TPU v7x, 512 devices: a whole 4x8x8 slice. The times are simulated.
512 devices in a mesh: wide: 64 (over z, x, y_hi), narrow: 8 (over y_lo, core).
Axes of the slice: x: 4, y: 8 (y_hi: 2, y_lo: 4; y = y_hi * 4 + y_lo), z: 8, core: 2. Of those that a mesh axis runs over, the one named last changes fastest.
Arguments:
- qkv: float32 [3, 2, 4096, 5120], P(None, None, 'wide', 'narrow'), may hold values from -30 to 30
- eta: float32 [8, 4096], P('narrow', 'wide'), may hold values from 0.01 to 0.1
- fast_weights: float32 [8, 640, 3, 384], P('narrow', 'wide'), may hold values from -0.25 to 0.25
- momentum: float32 [8, 640, 3, 384], P('narrow', 'wide'), may hold values from -50 to 50
- ttt_gain: float32 [5120], P('narrow'), may hold values from 0.5 to 1.5
Outputs:
- mixed: float32 [2, 4096, 5120], P(None, 'wide', 'narrow')
- new_weights: float32 [8, 640, 3, 384], P('narrow', 'wide')
- new_momentum: float32 [8, 640, 3, 384], P('narrow', 'wide')
All inputs are finite; a program needn't handle non-finite values.
Results may differ from a plain program's by a relative error of at most 0.0003.
Values sent between devices are 32-bit elements; how exact they have to be, the bound alone decides.
No kernel may reach another device: no remote copies, remote signals or barrier semaphores. Data moves between devices by JAX's collectives and lax.ppermute only.
A program may use at most 64 MiB of HBM per device.

v0:
```python
import math

import jax
import jax.numpy as jnp
import numpy as np
from jax import lax
from jax.sharding import PartitionSpec as P

D = 640
ATT = 128
WINDOW = 128


EPSILON = 1e-06
MOMENTUM_RATE = 0.9
STEP_SIZE = 0.03
PRECISION = lax.Precision.HIGHEST


def from_behind(block, axis, distance):
    devices = range(lax.axis_size(axis))
    route = [((i - distance) % len(devices), i) for i in devices]
    return lax.ppermute(block, axis, route)


def sent_together(arrays, axis, dim, along):
    both = jnp.concatenate(arrays, axis=along)
    whole, at, gathered = (lax.all_gather(both, axis, axis=dim, tiled=True), 0, [])
    for a in arrays:
        gathered.append(lax.slice_in_dim(whole, at, at + a.shape[along], axis=along))
        at += a.shape[along]
    return tuple(gathered)


def filled_up(lines, count):
    spare = -lines.shape[0] % count
    if not spare:
        return lines
    return jnp.concatenate([lines, jnp.zeros((spare, *lines.shape[1:]), lines.dtype)])


def total_of(shard, axis):
    lines = shard.reshape(-1, *shard.shape[1:][-1:])
    own = lax.psum_scatter(
        filled_up(lines, lax.axis_size(axis)), axis, scatter_dimension=0, tiled=True
    )
    whole = lax.all_gather(own, axis).reshape(-1, *lines.shape[1:])
    return lax.slice_in_dim(whole, 0, len(lines)).reshape(shard.shape)


def copy_for_each(shard, axis):
    copies = jnp.broadcast_to(shard, (lax.axis_size(axis), *shard.shape))
    return lax.all_to_all(copies, axis, split_axis=0, concat_axis=0, tiled=True)


def of_everyone(shard, axis):
    return copy_for_each(shard, axis).sum(axis=0)


def product(left, right):
    return jnp.dot(left, right, precision=PRECISION, preferred_element_type=jnp.float32)


def memory_read(inputs, weights):
    gate_pre = product(inputs, weights[:, 0, :])
    up_pre = product(inputs, weights[:, 1, :])
    hidden = jax.nn.silu(gate_pre) * up_pre
    return product(hidden, weights[:, 2, :].T)


def memory_gradient(key_rows, value_rows, rates, weights):
    gate_pre = product(key_rows, weights[:, 0, :])
    up_pre = product(key_rows, weights[:, 1, :])
    sigmoid = jax.nn.sigmoid(gate_pre)
    gated = gate_pre * sigmoid
    hidden = gated * up_pre
    weighted = rates[:, None] * value_rows
    back = -product(weighted, weights[:, 2, :])
    gate_back = back * up_pre * sigmoid * (1.0 + gate_pre * (1.0 - sigmoid))
    up_back = back * gated
    return (weighted, hidden, gate_back, up_back)


def renormalize(weights, moment):
    spread = jnp.sqrt(jnp.mean(moment * moment, axis=0) + EPSILON)
    moved = weights - STEP_SIZE * moment / spread
    ratio = jnp.sqrt(jnp.mean(weights * weights, axis=0) + EPSILON) / jnp.sqrt(
        jnp.mean(moved * moved, axis=0) + EPSILON
    )
    return moved * ratio


def window_attention(query_rows, key_rows, value_rows):
    groups, tok_rows, columns = query_rows.shape
    head_count = columns // ATT
    position = lax.axis_index("wide")
    reach = (WINDOW + tok_rows - 2) // tok_rows
    later_groups = jnp.arange(groups) >= 1
    key_parts, value_parts, offsets, live_parts = ([], [], [], [])
    for back in range(reach, 0, -1):
        keep = min(tok_rows, WINDOW - 1 - (back - 1) * tok_rows)
        got_keys, got_values = from_behind(
            (key_rows[:, tok_rows - keep :], value_rows[:, tok_rows - keep :]), "wide", back
        )
        same_group = position >= back
        key_parts.append(jnp.where(same_group, got_keys, jnp.roll(got_keys, 1, axis=0)))
        value_parts.append(jnp.where(same_group, got_values, jnp.roll(got_values, 1, axis=0)))
        offsets.append(np.arange(keep) + tok_rows - keep - back * tok_rows)
        live_parts.append(
            jnp.broadcast_to(jnp.logical_or(same_group, later_groups)[:, None], (groups, keep))
        )
    key_parts.append(key_rows)
    value_parts.append(value_rows)
    offsets.append(np.arange(tok_rows))
    live_parts.append(jnp.ones((groups, tok_rows), bool))
    near_keys = jnp.concatenate(key_parts, axis=1)
    near_values = jnp.concatenate(value_parts, axis=1)
    live = jnp.concatenate(live_parts, axis=1)
    offset = np.concatenate(offsets)
    distance = np.arange(tok_rows)[:, None] - offset[None, :]
    window_mask = jnp.asarray((distance >= 0) & (distance < WINDOW))
    allowed = live[:, None, None, :] & window_mask[None, None]
    span = near_keys.shape[1]
    queries4 = query_rows.reshape(groups, tok_rows, head_count, ATT)
    keys4 = near_keys.reshape(groups, span, head_count, ATT)
    values4 = near_values.reshape(groups, span, head_count, ATT)
    scores = jnp.einsum("cqhe,ckhe->chqk", queries4, keys4, precision=PRECISION) / math.sqrt(ATT)
    scores = jnp.where(allowed, scores, -1e30)
    highest = jnp.max(scores, axis=-1, keepdims=True)
    weights = jnp.exp(scores - highest)
    weights = weights / jnp.sum(weights, axis=-1, keepdims=True)
    output = jnp.einsum("chqk,ckhe->cqhe", weights, values4, precision=PRECISION)
    return output.reshape(groups, tok_rows, columns)


def local(qkv, eta, fast_weights, momentum, ttt_gain):
    query_rows, key_rows, value_rows = (qkv[0], qkv[1], qkv[2])
    attended = window_attention(query_rows, key_rows, value_rows)
    position = lax.axis_index("wide")
    readouts, updated_list, moment_list = ([], [], [])
    own_weights = fast_weights[0]
    own_moment = momentum[0]
    shard_rows = own_weights.shape[0]
    weights, moment_all = sent_together((own_weights, own_moment), "wide", 0, 1)
    first_keys = key_rows[0, :, 0:D]
    first_values = value_rows[0, :, 0:D]
    first_read = memory_read(query_rows[0, :, 0:D], weights)
    weighted, hidden, gate_back, up_back = memory_gradient(
        first_keys, first_values, eta[0], weights
    )
    total = total_of(
        jnp.stack(
            [
                product(first_keys.T, gate_back),
                product(first_keys.T, up_back),
                -product(weighted.T, hidden),
            ],
            axis=1,
        ),
        "wide",
    )
    moment_all = MOMENTUM_RATE * moment_all + total
    updated = renormalize(weights, moment_all)
    new_own = lax.dynamic_slice_in_dim(updated, position * shard_rows, shard_rows, 0)
    new_moment = lax.dynamic_slice_in_dim(moment_all, position * shard_rows, shard_rows, 0)
    second_read = memory_read(query_rows[1, :, 0:D], updated)
    readouts.append(jnp.stack([first_read, second_read]))
    updated_list.append(new_own)
    moment_list.append(new_moment)
    readout = readouts[0]
    squares = of_everyone(jnp.sum(readout * readout, axis=-1), "narrow")
    full_width = readout.shape[-1] * lax.axis_size("narrow")
    scale = jnp.sqrt(squares / full_width + EPSILON)
    mixed = attended + ttt_gain * (readout / scale[..., None])
    return (mixed, jnp.stack(updated_list), jnp.stack(moment_list))


def solution(mesh):
    return jax.shard_map(
        local,
        mesh=mesh,
        in_specs=(
            P(None, None, "wide", "narrow"),
            P("narrow", "wide"),
            P("narrow", "wide", None, None),
            P("narrow", "wide", None, None),
            P("narrow"),
        ),
        out_specs=(
            P(None, "wide", "narrow"),
            P("narrow", "wide", None, None),
            P("narrow", "wide", None, None),
        ),
        check_vma=False,
    )
```

profile of v0, /device:TPU:1, one launch (start us, length us, event | category | flops | bytes accessed | tf_op | source)
XLA Modules:
  0.0 715.4 jit_solution(17906317379520214605)
XLA Ops:
  8.9 191.2 %all-gather.5.cloned.1.call-done = f32[640,6,384]{2,1,0:T(8,128)} async-done(((f32[10,6,384]{2,1,0:T(8,128)}), f32[640,6,384]{2,1,0:T(8,128)}) %all-gather.5.cloned.1.call-update) | async-done | bytes 5898256 | tf_op jit(solution)/shard_map/all_gather | solution.py:28
  200.1 10.5 %fusion.82 = (f32[640,1,384]{2,1,0:T(1,128)S(1)}, f32[640,1,384]{2,1,0:T(1,128)S(1)}, f32[640,1,384]{2,1,0:T(1,128)S(1)}) fusion(f32[640,6,384]{2,1,0:T(8,128)} %all-gather.5.cloned.1.call-done), kind=kLoop, calls=%fused_computation.126 | loop fusion | bytes 5898240 | tf_op jit(solution)/shard_map/slice | solution.py:68
  216.1 3.7 copy.49
  219.8 4.3 reshape.79
  224.1 242.1 %fusion = f32[32,384]{1,0:T(8,128)S(1)} fusion(f32[1920,384]{1,0:T(8,128)S(1)} %reshape.79), kind=kCustom, calls=%all-reduce-scatter | all-reduce-scatter fusion | flops 786433 | bytes 3000320
  466.2 1.3 collective-permute-start.6
  467.5 1.3 collective-permute-start.5
  468.8 1.3 collective-permute-start.4
  470.1 1.3 collective-permute-start.7
  474.7 1.3 fusion.84
  476.0 5.4 collective-permute-start.3
  482.2 2.1 collective-permute-start.2
  484.3 6.0 collective-permute-start.1
  491.0 10.9 %collective-permute-start = (f32[2,63,640]{2,1,0:T(8,128)}, f32[2,63,640]{2,1,0:T(8,128)S(1)}, u32[]{:S(2)}, u32[]{:S(2)}) collective-permute-start(f32[2,63,640]{2,1,0:T(8,128)} %slice.118), channel_id=1, source_target_pairs={{496,0},{504,8},{0,16},{8,24},{16,32},{24,40},{32,48},{40,56},{48,... | collective-permute-start | bytes 967688 | tf_op jit(solution)/shard_map/ppermute | solution.py:23
  504.9 2.0 collective-permute-done
  507.4 3.4 fusion.89
  511.2 1.3 convolution_bitcast_fusion.2
  515.2 150.4 %all-gather.7.cloned.1.call-done = f32[64,30,384]{2,1,0:T(8,128)} async-done(((f32[1,30,384]{2,1,0:T(8,128)}), f32[64,30,384]{2,1,0:T(8,128)}) %all-gather.7.cloned.1.call-update) | async-done | bytes 2949136 | tf_op jit(solution)/shard_map/all_gather | solution.py:47
  665.6 5.7 reshape_reshape.3
  671.3 9.0 %multiply_reduce_fusion.2 = (f32[3,384]{1,0:T(4,128)S(1)}, f32[640,3,384]{2,1,0:T(4,128)S(1)}, f32[3,384]{1,0:T(4,128)S(1)}) fusion(f32[640,3,384]{2,1,0:T(4,128)} %reshape_reshape.3, f32[640,6,384]{2,1,0:T(8,128)} %all-gather.5.cloned.1.call-done), kind=kLoop, calls=%fused_computation.5 | loop fusion | flops 4421376 | bytes 11805696 | tf_op jit(solution)/shard_map/reduce_sum | solution.py:85
  680.3 4.3 multiply_reduce_fusion
  685.4 2.1 fusion.83
  690.9 10.7 %all-to-all-start = ((f32[8,1,128]{2,1,0:T(1,128)}), f32[8,1,128]{2,1,0:T(1,128)S(1)}, u32[]{:S(2)}, u32[]{:S(2)}) async-start(f32[8,1,128]{2,1,0:T(1,128)} %reshape.86), calls=%async_computation | async-start | bytes 8192 | tf_op jit(solution)/shard_map/all_to_all | solution.py:53
  703.8 2.7 all-to-all-done
  (100 shorter events, 26.0 us)
Async XLA Ops:
  7.2 203.5 %copy-start.7 = (f32[3,2,64,640]{3,2,1,0:T(8,128)S(1)}, f32[3,2,64,640]{3,2,1,0:T(8,128)}, u32[]{:S(2)}) copy-start(f32[3,2,64,640]{3,2,1,0:T(8,128)} %param.6) | copy-start | bytes 2949124
  7.2 192.9 %all-gather.5.cloned.1.call-start = ((), (), s32[]{:S(2)}) async-start(), calls=%async_computation.1 | async-start | bytes 7987200 | tf_op jit(solution)/shard_map/all_gather | solution.py:28
  8.9 203.3 %copy-start.12 = (f32[1,64]{1,0:T(1,128)S(1)}, f32[1,64]{1,0:T(1,128)}, u32[]{:S(2)}) copy-start(f32[1,64]{1,0:T(1,128)} %param.7) | copy-start | bytes 772
  8.9 656.7 %all-gather.7.cloned.1.call-start = ((), (), s32[]{:S(2)}) async-start(), calls=%async_computation.2 | async-start | bytes 3194880 | tf_op jit(solution)/shard_map/all_gather | solution.py:47
  210.6 5.3 copy-start.1
  210.6 5.3 copy-start.3
  210.6 5.3 copy-start.5
  224.1 278.1 %copy-start.10 = (pred[64,191]{1,0:T(32,128)(4,1)S(1)}, pred[64,191]{1,0:T(32,128)(4,1)}, u32[]{:S(2)}) copy-start(pred[64,191]{1,0:T(32,128)(4,1)} %constant.50.clone) | copy-start | bytes 36676
  466.2 7.2 collective-permute-start.6
  467.5 5.9 collective-permute-start.5
  468.8 4.6 collective-permute-start.4
  470.1 3.2 collective-permute-start.7
  476.0 31.3 %collective-permute-start.3 = (f32[2,64,640]{2,1,0:T(8,128)S(1)}, f32[2,64,640]{2,1,0:T(8,128)S(1)}, u32[]{:S(2)}, u32[]{:S(2)}) collective-permute-start(f32[2,64,640]{2,1,0:T(8,128)S(1)} %get-tuple-element.16), channel_id=1, source_target_pairs={{504,0},{0,8},{8,16},{16,24},{24,32},{32,40},{40,48},{48,56},{56,6... | collective-permute-start | bytes 983048 | tf_op jit(solution)/shard_map/ppermute | solution.py:23
  482.2 22.7 %collective-permute-start.2 = (f32[2,63,640]{2,1,0:T(8,128)}, f32[2,63,640]{2,1,0:T(8,128)S(1)}, u32[]{:S(2)}, u32[]{:S(2)}) collective-permute-start(f32[2,63,640]{2,1,0:T(8,128)} %slice.123), channel_id=1, source_target_pairs={{496,0},{504,8},{0,16},{8,24},{16,32},{24,40},{32,48},{40,56},{48,... | collective-permute-start | bytes 967688 | tf_op jit(solution)/shard_map/ppermute | solution.py:23
  484.3 26.8 %collective-permute-start.1 = (f32[2,64,640]{2,1,0:T(8,128)S(1)}, f32[2,64,640]{2,1,0:T(8,128)S(1)}, u32[]{:S(2)}, u32[]{:S(2)}) collective-permute-start(f32[2,64,640]{2,1,0:T(8,128)S(1)} %get-tuple-element.15), channel_id=1, source_target_pairs={{504,0},{0,8},{8,16},{16,24},{24,32},{32,40},{40,48},{48,56},{56,6... | collective-permute-start | bytes 983048 | tf_op jit(solution)/shard_map/ppermute | solution.py:23
  491.0 15.9 %collective-permute-start = (f32[2,63,640]{2,1,0:T(8,128)}, f32[2,63,640]{2,1,0:T(8,128)S(1)}, u32[]{:S(2)}, u32[]{:S(2)}) collective-permute-start(f32[2,63,640]{2,1,0:T(8,128)} %slice.118), channel_id=1, source_target_pairs={{496,0},{504,8},{0,16},{8,24},{16,32},{24,40},{32,48},{40,56},{48,... | collective-permute-start | bytes 967688 | tf_op jit(solution)/shard_map/ppermute | solution.py:23
  507.1 4.0 copy-start.9
  507.4 5.2 copy-start.6
  507.4 5.2 copy-start.8
  510.7 2.5 copy-start.4
  511.1 2.9 copy-start.2
  685.4 3.6 copy-start
  685.4 22.4 %copy-start.11 = (f32[640]{0:T(1024)S(1)}, f32[640]{0:T(1024)}, u32[]{:S(2)}) copy-start(f32[640]{0:T(1024)} %param.10) | copy-start | bytes 7684
  690.9 15.6 %all-to-all-start = ((f32[8,1,128]{2,1,0:T(1,128)}), f32[8,1,128]{2,1,0:T(1,128)S(1)}, u32[]{:S(2)}, u32[]{:S(2)}) async-start(f32[8,1,128]{2,1,0:T(1,128)} %reshape.86), calls=%async_computation | async-start | bytes 8192 | tf_op jit(solution)/shard_map/all_to_all | solution.py:53
Sparse Core Ops, SparseCore 0:
  13.1 186.8 all-gather.4
  474.8 190.7 all-gather.6
where the time goes:
time: 716 us; the launch traced here: 715 us
  waiting for transfers between devices  346 us (48%)
  blocking collectives  242 us (34%)
  starting transfers between devices  40.4 us (6%)
  local copies, waits for them, and re-layouts  39.2 us (5%)
  other arithmetic  17 us (2%)
  between operations  15.4 us (2%)
  matrix products  15.2 us (2%)
    unnamed x1, blocking collectives  242 us
    all_gather x1, waiting for transfers between devices, sent_together(): lax.all_gather(both, axis, axis=dim, tiled=True)  191 us
    all_gather x1, waiting for transfers between devices, total_of(): whole = lax.all_gather(own, axis).reshape(-1, *lines.shape[1:])  150 us
    ppermute x4, starting transfers between devices, from_behind(): return lax.ppermute(block, axis, route)  24.4 us
  transfers between devices with their start and end apart: 11, of which 4 were waited for; matrix products, arithmetic and copies ran while one was open for 2% of the time, Pallas kernels for 0%

commit v1 on v0

v1 whole, which is shorter than its diff:
```python
import functools
import math

import jax
import jax.numpy as jnp
from jax import lax
from jax.experimental import pallas as pl
from jax.experimental.pallas import tpu as pltpu
from jax.sharding import Mesh
from jax.sharding import PartitionSpec as P

ATT = 128
WINDOW = 128
EPSILON = 1e-06
MOMENTUM_RATE = 0.9
STEP_SIZE = 0.03
PRECISION = lax.Precision.HIGHEST

NZ, NX, NY = 8, 4, 2
BLOCKS = NZ * NX * NY
ROWS = 10
SLICE = 96
LANES = 128
TOK = 64
D = 640
H = 384
NARROW = 8
GROUPS = 2
VMEM_LIMIT = 24 * 1024 * 1024


def dot(left, right, dims=((1,), (0,))):
    return lax.dot_general(
        left, right, (dims, ((), ())), precision=PRECISION, preferred_element_type=jnp.float32
    )


def entry(group, sublane):
    q = group * 8 + sublane
    return (q // 3, q % 3) if q < 3 * ROWS else None


def call(body, outs, cost, *args, scratch=()):
    flops, nbytes = cost
    vmem = pl.BlockSpec(memory_space=pltpu.VMEM)
    return pl.pallas_call(
        body,
        out_shape=[jax.ShapeDtypeStruct(s, jnp.float32) for s in outs],
        in_specs=[pl.BlockSpec(memory_space=pltpu.SMEM) if a.dtype == jnp.int32 else vmem for a in args],
        out_specs=[vmem] * len(outs),
        scratch_shapes=[pltpu.VMEM(s, jnp.float32) for s in scratch],
        compiler_params=pltpu.CompilerParams(vmem_limit_bytes=VMEM_LIMIT),
        cost_estimate=pl.CostEstimate(flops=flops, bytes_accessed=nbytes, transcendentals=0),
    )(*args)


def to_column(row):
    n = row.shape[1]
    same = lax.broadcasted_iota(jnp.int32, (n, n), 0) == lax.broadcasted_iota(jnp.int32, (n, n), 1)
    return jnp.sum(jnp.where(same, row, 0.0), axis=1, keepdims=True)


def to_row(column):
    n = column.shape[0]
    same = lax.broadcasted_iota(jnp.int32, (n, n), 0) == lax.broadcasted_iota(jnp.int32, (n, n), 1)
    return jnp.sum(jnp.where(same, column, 0.0), axis=0, keepdims=True)


def own_packs(own_ref, flat_ref):
    flat_ref[24:32, :] = jnp.zeros((8, H), jnp.float32)
    for r in range(ROWS):
        flat_ref[3 * r : 3 * r + 3, :] = own_ref[r]
    return [
        jnp.concatenate(
            [flat_ref[8 * g : 8 * g + 8, SLICE * x : SLICE * (x + 1)] for g in range(4)], axis=1
        )
        for x in range(NX)
    ]


def prepare_body(fw_ref, mom_ref, eta_ref, key_ref, value_ref, send1_ref, sendx_ref, flat_ref):
    packs = own_packs(fw_ref, flat_ref)
    for z in range(NZ):
        for x in range(NX):
            for y in range(NY):
                for t in range(3):
                    send1_ref[(z * NX + x) * NY + y, 8 * t : 8 * t + 8, :] = packs[x][:, LANES * t : LANES * (t + 1)]
    keys = key_ref[...]
    weighted = to_column(eta_ref[...]) * value_ref[...]
    packs = own_packs(mom_ref, flat_ref)
    for x in range(NX):
        sendx_ref[x, 0:TOK, :] = keys
        sendx_ref[x, TOK : 2 * TOK, :] = weighted
        sendx_ref[x, 2 * TOK : 2 * TOK + 8, 0:H] = packs[x]
        sendx_ref[x, 2 * TOK : 2 * TOK + 8, H:D] = jnp.zeros((8, D - H), jnp.float32)


def widened(part):
    return jnp.concatenate([part, jnp.zeros((part.shape[0], LANES - SLICE), jnp.float32)], axis=1)


def unpack(recv_ref, out_refs, x_stride, y_stride, z_stride):
    for s in range(8):
        for x in range(NX):
            for y in range(NY):
                start = x * x_stride + y * y_stride + s
                rows = jnp.concatenate(
                    [recv_ref[pl.ds(start + 8 * t, NZ, stride=z_stride), :] for t in range(3)], axis=1
                )
                for g in range(4):
                    at = entry(g, s)
                    if at is None:
                        continue
                    r, i = at
                    out_refs[i][pl.ds((x * NY + y) * ROWS + r, NZ, stride=NX * NY * ROWS), :] = widened(
                        rows[:, SLICE * g : SLICE * (g + 1)]
                    )


def pack(in_refs, send_ref, x_stride, y_stride, z_stride):
    for s in range(8):
        for x in range(NX):
            for y in range(NY):
                parts = []
                for g in range(4):
                    at = entry(g, s)
                    if at is None:
                        parts.append(jnp.zeros((NZ, SLICE), jnp.float32))
                        continue
                    r, i = at
                    parts.append(in_refs[i][pl.ds((x * NY + y) * ROWS + r, NZ, stride=NX * NY * ROWS), :][:, :SLICE])
                rows = jnp.concatenate(parts, axis=1)
                start = x * x_stride + y * y_stride + s
                for t in range(3):
                    send_ref[pl.ds(start + 8 * t, NZ, stride=z_stride), :] = rows[:, LANES * t : LANES * (t + 1)]


def token_rows(ref, start):
    return jnp.concatenate([ref[x, start : start + TOK, :] for x in range(NX)], axis=0)


def gradient_body(recv1_ref, recvx_ref, w1_ref, w3_ref, w2_ref, send_ref, g1_ref, g3_ref, g2_ref):
    unpack(recv1_ref, (w1_ref, w3_ref, w2_ref), 48, 24, 192)
    keys = token_rows(recvx_ref, 0)
    weighted = token_rows(recvx_ref, TOK)
    pre = dot(keys, jnp.concatenate([w1_ref[...], w3_ref[...]], axis=1))
    gate_pre, up_pre = pre[:, :LANES], pre[:, LANES:]
    back = -dot(weighted, w2_ref[...])
    sigmoid = jax.nn.sigmoid(gate_pre)
    gated = gate_pre * sigmoid
    hidden = gated * up_pre
    gate_back = back * up_pre * sigmoid * (1.0 + gate_pre * (1.0 - sigmoid))
    up_back = back * gated
    both = dot(keys, jnp.concatenate([gate_back, up_back], axis=1), ((0,), (0,)))
    g1_ref[...] = both[:, :LANES]
    g3_ref[...] = both[:, LANES:]
    g2_ref[...] = -dot(weighted, hidden, ((0,), (0,)))
    pack((g1_ref, g3_ref, g2_ref), send_ref, 24, 96, 192)


def moment_body(recv2_ref, recvx_ref, send3_ref, own_ref):
    total = recv2_ref[0]
    for j in range(1, NZ * NY):
        total = total + recv2_ref[j]
    old = jnp.concatenate(
        [
            recvx_ref[x, 2 * TOK : 2 * TOK + 8, LANES * t : LANES * (t + 1)]
            for x in range(NX)
            for t in range(3)
        ],
        axis=0,
    )
    moment = MOMENTUM_RATE * old + total
    own_ref[...] = moment
    for j in range(NZ * NY):
        send3_ref[j] = moment


def hidden_of(inputs, w1, w3):
    pre = dot(inputs, jnp.concatenate([w1, w3], axis=1))
    gate_pre, up_pre = pre[:, :LANES], pre[:, LANES:]
    return gate_pre * jax.nn.sigmoid(gate_pre) * up_pre


def first_read_body(recvq_ref, w1_ref, w3_ref, w2_ref, moment_ref, send_ref):
    hidden = hidden_of(token_rows(recvq_ref, 0), w1_ref[...], w3_ref[...])
    partial = dot(hidden, w2_ref[...], ((1,), (1,)))
    for x in range(NX):
        send_ref[x, 0:TOK, :] = partial[x * TOK : (x + 1) * TOK]
        for t in range(3):
            send_ref[x, TOK : TOK + 8, LANES * t : LANES * (t + 1)] = moment_ref[24 * x + 8 * t : 24 * x + 8 * t + 8, :]
        send_ref[x, TOK : TOK + 8, H:D] = jnp.zeros((8, D - H), jnp.float32)


def renormalized(weights, moment):
    rate = STEP_SIZE / jnp.sqrt(jnp.mean(moment * moment, axis=0, keepdims=True) + EPSILON)
    moved = weights - moment * rate
    ratio = jnp.sqrt(jnp.mean(weights * weights, axis=0, keepdims=True) + EPSILON) / jnp.sqrt(
        jnp.mean(moved * moved, axis=0, keepdims=True) + EPSILON
    )
    return moved * ratio, rate, ratio


def second_read_body(recv3_ref, recvq_ref, w1_ref, w3_ref, w2_ref, send_ref, m1_ref, m3_ref, m2_ref):
    unpack(recv3_ref, (m1_ref, m3_ref, m2_ref), 24, 96, 192)
    new1, rate1, ratio1 = renormalized(w1_ref[...], m1_ref[...])
    new3, rate3, ratio3 = renormalized(w3_ref[...], m3_ref[...])
    new2, rate2, ratio2 = renormalized(w2_ref[...], m2_ref[...])
    hidden = hidden_of(token_rows(recvq_ref, TOK), new1, new3)
    partial = dot(hidden, new2, ((1,), (1,)))
    stats = [rate1, rate3, rate2, ratio1, ratio3, ratio2, jnp.zeros((2, LANES), jnp.float32)]
    stats = jnp.concatenate(stats, axis=0)
    for x in range(NX):
        send_ref[x, 0:TOK, :] = partial[x * TOK : (x + 1) * TOK]
        send_ref[x, TOK : TOK + 8, 0:LANES] = stats
        send_ref[x, TOK : TOK + 8, LANES:D] = jnp.zeros((8, D - LANES), jnp.float32)


def squares_body(first_ref, second_ref, readout_ref, send_ref):
    rows = []
    for c, ref in enumerate((first_ref, second_ref)):
        total = ref[0, 0:TOK, :]
        for x in range(1, NX):
            total = total + ref[x, 0:TOK, :]
        readout_ref[c] = total
        rows.append(to_row(jnp.sum(total * total, axis=1, keepdims=True)))
    row = jnp.concatenate(rows, axis=1)
    for n in range(NARROW):
        send_ref[n] = jnp.broadcast_to(row, (8, GROUPS * TOK))


def own_rows_body(first_ref, second_ref, fw_ref, new_w_ref, new_m_ref, flat_ref):
    for g in range(4):
        flat_ref[8 * g : 8 * g + 8, :] = jnp.concatenate(
            [first_ref[x, TOK : TOK + 8, SLICE * g : SLICE * (g + 1)] for x in range(NX)], axis=1
        )
    stats = jnp.concatenate([second_ref[x, TOK : TOK + 8, 0:SLICE] for x in range(NX)], axis=1)
    for r in range(ROWS):
        moment = flat_ref[3 * r : 3 * r + 3, :]
        new_m_ref[r] = moment
        new_w_ref[r] = (fw_ref[r] - moment * stats[0:3]) * stats[3:6]


def mix_body(recv_ref, readout_ref, attended_ref, gain_ref, mixed_ref):
    total = recv_ref[0, 0:1, :]
    for n in range(1, NARROW):
        total = total + recv_ref[n, 0:1, :]
    scale = to_column(1.0 / jnp.sqrt(total / (D * NARROW) + EPSILON))
    for c in range(GROUPS):
        mixed_ref[c] = attended_ref[c] + gain_ref[...] * (readout_ref[c] * scale[c * TOK : (c + 1) * TOK])


def attention_body(position_ref, q_ref, k_ref, v_ref, near_ref, far_ref, out_ref):
    position = position_ref[0]
    row = lax.broadcasted_iota(jnp.int32, (TOK, 3 * TOK), 0) + 2 * TOK
    col = lax.broadcasted_iota(jnp.int32, (TOK, 3 * TOK), 1)
    window = (row - col >= 0) & (row - col < WINDOW)
    for c in range(GROUPS):
        if c == 0:
            first = jnp.where(position >= 2, 0, jnp.where(position >= 1, TOK, 2 * TOK))
            allowed = window & (col >= first)
        else:
            allowed = window
        for h in range(D // ATT):
            at = slice(h * ATT, (h + 1) * ATT)
            parts = []
            for a in range(2):
                own = (k_ref, v_ref)[a]
                if c == 0:
                    far, near = far_ref[a, 0, :, at], near_ref[a, 0, :, at]
                else:
                    far = jnp.where(position >= 2, far_ref[a, 1, :, at], far_ref[a, 0, :, at])
                    near = jnp.where(position >= 1, near_ref[a, 1, :, at], near_ref[a, 0, :, at])
                parts.append(jnp.concatenate([far, near, own[c, :, at]], axis=0))
            keys, values = parts
            scores = dot(q_ref[c, :, at], keys, ((1,), (1,))) * (1.0 / math.sqrt(ATT))
            scores = jnp.where(allowed, scores, -1e30)
            weights = jnp.exp(scores - jnp.max(scores, axis=1, keepdims=True))
            weights = weights / jnp.sum(weights, axis=1, keepdims=True)
            out_ref[c, :, at] = dot(weights, values)


def behind(block, distance):
    axes = ("z", "x", "yh")
    return lax.ppermute(block, axes, [((i - distance) % BLOCKS, i) for i in range(BLOCKS)])


def exchange(pieces, axes):
    return lax.all_to_all(pieces, axes, split_axis=0, concat_axis=0, tiled=True)


def local(qkv, eta, fast_weights, momentum, ttt_gain):
    queries = qkv[0]
    own_weights, own_moment = fast_weights[0], momentum[0]
    position = (lax.axis_index("z") * NX + lax.axis_index("x")) * NY + lax.axis_index("yh")
    send1, sendx = call(
        prepare_body, [(BLOCKS, 24, LANES), (NX, 2 * TOK + 8, D)], (10**6, 3 * 10**6),
        own_weights, own_moment, eta, qkv[1, 0], qkv[2, 0], scratch=[(32, H)],
    )
    recvx = exchange(sendx, "x")
    recv1 = exchange(send1, ("z", "x", "yh"))
    near = behind(qkv[1:], 1)
    far = behind(qkv[1:], 2)
    w1, w3, w2, send2 = call(
        gradient_body, [(D, LANES)] * 3 + [(BLOCKS * 24, LANES)], (3 * 10**9, 4 * 10**6),
        recv1.reshape(BLOCKS * 24, LANES), recvx, scratch=[(D, LANES)] * 3,
    )
    recv2 = exchange(send2.reshape(NZ * NY, NX * 24, LANES), ("z", "yh"))
    recvq = exchange(jnp.broadcast_to(queries.reshape(1, 2 * TOK, D), (NX, 2 * TOK, D)), "x")
    (attended,) = call(
        attention_body, [(GROUPS, TOK, D)], (3 * 10**9, 4 * 10**6),
        jnp.reshape(position, (1,)).astype(jnp.int32), queries, qkv[1], qkv[2], near, far,
    )
    send3, moment = call(moment_body, [(NZ * NY, NX * 24, LANES), (NX * 24, LANES)], (10**6, 2 * 10**6), recv2, recvx)
    recv3 = exchange(send3, ("z", "yh"))
    (send_first,) = call(first_read_body, [(NX, TOK + 8, D)], (10**9, 3 * 10**6), recvq, w1, w3, w2, moment)
    first = exchange(send_first, "x")
    (send_second,) = call(
        second_read_body, [(NX, TOK + 8, D)], (10**9, 3 * 10**6),
        recv3.reshape(BLOCKS * 24, LANES), recvq, w1, w3, w2, scratch=[(D, LANES)] * 3,
    )
    second = exchange(send_second, "x")
    readout, send5 = call(
        squares_body, [(GROUPS, TOK, D), (NARROW, 8, GROUPS * TOK)], (10**6, 2 * 10**6), first, second
    )
    recv5 = exchange(send5, "narrow")
    new_weights, new_moment = call(
        own_rows_body, [(ROWS, 3, H), (ROWS, 3, H)], (10**6, 10**6), first, second, own_weights, scratch=[(32, H)]
    )
    (mixed,) = call(
        mix_body, [(GROUPS, TOK, D)], (10**6, 10**6), recv5, readout, attended, ttt_gain.reshape(1, D)
    )
    return mixed, new_weights[None], new_moment[None]


def solution(mesh):
    fine = Mesh(mesh.devices.reshape(NZ, NX, NY, NARROW), ("z", "x", "yh", "narrow"))
    wide = ("z", "x", "yh")
    return jax.shard_map(
        local,
        mesh=fine,
        in_specs=(
            P(None, None, wide, "narrow"),
            P("narrow", wide),
            P("narrow", wide, None, None),
            P("narrow", wide, None, None),
            P("narrow"),
        ),
        out_specs=(
            P(None, wide, "narrow"),
            P("narrow", wide, None, None),
            P("narrow", wide, None, None),
        ),
        check_vma=False,
    )
```

time: 716 us -> 234 us (0.33)
  waiting for transfers between devices: 346 us -> 77.5 us
  blocking collectives: 242 us -> 59.1 us
  local copies, waits for them, and re-layouts: 39.2 us -> 14.3 us
  Pallas kernels: 0 us -> 21.4 us
  starting transfers between devices: 40.4 us -> 59.7 us
  other arithmetic: 17 us -> 0 us
  matrix products: 15.2 us -> 0 us
  between operations: 15.4 us -> 0.89 us
    all_gather x2 -> x0, waiting for transfers between devices: 342 us -> none  [the longest x1 191 us: sent_together(): lax.all_gather(both, axis, axis=dim, tiled=True)]
    unnamed x1 -> x0, blocking collectives: 242 us -> none
    all_to_all x1 -> x6, waiting for transfers between devices: 2.67 us -> 77.5 us  [exchange(): return lax.all_to_all(pieces, axes, split_axis=0, concat_axis=0, tiled=True)]
    all_to_all x0 -> x2, blocking collectives: none -> 59.1 us  [exchange(): return lax.all_to_all(pieces, axes, split_axis=0, concat_axis=0, tiled=True)]
    all_to_all x1 -> x6, starting transfers between devices: 10.7 us -> 47.3 us  [exchange(): return lax.all_to_all(pieces, axes, split_axis=0, concat_axis=0, tiled=True)]
    pallas_call x0 -> x9, Pallas kernels: none -> 21.4 us  [call(): pl.pallas_call(body, out_shape=[jax.ShapeDtypeStruct(s, jnp.float32) for...]
    dot_general x14 -> x0, matrix products: 15.2 us -> none  [the longest x12 10.5 us: product(): jnp.dot(left, right, precision=PRECISION, preferred_element_type=jnp.floa...]
    reduce_sum x5 -> x0, other arithmetic: 13.7 us -> none  [the longest x1 8.97 us: renormalize(): spread = jnp.sqrt(jnp.mean(moment * moment, axis=0) + EPSILON)]
  transfers between devices with their start and end apart: 11 -> 8, of which waited for: 4 -> 4; matrix products, arithmetic and copies ran while one was open for 2% -> 2% of each run, Pallas kernels for 0% -> 7%
where the time goes in v1:
time: 234 us; the launch traced here: 233 us
  waiting for transfers between devices  77.5 us (33%)
  starting transfers between devices  59.7 us (26%)
  blocking collectives  59.1 us (25%)
  Pallas kernels  21.4 us (9%)
  local copies, waits for them, and re-layouts  14.3 us (6%)
    all_to_all x6, waiting for transfers between devices, exchange(): return lax.all_to_all(pieces, axes, split_axis=0, concat_axis=0, tiled=True)  77.5 us
    all_to_all x2, blocking collectives, exchange(): return lax.all_to_all(pieces, axes, split_axis=0, concat_axis=0, tiled=True)  59.1 us
    all_to_all x6, starting transfers between devices, exchange(): return lax.all_to_all(pieces, axes, split_axis=0, concat_axis=0, tiled=True)  47.3 us
    pallas_call x9, Pallas kernels, call(): pl.pallas_call(body, out_shape=[jax.ShapeDtypeStruct(s, jnp.float32) for...  21.4 us
    ppermute x2, starting transfers between devices, behind(): lax.ppermute(block, axes, [((i - distance) % BLOCKS, i) for i in range(BL...  12.4 us
    unnamed x40, local copies, waits for them, and re-layouts  9.13 us
  transfers between devices with their start and end apart: 8, of which 4 were waited for; matrix products, arithmetic and copies ran while one was open for 2% of the time, Pallas kernels for 7%

profile of v1, /device:TPU:1, one launch (start us, length us, event | category | flops | bytes accessed | tf_op | source)
XLA Modules:
  0.0 232.9 jit_solution(14038927202833968424)
XLA Ops:
  0.6 1.0 slice_bitcast_fusion.2
  4.1 18.5 %all_to_all.40.recvx_ref = f32[4,136,640]{2,1,0:T(8,128)S(1)} all-to-all(f32[4,136,640]{2,1,0:T(8,128)S(1)} %get-tuple-element.16), channel_id=1, replica_groups=mesh['z'=8,'x'=4,'yh'=2,'narrow'=8] {'x'}, dimensions={0} | all-to-all | bytes 2785280 | tf_op jit(solution)/shard_map/all_to_all | solution.py:289
  22.6 40.6 %all_to_all.41 = f32[64,24,128]{2,1,0:T(8,128)S(1)} all-to-all(f32[64,24,128]{2,1,0:T(8,128)S(1)} %get-tuple-element.15), channel_id=1, replica_groups=mesh['z'=8,'x'=4,'yh'=2,'narrow'=8] {'z','x','yh'}, dimensions={0} | all-to-all | bytes 1572864 | tf_op jit(solution)/shard_map/all_to_all | solution.py:289
  63.2 5.0 %shard_map.77 = (f32[640,128]{1,0:T(8,128)S(1)}, f32[640,128]{1,0:T(8,128)S(1)}, f32[640,128]{1,0:T(8,128)S(1)}, f32[1536,128]{1,0:T(8,128)}) custom-call(f32[1536,128]{1,0:T(8,128)S(1)} %bitcast.24, f32[4,136,640]{2,1,0:T(8,128)S(1)} %all_to_all.40.recvx_ref), custom_call_target="tpu_custom_call" | custom-call | flops 3000000000 | bytes 4000000 | tf_op jit(solution)/shard_map/pallas_call | solution.py:46
  70.4 11.1 %all-to-all-start.3 = ((f32[16,96,128]{2,1,0:T(8,128)}), f32[16,96,128]{2,1,0:T(8,128)S(1)}, u32[]{:S(2)}, u32[]{:S(2)}) async-start(f32[16,96,128]{2,1,0:T(8,128)} %bitcast.4), calls=%async_computation.3 | async-start | bytes 1572864 | tf_op jit(solution)/shard_map/all_to_all | solution.py:289
  81.5 1.0 slice_bitcast_fusion
  82.5 17.0 %all-to-all-done.3.recv2_ref = f32[16,96,128]{2,1,0:T(8,128)S(1)} async-done(((f32[16,96,128]{2,1,0:T(8,128)}), f32[16,96,128]{2,1,0:T(8,128)S(1)}, u32[]{:S(2)}, u32[]{:S(2)}) %all-to-all-start.3) | async-done | bytes 786464 | tf_op jit(solution)/shard_map/all_to_all | solution.py:289
  99.5 1.2 broadcast_in_dim.14
  100.6 3.5 %all-to-all-start = ((f32[4,128,640]{2,1,0:T(8,128)}), f32[4,128,640]{2,1,0:T(8,128)S(1)}, u32[]{:S(2)}, u32[]{:S(2)}) async-start(f32[4,128,640]{2,1,0:T(8,128)} %broadcast_in_dim.14), calls=%async_computation | async-start | bytes 2621440 | tf_op jit(solution)/shard_map/all_to_all | solution.py:289
  104.3 0.9 copy-done.1
  105.8 10.9 %all-to-all-done.recvq_ref = f32[4,128,640]{2,1,0:T(8,128)S(1)} async-done(((f32[4,128,640]{2,1,0:T(8,128)}), f32[4,128,640]{2,1,0:T(8,128)S(1)}, u32[]{:S(2)}, u32[]{:S(2)}) %all-to-all-start) | async-done | bytes 1310752 | tf_op jit(solution)/shard_map/all_to_all | solution.py:289
  116.7 17.1 %all-to-all-start.5 = ((f32[16,96,128]{2,1,0:T(8,128)}), f32[16,96,128]{2,1,0:T(8,128)S(1)}, u32[]{:S(2)}, u32[]{:S(2)}) async-start(f32[16,96,128]{2,1,0:T(8,128)} %copy-done.1), calls=%async_computation.5 | async-start | bytes 1572864 | tf_op jit(solution)/shard_map/all_to_all | solution.py:289
  133.8 2.4 %shard_map.79 = f32[4,72,640]{2,1,0:T(8,128)S(1)} custom-call(f32[4,128,640]{2,1,0:T(8,128)S(1)} %all-to-all-done.recvq_ref, f32[640,128]{1,0:T(8,128)S(1)} %copy-done.7, f32[640,128]{1,0:T(8,128)S(1)} %copy-done.9, f32[640,128]{1,0:T(8,128)S(1)} %copy-done.11, f32[96,128]{1,0:T(8,128)S(1)} %copy-done.15), custom_call_target="tpu_custom_call" | custom-call | flops 1000000000 | bytes 3000000 | tf_op jit(solution)/shard_map/pallas_call | solution.py:46
  137.1 20.2 %all-to-all-done.5 = f32[16,96,128]{2,1,0:T(8,128)S(1)} async-done(((f32[16,96,128]{2,1,0:T(8,128)}), f32[16,96,128]{2,1,0:T(8,128)S(1)}, u32[]{:S(2)}, u32[]{:S(2)}) %all-to-all-start.5) | async-done | bytes 786464 | tf_op jit(solution)/shard_map/all_to_all | solution.py:289
  157.2 3.5 %all-to-all-start.4 = ((f32[4,72,640]{2,1,0:T(8,128)}), f32[4,72,640]{2,1,0:T(8,128)S(1)}, u32[]{:S(2)}, u32[]{:S(2)}) async-start(f32[4,72,640]{2,1,0:T(8,128)} %copy-done.2), calls=%async_computation.4 | async-start | bytes 1474560 | tf_op jit(solution)/shard_map/all_to_all | solution.py:289
  160.7 2.0 slice.24
  162.8 9.1 %collective-permute-start = (f32[2,2,64,640]{3,2,1,0:T(8,128)}, f32[2,2,64,640]{3,2,1,0:T(8,128)}, u32[]{:S(2)}, u32[]{:S(2)}) collective-permute-start(f32[2,2,64,640]{3,2,1,0:T(8,128)} %slice.24), channel_id=1, source_target_pairs={{504,0},{0,8},{8,16},{16,24},{24,32},{32,40},{40,48},{48,56},{56,6... | collective-permute-start | bytes 1966088 | tf_op jit(solution)/shard_map/ppermute | solution.py:285
  171.9 3.3 %collective-permute-start.1 = (f32[2,2,64,640]{3,2,1,0:T(8,128)}, f32[2,2,64,640]{3,2,1,0:T(8,128)}, u32[]{:S(2)}, u32[]{:S(2)}) collective-permute-start(f32[2,2,64,640]{3,2,1,0:T(8,128)} %slice.24), channel_id=1, source_target_pairs={{496,0},{504,8},{0,16},{8,24},{16,32},{24,40},{32,48},{40,56},{48,... | collective-permute-start | bytes 1966088 | tf_op jit(solution)/shard_map/ppermute | solution.py:285
  175.2 3.4 %shard_map.80 = f32[4,72,640]{2,1,0:T(8,128)S(1)} custom-call(f32[1536,128]{1,0:T(8,128)S(1)} %bitcast.23, f32[4,128,640]{2,1,0:T(8,128)S(1)} %all-to-all-done.recvq_ref, f32[640,128]{1,0:T(8,128)S(1)} %copy-done.7, f32[640,128]{1,0:T(8,128)S(1)} %copy-done.9, f32[640,128]{1,0:T(8,128)S(1)} %copy-done.12), custom_call_target="tpu_custom_call" | custom-call | flops 1000000000 | bytes 3000000 | tf_op jit(solution)/shard_map/pallas_call | solution.py:46
  178.6 0.9 copy-done
  179.5 6.8 %all-to-all-start.6 = ((f32[4,72,640]{2,1,0:T(8,128)}), f32[4,72,640]{2,1,0:T(8,128)S(1)}, u32[]{:S(2)}, u32[]{:S(2)}) async-start(f32[4,72,640]{2,1,0:T(8,128)} %copy-done), calls=%async_computation.6 | async-start | bytes 1474560 | tf_op jit(solution)/shard_map/all_to_all | solution.py:289
  186.4 29.4 %all-to-all-done.6.second_ref = f32[4,72,640]{2,1,0:T(8,128)S(1)} async-done(((f32[4,72,640]{2,1,0:T(8,128)}), f32[4,72,640]{2,1,0:T(8,128)S(1)}, u32[]{:S(2)}, u32[]{:S(2)}) %all-to-all-start.6) | async-done | bytes 737312 | tf_op jit(solution)/shard_map/all_to_all | solution.py:289
  216.6 5.3 %all-to-all-start.7 = ((f32[8,8,128]{2,1,0:T(8,128)}), f32[8,8,128]{2,1,0:T(8,128)S(1)}, u32[]{:S(2)}, u32[]{:S(2)}) async-start(f32[8,8,128]{2,1,0:T(8,128)} %get-tuple-element.23), calls=%async_computation.7 | async-start | bytes 65536 | tf_op jit(solution)/shard_map/all_to_all | solution.py:289
  221.9 8.6 %shard_map.82.attended_ref = f32[2,64,640]{2,1,0:T(8,128)S(1)} custom-call(s32[1]{0:T(128)} %bitcast.6.position_ref, f32[2,64,640]{2,1,0:T(8,128)S(1)} %copy-done.4, f32[2,64,640]{2,1,0:T(8,128)S(1)} %copy-done.5, f32[2,64,640]{2,1,0:T(8,128)S(1)} %copy-done.3, f32[2,2,64,640]{3,2,1,0:T(8,128)} %collective-permute-done.near_ref, ...), custom_call_target="tpu_custom_call" | custom-call | flops 3000000000 | bytes 4000000 | tf_op jit(solution)/shard_map/pallas_call | solution.py:46
  (48 shorter events, 9.4 us)
Async XLA Ops:
  68.2 0.7 copy-start.6
  69.0 0.7 copy-start.8
  69.7 0.7 copy-start.10
  70.4 11.1 %copy-start.16 = (f32[3,2,64,640]{3,2,1,0:T(8,128)S(1)}, f32[3,2,64,640]{3,2,1,0:T(8,128)}, u32[]{:S(2)}) copy-start(f32[3,2,64,640]{3,2,1,0:T(8,128)} %param.5) | copy-start | bytes 2949124
  70.4 29.0 %all-to-all-start.3 = ((f32[16,96,128]{2,1,0:T(8,128)}), f32[16,96,128]{2,1,0:T(8,128)S(1)}, u32[]{:S(2)}, u32[]{:S(2)}) async-start(f32[16,96,128]{2,1,0:T(8,128)} %bitcast.4), calls=%async_computation.3 | async-start | bytes 1572864 | tf_op jit(solution)/shard_map/all_to_all | solution.py:289
  100.6 16.1 %all-to-all-start = ((f32[4,128,640]{2,1,0:T(8,128)}), f32[4,128,640]{2,1,0:T(8,128)S(1)}, u32[]{:S(2)}, u32[]{:S(2)}) async-start(f32[4,128,640]{2,1,0:T(8,128)} %broadcast_in_dim.14), calls=%async_computation | async-start | bytes 2621440 | tf_op jit(solution)/shard_map/all_to_all | solution.py:289
  104.3 0.9 copy-start.1
  105.8 28.0 %copy-start.7 = (f32[640,128]{1,0:T(8,128)S(1)}, f32[640,128]{1,0:T(8,128)}, u32[]{:S(2)}) copy-start(f32[640,128]{1,0:T(8,128)} %copy-done.6) | copy-start | bytes 983044
  105.8 28.0 %copy-start.9 = (f32[640,128]{1,0:T(8,128)S(1)}, f32[640,128]{1,0:T(8,128)}, u32[]{:S(2)}) copy-start(f32[640,128]{1,0:T(8,128)} %copy-done.8) | copy-start | bytes 983044
  105.8 28.0 %copy-start.11 = (f32[640,128]{1,0:T(8,128)S(1)}, f32[640,128]{1,0:T(8,128)}, u32[]{:S(2)}) copy-start(f32[640,128]{1,0:T(8,128)} %copy-done.10) | copy-start | bytes 983044
  116.7 17.1 %copy-start.15 = (f32[96,128]{1,0:T(8,128)S(1)}, f32[96,128]{1,0:T(8,128)}, u32[]{:S(2)}) copy-start(f32[96,128]{1,0:T(8,128)} %copy-done.14) | copy-start | bytes 147460
  116.7 40.5 %all-to-all-start.5 = ((f32[16,96,128]{2,1,0:T(8,128)}), f32[16,96,128]{2,1,0:T(8,128)S(1)}, u32[]{:S(2)}, u32[]{:S(2)}) async-start(f32[16,96,128]{2,1,0:T(8,128)} %copy-done.1), calls=%async_computation.5 | async-start | bytes 1572864 | tf_op jit(solution)/shard_map/all_to_all | solution.py:289
  136.2 0.9 copy-start.2
  157.2 22.3 %all-to-all-start.4 = ((f32[4,72,640]{2,1,0:T(8,128)}), f32[4,72,640]{2,1,0:T(8,128)S(1)}, u32[]{:S(2)}, u32[]{:S(2)}) async-start(f32[4,72,640]{2,1,0:T(8,128)} %copy-done.2), calls=%async_computation.4 | async-start | bytes 1474560 | tf_op jit(solution)/shard_map/all_to_all | solution.py:289
  160.7 14.5 %copy-start.12 = (f32[640,128]{1,0:T(8,128)S(1)}, f32[640,128]{1,0:T(8,128)}, u32[]{:S(2)}) copy-start(f32[640,128]{1,0:T(8,128)} %copy-done.10) | copy-start | bytes 983044
  162.8 59.1 %collective-permute-start = (f32[2,2,64,640]{3,2,1,0:T(8,128)}, f32[2,2,64,640]{3,2,1,0:T(8,128)}, u32[]{:S(2)}, u32[]{:S(2)}) collective-permute-start(f32[2,2,64,640]{3,2,1,0:T(8,128)} %slice.24), channel_id=1, source_target_pairs={{504,0},{0,8},{8,16},{16,24},{24,32},{32,40},{40,48},{48,56},{56,6... | collective-permute-start | bytes 1966088 | tf_op jit(solution)/shard_map/ppermute | solution.py:285
  171.9 50.0 %collective-permute-start.1 = (f32[2,2,64,640]{3,2,1,0:T(8,128)}, f32[2,2,64,640]{3,2,1,0:T(8,128)}, u32[]{:S(2)}, u32[]{:S(2)}) collective-permute-start(f32[2,2,64,640]{3,2,1,0:T(8,128)} %slice.24), channel_id=1, source_target_pairs={{496,0},{504,8},{0,16},{8,24},{16,32},{24,40},{32,48},{40,56},{48,... | collective-permute-start | bytes 1966088 | tf_op jit(solution)/shard_map/ppermute | solution.py:285
  178.6 0.9 copy-start
  179.5 6.8 %copy-start.17 = (f32[640]{0:T(1024)S(1)}, f32[640]{0:T(1024)}, u32[]{:S(2)}) copy-start(f32[640]{0:T(1024)} %param.9) | copy-start | bytes 7684
  179.5 42.4 %copy-start.3 = (f32[2,64,640]{2,1,0:T(8,128)S(1)}, f32[2,64,640]{2,1,0:T(8,128)}, u32[]{:S(2)}) copy-start(f32[2,64,640]{2,1,0:T(8,128)} %get-tuple-element.30.v_ref) | copy-start | bytes 983044
  179.5 42.4 %copy-start.4 = (f32[2,64,640]{2,1,0:T(8,128)S(1)}, f32[2,64,640]{2,1,0:T(8,128)}, u32[]{:S(2)}) copy-start(f32[2,64,640]{2,1,0:T(8,128)} %get-tuple-element.31.q_ref) | copy-start | bytes 983044
  179.5 42.4 %copy-start.5 = (f32[2,64,640]{2,1,0:T(8,128)S(1)}, f32[2,64,640]{2,1,0:T(8,128)}, u32[]{:S(2)}) copy-start(f32[2,64,640]{2,1,0:T(8,128)} %get-tuple-element.32.k_ref) | copy-start | bytes 983044
  179.5 36.3 %all-to-all-start.6 = ((f32[4,72,640]{2,1,0:T(8,128)}), f32[4,72,640]{2,1,0:T(8,128)S(1)}, u32[]{:S(2)}, u32[]{:S(2)}) async-start(f32[4,72,640]{2,1,0:T(8,128)} %copy-done), calls=%async_computation.6 | async-start | bytes 1474560 | tf_op jit(solution)/shard_map/all_to_all | solution.py:289
  216.6 15.4 %all-to-all-start.7 = ((f32[8,8,128]{2,1,0:T(8,128)}), f32[8,8,128]{2,1,0:T(8,128)S(1)}, u32[]{:S(2)}, u32[]{:S(2)}) async-start(f32[8,8,128]{2,1,0:T(8,128)} %get-tuple-element.23), calls=%async_computation.7 | async-start | bytes 65536 | tf_op jit(solution)/shard_map/all_to_all | solution.py:289
  (2 other events, 1.3 us)

commit v2 on v1

v2 whole, which is shorter than its diff:
```python
import functools
import math

import jax
import jax.numpy as jnp
from jax import lax
from jax.experimental import pallas as pl
from jax.experimental.pallas import tpu as pltpu
from jax.sharding import Mesh
from jax.sharding import PartitionSpec as P

ATT = 128
WINDOW = 128
EPSILON = 1e-06
MOMENTUM_RATE = 0.9
STEP_SIZE = 0.03
PRECISION = lax.Precision.HIGHEST

NZ, NX, NY = 8, 4, 2
BLOCKS = NZ * NX * NY
ROWS = 10
SLICE = 96
LANES = 128
TOK = 64
D = 640
H = 384
NARROW = 8
GROUPS = 2
VMEM_LIMIT = 16 * 1024 * 1024


def dot(left, right, dims=((1,), (0,))):
    return lax.dot_general(
        left, right, (dims, ((), ())), precision=PRECISION, preferred_element_type=jnp.float32
    )


def entry(group, sublane):
    q = group * 8 + sublane
    return (q // 3, q % 3) if q < 3 * ROWS else None


def call(body, outs, micros, *args, scratch=(), specs=None, after=(), grid=()):
    vmem = pl.BlockSpec(memory_space=pltpu.VMEM)
    specs = dict(specs or {})
    count, skipped, results = len(args), len(after), len(outs)

    def kernel(*refs):
        inputs, rest = refs[:count], refs[count + skipped :]
        targets, held, rest, sems = rest[:results], rest[results : 2 * results], rest[2 * results : -1], rest[-1]
        copies = [pltpu.make_async_copy(held[n], targets[n], sems.at[n]) for n in range(results)]
        started = set()

        def send(n):
            copies[n].start()
            started.add(n)

        body(*inputs, *held, *rest, send)
        for n in range(results):
            if n not in started:
                copies[n].start()
        for copy in copies:
            copy.wait()

    return pl.pallas_call(
        kernel,
        grid=grid,
        out_shape=[jax.ShapeDtypeStruct(s, jnp.float32) for s in outs],
        in_specs=[specs.get(n, vmem) for n in range(count)] + [pl.BlockSpec(memory_space=pl.ANY)] * skipped,
        out_specs=[pl.BlockSpec(memory_space=pltpu.HBM)] * results,
        scratch_shapes=[
            *(pltpu.VMEM(s, jnp.float32) for s in outs),
            *(pltpu.VMEM(s, jnp.float32) for s in scratch),
            pltpu.SemaphoreType.DMA((results,)),
        ],
        compiler_params=pltpu.CompilerParams(vmem_limit_bytes=VMEM_LIMIT),
        cost_estimate=pl.CostEstimate(flops=int(micros * 1e9), bytes_accessed=10**6, transcendentals=0),
    )(*args, *after)


def to_column(row):
    n = row.shape[1]
    same = lax.broadcasted_iota(jnp.int32, (n, n), 0) == lax.broadcasted_iota(jnp.int32, (n, n), 1)
    return jnp.sum(jnp.where(same, row, 0.0), axis=1, keepdims=True)


def to_row(column):
    n = column.shape[0]
    same = lax.broadcasted_iota(jnp.int32, (n, n), 0) == lax.broadcasted_iota(jnp.int32, (n, n), 1)
    return jnp.sum(jnp.where(same, column, 0.0), axis=0, keepdims=True)


def own_packs(own_ref, flat_ref):
    flat_ref[24:32, :] = jnp.zeros((8, H), jnp.float32)
    for q in range(3 * ROWS):
        flat_ref[q : q + 1, :] = own_ref[q]
    return [
        jnp.concatenate(
            [flat_ref[8 * g : 8 * g + 8, SLICE * x : SLICE * (x + 1)] for g in range(4)], axis=1
        )
        for x in range(NX)
    ]


def prepare_weights_body(fw_ref, send1_ref, flat_ref, send):
    packs = own_packs(fw_ref, flat_ref)
    for z in range(NZ):
        for x in range(NX):
            for y in range(NY):
                for t in range(3):
                    send1_ref[(z * NX + x) * NY + y, 8 * t : 8 * t + 8, :] = packs[x][:, LANES * t : LANES * (t + 1)]


def prepare_tokens_body(eta_ref, qkv_ref, mom_ref, pairs_ref, queries_ref, flat_ref, send):
    pairs_ref[0:TOK, :] = qkv_ref[1, 0]
    pairs_ref[TOK : 2 * TOK, :] = to_column(eta_ref[...]) * qkv_ref[2, 0]
    send(0)
    queries_ref[0:TOK, :] = qkv_ref[0, 0]
    queries_ref[TOK : 2 * TOK, :] = qkv_ref[0, 1]
    packs = own_packs(mom_ref, flat_ref)
    for x in range(NX):
        queries_ref[2 * TOK + 8 * x : 2 * TOK + 8 * x + 8, 0:H] = packs[x]
        queries_ref[2 * TOK + 8 * x : 2 * TOK + 8 * x + 8, H:D] = jnp.zeros((8, D - H), jnp.float32)


def widened(part):
    return jnp.concatenate([part, jnp.zeros((part.shape[0], LANES - SLICE), jnp.float32)], axis=1)


def unpack(recv_ref, out_ref, x_stride, y_stride, z_stride):
    for s in range(8):
        for x in range(NX):
            for y in range(NY):
                start = x * x_stride + y * y_stride + s
                rows = jnp.concatenate(
                    [recv_ref[pl.ds(start + 8 * t, NZ, stride=z_stride), :] for t in range(3)], axis=1
                )
                for g in range(4):
                    at = entry(g, s)
                    if at is None:
                        continue
                    r, i = at
                    out_ref[pl.ds(i * D + (x * NY + y) * ROWS + r, NZ, stride=NX * NY * ROWS), :] = widened(
                        rows[:, SLICE * g : SLICE * (g + 1)]
                    )


def pack(in_ref, send_ref, x_stride, y_stride, z_stride):
    for s in range(8):
        for x in range(NX):
            for y in range(NY):
                parts = []
                for g in range(4):
                    at = entry(g, s)
                    if at is None:
                        parts.append(jnp.zeros((NZ, SLICE), jnp.float32))
                        continue
                    r, i = at
                    parts.append(in_ref[pl.ds(i * D + (x * NY + y) * ROWS + r, NZ, stride=NX * NY * ROWS), :][:, :SLICE])
                rows = jnp.concatenate(parts, axis=1)
                start = x * x_stride + y * y_stride + s
                for t in range(3):
                    send_ref[pl.ds(start + 8 * t, NZ, stride=z_stride), :] = rows[:, LANES * t : LANES * (t + 1)]


def token_rows(refs, start):
    return jnp.concatenate([ref[start : start + TOK, :] for ref in refs], axis=0)


def matrix(ref, i):
    return ref[i * D : (i + 1) * D, :]


def gradient_body(recv1_ref, p0_ref, p1_ref, p2_ref, p3_ref, w_ref, send_ref, g_ref, send):
    unpack(recv1_ref, w_ref, 48, 24, 192)
    send(0)
    pairs = (p0_ref, p1_ref, p2_ref, p3_ref)
    keys = token_rows(pairs, 0)
    weighted = token_rows(pairs, TOK)
    pre = dot(keys, jnp.concatenate([matrix(w_ref, 0), matrix(w_ref, 1)], axis=1))
    gate_pre, up_pre = pre[:, :LANES], pre[:, LANES:]
    back = -dot(weighted, matrix(w_ref, 2))
    sigmoid = jax.nn.sigmoid(gate_pre)
    gated = gate_pre * sigmoid
    hidden = gated * up_pre
    gate_back = back * up_pre * sigmoid * (1.0 + gate_pre * (1.0 - sigmoid))
    up_back = back * gated
    both = dot(keys, jnp.concatenate([gate_back, up_back], axis=1), ((0,), (0,)))
    g_ref[0:D, :] = both[:, :LANES]
    g_ref[D : 2 * D, :] = both[:, LANES:]
    g_ref[2 * D : 3 * D, :] = -dot(weighted, hidden, ((0,), (0,)))
    pack(g_ref, send_ref, 24, 96, 192)


def source(x_ref, s):
    return lax.rem(x_ref[0] + NX - s, NX)


def moment_body(x_ref, recv2_ref, q0_ref, q1_ref, q2_ref, q3_ref, send3_ref, own_ref, send):
    total = recv2_ref[0]
    for j in range(1, NZ * NY):
        total = total + recv2_ref[j]
    own_ref[...] = total
    mine = pl.ds(pl.multiple_of(2 * TOK + 8 * x_ref[0], 8), 8)
    for s, ref in enumerate((q0_ref, q1_ref, q2_ref, q3_ref)):
        old = ref[mine, :]
        old = jnp.concatenate([old[:, LANES * t : LANES * (t + 1)] for t in range(3)], axis=0)
        rows = pl.ds(pl.multiple_of(24 * source(x_ref, s), 8), 24)
        own_ref[rows, :] = own_ref[rows, :] + MOMENTUM_RATE * old
    moment = own_ref[...]
    for j in range(NZ * NY):
        send3_ref[j] = moment


def hidden_of(inputs, w1, w3):
    pre = dot(inputs, jnp.concatenate([w1, w3], axis=1))
    gate_pre, up_pre = pre[:, :LANES], pre[:, LANES:]
    return gate_pre * jax.nn.sigmoid(gate_pre) * up_pre


def first_read_body(q0_ref, q1_ref, q2_ref, q3_ref, w_ref, *out_refs):
    out_refs = out_refs[:NX]
    hidden = hidden_of(token_rows((q0_ref, q1_ref, q2_ref, q3_ref), 0), matrix(w_ref, 0), matrix(w_ref, 1))
    partial = dot(hidden, matrix(w_ref, 2), ((1,), (1,)))
    for s in range(NX):
        out_refs[s][...] = partial[s * TOK : (s + 1) * TOK]


def renormalized(weights, moment):
    rate = STEP_SIZE / jnp.sqrt(jnp.mean(moment * moment, axis=0, keepdims=True) + EPSILON)
    moved = weights - moment * rate
    ratio = jnp.sqrt(jnp.mean(weights * weights, axis=0, keepdims=True) + EPSILON) / jnp.sqrt(
        jnp.mean(moved * moved, axis=0, keepdims=True) + EPSILON
    )
    return moved * ratio, rate, ratio


def second_read_body(x_ref, recv3_ref, q0_ref, q1_ref, q2_ref, q3_ref, w_ref, moment_ref, send_ref, m_ref, send):
    unpack(recv3_ref, m_ref, 24, 96, 192)
    new1, rate1, ratio1 = renormalized(matrix(w_ref, 0), matrix(m_ref, 0))
    new3, rate3, ratio3 = renormalized(matrix(w_ref, 1), matrix(m_ref, 1))
    new2, rate2, ratio2 = renormalized(matrix(w_ref, 2), matrix(m_ref, 2))
    hidden = hidden_of(token_rows((q0_ref, q1_ref, q2_ref, q3_ref), TOK), new1, new3)
    partial = dot(hidden, new2, ((1,), (1,)))
    stats = [rate1, rate3, rate2, ratio1, ratio3, ratio2, jnp.zeros((2, LANES), jnp.float32)]
    stats = jnp.concatenate(stats, axis=0)
    for x in range(NX):
        tail = [stats, *(moment_ref[24 * x + 8 * t : 24 * x + 8 * t + 8, :] for t in range(3))]
        tail.append(jnp.zeros((8, LANES), jnp.float32))
        send_ref[x, TOK : TOK + 8, :] = jnp.concatenate(tail, axis=1)
    for s in range(NX):
        send_ref[source(x_ref, s), 0:TOK, :] = partial[s * TOK : (s + 1) * TOK]


def squares_body(f0_ref, f1_ref, f2_ref, f3_ref, second_ref, readout_ref, send_ref, send):
    first = f0_ref[...] + f1_ref[...] + f2_ref[...] + f3_ref[...]
    second = second_ref[0, 0:TOK, :]
    for x in range(1, NX):
        second = second + second_ref[x, 0:TOK, :]
    readout_ref[0] = first
    readout_ref[1] = second
    row = jnp.concatenate(
        [to_row(jnp.sum(total * total, axis=1, keepdims=True)) for total in (first, second)], axis=1
    )
    for n in range(NARROW):
        send_ref[n] = jnp.broadcast_to(row, (8, GROUPS * TOK))


def own_rows_body(second_ref, fw_ref, new_w_ref, new_m_ref, flat_ref, send):
    for g in range(4):
        flat_ref[8 * g : 8 * g + 8, :] = jnp.concatenate(
            [
                second_ref[x, TOK : TOK + 8, LANES + SLICE * g : LANES + SLICE * (g + 1)]
                for x in range(NX)
            ],
            axis=1,
        )
    stats = jnp.concatenate([second_ref[x, TOK : TOK + 8, 0:SLICE] for x in range(NX)], axis=1)
    for q in range(3 * ROWS):
        i = q % 3
        moment = flat_ref[q : q + 1, :]
        new_m_ref[q] = moment
        new_w_ref[q] = (fw_ref[q] - moment * stats[i : i + 1]) * stats[3 + i : 4 + i]


def mix_body(recv_ref, readout_ref, attended_ref, gain_ref, mixed_ref, send):
    total = recv_ref[0, 0:1, :]
    for n in range(1, NARROW):
        total = total + recv_ref[n, 0:1, :]
    scale = to_column(1.0 / jnp.sqrt(total / (D * NARROW) + EPSILON))
    for c in range(GROUPS):
        mixed_ref[c] = attended_ref[c] + gain_ref[...] * (readout_ref[c] * scale[c * TOK : (c + 1) * TOK])


def attention_body(position_ref, qkv_ref, near_ref, far_ref, out_ref, send):
    position = position_ref[0]
    row = lax.broadcasted_iota(jnp.int32, (TOK, 3 * TOK), 0) + 2 * TOK
    col = lax.broadcasted_iota(jnp.int32, (TOK, 3 * TOK), 1)
    window = (row - col >= 0) & (row - col < WINDOW)
    for c in range(GROUPS):
        if c == 0:
            first = jnp.where(position >= 2, 0, jnp.where(position >= 1, TOK, 2 * TOK))
            allowed = window & (col >= first)
        else:
            allowed = window
        for h in range(D // ATT):
            at = slice(h * ATT, (h + 1) * ATT)
            parts = []
            for a in range(2):
                if c == 0:
                    far, near = far_ref[a, 0, :, at], near_ref[a, 0, :, at]
                else:
                    far = jnp.where(position >= 2, far_ref[a, 1, :, at], far_ref[a, 0, :, at])
                    near = jnp.where(position >= 1, near_ref[a, 1, :, at], near_ref[a, 0, :, at])
                parts.append(jnp.concatenate([far, near, qkv_ref[1 + a, c, :, at]], axis=0))
            keys, values = parts
            scores = dot(qkv_ref[0, c, :, at], keys, ((1,), (1,))) * (1.0 / math.sqrt(ATT))
            scores = jnp.where(allowed, scores, -1e30)
            weights = jnp.exp(scores - jnp.max(scores, axis=1, keepdims=True))
            weights = weights / jnp.sum(weights, axis=1, keepdims=True)
            out_ref[c, :, at] = dot(weights, values)


def behind(block, distance):
    axes = ("z", "x", "yh")
    return lax.ppermute(block, axes, [((i - distance) % BLOCKS, i) for i in range(BLOCKS)])


def from_neighbours(block):
    return [block] + [lax.ppermute(block, "x", [((i - s) % NX, i) for i in range(NX)]) for s in range(1, NX)]


def back_to_neighbours(blocks):
    return [blocks[0]] + [
        lax.ppermute(blocks[s], "x", [(i, (i - s) % NX) for i in range(NX)]) for s in range(1, NX)
    ]


def exchange(pieces, axes):
    return lax.all_to_all(pieces, axes, split_axis=0, concat_axis=0, tiled=True)


def scalar(value):
    return jnp.reshape(value, (1,)).astype(jnp.int32)


def local(qkv, eta, fast_weights, momentum, ttt_gain):
    own_weights, own_moment = fast_weights.reshape(3 * ROWS, 1, H), momentum.reshape(3 * ROWS, 1, H)
    x = lax.axis_index("x")
    position = scalar((lax.axis_index("z") * NX + x) * NY + lax.axis_index("yh"))
    x = scalar(x)
    smem = {0: pl.BlockSpec(memory_space=pltpu.SMEM)}
    near = behind(qkv[1:], 1)
    far = behind(qkv[1:], 2)
    (send1,) = call(prepare_weights_body, [(BLOCKS, 24, LANES)], 1, own_weights, scratch=[(32, H)])
    pairs, queries = call(
        prepare_tokens_body, [(2 * TOK, D), (2 * TOK + 32, D)], 1, eta, qkv, own_moment, scratch=[(32, H)]
    )
    recv1 = exchange(send1, ("z", "x", "yh"))
    pairs = from_neighbours(pairs)
    queries = from_neighbours(queries)
    weights, send2 = call(
        gradient_body, [(3 * D, LANES), (BLOCKS * 24, LANES)], 5,
        recv1.reshape(BLOCKS * 24, LANES), *pairs, scratch=[(3 * D, LANES)],
    )
    recv2 = exchange(send2.reshape(NZ * NY, NX * 24, LANES), ("z", "yh"))
    (attended,) = call(attention_body, [(GROUPS, TOK, D)], 9, position, qkv, near, far, specs=smem)
    send3, moment = call(
        moment_body, [(NZ * NY, NX * 24, LANES), (NX * 24, LANES)], 1, x, recv2, *queries,
        specs=smem, after=(attended,),
    )
    recv3 = exchange(send3, ("z", "yh"))
    first = call(first_read_body, [(TOK, D)] * NX, 3, *queries, weights)
    (send_second,) = call(
        second_read_body, [(NX, TOK + 8, D)], 4,
        x, recv3.reshape(BLOCKS * 24, LANES), *queries, weights, moment, scratch=[(3 * D, LANES)],
        specs=smem, after=(first[0],),
    )
    second = exchange(send_second, "x")
    first = back_to_neighbours(first)
    readout, send5 = call(
        squares_body, [(GROUPS, TOK, D), (NARROW, 8, GROUPS * TOK)], 1, *first, second
    )
    recv5 = exchange(send5, "narrow")
    new_weights, new_moment = call(
        own_rows_body, [(3 * ROWS, 1, H), (3 * ROWS, 1, H)], 1, second, own_weights, scratch=[(32, H)]
    )
    (mixed,) = call(
        mix_body, [(GROUPS, TOK, D)], 1, recv5, readout, attended, ttt_gain.reshape(1, D), after=(new_weights,)
    )
    return mixed, new_weights.reshape(1, ROWS, 3, H), new_moment.reshape(1, ROWS, 3, H)


def solution(mesh):
    fine = Mesh(mesh.devices.reshape(NZ, NX, NY, NARROW), ("z", "x", "yh", "narrow"))
    wide = ("z", "x", "yh")
    return jax.shard_map(
        local,
        mesh=fine,
        in_specs=(
            P(None, None, wide, "narrow"),
            P("narrow", wide),
            P("narrow", wide, None, None),
            P("narrow", wide, None, None),
            P("narrow"),
        ),
        out_specs=(
            P(None, wide, "narrow"),
            P("narrow", wide, None, None),
            P("narrow", wide, None, None),
        ),
        check_vma=False,
    )
```

time: 234 us -> 188 us (0.80)
  blocking collectives: 59.1 us -> 0 us
  starting transfers between devices: 59.7 us -> 109 us
  waiting for transfers between devices: 77.5 us -> 33 us
  Pallas kernels: 21.4 us -> 29.2 us
    all_to_all x6 -> x5, waiting for transfers between devices: 77.5 us -> 14.5 us  [exchange(): return lax.all_to_all(pieces, axes, split_axis=0, concat_axis=0, tiled=True)]
    all_to_all x2 -> x0, blocking collectives: 59.1 us -> none  [exchange(): return lax.all_to_all(pieces, axes, split_axis=0, concat_axis=0, tiled=True)]
    ppermute x0 -> x9, starting transfers between devices: none -> 28.4 us  [the longest x6 18.7 us: from_neighbours(): lax.ppermute(block, 'x', [((i - s) % NX, i) for i in range(NX)])]
    all_to_all x6 -> x5, starting transfers between devices: 47.3 us -> 71.4 us  [exchange(): return lax.all_to_all(pieces, axes, split_axis=0, concat_axis=0, tiled=True)]
    ppermute x0 -> x9, waiting for transfers between devices: none -> 18.5 us  [the longest x6 13.7 us: from_neighbours(): lax.ppermute(block, 'x', [((i - s) % NX, i) for i in range(NX)])]
    pallas_call x9 -> x10, Pallas kernels: 21.4 us -> 29.2 us  [call(): pl.pallas_call(kernel, grid=grid, out_shape=[jax.ShapeDtypeStruct(s, jnp....]
    unnamed x40 -> x42, local copies, waits for them, and re-layouts: 9.13 us -> 13.3 us
    ppermute x2, starting transfers between devices: 12.4 us -> 9.18 us  [behind(): lax.ppermute(block, axes, [((i - distance) % BLOCKS, i) for i in range(BL...]
  transfers between devices with their start and end apart: 8 -> 16, of which waited for: 4 -> 6; matrix products, arithmetic and copies ran while one was open for 2% -> 0% of each run, Pallas kernels for 7% -> 10%
where the time goes in v2:
time: 188 us; the launch traced here: 187 us
  starting transfers between devices  109 us (58%)
  waiting for transfers between devices  33 us (18%)
  Pallas kernels  29.2 us (16%)
  local copies, waits for them, and re-layouts  14.2 us (8%)
    all_to_all x5, starting transfers between devices, exchange(): return lax.all_to_all(pieces, axes, split_axis=0, concat_axis=0, tiled=True)  71.4 us
    pallas_call x10, Pallas kernels, call(): pl.pallas_call(kernel, grid=grid, out_shape=[jax.ShapeDtypeStruct(s, jnp....  29.2 us
    ppermute x6, starting transfers between devices, from_neighbours(): lax.ppermute(block, 'x', [((i - s) % NX, i) for i in range(NX)])  18.7 us
    all_to_all x5, waiting for transfers between devices, exchange(): return lax.all_to_all(pieces, axes, split_axis=0, concat_axis=0, tiled=True)  14.5 us
    ppermute x6, waiting for transfers between devices, from_neighbours(): lax.ppermute(block, 'x', [((i - s) % NX, i) for i in range(NX)])  13.7 us
    unnamed x42, local copies, waits for them, and re-layouts  13.3 us
    ppermute x3, starting transfers between devices, back_to_neighbours(): lax.ppermute(blocks[s], 'x', [(i, (i - s) % NX) for i in range(NX)])  9.67 us
    ppermute x2, starting transfers between devices, behind(): lax.ppermute(block, axes, [((i - distance) % BLOCKS, i) for i in range(BL...  9.18 us
  transfers between devices with their start and end apart: 16, of which 6 were waited for; matrix products, arithmetic and copies ran while one was open for 0% of the time, Pallas kernels for 10%

profile of v2, /device:TPU:1, one launch (start us, length us, event | category | flops | bytes accessed | tf_op | source)
XLA Modules:
  0.0 186.6 jit_solution(15493450560923259443)
XLA Ops:
  2.5 19.7 %all-to-all-start = ((f32[64,24,128]{2,1,0:T(8,128)}), f32[64,24,128]{2,1,0:T(8,128)S(1)}, u32[]{:S(2)}, u32[]{:S(2)}) async-start(f32[64,24,128]{2,1,0:T(8,128)} %shard_map.77), calls=%async_computation | async-start | bytes 1572864 | tf_op jit(solution)/shard_map/all_to_all | solution.py:340
  23.4 2.9 %collective-permute-start.3 = (f32[128,640]{1,0:T(8,128)S(1)}, f32[128,640]{1,0:T(8,128)S(1)}, u32[]{:S(2)}, u32[]{:S(2)}) collective-permute-start(f32[128,640]{1,0:T(8,128)S(1)} %get-tuple-element.18.refs_1_), channel_id=1, source_target_pairs={{48,0},{0,16},{16,32},{32,48},{49,1},{1,17},{17,33},{33,49},{50,2}... | collective-permute-start | bytes 983048 | tf_op jit(solution)/shard_map/ppermute | solution.py:330
  26.4 4.3 %collective-permute-start.4 = (f32[128,640]{1,0:T(8,128)S(1)}, f32[128,640]{1,0:T(8,128)S(1)}, u32[]{:S(2)}, u32[]{:S(2)}) collective-permute-start(f32[128,640]{1,0:T(8,128)S(1)} %get-tuple-element.18.refs_1_), channel_id=1, source_target_pairs={{32,0},{48,16},{0,32},{16,48},{33,1},{49,17},{1,33},{17,49},{34,2}... | collective-permute-start | bytes 983048 | tf_op jit(solution)/shard_map/ppermute | solution.py:330
  30.7 3.1 %collective-permute-start.5 = (f32[128,640]{1,0:T(8,128)S(1)}, f32[128,640]{1,0:T(8,128)S(1)}, u32[]{:S(2)}, u32[]{:S(2)}) collective-permute-start(f32[128,640]{1,0:T(8,128)S(1)} %get-tuple-element.18.refs_1_), channel_id=1, source_target_pairs={{16,0},{32,16},{48,32},{0,48},{17,1},{33,17},{49,33},{1,49},{18,2}... | collective-permute-start | bytes 983048 | tf_op jit(solution)/shard_map/ppermute | solution.py:330
  34.7 2.2 %collective-permute-start.10 = (f32[2,2,64,640]{3,2,1,0:T(8,128)}, f32[2,2,64,640]{3,2,1,0:T(8,128)S(1)}, u32[]{:S(2)}, u32[]{:S(2)}) collective-permute-start(f32[2,2,64,640]{3,2,1,0:T(8,128)} %slice.4), channel_id=1, source_target_pairs={{496,0},{504,8},{0,16},{8,24},{16,32},{24,40},{32,48},{40,56},{48,... | collective-permute-start | bytes 1966088 | tf_op jit(solution)/shard_map/ppermute | solution.py:326
  36.9 7.0 %collective-permute-start.9 = (f32[2,2,64,640]{3,2,1,0:T(8,128)}, f32[2,2,64,640]{3,2,1,0:T(8,128)S(1)}, u32[]{:S(2)}, u32[]{:S(2)}) collective-permute-start(f32[2,2,64,640]{3,2,1,0:T(8,128)} %slice.4), channel_id=1, source_target_pairs={{504,0},{0,8},{8,16},{16,24},{24,32},{32,40},{40,48},{48,56},{56,6... | collective-permute-start | bytes 1966088 | tf_op jit(solution)/shard_map/ppermute | solution.py:326
  44.6 13.5 %collective-permute-done.4.refs_3_ = f32[128,640]{1,0:T(8,128)S(1)} collective-permute-done((f32[128,640]{1,0:T(8,128)S(1)}, f32[128,640]{1,0:T(8,128)S(1)}, u32[]{:S(2)}, u32[]{:S(2)}) %collective-permute-start.4) | collective-permute-done | bytes 327712 | tf_op jit(solution)/shard_map/ppermute | solution.py:330
  63.4 5.4 %shard_map.78 = (f32[1920,128]{1,0:T(8,128)S(1)}, f32[1536,128]{1,0:T(8,128)}) custom-call(f32[1536,128]{1,0:T(8,128)S(1)} %bitcast.9, f32[128,640]{1,0:T(8,128)S(1)} %copy-done.2, f32[128,640]{1,0:T(8,128)S(1)} %copy-done.4, f32[128,640]{1,0:T(8,128)S(1)} %copy-done.6, f32[128,640]{1,0:T(8,128)S(1)} %copy-done.8), custom_call_target="tpu_custom_call" | custom-call | flops 5000000000 | bytes 1000000 | tf_op jit(solution)/shard_map/pallas_call | solution.py:65
  69.8 9.8 %all-to-all-start.1 = ((f32[16,96,128]{2,1,0:T(8,128)}), f32[16,96,128]{2,1,0:T(8,128)S(1)}, u32[]{:S(2)}, u32[]{:S(2)}) async-start(f32[16,96,128]{2,1,0:T(8,128)} %bitcast.4), calls=%async_computation.1 | async-start | bytes 1572864 | tf_op jit(solution)/shard_map/all_to_all | solution.py:340
  83.4 4.6 %collective-permute-start.2 = (f32[160,640]{1,0:T(8,128)S(1)}, f32[160,640]{1,0:T(8,128)}, u32[]{:S(2)}, u32[]{:S(2)}) collective-permute-start(f32[160,640]{1,0:T(8,128)S(1)} %get-tuple-element.17.refs_0_.refs_2_), channel_id=1, source_target_pairs={{16,0},{32,16},{48,32},{0,48},{17,1},{33,17},{49,33},{1,49},{18,2}... | collective-permute-start | bytes 1228808 | tf_op jit(solution)/shard_map/ppermute | solution.py:330
  88.0 7.5 %shard_map.80.refs_6_.refs_2_ = f32[2,64,640]{2,1,0:T(8,128)S(1)} custom-call(s32[1]{0:T(128)} %bitcast.5.refs_0_, f32[3,2,64,640]{3,2,1,0:T(8,128)S(1)} %copy-done, f32[2,2,64,640]{3,2,1,0:T(8,128)S(1)} %collective-permute-done.9.refs_2_, f32[2,2,64,640]{3,2,1,0:T(8,128)S(1)} %collective-permute-done.10.refs_3_), custom_call_target="tpu_custom_call" | custom-call | flops 8999999488 | bytes 1000000 | tf_op jit(solution)/shard_map/pallas_call | solution.py:65
  97.5 2.2 %shard_map.81 = (f32[16,96,128]{2,1,0:T(8,128)}, f32[96,128]{1,0:T(8,128)S(1)}) custom-call(s32[1]{0:T(128)} %bitcast.3.refs_0_, f32[16,96,128]{2,1,0:T(8,128)S(1)} %all-to-all-done.1.refs_1_, f32[160,640]{1,0:T(8,128)S(1)} %get-tuple-element.17.refs_0_.refs_2_, f32[160,640]{1,0:T(8,128)} %collective-permute-done.refs_1_.refs_3_, ...), custom_call_target="tpu_custom_call" | custom-call | flops 1000000000 | bytes 1000000 | tf_op jit(solution)/shard_map/pallas_call | solution.py:65
  99.7 11.7 %all-to-all-start.2 = ((f32[16,96,128]{2,1,0:T(8,128)}), f32[16,96,128]{2,1,0:T(8,128)S(1)}, u32[]{:S(2)}, u32[]{:S(2)}) async-start(f32[16,96,128]{2,1,0:T(8,128)} %get-tuple-element.25), calls=%async_computation.2 | async-start | bytes 1572864 | tf_op jit(solution)/shard_map/all_to_all | solution.py:340
  112.6 4.5 %shard_map.79 = (f32[64,640]{1,0:T(8,128)S(1)}, f32[64,640]{1,0:T(8,128)S(1)}, f32[64,640]{1,0:T(8,128)S(1)}, f32[64,640]{1,0:T(8,128)S(1)}) custom-call(f32[160,640]{1,0:T(8,128)S(1)} %get-tuple-element.17.refs_0_.refs_2_, f32[160,640]{1,0:T(8,128)} %collective-permute-done.refs_1_.refs_3_, f32[160,640]{1,0:T(8,128)} %collective-permute-done.1.refs_2_.refs_4_, ...), custom_call_target="tpu_custom_call" | custom-call | flops 3000000000 | bytes 1000000 | tf_op jit(solution)/shard_map/pallas_call | solution.py:65
  117.1 10.3 %all-to-all-done.2 = f32[16,96,128]{2,1,0:T(8,128)S(1)} async-done(((f32[16,96,128]{2,1,0:T(8,128)}), f32[16,96,128]{2,1,0:T(8,128)S(1)}, u32[]{:S(2)}, u32[]{:S(2)}) %all-to-all-start.2) | async-done | bytes 786464 | tf_op jit(solution)/shard_map/all_to_all | solution.py:340
  128.6 5.5 %shard_map.82 = f32[4,72,640]{2,1,0:T(8,128)} custom-call(s32[1]{0:T(128)} %bitcast.3.refs_0_, f32[1536,128]{1,0:T(8,128)S(1)} %bitcast.10, f32[160,640]{1,0:T(8,128)S(1)} %get-tuple-element.17.refs_0_.refs_2_, f32[160,640]{1,0:T(8,128)} %collective-permute-done.refs_1_.refs_3_, f32[160,640]{1,0:T(8,128)} %collective-permute-done.1.refs_2_.refs_4_, ...), custom_call_target="tpu_custom_call" | custom-call | flops 4000000000 | bytes 1000000 | tf_op jit(solution)/shard_map/pallas_call | solution.py:65
  134.1 3.5 %all-to-all-start.3 = ((f32[4,72,640]{2,1,0:T(8,128)}), f32[4,72,640]{2,1,0:T(8,128)S(1)}, u32[]{:S(2)}, u32[]{:S(2)}) async-start(f32[4,72,640]{2,1,0:T(8,128)} %shard_map.82), calls=%async_computation.3 | async-start | bytes 1474560 | tf_op jit(solution)/shard_map/all_to_all | solution.py:340
  137.6 4.7 %collective-permute-start.6 = (f32[64,640]{1,0:T(8,128)S(1)}, f32[64,640]{1,0:T(8,128)S(1)}, u32[]{:S(2)}, u32[]{:S(2)}) collective-permute-start(f32[64,640]{1,0:T(8,128)S(1)} %get-tuple-element.21), channel_id=1, source_target_pairs={{0,48},{16,0},{32,16},{48,32},{1,49},{17,1},{33,17},{49,33},{2,50}... | collective-permute-start | bytes 491528 | tf_op jit(solution)/shard_map/ppermute | solution.py:335
  142.3 2.5 %collective-permute-start.7 = (f32[64,640]{1,0:T(8,128)S(1)}, f32[64,640]{1,0:T(8,128)S(1)}, u32[]{:S(2)}, u32[]{:S(2)}) collective-permute-start(f32[64,640]{1,0:T(8,128)S(1)} %get-tuple-element.22), channel_id=1, source_target_pairs={{0,32},{16,48},{32,0},{48,16},{1,33},{17,49},{33,1},{49,17},{2,34}... | collective-permute-start | bytes 491528 | tf_op jit(solution)/shard_map/ppermute | solution.py:335
  144.8 2.5 %collective-permute-start.8 = (f32[64,640]{1,0:T(8,128)S(1)}, f32[64,640]{1,0:T(8,128)S(1)}, u32[]{:S(2)}, u32[]{:S(2)}) collective-permute-start(f32[64,640]{1,0:T(8,128)S(1)} %get-tuple-element.23), channel_id=1, source_target_pairs={{0,16},{16,32},{32,48},{48,0},{1,17},{17,33},{33,49},{49,1},{2,18}... | collective-permute-start | bytes 491528 | tf_op jit(solution)/shard_map/ppermute | solution.py:335
  147.3 2.5 %collective-permute-done.7.refs_2_ = f32[64,640]{1,0:T(8,128)S(1)} collective-permute-done((f32[64,640]{1,0:T(8,128)S(1)}, f32[64,640]{1,0:T(8,128)S(1)}, u32[]{:S(2)}, u32[]{:S(2)}) %collective-permute-start.7) | collective-permute-done | bytes 163872 | tf_op jit(solution)/shard_map/ppermute | solution.py:335
  149.9 2.2 %collective-permute-done.8.refs_3_ = f32[64,640]{1,0:T(8,128)S(1)} collective-permute-done((f32[64,640]{1,0:T(8,128)S(1)}, f32[64,640]{1,0:T(8,128)S(1)}, u32[]{:S(2)}, u32[]{:S(2)}) %collective-permute-start.8) | collective-permute-done | bytes 163872 | tf_op jit(solution)/shard_map/ppermute | solution.py:335
  153.0 26.7 %all-to-all-start.4 = ((f32[8,8,128]{2,1,0:T(8,128)}), f32[8,8,128]{2,1,0:T(8,128)S(1)}, u32[]{:S(2)}, u32[]{:S(2)}) async-start(f32[8,8,128]{2,1,0:T(8,128)} %get-tuple-element.27), calls=%async_computation.4 | async-start | bytes 65536 | tf_op jit(solution)/shard_map/all_to_all | solution.py:340
  180.5 4.2 %all-to-all-done.4.refs_0_ = f32[8,8,128]{2,1,0:T(8,128)S(1)} async-done(((f32[8,8,128]{2,1,0:T(8,128)}), f32[8,8,128]{2,1,0:T(8,128)S(1)}, u32[]{:S(2)}, u32[]{:S(2)}) %all-to-all-start.4) | async-done | bytes 32800 | tf_op jit(solution)/shard_map/all_to_all | solution.py:340
  (62 shorter events, 22.5 us)
Async XLA Ops:
  2.5 19.8 %copy-start = (f32[3,2,64,640]{3,2,1,0:T(8,128)S(1)}, f32[3,2,64,640]{3,2,1,0:T(8,128)}, u32[]{:S(2)}) copy-start(f32[3,2,64,640]{3,2,1,0:T(8,128)} %refs_1_.3) | copy-start | bytes 2949124
  2.5 19.8 %copy-start.9 = (f32[1,10,3,384]{3,0,2,1:T(1,128)S(1)}, f32[1,10,3,384]{3,0,2,1:T(1,128)}, u32[]{:S(2)}) copy-start(f32[1,10,3,384]{3,0,2,1:T(1,128)} %param.8) | copy-start | bytes 138244
  2.5 57.0 %all-to-all-start = ((f32[64,24,128]{2,1,0:T(8,128)}), f32[64,24,128]{2,1,0:T(8,128)S(1)}, u32[]{:S(2)}, u32[]{:S(2)}) async-start(f32[64,24,128]{2,1,0:T(8,128)} %shard_map.77), calls=%async_computation | async-start | bytes 1572864 | tf_op jit(solution)/shard_map/all_to_all | solution.py:340
  23.4 11.2 %copy-start.1 = (f32[128,640]{1,0:T(8,128)}, f32[128,640]{1,0:T(8,128)S(1)}, u32[]{:S(2)}) copy-start(f32[128,640]{1,0:T(8,128)S(1)} %get-tuple-element.18.refs_1_) | copy-start | bytes 983044
  23.4 20.4 %collective-permute-start.3 = (f32[128,640]{1,0:T(8,128)S(1)}, f32[128,640]{1,0:T(8,128)S(1)}, u32[]{:S(2)}, u32[]{:S(2)}) collective-permute-start(f32[128,640]{1,0:T(8,128)S(1)} %get-tuple-element.18.refs_1_), channel_id=1, source_target_pairs={{48,0},{0,16},{16,32},{32,48},{49,1},{1,17},{17,33},{33,49},{50,2}... | collective-permute-start | bytes 983048 | tf_op jit(solution)/shard_map/ppermute | solution.py:330
  26.4 31.7 %collective-permute-start.4 = (f32[128,640]{1,0:T(8,128)S(1)}, f32[128,640]{1,0:T(8,128)S(1)}, u32[]{:S(2)}, u32[]{:S(2)}) collective-permute-start(f32[128,640]{1,0:T(8,128)S(1)} %get-tuple-element.18.refs_1_), channel_id=1, source_target_pairs={{32,0},{48,16},{0,32},{16,48},{33,1},{49,17},{1,33},{17,49},{34,2}... | collective-permute-start | bytes 983048 | tf_op jit(solution)/shard_map/ppermute | solution.py:330
  30.7 28.1 %collective-permute-start.5 = (f32[128,640]{1,0:T(8,128)S(1)}, f32[128,640]{1,0:T(8,128)S(1)}, u32[]{:S(2)}, u32[]{:S(2)}) collective-permute-start(f32[128,640]{1,0:T(8,128)S(1)} %get-tuple-element.18.refs_1_), channel_id=1, source_target_pairs={{16,0},{32,16},{48,32},{0,48},{17,1},{33,17},{49,33},{1,49},{18,2}... | collective-permute-start | bytes 983048 | tf_op jit(solution)/shard_map/ppermute | solution.py:330
  34.7 53.3 %collective-permute-start.10 = (f32[2,2,64,640]{3,2,1,0:T(8,128)}, f32[2,2,64,640]{3,2,1,0:T(8,128)S(1)}, u32[]{:S(2)}, u32[]{:S(2)}) collective-permute-start(f32[2,2,64,640]{3,2,1,0:T(8,128)} %slice.4), channel_id=1, source_target_pairs={{496,0},{504,8},{0,16},{8,24},{16,32},{24,40},{32,48},{40,56},{48,... | collective-permute-start | bytes 1966088 | tf_op jit(solution)/shard_map/ppermute | solution.py:326
  36.9 51.1 %collective-permute-start.9 = (f32[2,2,64,640]{3,2,1,0:T(8,128)}, f32[2,2,64,640]{3,2,1,0:T(8,128)S(1)}, u32[]{:S(2)}, u32[]{:S(2)}) collective-permute-start(f32[2,2,64,640]{3,2,1,0:T(8,128)} %slice.4), channel_id=1, source_target_pairs={{504,0},{0,8},{8,16},{16,24},{24,32},{32,40},{40,48},{48,56},{56,6... | collective-permute-start | bytes 1966088 | tf_op jit(solution)/shard_map/ppermute | solution.py:326
  69.8 26.7 %all-to-all-start.1 = ((f32[16,96,128]{2,1,0:T(8,128)}), f32[16,96,128]{2,1,0:T(8,128)S(1)}, u32[]{:S(2)}, u32[]{:S(2)}) async-start(f32[16,96,128]{2,1,0:T(8,128)} %bitcast.4), calls=%async_computation.1 | async-start | bytes 1572864 | tf_op jit(solution)/shard_map/all_to_all | solution.py:340
  79.6 16.7 %collective-permute-start = (f32[160,640]{1,0:T(8,128)S(1)}, f32[160,640]{1,0:T(8,128)}, u32[]{:S(2)}, u32[]{:S(2)}) collective-permute-start(f32[160,640]{1,0:T(8,128)S(1)} %get-tuple-element.17.refs_0_.refs_2_), channel_id=1, source_target_pairs={{48,0},{0,16},{16,32},{32,48},{49,1},{1,17},{17,33},{33,49},{50,2}... | collective-permute-start | bytes 1228808 | tf_op jit(solution)/shard_map/ppermute | solution.py:330
  81.5 14.8 %collective-permute-start.1 = (f32[160,640]{1,0:T(8,128)S(1)}, f32[160,640]{1,0:T(8,128)}, u32[]{:S(2)}, u32[]{:S(2)}) collective-permute-start(f32[160,640]{1,0:T(8,128)S(1)} %get-tuple-element.17.refs_0_.refs_2_), channel_id=1, source_target_pairs={{32,0},{48,16},{0,32},{16,48},{33,1},{49,17},{1,33},{17,49},{34,2}... | collective-permute-start | bytes 1228808 | tf_op jit(solution)/shard_map/ppermute | solution.py:330
  83.4 13.1 %collective-permute-start.2 = (f32[160,640]{1,0:T(8,128)S(1)}, f32[160,640]{1,0:T(8,128)}, u32[]{:S(2)}, u32[]{:S(2)}) collective-permute-start(f32[160,640]{1,0:T(8,128)S(1)} %get-tuple-element.17.refs_0_.refs_2_), channel_id=1, source_target_pairs={{16,0},{32,16},{48,32},{0,48},{17,1},{33,17},{49,33},{1,49},{18,2}... | collective-permute-start | bytes 1228808 | tf_op jit(solution)/shard_map/ppermute | solution.py:330
  99.7 27.6 %all-to-all-start.2 = ((f32[16,96,128]{2,1,0:T(8,128)}), f32[16,96,128]{2,1,0:T(8,128)S(1)}, u32[]{:S(2)}, u32[]{:S(2)}) async-start(f32[16,96,128]{2,1,0:T(8,128)} %get-tuple-element.25), calls=%async_computation.2 | async-start | bytes 1572864 | tf_op jit(solution)/shard_map/all_to_all | solution.py:340
  111.4 1.2 copy-start.18
  127.4 1.2 copy-start.19
  134.1 18.0 %all-to-all-start.3 = ((f32[4,72,640]{2,1,0:T(8,128)}), f32[4,72,640]{2,1,0:T(8,128)S(1)}, u32[]{:S(2)}, u32[]{:S(2)}) async-start(f32[4,72,640]{2,1,0:T(8,128)} %shard_map.82), calls=%async_computation.3 | async-start | bytes 1474560 | tf_op jit(solution)/shard_map/all_to_all | solution.py:340
  137.6 9.7 %copy-start.20 = (f32[640]{0:T(1024)S(1)}, f32[640]{0:T(1024)}, u32[]{:S(2)}) copy-start(f32[640]{0:T(1024)} %param.9) | copy-start | bytes 7684
  137.6 9.7 %collective-permute-start.6 = (f32[64,640]{1,0:T(8,128)S(1)}, f32[64,640]{1,0:T(8,128)S(1)}, u32[]{:S(2)}, u32[]{:S(2)}) collective-permute-start(f32[64,640]{1,0:T(8,128)S(1)} %get-tuple-element.21), channel_id=1, source_target_pairs={{0,48},{16,0},{32,16},{48,32},{1,49},{17,1},{33,17},{49,33},{2,50}... | collective-permute-start | bytes 491528 | tf_op jit(solution)/shard_map/ppermute | solution.py:335
  142.3 7.6 %collective-permute-start.7 = (f32[64,640]{1,0:T(8,128)S(1)}, f32[64,640]{1,0:T(8,128)S(1)}, u32[]{:S(2)}, u32[]{:S(2)}) collective-permute-start(f32[64,640]{1,0:T(8,128)S(1)} %get-tuple-element.22), channel_id=1, source_target_pairs={{0,32},{16,48},{32,0},{48,16},{1,33},{17,49},{33,1},{49,17},{2,34}... | collective-permute-start | bytes 491528 | tf_op jit(solution)/shard_map/ppermute | solution.py:335
  144.8 7.3 %collective-permute-start.8 = (f32[64,640]{1,0:T(8,128)S(1)}, f32[64,640]{1,0:T(8,128)S(1)}, u32[]{:S(2)}, u32[]{:S(2)}) collective-permute-start(f32[64,640]{1,0:T(8,128)S(1)} %get-tuple-element.23), channel_id=1, source_target_pairs={{0,16},{16,32},{32,48},{48,0},{1,17},{17,33},{33,49},{49,1},{2,18}... | collective-permute-start | bytes 491528 | tf_op jit(solution)/shard_map/ppermute | solution.py:335
  153.0 26.8 %copy-start.11 = (f32[1,10,3,384]{3,0,2,1:T(1,128)S(1)}, f32[1,10,3,384]{3,0,2,1:T(1,128)}, u32[]{:S(2)}) copy-start(f32[1,10,3,384]{3,0,2,1:T(1,128)} %param.7) | copy-start | bytes 138244
  153.0 31.7 %all-to-all-start.4 = ((f32[8,8,128]{2,1,0:T(8,128)}), f32[8,8,128]{2,1,0:T(8,128)S(1)}, u32[]{:S(2)}, u32[]{:S(2)}) async-start(f32[8,8,128]{2,1,0:T(8,128)} %get-tuple-element.27), calls=%async_computation.4 | async-start | bytes 65536 | tf_op jit(solution)/shard_map/all_to_all | solution.py:340
  179.8 5.0 %copy-start.16 = (f32[2,64,640]{2,1,0:T(8,128)S(1)}, f32[2,64,640]{2,1,0:T(8,128)}, u32[]{:S(2)}) copy-start(f32[2,64,640]{2,1,0:T(8,128)} %copy-done.14) | copy-start | bytes 983044
  (13 other events, 11.0 us)

commit v3 on v2

v3 whole, which is shorter than its diff:
```python
import functools
import math

import jax
import jax.numpy as jnp
from jax import lax
from jax.experimental import pallas as pl
from jax.experimental.pallas import tpu as pltpu
from jax.sharding import Mesh
from jax.sharding import PartitionSpec as P

ATT = 128
WINDOW = 128
EPSILON = 1e-06
MOMENTUM_RATE = 0.9
STEP_SIZE = 0.03
PRECISION = lax.Precision.HIGHEST

NZ, NX, NY = 8, 4, 2
BLOCKS = NZ * NX * NY
ROWS = 10
SLICE = 96
LANES = 128
TOK = 64
D = 640
H = 384
NARROW = 8
GROUPS = 2
VMEM_LIMIT = 58 * 1024 * 1024
ROOM = 8 * 1024 * 1024


def dot(left, right, dims=((1,), (0,))):
    return lax.dot_general(
        left, right, (dims, ((), ())), precision=PRECISION, preferred_element_type=jnp.float32
    )


def entry(group, sublane):
    q = group * 8 + sublane
    return (q // 3, q % 3) if q < 3 * ROWS else None


def call(body, outs, micros, *args, lazy=(), after=(), scratch=(), smem=(), fan=(), room=0):
    vmem, anywhere = pl.BlockSpec(memory_space=pltpu.VMEM), pl.BlockSpec(memory_space=pl.ANY)
    held = [outs[n][1:] if n in fan else outs[n] for n in range(len(outs))]
    lazy_shapes = [a.shape if at is None else a.shape[1:] for a, at in lazy]
    sizes = (len(args), len(lazy), len(after), len(outs), len(outs), len(lazy), len(scratch))
    fetches = max(len(lazy), 1)
    sends = sum(outs[n][0] if n in fan else 1 for n in range(len(outs)))

    def kernel(*refs):
        split, at = [], 0
        for size in sizes:
            split.append(refs[at : at + size])
            at += size
        inputs, sources, _, targets, results, fetched, spare = split
        in_sems, out_sems = refs[at:]
        incoming = [
            pltpu.make_async_copy(ref if lazy[n][1] is None else ref.at[lazy[n][1]], fetched[n], in_sems.at[n])
            for n, ref in enumerate(sources)
        ]
        for copy in incoming:
            copy.start()
        outgoing, base = [], 0
        for n in range(len(outs)):
            places = [targets[n].at[j] for j in range(outs[n][0])] if n in fan else [targets[n]]
            outgoing.append(
                [pltpu.make_async_copy(results[n], place, out_sems.at[base + j]) for j, place in enumerate(places)]
            )
            base += len(places)
        sent = set()

        def need():
            for copy in incoming:
                copy.wait()

        def send(n):
            sent.add(n)
            for copy in outgoing[n]:
                copy.start()

        body(inputs, fetched, results, spare, need, send)
        for n in range(len(outs)):
            if n not in sent:
                send(n)
        for copies in outgoing:
            for copy in copies:
                copy.wait()

    return pl.pallas_call(
        kernel,
        out_shape=[jax.ShapeDtypeStruct(s, jnp.float32) for s in outs],
        in_specs=[pl.BlockSpec(memory_space=pltpu.SMEM) if n in smem else vmem for n in range(len(args))]
        + [anywhere] * (len(lazy) + len(after)),
        out_specs=[anywhere] * len(outs),
        scratch_shapes=[
            *(pltpu.VMEM(tuple(s), jnp.float32) for s in (*held, *lazy_shapes, *scratch)),
            pltpu.SemaphoreType.DMA((fetches,)),
            pltpu.SemaphoreType.DMA((sends,)),
        ],
        compiler_params=pltpu.CompilerParams(vmem_limit_bytes=VMEM_LIMIT - room),
        cost_estimate=pl.CostEstimate(flops=int(micros * 1e9), bytes_accessed=10**6, transcendentals=0),
    )(*args, *(a for a, _ in lazy), *after)


def to_column(row):
    n = row.shape[1]
    same = lax.broadcasted_iota(jnp.int32, (n, n), 0) == lax.broadcasted_iota(jnp.int32, (n, n), 1)
    return jnp.sum(jnp.where(same, row, 0.0), axis=1, keepdims=True)


def to_row(column):
    n = column.shape[0]
    same = lax.broadcasted_iota(jnp.int32, (n, n), 0) == lax.broadcasted_iota(jnp.int32, (n, n), 1)
    return jnp.sum(jnp.where(same, column, 0.0), axis=0, keepdims=True)


def own_packs(own_ref, flat_ref):
    flat_ref[24:32, :] = jnp.zeros((8, H), jnp.float32)
    for q in range(3 * ROWS):
        flat_ref[q : q + 1, :] = own_ref[q]
    return [
        jnp.concatenate(
            [flat_ref[8 * g : 8 * g + 8, SLICE * x : SLICE * (x + 1)] for g in range(4)], axis=1
        )
        for x in range(NX)
    ]


def prepare_weights_body(args, lazy, results, scratch, need, send):
    packs = own_packs(args[0], scratch[0])
    for z in range(NZ):
        for x in range(NX):
            for y in range(NY):
                for t in range(3):
                    results[0][(z * NX + x) * NY + y, 8 * t : 8 * t + 8, :] = packs[x][:, LANES * t : LANES * (t + 1)]


def prepare_pairs_body(args, lazy, results, scratch, need, send):
    eta_ref, qkv_ref = args
    results[0][0:TOK, :] = qkv_ref[1, 0]
    results[0][TOK : 2 * TOK, :] = to_column(eta_ref[...]) * qkv_ref[2, 0]


def prepare_queries_body(args, lazy, results, scratch, need, send):
    (mom_ref,), (qkv_ref,), (queries_ref, tail_ref) = args, lazy, results
    packs = own_packs(mom_ref, scratch[0])
    for x in range(NX):
        queries_ref[2 * TOK + 8 * x : 2 * TOK + 8 * x + 8, 0:H] = packs[x]
        queries_ref[2 * TOK + 8 * x : 2 * TOK + 8 * x + 8, H:D] = jnp.zeros((8, D - H), jnp.float32)
    need()
    queries_ref[0:TOK, :] = qkv_ref[0, 0]
    queries_ref[TOK : 2 * TOK, :] = qkv_ref[0, 1]
    send(0)
    for a in range(2):
        tail_ref[a] = qkv_ref[1 + a, 0]


def prepare_tails_body(args, lazy, results, scratch, need, send):
    (position_ref,), (qkv_ref,) = args, lazy
    position = position_ref[0]
    need()
    for distance, ref in zip((1, 2), results):
        for a in range(2):
            ref[a] = jnp.where(position >= BLOCKS - distance, qkv_ref[1 + a, 0], qkv_ref[1 + a, 1])


def widened(part):
    return jnp.concatenate([part, jnp.zeros((part.shape[0], LANES - SLICE), jnp.float32)], axis=1)


def unpack(recv_ref, out_ref, x_stride, y_stride, z_stride):
    for s in range(8):
        for x in range(NX):
            for y in range(NY):
                start = x * x_stride + y * y_stride + s
                rows = jnp.concatenate(
                    [recv_ref[pl.ds(start + 8 * t, NZ, stride=z_stride), :] for t in range(3)], axis=1
                )
                for g in range(4):
                    at = entry(g, s)
                    if at is None:
                        continue
                    r, i = at
                    out_ref[pl.ds(i * D + (x * NY + y) * ROWS + r, NZ, stride=NX * NY * ROWS), :] = widened(
                        rows[:, SLICE * g : SLICE * (g + 1)]
                    )


def pack(in_ref, send_ref, x_stride, y_stride, z_stride):
    for s in range(8):
        for x in range(NX):
            for y in range(NY):
                parts = []
                for g in range(4):
                    at = entry(g, s)
                    if at is None:
                        parts.append(jnp.zeros((NZ, SLICE), jnp.float32))
                        continue
                    r, i = at
                    parts.append(in_ref[pl.ds(i * D + (x * NY + y) * ROWS + r, NZ, stride=NX * NY * ROWS), :][:, :SLICE])
                rows = jnp.concatenate(parts, axis=1)
                start = x * x_stride + y * y_stride + s
                for t in range(3):
                    send_ref[pl.ds(start + 8 * t, NZ, stride=z_stride), :] = rows[:, LANES * t : LANES * (t + 1)]


def token_rows(refs, start):
    return jnp.concatenate([ref[start : start + TOK, :] for ref in refs], axis=0)


def matrix(ref, i):
    return ref[i * D : (i + 1) * D, :]


def gradient_body(args, pairs, results, scratch, need, send):
    (recv_ref,), (w_ref, send_ref), (g_ref,) = args, results, scratch
    unpack(recv_ref, w_ref, 48, 24, 192)
    send(0)
    need()
    keys = token_rows(pairs, 0)
    weighted = token_rows(pairs, TOK)
    pre = dot(keys, jnp.concatenate([matrix(w_ref, 0), matrix(w_ref, 1)], axis=1))
    gate_pre, up_pre = pre[:, :LANES], pre[:, LANES:]
    back = -dot(weighted, matrix(w_ref, 2))
    sigmoid = jax.nn.sigmoid(gate_pre)
    gated = gate_pre * sigmoid
    hidden = gated * up_pre
    gate_back = back * up_pre * sigmoid * (1.0 + gate_pre * (1.0 - sigmoid))
    up_back = back * gated
    both = dot(keys, jnp.concatenate([gate_back, up_back], axis=1), ((0,), (0,)))
    g_ref[0:D, :] = both[:, :LANES]
    g_ref[D : 2 * D, :] = both[:, LANES:]
    g_ref[2 * D : 3 * D, :] = -dot(weighted, hidden, ((0,), (0,)))
    pack(g_ref, send_ref, 24, 96, 192)


def source(x_ref, s):
    return lax.rem(x_ref[0] + NX - s, NX)


def moment_body(args, queries, results, scratch, need, send):
    (x_ref, recv_ref), (own_ref,) = args, results
    total = recv_ref[0]
    for j in range(1, NZ * NY):
        total = total + recv_ref[j]
    own_ref[...] = total
    need()
    mine = pl.ds(pl.multiple_of(2 * TOK + 8 * x_ref[0], 8), 8)
    for s, ref in enumerate(queries):
        old = ref[mine, :]
        old = jnp.concatenate([old[:, LANES * t : LANES * (t + 1)] for t in range(3)], axis=0)
        rows = pl.ds(pl.multiple_of(24 * source(x_ref, s), 8), 24)
        own_ref[rows, :] = own_ref[rows, :] + MOMENTUM_RATE * old


def hidden_of(inputs, w1, w3):
    pre = dot(inputs, jnp.concatenate([w1, w3], axis=1))
    gate_pre, up_pre = pre[:, :LANES], pre[:, LANES:]
    return gate_pre * jax.nn.sigmoid(gate_pre) * up_pre


def first_read_body(args, lazy, results, scratch, need, send):
    need()
    *queries, w_ref = lazy
    hidden = hidden_of(token_rows(queries, 0), matrix(w_ref, 0), matrix(w_ref, 1))
    partial = dot(hidden, matrix(w_ref, 2), ((1,), (1,)))
    for s in range(NX):
        results[s][...] = partial[s * TOK : (s + 1) * TOK]


def renormalized(weights, moment):
    rate = STEP_SIZE / jnp.sqrt(jnp.mean(moment * moment, axis=0, keepdims=True) + EPSILON)
    moved = weights - moment * rate
    ratio = jnp.sqrt(jnp.mean(weights * weights, axis=0, keepdims=True) + EPSILON) / jnp.sqrt(
        jnp.mean(moved * moved, axis=0, keepdims=True) + EPSILON
    )
    return moved * ratio, rate, ratio


def second_read_body(args, lazy, results, scratch, need, send):
    (x_ref, recv_ref), (*queries, w_ref, moment_ref), (send_ref,), (m_ref,) = args, lazy, results, scratch
    unpack(recv_ref, m_ref, 24, 96, 192)
    need()
    new1, rate1, ratio1 = renormalized(matrix(w_ref, 0), matrix(m_ref, 0))
    new3, rate3, ratio3 = renormalized(matrix(w_ref, 1), matrix(m_ref, 1))
    new2, rate2, ratio2 = renormalized(matrix(w_ref, 2), matrix(m_ref, 2))
    hidden = hidden_of(token_rows(queries, TOK), new1, new3)
    partial = dot(hidden, new2, ((1,), (1,)))
    stats = [rate1, rate3, rate2, ratio1, ratio3, ratio2, jnp.zeros((2, LANES), jnp.float32)]
    stats = jnp.concatenate(stats, axis=0)
    for x in range(NX):
        tail = [stats, *(moment_ref[24 * x + 8 * t : 24 * x + 8 * t + 8, :] for t in range(3))]
        tail.append(jnp.zeros((8, LANES), jnp.float32))
        send_ref[x, TOK : TOK + 8, :] = jnp.concatenate(tail, axis=1)
    for s in range(NX):
        send_ref[source(x_ref, s), 0:TOK, :] = partial[s * TOK : (s + 1) * TOK]


def squares_body(args, lazy, results, scratch, need, send):
    (second_ref,), (readout_ref, send_ref) = args, results
    need()
    first = lazy[0][...] + lazy[1][...] + lazy[2][...] + lazy[3][...]
    second = second_ref[0, 0:TOK, :]
    for x in range(1, NX):
        second = second + second_ref[x, 0:TOK, :]
    readout_ref[0] = first
    readout_ref[1] = second
    row = jnp.concatenate(
        [to_row(jnp.sum(total * total, axis=1, keepdims=True)) for total in (first, second)], axis=1
    )
    send_ref[...] = jnp.broadcast_to(row, (8, GROUPS * TOK))


def own_rows_body(args, lazy, results, scratch, need, send):
    (second_ref, fw_ref), (new_w_ref, new_m_ref), (flat_ref,) = args, results, scratch
    for g in range(4):
        flat_ref[8 * g : 8 * g + 8, :] = jnp.concatenate(
            [
                second_ref[x, TOK : TOK + 8, LANES + SLICE * g : LANES + SLICE * (g + 1)]
                for x in range(NX)
            ],
            axis=1,
        )
    stats = jnp.concatenate([second_ref[x, TOK : TOK + 8, 0:SLICE] for x in range(NX)], axis=1)
    for q in range(3 * ROWS):
        i = q % 3
        moment = flat_ref[q : q + 1, :]
        new_m_ref[q] = moment
        new_w_ref[q] = (fw_ref[q] - moment * stats[i : i + 1]) * stats[3 + i : 4 + i]


def mix_body(args, lazy, results, scratch, need, send):
    (recv_ref, gain_ref), (readout_ref, *attended_refs), (mixed_ref,) = args, lazy, results
    total = recv_ref[0, 0:1, :]
    for n in range(1, NARROW):
        total = total + recv_ref[n, 0:1, :]
    scale = to_column(1.0 / jnp.sqrt(total / (D * NARROW) + EPSILON))
    need()
    for c in range(GROUPS):
        mixed_ref[c] = attended_refs[c][...] + gain_ref[...] * (readout_ref[c] * scale[c * TOK : (c + 1) * TOK])


def attention_body(c, args, lazy, results, scratch, need, send):
    (position_ref,), (qkv_ref, near_ref, far_ref), (out_ref,) = args, lazy, results
    position = position_ref[0]
    row = lax.broadcasted_iota(jnp.int32, (TOK, 3 * TOK), 0) + 2 * TOK
    col = lax.broadcasted_iota(jnp.int32, (TOK, 3 * TOK), 1)
    allowed = (row - col >= 0) & (row - col < WINDOW)
    if c == 0:
        first = jnp.where(position >= 2, 0, jnp.where(position >= 1, TOK, 2 * TOK))
        allowed = allowed & (col >= first)
    need()
    for h in range(D // ATT):
        at = slice(h * ATT, (h + 1) * ATT)
        keys, values = (
            jnp.concatenate([far_ref[a, :, at], near_ref[a, :, at], qkv_ref[1 + a, c, :, at]], axis=0)
            for a in range(2)
        )
        scores = dot(qkv_ref[0, c, :, at], keys, ((1,), (1,))) * (1.0 / math.sqrt(ATT))
        scores = jnp.where(allowed, scores, -1e30)
        weights = jnp.exp(scores - jnp.max(scores, axis=1, keepdims=True))
        weights = weights / jnp.sum(weights, axis=1, keepdims=True)
        out_ref[:, at] = dot(weights, values)


def behind(block, distance):
    axes = ("z", "x", "yh")
    return lax.ppermute(block, axes, [((i - distance) % BLOCKS, i) for i in range(BLOCKS)])


def from_neighbours(block):
    return [block] + [lax.ppermute(block, "x", [((i - s) % NX, i) for i in range(NX)]) for s in range(1, NX)]


def back_to_neighbours(blocks):
    return [blocks[0]] + [
        lax.ppermute(blocks[s], "x", [(i, (i - s) % NX) for i in range(NX)]) for s in range(1, NX)
    ]


def exchange(pieces, axes):
    return lax.all_to_all(pieces, axes, split_axis=0, concat_axis=0, tiled=True)


def scalar(value):
    return jnp.reshape(value, (1,)).astype(jnp.int32)


def whole(*arrays):
    return [(a, None) for a in arrays]


def local(qkv, eta, fast_weights, momentum, ttt_gain):
    own_weights, own_moment = fast_weights.reshape(3 * ROWS, 1, H), momentum.reshape(3 * ROWS, 1, H)
    x = lax.axis_index("x")
    position = scalar((lax.axis_index("z") * NX + x) * NY + lax.axis_index("yh"))
    x = scalar(x)
    everyone, cross = ("z", "x", "yh"), ("z", "yh")
    (send1,) = call(prepare_weights_body, [(BLOCKS, 24, LANES)], 1, own_weights, scratch=[(32, H)])
    (pairs,) = call(prepare_pairs_body, [(2 * TOK, D)], 1, eta, qkv)
    recv1 = exchange(send1, everyone).reshape(BLOCKS * 24, LANES)
    pairs = from_neighbours(pairs)
    weights, send2 = call(
        gradient_body, [(3 * D, LANES), (BLOCKS * 24, LANES)], 5, recv1, lazy=whole(*pairs),
        scratch=[(3 * D, LANES)], room=ROOM - 1024 * 1024,
    )
    recv2 = exchange(send2.reshape(NZ * NY, NX * 24, LANES), cross)
    queries, tail = call(
        prepare_queries_body, [(2 * TOK + 32, D), (2, TOK, D)], 1, own_moment, lazy=whole(qkv), scratch=[(32, H)],
        after=(weights,),
    )
    queries = from_neighbours(queries)
    near0, far0 = behind(tail, 1), behind(tail, 2)
    (send3,) = call(
        moment_body, [(NZ * NY, NX * 24, LANES)], 2, x, recv2, lazy=whole(*queries), smem=(0,), fan=(0,), room=ROOM
    )
    recv3 = exchange(send3, cross).reshape(BLOCKS * 24, LANES)
    near1, far1 = call(
        prepare_tails_body, [(2, TOK, D)] * 2, 1, position, lazy=whole(qkv), smem=(0,), after=(send3,)
    )
    near1, far1 = behind(near1, 1), behind(far1, 2)
    first = back_to_neighbours(
        call(first_read_body, [(TOK, D)] * NX, 4, lazy=whole(*queries, weights), after=(send3,))
    )
    (attended0,) = call(
        functools.partial(attention_body, 0), [(TOK, D)], 4, position, lazy=whole(qkv, near0, far0), smem=(0,),
        after=(send3,),
    )
    (send_second,) = call(
        second_read_body, [(NX, TOK + 8, D)], 5, x, recv3,
        lazy=[*whole(*queries, weights), (send3, 0)], scratch=[(3 * D, LANES)], smem=(0,),
        after=(*first[1:], attended0), room=ROOM,
    )
    second = exchange(send_second, "x")
    (attended1,) = call(
        functools.partial(attention_body, 1), [(TOK, D)], 4, position, lazy=whole(qkv, near1, far1), smem=(0,),
        after=(send_second,),
    )
    readout, send5 = call(
        squares_body, [(GROUPS, TOK, D), (NARROW, 8, GROUPS * TOK)], 1, second, lazy=whole(*first), fan=(1,),
        after=(attended1,), room=ROOM,
    )
    recv5 = exchange(send5, "narrow")
    new_weights, new_moment = call(
        own_rows_body, [(3 * ROWS, 1, H), (3 * ROWS, 1, H)], 1, second, own_weights, scratch=[(32, H)],
        after=(send5,),
    )
    (mixed,) = call(
        mix_body, [(GROUPS, TOK, D)], 1, recv5, ttt_gain.reshape(1, D), lazy=whole(readout, attended0, attended1),
        after=(new_weights,), room=ROOM,
    )
    return mixed, new_weights.reshape(1, ROWS, 3, H), new_moment.reshape(1, ROWS, 3, H)


def solution(mesh):
    fine = Mesh(mesh.devices.reshape(NZ, NX, NY, NARROW), ("z", "x", "yh", "narrow"))
    wide = ("z", "x", "yh")
    return jax.shard_map(
        local,
        mesh=fine,
        in_specs=(
            P(None, None, wide, "narrow"),
            P("narrow", wide),
            P("narrow", wide, None, None),
            P("narrow", wide, None, None),
            P("narrow"),
        ),
        out_specs=(
            P(None, wide, "narrow"),
            P("narrow", wide, None, None),
            P("narrow", wide, None, None),
        ),
        check_vma=False,
    )
```

time: 188 us -> 210 us (1.12); the launches traced: 187 us -> 206 us
  Pallas kernels: 29.2 us -> 44.4 us
  waiting for transfers between devices: 33 us -> 47.9 us
  local copies, waits for them, and re-layouts: 14.2 us -> 4.98 us
    ppermute x6, waiting for transfers between devices: 13.7 us -> 30.8 us  [from_neighbours(): lax.ppermute(block, 'x', [((i - s) % NX, i) for i in range(NX)])]
    pallas_call x10 -> x13, Pallas kernels: 29.2 us -> 44.4 us  [call(): pl.pallas_call(kernel, out_shape=[jax.ShapeDtypeStruct(s, jnp.float32) fo...]
    ppermute x2 -> x4, waiting for transfers between devices: 0.01 us -> 12.9 us  [behind(): lax.ppermute(block, axes, [((i - distance) % BLOCKS, i) for i in range(BL...]
    all_to_all x5, waiting for transfers between devices: 14.5 us -> 4.24 us  [exchange(): return lax.all_to_all(pieces, axes, split_axis=0, concat_axis=0, tiled=True)]
    all_to_all x5, starting transfers between devices: 71.4 us -> 61.9 us  [exchange(): return lax.all_to_all(pieces, axes, split_axis=0, concat_axis=0, tiled=True)]
    unnamed x42, local copies, waits for them, and re-layouts: 13.3 us -> 4.98 us
    ppermute x2 -> x4, starting transfers between devices: 9.18 us -> 16.5 us  [behind(): lax.ppermute(block, axes, [((i - distance) % BLOCKS, i) for i in range(BL...]
    ppermute x3, waiting for transfers between devices: 4.75 us -> 0.01 us  [back_to_neighbours(): lax.ppermute(blocks[s], 'x', [(i, (i - s) % NX) for i in range(NX)])]
  transfers between devices with their start and end apart: 16 -> 18, of which waited for: 6 -> 10; matrix products, arithmetic and copies ran while one was open for 0% -> 0% of each run, Pallas kernels for 10% -> 15%
where the time goes in v3:
time: 210 us; the launch traced here: 206 us
  starting transfers between devices  107 us (51%)
  waiting for transfers between devices  47.9 us (23%)
  Pallas kernels  44.4 us (21%)
  local copies, waits for them, and re-layouts  4.98 us (2%)
    all_to_all x5, starting transfers between devices, exchange(): return lax.all_to_all(pieces, axes, split_axis=0, concat_axis=0, tiled=True)  61.9 us
    pallas_call x13, Pallas kernels, call(): pl.pallas_call(kernel, out_shape=[jax.ShapeDtypeStruct(s, jnp.float32) fo...  44.4 us
    ppermute x6, waiting for transfers between devices, from_neighbours(): lax.ppermute(block, 'x', [((i - s) % NX, i) for i in range(NX)])  30.8 us
    ppermute x6, starting transfers between devices, from_neighbours(): lax.ppermute(block, 'x', [((i - s) % NX, i) for i in range(NX)])  21.1 us
    ppermute x4, starting transfers between devices, behind(): lax.ppermute(block, axes, [((i - distance) % BLOCKS, i) for i in range(BL...  16.5 us
    ppermute x4, waiting for transfers between devices, behind(): lax.ppermute(block, axes, [((i - distance) % BLOCKS, i) for i in range(BL...  12.9 us
    ppermute x3, starting transfers between devices, back_to_neighbours(): lax.ppermute(blocks[s], 'x', [(i, (i - s) % NX) for i in range(NX)])  7.74 us
    unnamed x42, local copies, waits for them, and re-layouts  4.98 us
  transfers between devices with their start and end apart: 18, of which 10 were waited for; matrix products, arithmetic and copies ran while one was open for 0% of the time, Pallas kernels for 15%

profile of v3, /device:TPU:1, one launch (start us, length us, event | category | flops | bytes accessed | tf_op | source)
XLA Modules:
  0.0 205.9 jit_solution(13105123639104763414)
XLA Ops:
  2.5 19.6 %all-to-all-start = ((f32[64,24,128]{2,1,0:T(8,128)}), f32[64,24,128]{2,1,0:T(8,128)S(1)}, u32[]{:S(2)}, u32[]{:S(2)}) async-start(f32[64,24,128]{2,1,0:T(8,128)} %shard_map.76), calls=%async_computation | async-start | bytes 1572864 | tf_op jit(solution)/shard_map/all_to_all | solution.py:384
  24.2 2.9 %collective-permute-start = (f32[128,640]{1,0:T(8,128)}, f32[128,640]{1,0:T(8,128)S(1)}, u32[]{:S(2)}, u32[]{:S(2)}) collective-permute-start(f32[128,640]{1,0:T(8,128)} %shard_map.77.refs_1_), channel_id=1, source_target_pairs={{48,0},{0,16},{16,32},{32,48},{49,1},{1,17},{17,33},{33,49},{50,2}... | collective-permute-start | bytes 983048 | tf_op jit(solution)/shard_map/ppermute | solution.py:374
  27.1 4.3 %collective-permute-start.1 = (f32[128,640]{1,0:T(8,128)}, f32[128,640]{1,0:T(8,128)S(1)}, u32[]{:S(2)}, u32[]{:S(2)}) collective-permute-start(f32[128,640]{1,0:T(8,128)} %shard_map.77.refs_1_), channel_id=1, source_target_pairs={{32,0},{48,16},{0,32},{16,48},{33,1},{49,17},{1,33},{17,49},{34,2}... | collective-permute-start | bytes 983048 | tf_op jit(solution)/shard_map/ppermute | solution.py:374
  31.4 3.1 %collective-permute-start.2 = (f32[128,640]{1,0:T(8,128)}, f32[128,640]{1,0:T(8,128)S(1)}, u32[]{:S(2)}, u32[]{:S(2)}) collective-permute-start(f32[128,640]{1,0:T(8,128)} %shard_map.77.refs_1_), channel_id=1, source_target_pairs={{16,0},{32,16},{48,32},{0,48},{17,1},{33,17},{49,33},{1,49},{18,2}... | collective-permute-start | bytes 983048 | tf_op jit(solution)/shard_map/ppermute | solution.py:374
  34.5 7.5 %collective-permute-done.refs_2_ = f32[128,640]{1,0:T(8,128)S(1)} collective-permute-done((f32[128,640]{1,0:T(8,128)}, f32[128,640]{1,0:T(8,128)S(1)}, u32[]{:S(2)}, u32[]{:S(2)}) %collective-permute-start) | collective-permute-done | bytes 327712 | tf_op jit(solution)/shard_map/ppermute | solution.py:374
  42.0 8.9 %collective-permute-done.1.refs_3_ = f32[128,640]{1,0:T(8,128)S(1)} collective-permute-done((f32[128,640]{1,0:T(8,128)}, f32[128,640]{1,0:T(8,128)S(1)}, u32[]{:S(2)}, u32[]{:S(2)}) %collective-permute-start.1) | collective-permute-done | bytes 327712 | tf_op jit(solution)/shard_map/ppermute | solution.py:374
  52.0 5.5 %shard_map.78 = (f32[1920,128]{1,0:T(8,128)}, f32[1536,128]{1,0:T(8,128)}) custom-call(f32[1536,128]{1,0:T(8,128)S(1)} %bitcast.10, f32[128,640]{1,0:T(8,128)S(1)} %copy-done.9, f32[128,640]{1,0:T(8,128)S(1)} %collective-permute-done.refs_2_, f32[128,640]{1,0:T(8,128)S(1)} %collective-permute-done.1.refs_3_, f32[128,640]{1,0:T(8,128)S(1)} %collective-permute-done.2.refs_4_), custom_call_target="tpu_custom_call" | custom-call | flops 5000000000 | bytes 1000000 | tf_op jit(solution)/shard_map/pallas_call | solution.py:91
  57.5 9.9 %all-to-all-start.1 = ((f32[16,96,128]{2,1,0:T(8,128)}), f32[16,96,128]{2,1,0:T(8,128)S(1)}, u32[]{:S(2)}, u32[]{:S(2)}) async-start(f32[16,96,128]{2,1,0:T(8,128)} %bitcast.3), calls=%async_computation.1 | async-start | bytes 1572864 | tf_op jit(solution)/shard_map/all_to_all | solution.py:384
  67.5 2.9 %shard_map.79 = (f32[160,640]{1,0:T(8,128)}, f32[2,64,640]{2,1,0:T(8,128)}) custom-call(f32[30,1,384]{2,1,0:T(1,128)} %bitcast.12, f32[3,2,64,640]{3,2,1,0:T(8,128)} %refs_1_.9, f32[1920,128]{1,0:T(8,128)} %get-tuple-element.18.refs_2_.refs_4_.refs_6_), custom_call_target="tpu_custom_call" | custom-call | flops 1000000000 | bytes 1000000 | tf_op jit(solution)/shard_map/pallas_call | solution.py:91
  70.4 4.6 %collective-permute-start.3 = (f32[160,640]{1,0:T(8,128)}, f32[160,640]{1,0:T(8,128)S(1)}, u32[]{:S(2)}, u32[]{:S(2)}) collective-permute-start(f32[160,640]{1,0:T(8,128)} %get-tuple-element.19.refs_2_.refs_0_), channel_id=1, source_target_pairs={{48,0},{0,16},{16,32},{32,48},{49,1},{1,17},{17,33},{33,49},{50,2}... | collective-permute-start | bytes 1228808 | tf_op jit(solution)/shard_map/ppermute | solution.py:374
  77.6 3.6 %collective-permute-start.5 = (f32[160,640]{1,0:T(8,128)}, f32[160,640]{1,0:T(8,128)S(1)}, u32[]{:S(2)}, u32[]{:S(2)}) collective-permute-start(f32[160,640]{1,0:T(8,128)} %get-tuple-element.19.refs_2_.refs_0_), channel_id=1, source_target_pairs={{16,0},{32,16},{48,32},{0,48},{17,1},{33,17},{49,33},{1,49},{18,2}... | collective-permute-start | bytes 1228808 | tf_op jit(solution)/shard_map/ppermute | solution.py:374
  83.4 9.6 %collective-permute-done.4.refs_4_.refs_2_ = f32[160,640]{1,0:T(8,128)S(1)} collective-permute-done((f32[160,640]{1,0:T(8,128)}, f32[160,640]{1,0:T(8,128)S(1)}, u32[]{:S(2)}, u32[]{:S(2)}) %collective-permute-start.4) | collective-permute-done | bytes 409632 | tf_op jit(solution)/shard_map/ppermute | solution.py:374
  98.6 11.6 %all-to-all-start.2 = ((f32[16,96,128]{2,1,0:T(8,128)}), f32[16,96,128]{2,1,0:T(8,128)S(1)}, u32[]{:S(2)}, u32[]{:S(2)}) async-start(f32[16,96,128]{2,1,0:T(8,128)} %shard_map.80.refs_5_.refs_4_.refs_7_.refs_2_), calls=%async_computation.2 | async-start | bytes 1572864 | tf_op jit(solution)/shard_map/all_to_all | solution.py:384
  110.2 5.2 %collective-permute-start.10 = (f32[2,64,640]{2,1,0:T(8,128)S(1)}, f32[2,64,640]{2,1,0:T(8,128)S(1)}, u32[]{:S(2)}, u32[]{:S(2)}) collective-permute-start(f32[2,64,640]{2,1,0:T(8,128)S(1)} %copy-done.17), channel_id=1, source_target_pairs={{496,0},{504,8},{0,16},{8,24},{16,32},{24,40},{32,48},{40,56},{48,... | collective-permute-start | bytes 983048 | tf_op jit(solution)/shard_map/ppermute | solution.py:370
  115.5 7.2 %collective-permute-start.9 = (f32[2,64,640]{2,1,0:T(8,128)S(1)}, f32[2,64,640]{2,1,0:T(8,128)S(1)}, u32[]{:S(2)}, u32[]{:S(2)}) collective-permute-start(f32[2,64,640]{2,1,0:T(8,128)S(1)} %copy-done.17), channel_id=1, source_target_pairs={{504,0},{0,8},{8,16},{16,24},{24,32},{32,40},{40,48},{48,56},{56,6... | collective-permute-start | bytes 983048 | tf_op jit(solution)/shard_map/ppermute | solution.py:370
  122.6 5.0 %shard_map.81 = (f32[64,640]{1,0:T(8,128)}, f32[64,640]{1,0:T(8,128)}, f32[64,640]{1,0:T(8,128)}, f32[64,640]{1,0:T(8,128)}) custom-call(f32[160,640]{1,0:T(8,128)} %get-tuple-element.19.refs_2_.refs_0_, f32[160,640]{1,0:T(8,128)} %copy-done.3, f32[160,640]{1,0:T(8,128)} %copy-done.5, f32[160,640]{1,0:T(8,128)} %copy-done.7, ...), custom_call_target="tpu_custom_call" | custom-call | flops 4000000000 | bytes 1000000 | tf_op jit(solution)/shard_map/pallas_call | solution.py:91
  129.8 3.5 %collective-permute-start.7 = (f32[64,640]{1,0:T(8,128)}, f32[64,640]{1,0:T(8,128)S(1)}, u32[]{:S(2)}, u32[]{:S(2)}) collective-permute-start(f32[64,640]{1,0:T(8,128)} %get-tuple-element.21), channel_id=1, source_target_pairs={{0,32},{16,48},{32,0},{48,16},{1,33},{17,49},{33,1},{49,17},{2,34}... | collective-permute-start | bytes 491528 | tf_op jit(solution)/shard_map/ppermute | solution.py:379
  137.5 11.9 %collective-permute-done.10.refs_3_ = f32[2,64,640]{2,1,0:T(8,128)S(1)} collective-permute-done((f32[2,64,640]{2,1,0:T(8,128)S(1)}, f32[2,64,640]{2,1,0:T(8,128)S(1)}, u32[]{:S(2)}, u32[]{:S(2)}) %collective-permute-start.10) | collective-permute-done | bytes 327712 | tf_op jit(solution)/shard_map/ppermute | solution.py:370
  153.6 5.8 %shard_map.82.refs_11_.refs_3_ = f32[64,640]{1,0:T(8,128)} custom-call(s32[1]{0:T(128)} %bitcast.6.refs_0_, f32[3,2,64,640]{3,2,1,0:T(8,128)} %refs_1_.9, f32[2,64,640]{2,1,0:T(8,128)} %copy-done.20, f32[2,64,640]{2,1,0:T(8,128)} %copy-done.19, f32[16,96,128]{2,1,0:T(8,128)} %shard_map.80.refs_5_.refs_4_.refs_7_.refs_2_), custom_call_target="tpu_custom_call" | custom-call | flops 4000000000 | bytes 1000000 | tf_op jit(solution)/shard_map/pallas_call | solution.py:91
  160.4 6.3 %shard_map.83.refs_4_ = f32[4,72,640]{2,1,0:T(8,128)} custom-call(s32[1]{0:T(128)} %bitcast.refs_0_, f32[1536,128]{1,0:T(8,128)S(1)} %bitcast.9, f32[160,640]{1,0:T(8,128)S(1)} %copy-done.2, f32[160,640]{1,0:T(8,128)S(1)} %copy-done.4, f32[160,640]{1,0:T(8,128)S(1)} %copy-done.6, f32[160,640]{1,0:T(8,128)S(1)} %copy-done.8, ...), custom_call_target="tpu_custom_call" | custom-call | flops 5000000000 | bytes 1000000 | tf_op jit(solution)/shard_map/pallas_call | solution.py:91
  166.7 3.9 %all-to-all-start.3 = ((f32[4,72,640]{2,1,0:T(8,128)}), f32[4,72,640]{2,1,0:T(8,128)S(1)}, u32[]{:S(2)}, u32[]{:S(2)}) async-start(f32[4,72,640]{2,1,0:T(8,128)} %shard_map.83.refs_4_), calls=%async_computation.3 | async-start | bytes 1474560 | tf_op jit(solution)/shard_map/all_to_all | solution.py:384
  171.7 5.8 %shard_map.85.refs_5_.refs_4_ = f32[64,640]{1,0:T(8,128)} custom-call(s32[1]{0:T(128)} %bitcast.6.refs_0_, f32[3,2,64,640]{3,2,1,0:T(8,128)} %refs_1_.9, f32[2,64,640]{2,1,0:T(8,128)} %copy-done.18, f32[2,64,640]{2,1,0:T(8,128)} %collective-permute-done.12.refs_3_, f32[4,72,640]{2,1,0:T(8,128)} %shard_map.83.refs_4_), custom_call_target="tpu_custom_call" | custom-call | flops 4000000000 | bytes 1000000 | tf_op jit(solution)/shard_map/pallas_call | solution.py:91
  181.6 16.9 %all-to-all-start.4 = ((f32[8,8,128]{2,1,0:T(8,128)}), f32[8,8,128]{2,1,0:T(8,128)S(1)}, u32[]{:S(2)}, u32[]{:S(2)}) async-start(f32[8,8,128]{2,1,0:T(8,128)} %get-tuple-element.27.refs_2_), calls=%async_computation.4 | async-start | bytes 65536 | tf_op jit(solution)/shard_map/all_to_all | solution.py:384
  200.5 3.0 %all-to-all-done.4.refs_0_ = f32[8,8,128]{2,1,0:T(8,128)S(1)} async-done(((f32[8,8,128]{2,1,0:T(8,128)}), f32[8,8,128]{2,1,0:T(8,128)S(1)}, u32[]{:S(2)}, u32[]{:S(2)}) %all-to-all-start.4) | async-done | bytes 32800 | tf_op jit(solution)/shard_map/all_to_all | solution.py:384
  (68 shorter events, 36.2 us)
Async XLA Ops:
  2.5 48.6 %all-to-all-start = ((f32[64,24,128]{2,1,0:T(8,128)}), f32[64,24,128]{2,1,0:T(8,128)S(1)}, u32[]{:S(2)}, u32[]{:S(2)}) async-start(f32[64,24,128]{2,1,0:T(8,128)} %shard_map.76), calls=%async_computation | async-start | bytes 1572864 | tf_op jit(solution)/shard_map/all_to_all | solution.py:384
  24.2 17.8 %collective-permute-start = (f32[128,640]{1,0:T(8,128)}, f32[128,640]{1,0:T(8,128)S(1)}, u32[]{:S(2)}, u32[]{:S(2)}) collective-permute-start(f32[128,640]{1,0:T(8,128)} %shard_map.77.refs_1_), channel_id=1, source_target_pairs={{48,0},{0,16},{16,32},{32,48},{49,1},{1,17},{17,33},{33,49},{50,2}... | collective-permute-start | bytes 983048 | tf_op jit(solution)/shard_map/ppermute | solution.py:374
  27.1 23.8 %collective-permute-start.1 = (f32[128,640]{1,0:T(8,128)}, f32[128,640]{1,0:T(8,128)S(1)}, u32[]{:S(2)}, u32[]{:S(2)}) collective-permute-start(f32[128,640]{1,0:T(8,128)} %shard_map.77.refs_1_), channel_id=1, source_target_pairs={{32,0},{48,16},{0,32},{16,48},{33,1},{49,17},{1,33},{17,49},{34,2}... | collective-permute-start | bytes 983048 | tf_op jit(solution)/shard_map/ppermute | solution.py:374
  31.4 19.6 %collective-permute-start.2 = (f32[128,640]{1,0:T(8,128)}, f32[128,640]{1,0:T(8,128)S(1)}, u32[]{:S(2)}, u32[]{:S(2)}) collective-permute-start(f32[128,640]{1,0:T(8,128)} %shard_map.77.refs_1_), channel_id=1, source_target_pairs={{16,0},{32,16},{48,32},{0,48},{17,1},{33,17},{49,33},{1,49},{18,2}... | collective-permute-start | bytes 983048 | tf_op jit(solution)/shard_map/ppermute | solution.py:374
  57.5 37.9 %all-to-all-start.1 = ((f32[16,96,128]{2,1,0:T(8,128)}), f32[16,96,128]{2,1,0:T(8,128)S(1)}, u32[]{:S(2)}, u32[]{:S(2)}) async-start(f32[16,96,128]{2,1,0:T(8,128)} %bitcast.3), calls=%async_computation.1 | async-start | bytes 1572864 | tf_op jit(solution)/shard_map/all_to_all | solution.py:384
  70.4 13.0 %collective-permute-start.3 = (f32[160,640]{1,0:T(8,128)}, f32[160,640]{1,0:T(8,128)S(1)}, u32[]{:S(2)}, u32[]{:S(2)}) collective-permute-start(f32[160,640]{1,0:T(8,128)} %get-tuple-element.19.refs_2_.refs_0_), channel_id=1, source_target_pairs={{48,0},{0,16},{16,32},{32,48},{49,1},{1,17},{17,33},{33,49},{50,2}... | collective-permute-start | bytes 1228808 | tf_op jit(solution)/shard_map/ppermute | solution.py:374
  75.0 18.0 %collective-permute-start.4 = (f32[160,640]{1,0:T(8,128)}, f32[160,640]{1,0:T(8,128)S(1)}, u32[]{:S(2)}, u32[]{:S(2)}) collective-permute-start(f32[160,640]{1,0:T(8,128)} %get-tuple-element.19.refs_2_.refs_0_), channel_id=1, source_target_pairs={{32,0},{48,16},{0,32},{16,48},{33,1},{49,17},{1,33},{17,49},{34,2}... | collective-permute-start | bytes 1228808 | tf_op jit(solution)/shard_map/ppermute | solution.py:374
  77.6 17.9 %collective-permute-start.5 = (f32[160,640]{1,0:T(8,128)}, f32[160,640]{1,0:T(8,128)S(1)}, u32[]{:S(2)}, u32[]{:S(2)}) collective-permute-start(f32[160,640]{1,0:T(8,128)} %get-tuple-element.19.refs_2_.refs_0_), channel_id=1, source_target_pairs={{16,0},{32,16},{48,32},{0,48},{17,1},{33,17},{49,33},{1,49},{18,2}... | collective-permute-start | bytes 1228808 | tf_op jit(solution)/shard_map/ppermute | solution.py:374
  83.4 15.2 %copy-start.3 = (f32[160,640]{1,0:T(8,128)}, f32[160,640]{1,0:T(8,128)S(1)}, u32[]{:S(2)}) copy-start(f32[160,640]{1,0:T(8,128)S(1)} %collective-permute-done.3.refs_3_.refs_1_) | copy-start | bytes 1228804
  98.6 11.6 %copy-start.17 = (f32[2,64,640]{2,1,0:T(8,128)S(1)}, f32[2,64,640]{2,1,0:T(8,128)}, u32[]{:S(2)}) copy-start(f32[2,64,640]{2,1,0:T(8,128)} %get-tuple-element.23) | copy-start | bytes 983044
  98.6 60.8 %all-to-all-start.2 = ((f32[16,96,128]{2,1,0:T(8,128)}), f32[16,96,128]{2,1,0:T(8,128)S(1)}, u32[]{:S(2)}, u32[]{:S(2)}) async-start(f32[16,96,128]{2,1,0:T(8,128)} %shard_map.80.refs_5_.refs_4_.refs_7_.refs_2_), calls=%async_computation.2 | async-start | bytes 1572864 | tf_op jit(solution)/shard_map/all_to_all | solution.py:384
  110.2 39.2 %collective-permute-start.10 = (f32[2,64,640]{2,1,0:T(8,128)S(1)}, f32[2,64,640]{2,1,0:T(8,128)S(1)}, u32[]{:S(2)}, u32[]{:S(2)}) collective-permute-start(f32[2,64,640]{2,1,0:T(8,128)S(1)} %copy-done.17), channel_id=1, source_target_pairs={{496,0},{504,8},{0,16},{8,24},{16,32},{24,40},{32,48},{40,56},{48,... | collective-permute-start | bytes 983048 | tf_op jit(solution)/shard_map/ppermute | solution.py:370
  115.5 35.8 %collective-permute-start.9 = (f32[2,64,640]{2,1,0:T(8,128)S(1)}, f32[2,64,640]{2,1,0:T(8,128)S(1)}, u32[]{:S(2)}, u32[]{:S(2)}) collective-permute-start(f32[2,64,640]{2,1,0:T(8,128)S(1)} %copy-done.17), channel_id=1, source_target_pairs={{504,0},{0,8},{8,16},{16,24},{24,32},{32,40},{40,48},{48,56},{56,6... | collective-permute-start | bytes 983048 | tf_op jit(solution)/shard_map/ppermute | solution.py:370
  127.6 31.8 %collective-permute-start.6 = (f32[64,640]{1,0:T(8,128)}, f32[64,640]{1,0:T(8,128)S(1)}, u32[]{:S(2)}, u32[]{:S(2)}) collective-permute-start(f32[64,640]{1,0:T(8,128)} %get-tuple-element.20), channel_id=1, source_target_pairs={{0,48},{16,0},{32,16},{48,32},{1,49},{17,1},{33,17},{49,33},{2,50}... | collective-permute-start | bytes 491528 | tf_op jit(solution)/shard_map/ppermute | solution.py:379
  129.8 29.6 %collective-permute-start.7 = (f32[64,640]{1,0:T(8,128)}, f32[64,640]{1,0:T(8,128)S(1)}, u32[]{:S(2)}, u32[]{:S(2)}) collective-permute-start(f32[64,640]{1,0:T(8,128)} %get-tuple-element.21), channel_id=1, source_target_pairs={{0,32},{16,48},{32,0},{48,16},{1,33},{17,49},{33,1},{49,17},{2,34}... | collective-permute-start | bytes 491528 | tf_op jit(solution)/shard_map/ppermute | solution.py:379
  133.3 26.2 %collective-permute-start.8 = (f32[64,640]{1,0:T(8,128)}, f32[64,640]{1,0:T(8,128)S(1)}, u32[]{:S(2)}, u32[]{:S(2)}) collective-permute-start(f32[64,640]{1,0:T(8,128)} %get-tuple-element.22), channel_id=1, source_target_pairs={{0,16},{16,32},{32,48},{48,0},{1,17},{17,33},{33,49},{49,1},{2,18}... | collective-permute-start | bytes 491528 | tf_op jit(solution)/shard_map/ppermute | solution.py:379
  149.4 21.2 %collective-permute-start.11 = (f32[2,64,640]{2,1,0:T(8,128)}, f32[2,64,640]{2,1,0:T(8,128)S(1)}, u32[]{:S(2)}, u32[]{:S(2)}) collective-permute-start(f32[2,64,640]{2,1,0:T(8,128)} %get-tuple-element.25), channel_id=1, source_target_pairs={{504,0},{0,8},{8,16},{16,24},{24,32},{32,40},{40,48},{48,56},{56,6... | collective-permute-start | bytes 983048 | tf_op jit(solution)/shard_map/ppermute | solution.py:370
  151.3 8.1 %copy-start.2 = (f32[160,640]{1,0:T(8,128)S(1)}, f32[160,640]{1,0:T(8,128)}, u32[]{:S(2)}) copy-start(f32[160,640]{1,0:T(8,128)} %get-tuple-element.19.refs_2_.refs_0_) | copy-start | bytes 1228804
  151.3 8.1 %copy-start.4 = (f32[160,640]{1,0:T(8,128)S(1)}, f32[160,640]{1,0:T(8,128)}, u32[]{:S(2)}) copy-start(f32[160,640]{1,0:T(8,128)} %copy-done.3) | copy-start | bytes 1228804
  151.3 8.1 %copy-start.6 = (f32[160,640]{1,0:T(8,128)S(1)}, f32[160,640]{1,0:T(8,128)}, u32[]{:S(2)}) copy-start(f32[160,640]{1,0:T(8,128)} %copy-done.5) | copy-start | bytes 1228804
  151.4 8.1 %copy-start.8 = (f32[160,640]{1,0:T(8,128)S(1)}, f32[160,640]{1,0:T(8,128)}, u32[]{:S(2)}) copy-start(f32[160,640]{1,0:T(8,128)} %copy-done.7) | copy-start | bytes 1228804
  151.4 20.3 %collective-permute-start.12 = (f32[2,64,640]{2,1,0:T(8,128)}, f32[2,64,640]{2,1,0:T(8,128)}, u32[]{:S(2)}, u32[]{:S(2)}) collective-permute-start(f32[2,64,640]{2,1,0:T(8,128)} %get-tuple-element.26), channel_id=1, source_target_pairs={{496,0},{504,8},{0,16},{8,24},{16,32},{24,40},{32,48},{40,56},{48,... | collective-permute-start | bytes 983048 | tf_op jit(solution)/shard_map/ppermute | solution.py:370
  166.7 12.0 %all-to-all-start.3 = ((f32[4,72,640]{2,1,0:T(8,128)}), f32[4,72,640]{2,1,0:T(8,128)S(1)}, u32[]{:S(2)}, u32[]{:S(2)}) async-start(f32[4,72,640]{2,1,0:T(8,128)} %shard_map.83.refs_4_), calls=%async_computation.3 | async-start | bytes 1474560 | tf_op jit(solution)/shard_map/all_to_all | solution.py:384
  181.6 21.9 %all-to-all-start.4 = ((f32[8,8,128]{2,1,0:T(8,128)}), f32[8,8,128]{2,1,0:T(8,128)S(1)}, u32[]{:S(2)}, u32[]{:S(2)}) async-start(f32[8,8,128]{2,1,0:T(8,128)} %get-tuple-element.27.refs_2_), calls=%async_computation.4 | async-start | bytes 65536 | tf_op jit(solution)/shard_map/all_to_all | solution.py:384
  (15 other events, 46.1 us)

commit v4 on v3

--- a/solution.py
+++ b/solution.py
@@ -28,6 +28,7 @@
 GROUPS = 2
 VMEM_LIMIT = 58 * 1024 * 1024
 ROOM = 8 * 1024 * 1024
+SMALL = 42 * 1024 * 1024
 
 
 def dot(left, right, dims=((1,), (0,))):
@@ -44,7 +45,7 @@
 def call(body, outs, micros, *args, lazy=(), after=(), scratch=(), smem=(), fan=(), room=0):
     vmem, anywhere = pl.BlockSpec(memory_space=pltpu.VMEM), pl.BlockSpec(memory_space=pl.ANY)
     held = [outs[n][1:] if n in fan else outs[n] for n in range(len(outs))]
-    lazy_shapes = [a.shape if at is None else a.shape[1:] for a, at in lazy]
+    lazy_shapes = [a.shape if at is None else (at[1], *a.shape[1:]) for a, at in lazy]
     sizes = (len(args), len(lazy), len(after), len(outs), len(outs), len(lazy), len(scratch))
     fetches = max(len(lazy), 1)
     sends = sum(outs[n][0] if n in fan else 1 for n in range(len(outs)))
@@ -57,7 +58,7 @@
         inputs, sources, _, targets, results, fetched, spare = split
         in_sems, out_sems = refs[at:]
         incoming = [
-            pltpu.make_async_copy(ref if lazy[n][1] is None else ref.at[lazy[n][1]], fetched[n], in_sems.at[n])
+            pltpu.make_async_copy(ref if lazy[n][1] is None else ref.at[pl.ds(*lazy[n][1])], fetched[n], in_sems.at[n])
             for n, ref in enumerate(sources)
         ]
         for copy in incoming:
@@ -128,13 +129,17 @@
     ]
 
 
-def prepare_weights_body(args, lazy, results, scratch, need, send):
-    packs = own_packs(args[0], scratch[0])
-    for z in range(NZ):
-        for x in range(NX):
+def prepare_packs_body(args, lazy, results, scratch, need, send):
+    for half, ref in enumerate(args):
+        for x, block in enumerate(own_packs(ref, scratch[0])):
             for y in range(NY):
                 for t in range(3):
-                    results[0][(z * NX + x) * NY + y, 8 * t : 8 * t + 8, :] = packs[x][:, LANES * t : LANES * (t + 1)]
+                    rows = slice(24 * half + 8 * t, 24 * half + 8 * t + 8)
+                    results[0][x * NY + y, rows, :] = block[:, LANES * t : LANES * (t + 1)]
+
+
+def spread_body(args, lazy, results, scratch, need, send):
+    results[0][...] = args[0][:, 0:24, :]
 
 
 def prepare_pairs_body(args, lazy, results, scratch, need, send):
@@ -144,26 +149,10 @@
 
 
 def prepare_queries_body(args, lazy, results, scratch, need, send):
-    (mom_ref,), (qkv_ref,), (queries_ref, tail_ref) = args, lazy, results
-    packs = own_packs(mom_ref, scratch[0])
-    for x in range(NX):
-        queries_ref[2 * TOK + 8 * x : 2 * TOK + 8 * x + 8, 0:H] = packs[x]
-        queries_ref[2 * TOK + 8 * x : 2 * TOK + 8 * x + 8, H:D] = jnp.zeros((8, D - H), jnp.float32)
-    need()
-    queries_ref[0:TOK, :] = qkv_ref[0, 0]
-    queries_ref[TOK : 2 * TOK, :] = qkv_ref[0, 1]
-    send(0)
-    for a in range(2):
-        tail_ref[a] = qkv_ref[1 + a, 0]
-
-
-def prepare_tails_body(args, lazy, results, scratch, need, send):
-    (position_ref,), (qkv_ref,) = args, lazy
-    position = position_ref[0]
-    need()
-    for distance, ref in zip((1, 2), results):
-        for a in range(2):
-            ref[a] = jnp.where(position >= BLOCKS - distance, qkv_ref[1 + a, 0], qkv_ref[1 + a, 1])
+    need()
+    (queries_ref,) = results
+    queries_ref[0:TOK, :] = lazy[0][0, 0]
+    queries_ref[TOK : 2 * TOK, :] = lazy[0][0, 1]
 
 
 def widened(part):
@@ -240,19 +229,13 @@
     return lax.rem(x_ref[0] + NX - s, NX)
 
 
-def moment_body(args, queries, results, scratch, need, send):
-    (x_ref, recv_ref), (own_ref,) = args, results
+def moment_body(args, lazy, results, scratch, need, send):
+    (yh_ref, recv_ref, packs_ref), (own_ref,) = args, results
     total = recv_ref[0]
     for j in range(1, NZ * NY):
         total = total + recv_ref[j]
-    own_ref[...] = total
-    need()
-    mine = pl.ds(pl.multiple_of(2 * TOK + 8 * x_ref[0], 8), 8)
-    for s, ref in enumerate(queries):
-        old = ref[mine, :]
-        old = jnp.concatenate([old[:, LANES * t : LANES * (t + 1)] for t in range(3)], axis=0)
-        rows = pl.ds(pl.multiple_of(24 * source(x_ref, s), 8), 24)
-        own_ref[rows, :] = own_ref[rows, :] + MOMENTUM_RATE * old
+    old = jnp.concatenate([packs_ref[x * NY + yh_ref[0], 24:48, :] for x in range(NX)], axis=0)
+    own_ref[...] = total + MOMENTUM_RATE * old
 
 
 def hidden_of(inputs, w1, w3):
@@ -286,12 +269,12 @@
     new1, rate1, ratio1 = renormalized(matrix(w_ref, 0), matrix(m_ref, 0))
     new3, rate3, ratio3 = renormalized(matrix(w_ref, 1), matrix(m_ref, 1))
     new2, rate2, ratio2 = renormalized(matrix(w_ref, 2), matrix(m_ref, 2))
-    hidden = hidden_of(token_rows(queries, TOK), new1, new3)
+    hidden = hidden_of(token_rows(queries, 0), new1, new3)
     partial = dot(hidden, new2, ((1,), (1,)))
     stats = [rate1, rate3, rate2, ratio1, ratio3, ratio2, jnp.zeros((2, LANES), jnp.float32)]
     stats = jnp.concatenate(stats, axis=0)
     for x in range(NX):
-        tail = [stats, *(moment_ref[24 * x + 8 * t : 24 * x + 8 * t + 8, :] for t in range(3))]
+        tail = [stats, *(moment_ref[0, 24 * x + 8 * t : 24 * x + 8 * t + 8, :] for t in range(3))]
         tail.append(jnp.zeros((8, LANES), jnp.float32))
         send_ref[x, TOK : TOK + 8, :] = jnp.concatenate(tail, axis=1)
     for s in range(NX):
@@ -332,37 +315,40 @@
 
 
 def mix_body(args, lazy, results, scratch, need, send):
-    (recv_ref, gain_ref), (readout_ref, *attended_refs), (mixed_ref,) = args, lazy, results
+    (recv_ref, gain_ref, readout_ref, attended_ref), (mixed_ref,) = args, results
     total = recv_ref[0, 0:1, :]
     for n in range(1, NARROW):
         total = total + recv_ref[n, 0:1, :]
     scale = to_column(1.0 / jnp.sqrt(total / (D * NARROW) + EPSILON))
-    need()
     for c in range(GROUPS):
-        mixed_ref[c] = attended_refs[c][...] + gain_ref[...] * (readout_ref[c] * scale[c * TOK : (c + 1) * TOK])
-
-
-def attention_body(c, args, lazy, results, scratch, need, send):
+        mixed_ref[c] = attended_ref[c] + gain_ref[...] * (readout_ref[c] * scale[c * TOK : (c + 1) * TOK])
+
+
+def attention_body(args, lazy, results, scratch, need, send):
     (position_ref,), (qkv_ref, near_ref, far_ref), (out_ref,) = args, lazy, results
     position = position_ref[0]
     row = lax.broadcasted_iota(jnp.int32, (TOK, 3 * TOK), 0) + 2 * TOK
     col = lax.broadcasted_iota(jnp.int32, (TOK, 3 * TOK), 1)
-    allowed = (row - col >= 0) & (row - col < WINDOW)
-    if c == 0:
-        first = jnp.where(position >= 2, 0, jnp.where(position >= 1, TOK, 2 * TOK))
-        allowed = allowed & (col >= first)
-    need()
-    for h in range(D // ATT):
-        at = slice(h * ATT, (h + 1) * ATT)
-        keys, values = (
-            jnp.concatenate([far_ref[a, :, at], near_ref[a, :, at], qkv_ref[1 + a, c, :, at]], axis=0)
-            for a in range(2)
-        )
-        scores = dot(qkv_ref[0, c, :, at], keys, ((1,), (1,))) * (1.0 / math.sqrt(ATT))
-        scores = jnp.where(allowed, scores, -1e30)
-        weights = jnp.exp(scores - jnp.max(scores, axis=1, keepdims=True))
-        weights = weights / jnp.sum(weights, axis=1, keepdims=True)
-        out_ref[:, at] = dot(weights, values)
+    window = (row - col >= 0) & (row - col < WINDOW)
+    first = jnp.where(position >= 2, 0, jnp.where(position >= 1, TOK, 2 * TOK))
+    need()
+    for c in range(GROUPS):
+        allowed = window & (col >= first) if c == 0 else window
+        for h in range(D // ATT):
+            at = slice(h * ATT, (h + 1) * ATT)
+            parts = []
+            for a in range(2):
+                far, near = far_ref[a, c, :, at], near_ref[a, c, :, at]
+                if c == 1:
+                    far = jnp.where(position >= 2, far, far_ref[a, 0, :, at])
+                    near = jnp.where(position >= 1, near, near_ref[a, 0, :, at])
+                parts.append(jnp.concatenate([far, near, qkv_ref[1 + a, c, :, at]], axis=0))
+            keys, values = parts
+            scores = dot(qkv_ref[0, c, :, at], keys, ((1,), (1,))) * (1.0 / math.sqrt(ATT))
+            scores = jnp.where(allowed, scores, -1e30)
+            weights = jnp.exp(scores - jnp.max(scores, axis=1, keepdims=True))
+            weights = weights / jnp.sum(weights, axis=1, keepdims=True)
+            out_ref[c, :, at] = dot(weights, values)
 
 
 def behind(block, distance):
@@ -394,62 +380,58 @@
 
 def local(qkv, eta, fast_weights, momentum, ttt_gain):
     own_weights, own_moment = fast_weights.reshape(3 * ROWS, 1, H), momentum.reshape(3 * ROWS, 1, H)
-    x = lax.axis_index("x")
-    position = scalar((lax.axis_index("z") * NX + x) * NY + lax.axis_index("yh"))
-    x = scalar(x)
-    everyone, cross = ("z", "x", "yh"), ("z", "yh")
-    (send1,) = call(prepare_weights_body, [(BLOCKS, 24, LANES)], 1, own_weights, scratch=[(32, H)])
-    (pairs,) = call(prepare_pairs_body, [(2 * TOK, D)], 1, eta, qkv)
-    recv1 = exchange(send1, everyone).reshape(BLOCKS * 24, LANES)
+    x, yh = lax.axis_index("x"), lax.axis_index("yh")
+    position = scalar((lax.axis_index("z") * NX + x) * NY + yh)
+    x, yh = scalar(x), scalar(yh)
+    (packs,) = call(
+        prepare_packs_body, [(NX * NY, 48, LANES)], 1, own_weights, own_moment, scratch=[(32, H)], room=SMALL
+    )
+    (pairs,) = call(prepare_pairs_body, [(2 * TOK, D)], 1, eta, qkv, room=SMALL)
+    packs = exchange(packs, ("x", "yh"))
+    (spread,) = call(spread_body, [(NZ, NX * NY, 24, LANES)], 1, packs, fan=(0,), room=SMALL)
+    recv1 = exchange(spread.reshape(NZ, NX * NY * 24, LANES), "z").reshape(BLOCKS * 24, LANES)
     pairs = from_neighbours(pairs)
+    near, far = behind(qkv[1:], 1), behind(qkv[1:], 2)
     weights, send2 = call(
         gradient_body, [(3 * D, LANES), (BLOCKS * 24, LANES)], 5, recv1, lazy=whole(*pairs),
         scratch=[(3 * D, LANES)], room=ROOM - 1024 * 1024,
     )
-    recv2 = exchange(send2.reshape(NZ * NY, NX * 24, LANES), cross)
-    queries, tail = call(
-        prepare_queries_body, [(2 * TOK + 32, D), (2, TOK, D)], 1, own_moment, lazy=whole(qkv), scratch=[(32, H)],
-        after=(weights,),
-    )
+    recv2 = exchange(send2.reshape(NZ * NY, NX * 24, LANES), ("z", "yh"))
+    (queries,) = call(prepare_queries_body, [(2 * TOK, D)], 1, lazy=[(qkv, (0, 1))], after=(weights,))
     queries = from_neighbours(queries)
-    near0, far0 = behind(tail, 1), behind(tail, 2)
+    (attended,) = call(
+        attention_body, [(GROUPS, TOK, D)], 8, position, lazy=whole(qkv, near, far), smem=(0,)
+    )
     (send3,) = call(
-        moment_body, [(NZ * NY, NX * 24, LANES)], 2, x, recv2, lazy=whole(*queries), smem=(0,), fan=(0,), room=ROOM
-    )
-    recv3 = exchange(send3, cross).reshape(BLOCKS * 24, LANES)
-    near1, far1 = call(
-        prepare_tails_body, [(2, TOK, D)] * 2, 1, position, lazy=whole(qkv), smem=(0,), after=(send3,)
-    )
-    near1, far1 = behind(near1, 1), behind(far1, 2)
+        moment_body, [(NZ * NY, NX * 24, LANES)], 2, yh, recv2, packs, smem=(0,), fan=(0,),
+        after=(attended, *queries[1:]),
+        room=ROOM,
+    )
+    recv3 = exchange(send3, ("z", "yh")).reshape(BLOCKS * 24, LANES)
     first = back_to_neighbours(
-        call(first_read_body, [(TOK, D)] * NX, 4, lazy=whole(*queries, weights), after=(send3,))
-    )
-    (attended0,) = call(
-        functools.partial(attention_body, 0), [(TOK, D)], 4, position, lazy=whole(qkv, near0, far0), smem=(0,),
-        after=(send3,),
+        call(
+            first_read_body, [(TOK, D)] * NX, 4, lazy=[*((q, (0, TOK)) for q in queries), (weights, None)],
+            after=(send3,),
+        )
     )
     (send_second,) = call(
         second_read_body, [(NX, TOK + 8, D)], 5, x, recv3,
-        lazy=[*whole(*queries, weights), (send3, 0)], scratch=[(3 * D, LANES)], smem=(0,),
-        after=(*first[1:], attended0), room=ROOM,
+        lazy=[*((q, (TOK, TOK)) for q in queries), (weights, None), (send3, (0, 1))], scratch=[(3 * D, LANES)],
+        smem=(0,), after=first[1:], room=ROOM,
     )
     second = exchange(send_second, "x")
-    (attended1,) = call(
-        functools.partial(attention_body, 1), [(TOK, D)], 4, position, lazy=whole(qkv, near1, far1), smem=(0,),
-        after=(send_second,),
-    )
     readout, send5 = call(
         squares_body, [(GROUPS, TOK, D), (NARROW, 8, GROUPS * TOK)], 1, second, lazy=whole(*first), fan=(1,),
-        after=(attended1,), room=ROOM,
+        room=SMALL,
     )
     recv5 = exchange(send5, "narrow")
     new_weights, new_moment = call(
         own_rows_body, [(3 * ROWS, 1, H), (3 * ROWS, 1, H)], 1, second, own_weights, scratch=[(32, H)],
-        after=(send5,),
+        after=(send5,), room=SMALL,
     )
     (mixed,) = call(
-        mix_body, [(GROUPS, TOK, D)], 1, recv5, ttt_gain.reshape(1, D), lazy=whole(readout, attended0, attended1),
-        after=(new_weights,), room=ROOM,
+        mix_body, [(GROUPS, TOK, D)], 1, recv5, ttt_gain.reshape(1, D), readout, attended, after=(new_weights,),
+        room=SMALL,
     )
     return mixed, new_weights.reshape(1, ROWS, 3, H), new_moment.reshape(1, ROWS, 3, H)
 

time: 210 us -> 209 us (level); the launches traced: 206 us -> 208 us
  blocking collectives: 0 us -> 19.7 us
  starting transfers between devices: 107 us -> 87.5 us
  waiting for transfers between devices: 47.9 us -> 61.4 us
  Pallas kernels: 44.4 us -> 34.3 us
    all_to_all x0 -> x1, blocking collectives: none -> 19.7 us  [exchange(): return lax.all_to_all(pieces, axes, split_axis=0, concat_axis=0, tiled=True)]
    ppermute x6, waiting for transfers between devices: 30.8 us -> 11.9 us  [from_neighbours(): lax.ppermute(block, 'x', [((i - s) % NX, i) for i in range(NX)])]
    ppermute x4 -> x2, waiting for transfers between devices: 12.9 us -> 31.7 us  [behind(): lax.ppermute(block, axes, [((i - distance) % BLOCKS, i) for i in range(BL...]
    all_to_all x5, starting transfers between devices: 61.9 us -> 47.3 us  [exchange(): return lax.all_to_all(pieces, axes, split_axis=0, concat_axis=0, tiled=True)]
    pallas_call x13 -> x12, Pallas kernels: 44.4 us -> 34.3 us  [call(): pl.pallas_call(kernel, out_shape=[jax.ShapeDtypeStruct(s, jnp.float32) fo...]
    all_to_all x5, waiting for transfers between devices: 4.24 us -> 13.1 us  [exchange(): return lax.all_to_all(pieces, axes, split_axis=0, concat_axis=0, tiled=True)]
    ppermute x4 -> x2, starting transfers between devices: 16.5 us -> 9.27 us  [behind(): lax.ppermute(block, axes, [((i - distance) % BLOCKS, i) for i in range(BL...]
    ppermute x3, waiting for transfers between devices: 0.01 us -> 4.78 us  [back_to_neighbours(): lax.ppermute(blocks[s], 'x', [(i, (i - s) % NX) for i in range(NX)])]
  transfers between devices with their start and end apart: 18 -> 16, of which waited for: 10 -> 8; matrix products, arithmetic and copies ran while one was open for 0% -> 0% of each run, Pallas kernels for 15% -> 8%
where the time goes in v4:
time: 209 us; the launch traced here: 208 us
  starting transfers between devices  87.5 us (42%)
  waiting for transfers between devices  61.4 us (29%)
  Pallas kernels  34.3 us (16%)
  blocking collectives  19.7 us (9%)
  local copies, waits for them, and re-layouts  3.68 us (2%)
    all_to_all x5, starting transfers between devices, exchange(): return lax.all_to_all(pieces, axes, split_axis=0, concat_axis=0, tiled=True)  47.3 us
    pallas_call x12, Pallas kernels, call(): pl.pallas_call(kernel, out_shape=[jax.ShapeDtypeStruct(s, jnp.float32) fo...  34.3 us
    ppermute x2, waiting for transfers between devices, behind(): lax.ppermute(block, axes, [((i - distance) % BLOCKS, i) for i in range(BL...  31.7 us
    ppermute x6, starting transfers between devices, from_neighbours(): lax.ppermute(block, 'x', [((i - s) % NX, i) for i in range(NX)])  20.9 us
    all_to_all x1, blocking collectives, exchange(): return lax.all_to_all(pieces, axes, split_axis=0, concat_axis=0, tiled=True)  19.7 us
    all_to_all x5, waiting for transfers between devices, exchange(): return lax.all_to_all(pieces, axes, split_axis=0, concat_axis=0, tiled=True)  13.1 us
    ppermute x6, waiting for transfers between devices, from_neighbours(): lax.ppermute(block, 'x', [((i - s) % NX, i) for i in range(NX)])  11.9 us
    ppermute x3, starting transfers between devices, back_to_neighbours(): lax.ppermute(blocks[s], 'x', [(i, (i - s) % NX) for i in range(NX)])  10 us
  transfers between devices with their start and end apart: 16, of which 8 were waited for; matrix products, arithmetic and copies ran while one was open for 0% of the time, Pallas kernels for 8%

profile of v4, /device:TPU:1, one launch (start us, length us, event | category | flops | bytes accessed | tf_op | source)
XLA Modules:
  0.0 207.9 jit_solution(5925207752939978237)
XLA Ops:
  2.6 19.7 %all_to_all.30.refs_0_.refs_2_ = f32[8,48,128]{2,1,0:T(8,128)S(1)} all-to-all(f32[8,48,128]{2,1,0:T(8,128)S(1)} %shard_map.76), channel_id=1, replica_groups=mesh['z'=8,'x'=4,'yh'=2,'narrow'=8] {'x','yh'}, dimensions={0} | all-to-all | bytes 393216 | tf_op jit(solution)/shard_map/all_to_all | solution.py:370
  23.4 10.2 %all-to-all-start.1 = ((f32[8,192,128]{2,1,0:T(8,128)}), f32[8,192,128]{2,1,0:T(8,128)S(1)}, u32[]{:S(2)}, u32[]{:S(2)}) async-start(f32[8,192,128]{2,1,0:T(8,128)} %bitcast.4), calls=%async_computation.1 | async-start | bytes 1572864 | tf_op jit(solution)/shard_map/all_to_all | solution.py:370
  35.7 3.7 %collective-permute-start.1 = (f32[128,640]{1,0:T(8,128)S(1)}, f32[128,640]{1,0:T(8,128)S(1)}, u32[]{:S(2)}, u32[]{:S(2)}) collective-permute-start(f32[128,640]{1,0:T(8,128)S(1)} %shard_map.78.refs_1_), channel_id=1, source_target_pairs={{32,0},{48,16},{0,32},{16,48},{33,1},{49,17},{1,33},{17,49},{34,2}... | collective-permute-start | bytes 983048 | tf_op jit(solution)/shard_map/ppermute | solution.py:360
  39.4 3.1 %collective-permute-start.2 = (f32[128,640]{1,0:T(8,128)S(1)}, f32[128,640]{1,0:T(8,128)S(1)}, u32[]{:S(2)}, u32[]{:S(2)}) collective-permute-start(f32[128,640]{1,0:T(8,128)S(1)} %shard_map.78.refs_1_), channel_id=1, source_target_pairs={{16,0},{32,16},{48,32},{0,48},{17,1},{33,17},{49,33},{1,49},{18,2}... | collective-permute-start | bytes 983048 | tf_op jit(solution)/shard_map/ppermute | solution.py:360
  42.5 2.3 %collective-permute-done.refs_2_ = f32[128,640]{1,0:T(8,128)S(1)} collective-permute-done((f32[128,640]{1,0:T(8,128)S(1)}, f32[128,640]{1,0:T(8,128)S(1)}, u32[]{:S(2)}, u32[]{:S(2)}) %collective-permute-start) | collective-permute-done | bytes 327712 | tf_op jit(solution)/shard_map/ppermute | solution.py:360
  44.8 5.0 %collective-permute-done.1.refs_3_ = f32[128,640]{1,0:T(8,128)S(1)} collective-permute-done((f32[128,640]{1,0:T(8,128)S(1)}, f32[128,640]{1,0:T(8,128)S(1)}, u32[]{:S(2)}, u32[]{:S(2)}) %collective-permute-start.1) | collective-permute-done | bytes 327712 | tf_op jit(solution)/shard_map/ppermute | solution.py:360
  49.8 4.5 %collective-permute-done.2.refs_4_ = f32[128,640]{1,0:T(8,128)S(1)} collective-permute-done((f32[128,640]{1,0:T(8,128)S(1)}, f32[128,640]{1,0:T(8,128)S(1)}, u32[]{:S(2)}, u32[]{:S(2)}) %collective-permute-start.2) | collective-permute-done | bytes 327712 | tf_op jit(solution)/shard_map/ppermute | solution.py:360
  55.2 5.5 %shard_map.79 = (f32[1920,128]{1,0:T(8,128)}, f32[1536,128]{1,0:T(8,128)}) custom-call(f32[1536,128]{1,0:T(8,128)S(1)} %bitcast.12, f32[128,640]{1,0:T(8,128)S(1)} %shard_map.78.refs_1_, f32[128,640]{1,0:T(8,128)S(1)} %collective-permute-done.refs_2_, f32[128,640]{1,0:T(8,128)S(1)} %collective-permute-done.1.refs_3_, ...), custom_call_target="tpu_custom_call" | custom-call | flops 5000000000 | bytes 1000000 | tf_op jit(solution)/shard_map/pallas_call | solution.py:92
  60.7 6.6 %all-to-all-start.2 = ((f32[16,96,128]{2,1,0:T(8,128)}), f32[16,96,128]{2,1,0:T(8,128)S(1)}, u32[]{:S(2)}, u32[]{:S(2)}) async-start(f32[16,96,128]{2,1,0:T(8,128)} %bitcast.6), calls=%async_computation.2 | async-start | bytes 1572864 | tf_op jit(solution)/shard_map/all_to_all | solution.py:370
  67.4 7.2 %collective-permute-start.3 = (f32[2,2,64,640]{3,2,1,0:T(8,128)S(1)}, f32[2,2,64,640]{3,2,1,0:T(8,128)}, u32[]{:S(2)}, u32[]{:S(2)}) collective-permute-start(f32[2,2,64,640]{3,2,1,0:T(8,128)S(1)} %slice.4), channel_id=1, source_target_pairs={{504,0},{0,8},{8,16},{16,24},{24,32},{32,40},{40,48},{48,56},{56,6... | collective-permute-start | bytes 1966088 | tf_op jit(solution)/shard_map/ppermute | solution.py:356
  80.4 6.5 %collective-permute-start.6 = (f32[128,640]{1,0:T(8,128)}, f32[128,640]{1,0:T(8,128)S(1)}, u32[]{:S(2)}, u32[]{:S(2)}) collective-permute-start(f32[128,640]{1,0:T(8,128)} %shard_map.81.refs_0_.refs_2_), channel_id=1, source_target_pairs={{32,0},{48,16},{0,32},{16,48},{33,1},{49,17},{1,33},{17,49},{34,2}... | collective-permute-start | bytes 983048 | tf_op jit(solution)/shard_map/ppermute | solution.py:360
  86.8 3.8 %collective-permute-start.7 = (f32[128,640]{1,0:T(8,128)}, f32[128,640]{1,0:T(8,128)S(1)}, u32[]{:S(2)}, u32[]{:S(2)}) collective-permute-start(f32[128,640]{1,0:T(8,128)} %shard_map.81.refs_0_.refs_2_), channel_id=1, source_target_pairs={{16,0},{32,16},{48,32},{0,48},{17,1},{33,17},{49,33},{1,49},{18,2}... | collective-permute-start | bytes 983048 | tf_op jit(solution)/shard_map/ppermute | solution.py:360
  90.7 31.7 %collective-permute-done.3.refs_2_ = f32[2,2,64,640]{3,2,1,0:T(8,128)} collective-permute-done((f32[2,2,64,640]{3,2,1,0:T(8,128)S(1)}, f32[2,2,64,640]{3,2,1,0:T(8,128)}, u32[]{:S(2)}, u32[]{:S(2)}) %collective-permute-start.3) | collective-permute-done | bytes 655392 | tf_op jit(solution)/shard_map/ppermute | solution.py:356
  122.3 9.7 %shard_map.80.refs_3_ = f32[2,64,640]{2,1,0:T(8,128)} custom-call(s32[1]{0:T(128)} %bitcast.7.refs_0_, f32[3,2,64,640]{3,2,1,0:T(8,128)} %refs_0_.3, f32[2,2,64,640]{3,2,1,0:T(8,128)} %collective-permute-done.3.refs_2_, f32[2,2,64,640]{3,2,1,0:T(8,128)} %collective-permute-done.4.refs_3_), custom_call_target="tpu_custom_call" | custom-call | flops 8000000000 | bytes 1000000 | tf_op jit(solution)/shard_map/pallas_call | solution.py:92
  134.5 4.1 %all-to-all-start.3 = ((f32[16,96,128]{2,1,0:T(8,128)}), f32[16,96,128]{2,1,0:T(8,128)S(1)}, u32[]{:S(2)}, u32[]{:S(2)}) async-start(f32[16,96,128]{2,1,0:T(8,128)} %shard_map.82.refs_5_.refs_7_), calls=%async_computation.3 | async-start | bytes 1572864 | tf_op jit(solution)/shard_map/all_to_all | solution.py:370
  138.6 4.9 %shard_map.83 = (f32[64,640]{1,0:T(8,128)}, f32[64,640]{1,0:T(8,128)}, f32[64,640]{1,0:T(8,128)}, f32[64,640]{1,0:T(8,128)}) custom-call(f32[128,640]{1,0:T(8,128)} %shard_map.81.refs_0_.refs_2_, f32[128,640]{1,0:T(8,128)} %copy-done.2, f32[128,640]{1,0:T(8,128)} %copy-done.4, f32[128,640]{1,0:T(8,128)} %copy-done.6, ...), custom_call_target="tpu_custom_call" | custom-call | flops 4000000000 | bytes 1000000 | tf_op jit(solution)/shard_map/pallas_call | solution.py:92
  145.4 4.8 %collective-permute-start.8 = (f32[64,640]{1,0:T(8,128)}, f32[64,640]{1,0:T(8,128)S(1)}, u32[]{:S(2)}, u32[]{:S(2)}) collective-permute-start(f32[64,640]{1,0:T(8,128)} %get-tuple-element.15), channel_id=1, source_target_pairs={{0,48},{16,0},{32,16},{48,32},{1,49},{17,1},{33,17},{49,33},{2,50}... | collective-permute-start | bytes 491528 | tf_op jit(solution)/shard_map/ppermute | solution.py:365
  150.3 3.3 %collective-permute-start.9 = (f32[64,640]{1,0:T(8,128)}, f32[64,640]{1,0:T(8,128)S(1)}, u32[]{:S(2)}, u32[]{:S(2)}) collective-permute-start(f32[64,640]{1,0:T(8,128)} %get-tuple-element.16), channel_id=1, source_target_pairs={{0,32},{16,48},{32,0},{48,16},{1,33},{17,49},{33,1},{49,17},{2,34}... | collective-permute-start | bytes 491528 | tf_op jit(solution)/shard_map/ppermute | solution.py:365
  153.6 4.8 %collective-permute-done.9.refs_9_.refs_3_ = f32[64,640]{1,0:T(8,128)S(1)} collective-permute-done((f32[64,640]{1,0:T(8,128)}, f32[64,640]{1,0:T(8,128)S(1)}, u32[]{:S(2)}, u32[]{:S(2)}) %collective-permute-start.9) | collective-permute-done | bytes 163872 | tf_op jit(solution)/shard_map/ppermute | solution.py:365
  158.4 6.3 %shard_map.84 = f32[4,72,640]{2,1,0:T(8,128)} custom-call(s32[1]{0:T(128)} %bitcast.refs_0_, f32[1536,128]{1,0:T(8,128)S(1)} %bitcast.11, f32[128,640]{1,0:T(8,128)S(1)} %copy-done.1, f32[128,640]{1,0:T(8,128)S(1)} %copy-done.3, f32[128,640]{1,0:T(8,128)S(1)} %copy-done.5, f32[128,640]{1,0:T(8,128)S(1)} %copy-done.7, ...), custom_call_target="tpu_custom_call" | custom-call | flops 5000000000 | bytes 1000000 | tf_op jit(solution)/shard_map/pallas_call | solution.py:92
  164.7 4.1 %all-to-all-start.4 = ((f32[4,72,640]{2,1,0:T(8,128)}), f32[4,72,640]{2,1,0:T(8,128)S(1)}, u32[]{:S(2)}, u32[]{:S(2)}) async-start(f32[4,72,640]{2,1,0:T(8,128)} %shard_map.84), calls=%async_computation.4 | async-start | bytes 1474560 | tf_op jit(solution)/shard_map/all_to_all | solution.py:370
  168.8 8.1 %all-to-all-done.4.refs_0_ = f32[4,72,640]{2,1,0:T(8,128)S(1)} async-done(((f32[4,72,640]{2,1,0:T(8,128)}), f32[4,72,640]{2,1,0:T(8,128)S(1)}, u32[]{:S(2)}, u32[]{:S(2)}) %all-to-all-start.4) | async-done | bytes 737312 | tf_op jit(solution)/shard_map/all_to_all | solution.py:370
  178.7 22.3 %all-to-all-start.5 = ((f32[8,8,128]{2,1,0:T(8,128)}), f32[8,8,128]{2,1,0:T(8,128)S(1)}, u32[]{:S(2)}, u32[]{:S(2)}) async-start(f32[8,8,128]{2,1,0:T(8,128)} %get-tuple-element.19.refs_2_), calls=%async_computation.5 | async-start | bytes 65536 | tf_op jit(solution)/shard_map/all_to_all | solution.py:370
  201.9 4.2 %all-to-all-done.5.refs_0_ = f32[8,8,128]{2,1,0:T(8,128)S(1)} async-done(((f32[8,8,128]{2,1,0:T(8,128)}), f32[8,8,128]{2,1,0:T(8,128)S(1)}, u32[]{:S(2)}, u32[]{:S(2)}) %all-to-all-start.5) | async-done | bytes 32800 | tf_op jit(solution)/shard_map/all_to_all | solution.py:370
  (57 shorter events, 20.3 us)
Async XLA Ops:
  23.3 10.2 %copy-start = (f32[3,2,64,640]{3,2,1,0:T(8,128)S(1)}, f32[3,2,64,640]{3,2,1,0:T(8,128)}, u32[]{:S(2)}) copy-start(f32[3,2,64,640]{3,2,1,0:T(8,128)} %refs_0_.3) | copy-start | bytes 2949124
  23.3 10.2 %copy-start.11 = (f32[1,64]{1,0:T(1,128)S(1)}, f32[1,64]{1,0:T(1,128)}, u32[]{:S(2)}) copy-start(f32[1,64]{1,0:T(1,128)} %refs_0_.2) | copy-start | bytes 772
  23.4 31.8 %all-to-all-start.1 = ((f32[8,192,128]{2,1,0:T(8,128)}), f32[8,192,128]{2,1,0:T(8,128)S(1)}, u32[]{:S(2)}, u32[]{:S(2)}) async-start(f32[8,192,128]{2,1,0:T(8,128)} %bitcast.4), calls=%async_computation.1 | async-start | bytes 1572864 | tf_op jit(solution)/shard_map/all_to_all | solution.py:370
  33.8 11.0 %collective-permute-start = (f32[128,640]{1,0:T(8,128)S(1)}, f32[128,640]{1,0:T(8,128)S(1)}, u32[]{:S(2)}, u32[]{:S(2)}) collective-permute-start(f32[128,640]{1,0:T(8,128)S(1)} %shard_map.78.refs_1_), channel_id=1, source_target_pairs={{48,0},{0,16},{16,32},{32,48},{49,1},{1,17},{17,33},{33,49},{50,2}... | collective-permute-start | bytes 983048 | tf_op jit(solution)/shard_map/ppermute | solution.py:360
  35.7 14.1 %collective-permute-start.1 = (f32[128,640]{1,0:T(8,128)S(1)}, f32[128,640]{1,0:T(8,128)S(1)}, u32[]{:S(2)}, u32[]{:S(2)}) collective-permute-start(f32[128,640]{1,0:T(8,128)S(1)} %shard_map.78.refs_1_), channel_id=1, source_target_pairs={{32,0},{48,16},{0,32},{16,48},{33,1},{49,17},{1,33},{17,49},{34,2}... | collective-permute-start | bytes 983048 | tf_op jit(solution)/shard_map/ppermute | solution.py:360
  39.4 15.0 %collective-permute-start.2 = (f32[128,640]{1,0:T(8,128)S(1)}, f32[128,640]{1,0:T(8,128)S(1)}, u32[]{:S(2)}, u32[]{:S(2)}) collective-permute-start(f32[128,640]{1,0:T(8,128)S(1)} %shard_map.78.refs_1_), channel_id=1, source_target_pairs={{16,0},{32,16},{48,32},{0,48},{17,1},{33,17},{49,33},{1,49},{18,2}... | collective-permute-start | bytes 983048 | tf_op jit(solution)/shard_map/ppermute | solution.py:360
  60.7 71.4 %all-to-all-start.2 = ((f32[16,96,128]{2,1,0:T(8,128)}), f32[16,96,128]{2,1,0:T(8,128)S(1)}, u32[]{:S(2)}, u32[]{:S(2)}) async-start(f32[16,96,128]{2,1,0:T(8,128)} %bitcast.6), calls=%async_computation.2 | async-start | bytes 1572864 | tf_op jit(solution)/shard_map/all_to_all | solution.py:370
  67.4 54.9 %collective-permute-start.3 = (f32[2,2,64,640]{3,2,1,0:T(8,128)S(1)}, f32[2,2,64,640]{3,2,1,0:T(8,128)}, u32[]{:S(2)}, u32[]{:S(2)}) collective-permute-start(f32[2,2,64,640]{3,2,1,0:T(8,128)S(1)} %slice.4), channel_id=1, source_target_pairs={{504,0},{0,8},{8,16},{16,24},{24,32},{32,40},{40,48},{48,56},{56,6... | collective-permute-start | bytes 1966088 | tf_op jit(solution)/shard_map/ppermute | solution.py:356
  74.6 47.7 %collective-permute-start.4 = (f32[2,2,64,640]{3,2,1,0:T(8,128)S(1)}, f32[2,2,64,640]{3,2,1,0:T(8,128)}, u32[]{:S(2)}, u32[]{:S(2)}) collective-permute-start(f32[2,2,64,640]{3,2,1,0:T(8,128)S(1)} %slice.4), channel_id=1, source_target_pairs={{496,0},{504,8},{0,16},{8,24},{16,32},{24,40},{32,48},{40,56},{48,... | collective-permute-start | bytes 1966088 | tf_op jit(solution)/shard_map/ppermute | solution.py:356
  78.4 53.6 %collective-permute-start.5 = (f32[128,640]{1,0:T(8,128)}, f32[128,640]{1,0:T(8,128)S(1)}, u32[]{:S(2)}, u32[]{:S(2)}) collective-permute-start(f32[128,640]{1,0:T(8,128)} %shard_map.81.refs_0_.refs_2_), channel_id=1, source_target_pairs={{48,0},{0,16},{16,32},{32,48},{49,1},{1,17},{17,33},{33,49},{50,2}... | collective-permute-start | bytes 983048 | tf_op jit(solution)/shard_map/ppermute | solution.py:360
  80.4 51.7 %collective-permute-start.6 = (f32[128,640]{1,0:T(8,128)}, f32[128,640]{1,0:T(8,128)S(1)}, u32[]{:S(2)}, u32[]{:S(2)}) collective-permute-start(f32[128,640]{1,0:T(8,128)} %shard_map.81.refs_0_.refs_2_), channel_id=1, source_target_pairs={{32,0},{48,16},{0,32},{16,48},{33,1},{49,17},{1,33},{17,49},{34,2}... | collective-permute-start | bytes 983048 | tf_op jit(solution)/shard_map/ppermute | solution.py:360
  86.8 45.2 %collective-permute-start.7 = (f32[128,640]{1,0:T(8,128)}, f32[128,640]{1,0:T(8,128)S(1)}, u32[]{:S(2)}, u32[]{:S(2)}) collective-permute-start(f32[128,640]{1,0:T(8,128)} %shard_map.81.refs_0_.refs_2_), channel_id=1, source_target_pairs={{16,0},{32,16},{48,32},{0,48},{17,1},{33,17},{49,33},{1,49},{18,2}... | collective-permute-start | bytes 983048 | tf_op jit(solution)/shard_map/ppermute | solution.py:360
  134.5 23.9 %all-to-all-start.3 = ((f32[16,96,128]{2,1,0:T(8,128)}), f32[16,96,128]{2,1,0:T(8,128)S(1)}, u32[]{:S(2)}, u32[]{:S(2)}) async-start(f32[16,96,128]{2,1,0:T(8,128)} %shard_map.82.refs_5_.refs_7_), calls=%async_computation.3 | async-start | bytes 1572864 | tf_op jit(solution)/shard_map/all_to_all | solution.py:370
  138.6 19.8 %copy-start.1 = (f32[128,640]{1,0:T(8,128)S(1)}, f32[128,640]{1,0:T(8,128)}, u32[]{:S(2)}) copy-start(f32[128,640]{1,0:T(8,128)} %shard_map.81.refs_0_.refs_2_) | copy-start | bytes 983044
  138.6 19.7 %copy-start.3 = (f32[128,640]{1,0:T(8,128)S(1)}, f32[128,640]{1,0:T(8,128)}, u32[]{:S(2)}) copy-start(f32[128,640]{1,0:T(8,128)} %copy-done.2) | copy-start | bytes 983044
  138.6 19.7 %copy-start.5 = (f32[128,640]{1,0:T(8,128)S(1)}, f32[128,640]{1,0:T(8,128)}, u32[]{:S(2)}) copy-start(f32[128,640]{1,0:T(8,128)} %copy-done.4) | copy-start | bytes 983044
  138.6 19.7 %copy-start.7 = (f32[128,640]{1,0:T(8,128)S(1)}, f32[128,640]{1,0:T(8,128)}, u32[]{:S(2)}) copy-start(f32[128,640]{1,0:T(8,128)} %copy-done.6) | copy-start | bytes 983044
  143.5 10.0 %collective-permute-start.10 = (f32[64,640]{1,0:T(8,128)}, f32[64,640]{1,0:T(8,128)S(1)}, u32[]{:S(2)}, u32[]{:S(2)}) collective-permute-start(f32[64,640]{1,0:T(8,128)} %get-tuple-element.17), channel_id=1, source_target_pairs={{0,16},{16,32},{32,48},{48,0},{1,17},{17,33},{33,49},{49,1},{2,18}... | collective-permute-start | bytes 491528 | tf_op jit(solution)/shard_map/ppermute | solution.py:365
  145.4 8.1 %collective-permute-start.8 = (f32[64,640]{1,0:T(8,128)}, f32[64,640]{1,0:T(8,128)S(1)}, u32[]{:S(2)}, u32[]{:S(2)}) collective-permute-start(f32[64,640]{1,0:T(8,128)} %get-tuple-element.15), channel_id=1, source_target_pairs={{0,48},{16,0},{32,16},{48,32},{1,49},{17,1},{33,17},{49,33},{2,50}... | collective-permute-start | bytes 491528 | tf_op jit(solution)/shard_map/ppermute | solution.py:365
  150.3 8.1 %collective-permute-start.9 = (f32[64,640]{1,0:T(8,128)}, f32[64,640]{1,0:T(8,128)S(1)}, u32[]{:S(2)}, u32[]{:S(2)}) collective-permute-start(f32[64,640]{1,0:T(8,128)} %get-tuple-element.16), channel_id=1, source_target_pairs={{0,32},{16,48},{32,0},{48,16},{1,33},{17,49},{33,1},{49,17},{2,34}... | collective-permute-start | bytes 491528 | tf_op jit(solution)/shard_map/ppermute | solution.py:365
  164.7 12.2 %copy-start.15 = (f32[64,640]{1,0:T(8,128)S(1)}, f32[64,640]{1,0:T(8,128)}, u32[]{:S(2)}) copy-start(f32[64,640]{1,0:T(8,128)} %get-tuple-element.18.refs_1_) | copy-start | bytes 491524
  164.7 12.2 %all-to-all-start.4 = ((f32[4,72,640]{2,1,0:T(8,128)}), f32[4,72,640]{2,1,0:T(8,128)S(1)}, u32[]{:S(2)}, u32[]{:S(2)}) async-start(f32[4,72,640]{2,1,0:T(8,128)} %shard_map.84), calls=%async_computation.4 | async-start | bytes 1474560 | tf_op jit(solution)/shard_map/all_to_all | solution.py:370
  178.7 22.3 %copy-start.10 = (f32[1,10,3,384]{3,0,2,1:T(1,128)S(1)}, f32[1,10,3,384]{3,0,2,1:T(1,128)}, u32[]{:S(2)}) copy-start(f32[1,10,3,384]{3,0,2,1:T(1,128)} %param.7) | copy-start | bytes 138244
  178.7 27.3 %all-to-all-start.5 = ((f32[8,8,128]{2,1,0:T(8,128)}), f32[8,8,128]{2,1,0:T(8,128)S(1)}, u32[]{:S(2)}, u32[]{:S(2)}) async-start(f32[8,8,128]{2,1,0:T(8,128)} %get-tuple-element.19.refs_2_), calls=%async_computation.5 | async-start | bytes 65536 | tf_op jit(solution)/shard_map/all_to_all | solution.py:370
  (9 other events, 19.8 us)

commit v5 on v4

--- a/solution.py
+++ b/solution.py
@@ -394,7 +394,7 @@
     near, far = behind(qkv[1:], 1), behind(qkv[1:], 2)
     weights, send2 = call(
         gradient_body, [(3 * D, LANES), (BLOCKS * 24, LANES)], 5, recv1, lazy=whole(*pairs),
-        scratch=[(3 * D, LANES)], room=ROOM - 1024 * 1024,
+        scratch=[(3 * D, LANES)], after=(near, far), room=ROOM - 1024 * 1024,
     )
     recv2 = exchange(send2.reshape(NZ * NY, NX * 24, LANES), ("z", "yh"))
     (queries,) = call(prepare_queries_body, [(2 * TOK, D)], 1, lazy=[(qkv, (0, 1))], after=(weights,))

time: 209 us -> 206 us (0.986)
  starting transfers between devices: 87.5 us -> 83.2 us
    ppermute x2, waiting for transfers between devices: 31.7 us -> 0.01 us  [behind(): lax.ppermute(block, axes, [((i - distance) % BLOCKS, i) for i in range(BL...]
    ppermute x6, waiting for transfers between devices: 11.9 us -> 40.3 us  [from_neighbours(): lax.ppermute(block, 'x', [((i - s) % NX, i) for i in range(NX)])]
    ppermute x2, starting transfers between devices: 9.27 us -> 4.84 us  [behind(): lax.ppermute(block, axes, [((i - distance) % BLOCKS, i) for i in range(BL...]
    all_to_all x5, waiting for transfers between devices: 13.1 us -> 15.9 us  [exchange(): return lax.all_to_all(pieces, axes, split_axis=0, concat_axis=0, tiled=True)]
  transfers between devices with their start and end apart: 16 -> 16, of which waited for: 8 -> 7; matrix products, arithmetic and copies ran while one was open for 0% -> 0% of each run, Pallas kernels for 8% -> 8%
where the time goes in v5:
time: 206 us; the launch traced here: 205 us
  starting transfers between devices  83.2 us (40%)
  waiting for transfers between devices  61.1 us (30%)
  Pallas kernels  35.9 us (17%)
  blocking collectives  19.7 us (10%)
  local copies, waits for them, and re-layouts  3.57 us (2%)
    all_to_all x5, starting transfers between devices, exchange(): return lax.all_to_all(pieces, axes, split_axis=0, concat_axis=0, tiled=True)  49.1 us
    ppermute x6, waiting for transfers between devices, from_neighbours(): lax.ppermute(block, 'x', [((i - s) % NX, i) for i in range(NX)])  40.3 us
    pallas_call x12, Pallas kernels, call(): pl.pallas_call(kernel, out_shape=[jax.ShapeDtypeStruct(s, jnp.float32) fo...  35.9 us
    all_to_all x1, blocking collectives, exchange(): return lax.all_to_all(pieces, axes, split_axis=0, concat_axis=0, tiled=True)  19.7 us
    ppermute x6, starting transfers between devices, from_neighbours(): lax.ppermute(block, 'x', [((i - s) % NX, i) for i in range(NX)])  18.9 us
    all_to_all x5, waiting for transfers between devices, exchange(): return lax.all_to_all(pieces, axes, split_axis=0, concat_axis=0, tiled=True)  15.9 us
    ppermute x3, starting transfers between devices, back_to_neighbours(): lax.ppermute(blocks[s], 'x', [(i, (i - s) % NX) for i in range(NX)])  10.4 us
    ppermute x3, waiting for transfers between devices, back_to_neighbours(): lax.ppermute(blocks[s], 'x', [(i, (i - s) % NX) for i in range(NX)])  4.96 us
  transfers between devices with their start and end apart: 16, of which 7 were waited for; matrix products, arithmetic and copies ran while one was open for 0% of the time, Pallas kernels for 8%

profile of v5, /device:TPU:1, one launch (start us, length us, event | category | flops | bytes accessed | tf_op | source)
XLA Modules:
  0.0 204.7 jit_solution(6362488184993546274)
XLA Ops:
  2.6 19.7 %all_to_all.30.refs_0_.refs_2_ = f32[8,48,128]{2,1,0:T(8,128)S(1)} all-to-all(f32[8,48,128]{2,1,0:T(8,128)S(1)} %shard_map.76), channel_id=1, replica_groups=mesh['z'=8,'x'=4,'yh'=2,'narrow'=8] {'x','yh'}, dimensions={0} | all-to-all | bytes 393216 | tf_op jit(solution)/shard_map/all_to_all | solution.py:370
  23.4 10.2 %all-to-all-start.1 = ((f32[8,192,128]{2,1,0:T(8,128)}), f32[8,192,128]{2,1,0:T(8,128)}, u32[]{:S(2)}, u32[]{:S(2)}) async-start(f32[8,192,128]{2,1,0:T(8,128)} %bitcast.4), calls=%async_computation.1 | async-start | bytes 1572864 | tf_op jit(solution)/shard_map/all_to_all | solution.py:370
  33.6 2.6 %collective-permute-start.3 = (f32[2,2,64,640]{3,2,1,0:T(8,128)S(1)}, f32[2,2,64,640]{3,2,1,0:T(8,128)S(1)}, u32[]{:S(2)}, u32[]{:S(2)}) collective-permute-start(f32[2,2,64,640]{3,2,1,0:T(8,128)S(1)} %slice.4), channel_id=1, source_target_pairs={{504,0},{0,8},{8,16},{16,24},{24,32},{32,40},{40,48},{48,56},{56,6... | collective-permute-start | bytes 1966088 | tf_op jit(solution)/shard_map/ppermute | solution.py:356
  36.3 2.2 %collective-permute-start.4 = (f32[2,2,64,640]{3,2,1,0:T(8,128)S(1)}, f32[2,2,64,640]{3,2,1,0:T(8,128)S(1)}, u32[]{:S(2)}, u32[]{:S(2)}) collective-permute-start(f32[2,2,64,640]{3,2,1,0:T(8,128)S(1)} %slice.4), channel_id=1, source_target_pairs={{496,0},{504,8},{0,16},{8,24},{16,32},{24,40},{32,48},{40,56},{48,... | collective-permute-start | bytes 1966088 | tf_op jit(solution)/shard_map/ppermute | solution.py:356
  40.6 6.6 %collective-permute-start.1 = (f32[128,640]{1,0:T(8,128)S(1)}, f32[128,640]{1,0:T(8,128)S(1)}, u32[]{:S(2)}, u32[]{:S(2)}) collective-permute-start(f32[128,640]{1,0:T(8,128)S(1)} %shard_map.78.refs_1_), channel_id=1, source_target_pairs={{32,0},{48,16},{0,32},{16,48},{33,1},{49,17},{1,33},{17,49},{34,2}... | collective-permute-start | bytes 983048 | tf_op jit(solution)/shard_map/ppermute | solution.py:360
  49.2 22.1 %collective-permute-done.refs_2_ = f32[128,640]{1,0:T(8,128)S(1)} collective-permute-done((f32[128,640]{1,0:T(8,128)S(1)}, f32[128,640]{1,0:T(8,128)S(1)}, u32[]{:S(2)}, u32[]{:S(2)}) %collective-permute-start) | collective-permute-done | bytes 327712 | tf_op jit(solution)/shard_map/ppermute | solution.py:360
  71.3 15.7 %collective-permute-done.1.refs_3_ = f32[128,640]{1,0:T(8,128)S(1)} collective-permute-done((f32[128,640]{1,0:T(8,128)S(1)}, f32[128,640]{1,0:T(8,128)S(1)}, u32[]{:S(2)}, u32[]{:S(2)}) %collective-permute-start.1) | collective-permute-done | bytes 327712 | tf_op jit(solution)/shard_map/ppermute | solution.py:360
  87.1 7.1 %shard_map.79 = (f32[1920,128]{1,0:T(8,128)}, f32[1536,128]{1,0:T(8,128)}) custom-call(f32[1536,128]{1,0:T(8,128)} %bitcast.5.refs_0_, f32[128,640]{1,0:T(8,128)S(1)} %shard_map.78.refs_1_, f32[128,640]{1,0:T(8,128)S(1)} %collective-permute-done.refs_2_, f32[128,640]{1,0:T(8,128)S(1)} %collective-permute-done.1.refs_3_, ...), custom_call_target="tpu_custom_call" | custom-call | flops 5000000000 | bytes 1000000 | tf_op jit(solution)/shard_map/pallas_call | solution.py:92
  94.2 5.2 %all-to-all-start.2 = ((f32[16,96,128]{2,1,0:T(8,128)}), f32[16,96,128]{2,1,0:T(8,128)S(1)}, u32[]{:S(2)}, u32[]{:S(2)}) async-start(f32[16,96,128]{2,1,0:T(8,128)} %bitcast.16), calls=%async_computation.2 | async-start | bytes 1572864 | tf_op jit(solution)/shard_map/all_to_all | solution.py:370
  105.0 4.6 %collective-permute-start.7 = (f32[128,640]{1,0:T(8,128)}, f32[128,640]{1,0:T(8,128)S(1)}, u32[]{:S(2)}, u32[]{:S(2)}) collective-permute-start(f32[128,640]{1,0:T(8,128)} %shard_map.81.refs_0_.refs_2_), channel_id=1, source_target_pairs={{16,0},{32,16},{48,32},{0,48},{17,1},{33,17},{49,33},{1,49},{18,2}... | collective-permute-start | bytes 983048 | tf_op jit(solution)/shard_map/ppermute | solution.py:360
  109.6 9.7 %shard_map.80.refs_3_ = f32[2,64,640]{2,1,0:T(8,128)} custom-call(s32[1]{0:T(128)} %bitcast.7.refs_0_, f32[3,2,64,640]{3,2,1,0:T(8,128)} %refs_0_.3, f32[2,2,64,640]{3,2,1,0:T(8,128)} %copy-done.1, f32[2,2,64,640]{3,2,1,0:T(8,128)} %copy-done.2), custom_call_target="tpu_custom_call" | custom-call | flops 8000000000 | bytes 1000000 | tf_op jit(solution)/shard_map/pallas_call | solution.py:92
  119.3 2.4 %collective-permute-done.7.refs_6_.refs_3_.refs_5_ = f32[128,640]{1,0:T(8,128)S(1)} collective-permute-done((f32[128,640]{1,0:T(8,128)}, f32[128,640]{1,0:T(8,128)S(1)}, u32[]{:S(2)}, u32[]{:S(2)}) %collective-permute-start.7) | collective-permute-done | bytes 327712 | tf_op jit(solution)/shard_map/ppermute | solution.py:360
  124.0 11.2 %all-to-all-start.3 = ((f32[16,96,128]{2,1,0:T(8,128)}), f32[16,96,128]{2,1,0:T(8,128)S(1)}, u32[]{:S(2)}, u32[]{:S(2)}) async-start(f32[16,96,128]{2,1,0:T(8,128)} %shard_map.82.refs_5_.refs_7_), calls=%async_computation.3 | async-start | bytes 1572864 | tf_op jit(solution)/shard_map/all_to_all | solution.py:370
  135.2 4.9 %shard_map.83 = (f32[64,640]{1,0:T(8,128)}, f32[64,640]{1,0:T(8,128)}, f32[64,640]{1,0:T(8,128)}, f32[64,640]{1,0:T(8,128)}) custom-call(f32[128,640]{1,0:T(8,128)} %shard_map.81.refs_0_.refs_2_, f32[128,640]{1,0:T(8,128)} %copy-done.4, f32[128,640]{1,0:T(8,128)} %copy-done.6, f32[128,640]{1,0:T(8,128)} %copy-done.8, ...), custom_call_target="tpu_custom_call" | custom-call | flops 4000000000 | bytes 1000000 | tf_op jit(solution)/shard_map/pallas_call | solution.py:92
  140.1 2.0 collective-permute-start.10
  142.1 5.3 %collective-permute-start.8 = (f32[64,640]{1,0:T(8,128)}, f32[64,640]{1,0:T(8,128)S(1)}, u32[]{:S(2)}, u32[]{:S(2)}) collective-permute-start(f32[64,640]{1,0:T(8,128)} %get-tuple-element.15), channel_id=1, source_target_pairs={{0,48},{16,0},{32,16},{48,32},{1,49},{17,1},{33,17},{49,33},{2,50}... | collective-permute-start | bytes 491528 | tf_op jit(solution)/shard_map/ppermute | solution.py:365
  147.4 3.1 %collective-permute-start.9 = (f32[64,640]{1,0:T(8,128)}, f32[64,640]{1,0:T(8,128)S(1)}, u32[]{:S(2)}, u32[]{:S(2)}) collective-permute-start(f32[64,640]{1,0:T(8,128)} %get-tuple-element.16), channel_id=1, source_target_pairs={{0,32},{16,48},{32,0},{48,16},{1,33},{17,49},{33,1},{49,17},{2,34}... | collective-permute-start | bytes 491528 | tf_op jit(solution)/shard_map/ppermute | solution.py:365
  150.5 5.0 %collective-permute-done.9.refs_9_.refs_3_ = f32[64,640]{1,0:T(8,128)S(1)} collective-permute-done((f32[64,640]{1,0:T(8,128)}, f32[64,640]{1,0:T(8,128)S(1)}, u32[]{:S(2)}, u32[]{:S(2)}) %collective-permute-start.9) | collective-permute-done | bytes 163872 | tf_op jit(solution)/shard_map/ppermute | solution.py:365
  155.5 2.0 all-to-all-done.3
  157.5 6.3 %shard_map.84 = f32[4,72,640]{2,1,0:T(8,128)} custom-call(s32[1]{0:T(128)} %bitcast.refs_0_, f32[1536,128]{1,0:T(8,128)S(1)} %bitcast.11, f32[128,640]{1,0:T(8,128)S(1)} %copy-done.3, f32[128,640]{1,0:T(8,128)S(1)} %copy-done.5, f32[128,640]{1,0:T(8,128)S(1)} %copy-done.7, f32[128,640]{1,0:T(8,128)S(1)} %copy-done.9, ...), custom_call_target="tpu_custom_call" | custom-call | flops 5000000000 | bytes 1000000 | tf_op jit(solution)/shard_map/pallas_call | solution.py:92
  163.8 7.8 %all-to-all-start.4 = ((f32[4,72,640]{2,1,0:T(8,128)}), f32[4,72,640]{2,1,0:T(8,128)S(1)}, u32[]{:S(2)}, u32[]{:S(2)}) async-start(f32[4,72,640]{2,1,0:T(8,128)} %shard_map.84), calls=%async_computation.4 | async-start | bytes 1474560 | tf_op jit(solution)/shard_map/all_to_all | solution.py:370
  171.6 9.7 %all-to-all-done.4.refs_0_ = f32[4,72,640]{2,1,0:T(8,128)S(1)} async-done(((f32[4,72,640]{2,1,0:T(8,128)}), f32[4,72,640]{2,1,0:T(8,128)S(1)}, u32[]{:S(2)}, u32[]{:S(2)}) %all-to-all-start.4) | async-done | bytes 737312 | tf_op jit(solution)/shard_map/all_to_all | solution.py:370
  183.2 14.7 %all-to-all-start.5 = ((f32[8,8,128]{2,1,0:T(8,128)}), f32[8,8,128]{2,1,0:T(8,128)S(1)}, u32[]{:S(2)}, u32[]{:S(2)}) async-start(f32[8,8,128]{2,1,0:T(8,128)} %get-tuple-element.19.refs_2_), calls=%async_computation.5 | async-start | bytes 65536 | tf_op jit(solution)/shard_map/all_to_all | solution.py:370
  198.7 4.2 %all-to-all-done.5.refs_0_ = f32[8,8,128]{2,1,0:T(8,128)S(1)} async-done(((f32[8,8,128]{2,1,0:T(8,128)}), f32[8,8,128]{2,1,0:T(8,128)S(1)}, u32[]{:S(2)}, u32[]{:S(2)}) %all-to-all-start.5) | async-done | bytes 32800 | tf_op jit(solution)/shard_map/all_to_all | solution.py:370
  (61 shorter events, 19.2 us)
Async XLA Ops:
  23.3 10.2 %copy-start = (f32[3,2,64,640]{3,2,1,0:T(8,128)S(1)}, f32[3,2,64,640]{3,2,1,0:T(8,128)}, u32[]{:S(2)}) copy-start(f32[3,2,64,640]{3,2,1,0:T(8,128)} %refs_0_.3) | copy-start | bytes 2949124
  23.4 63.7 %all-to-all-start.1 = ((f32[8,192,128]{2,1,0:T(8,128)}), f32[8,192,128]{2,1,0:T(8,128)}, u32[]{:S(2)}, u32[]{:S(2)}) async-start(f32[8,192,128]{2,1,0:T(8,128)} %bitcast.4), calls=%async_computation.1 | async-start | bytes 1572864 | tf_op jit(solution)/shard_map/all_to_all | solution.py:370
  33.6 53.4 %collective-permute-start.3 = (f32[2,2,64,640]{3,2,1,0:T(8,128)S(1)}, f32[2,2,64,640]{3,2,1,0:T(8,128)S(1)}, u32[]{:S(2)}, u32[]{:S(2)}) collective-permute-start(f32[2,2,64,640]{3,2,1,0:T(8,128)S(1)} %slice.4), channel_id=1, source_target_pairs={{504,0},{0,8},{8,16},{16,24},{24,32},{32,40},{40,48},{48,56},{56,6... | collective-permute-start | bytes 1966088 | tf_op jit(solution)/shard_map/ppermute | solution.py:356
  36.3 50.8 %collective-permute-start.4 = (f32[2,2,64,640]{3,2,1,0:T(8,128)S(1)}, f32[2,2,64,640]{3,2,1,0:T(8,128)S(1)}, u32[]{:S(2)}, u32[]{:S(2)}) collective-permute-start(f32[2,2,64,640]{3,2,1,0:T(8,128)S(1)} %slice.4), channel_id=1, source_target_pairs={{496,0},{504,8},{0,16},{8,24},{16,32},{24,40},{32,48},{40,56},{48,... | collective-permute-start | bytes 1966088 | tf_op jit(solution)/shard_map/ppermute | solution.py:356
  38.7 32.6 %collective-permute-start = (f32[128,640]{1,0:T(8,128)S(1)}, f32[128,640]{1,0:T(8,128)S(1)}, u32[]{:S(2)}, u32[]{:S(2)}) collective-permute-start(f32[128,640]{1,0:T(8,128)S(1)} %shard_map.78.refs_1_), channel_id=1, source_target_pairs={{48,0},{0,16},{16,32},{32,48},{49,1},{1,17},{17,33},{33,49},{50,2}... | collective-permute-start | bytes 983048 | tf_op jit(solution)/shard_map/ppermute | solution.py:360
  40.6 46.4 %collective-permute-start.1 = (f32[128,640]{1,0:T(8,128)S(1)}, f32[128,640]{1,0:T(8,128)S(1)}, u32[]{:S(2)}, u32[]{:S(2)}) collective-permute-start(f32[128,640]{1,0:T(8,128)S(1)} %shard_map.78.refs_1_), channel_id=1, source_target_pairs={{32,0},{48,16},{0,32},{16,48},{33,1},{49,17},{1,33},{17,49},{34,2}... | collective-permute-start | bytes 983048 | tf_op jit(solution)/shard_map/ppermute | solution.py:360
  47.3 39.8 %collective-permute-start.2 = (f32[128,640]{1,0:T(8,128)S(1)}, f32[128,640]{1,0:T(8,128)S(1)}, u32[]{:S(2)}, u32[]{:S(2)}) collective-permute-start(f32[128,640]{1,0:T(8,128)S(1)} %shard_map.78.refs_1_), channel_id=1, source_target_pairs={{16,0},{32,16},{48,32},{0,48},{17,1},{33,17},{49,33},{1,49},{18,2}... | collective-permute-start | bytes 983048 | tf_op jit(solution)/shard_map/ppermute | solution.py:360
  94.2 27.6 %all-to-all-start.2 = ((f32[16,96,128]{2,1,0:T(8,128)}), f32[16,96,128]{2,1,0:T(8,128)S(1)}, u32[]{:S(2)}, u32[]{:S(2)}) async-start(f32[16,96,128]{2,1,0:T(8,128)} %bitcast.16), calls=%async_computation.2 | async-start | bytes 1572864 | tf_op jit(solution)/shard_map/all_to_all | solution.py:370
  101.1 18.2 %collective-permute-start.5 = (f32[128,640]{1,0:T(8,128)}, f32[128,640]{1,0:T(8,128)S(1)}, u32[]{:S(2)}, u32[]{:S(2)}) collective-permute-start(f32[128,640]{1,0:T(8,128)} %shard_map.81.refs_0_.refs_2_), channel_id=1, source_target_pairs={{48,0},{0,16},{16,32},{32,48},{49,1},{1,17},{17,33},{33,49},{50,2}... | collective-permute-start | bytes 983048 | tf_op jit(solution)/shard_map/ppermute | solution.py:360
  103.1 16.3 %collective-permute-start.6 = (f32[128,640]{1,0:T(8,128)}, f32[128,640]{1,0:T(8,128)S(1)}, u32[]{:S(2)}, u32[]{:S(2)}) collective-permute-start(f32[128,640]{1,0:T(8,128)} %shard_map.81.refs_0_.refs_2_), channel_id=1, source_target_pairs={{32,0},{48,16},{0,32},{16,48},{33,1},{49,17},{1,33},{17,49},{34,2}... | collective-permute-start | bytes 983048 | tf_op jit(solution)/shard_map/ppermute | solution.py:360
  105.0 16.8 %collective-permute-start.7 = (f32[128,640]{1,0:T(8,128)}, f32[128,640]{1,0:T(8,128)S(1)}, u32[]{:S(2)}, u32[]{:S(2)}) collective-permute-start(f32[128,640]{1,0:T(8,128)} %shard_map.81.refs_0_.refs_2_), channel_id=1, source_target_pairs={{16,0},{32,16},{48,32},{0,48},{17,1},{33,17},{49,33},{1,49},{18,2}... | collective-permute-start | bytes 983048 | tf_op jit(solution)/shard_map/ppermute | solution.py:360
  124.0 33.5 %all-to-all-start.3 = ((f32[16,96,128]{2,1,0:T(8,128)}), f32[16,96,128]{2,1,0:T(8,128)S(1)}, u32[]{:S(2)}, u32[]{:S(2)}) async-start(f32[16,96,128]{2,1,0:T(8,128)} %shard_map.82.refs_5_.refs_7_), calls=%async_computation.3 | async-start | bytes 1572864 | tf_op jit(solution)/shard_map/all_to_all | solution.py:370
  135.2 22.3 %copy-start.3 = (f32[128,640]{1,0:T(8,128)S(1)}, f32[128,640]{1,0:T(8,128)}, u32[]{:S(2)}) copy-start(f32[128,640]{1,0:T(8,128)} %shard_map.81.refs_0_.refs_2_) | copy-start | bytes 983044
  135.2 22.3 %copy-start.5 = (f32[128,640]{1,0:T(8,128)S(1)}, f32[128,640]{1,0:T(8,128)}, u32[]{:S(2)}) copy-start(f32[128,640]{1,0:T(8,128)} %copy-done.4) | copy-start | bytes 983044
  135.2 22.3 %copy-start.7 = (f32[128,640]{1,0:T(8,128)S(1)}, f32[128,640]{1,0:T(8,128)}, u32[]{:S(2)}) copy-start(f32[128,640]{1,0:T(8,128)} %copy-done.6) | copy-start | bytes 983044
  135.2 22.3 %copy-start.9 = (f32[128,640]{1,0:T(8,128)S(1)}, f32[128,640]{1,0:T(8,128)}, u32[]{:S(2)}) copy-start(f32[128,640]{1,0:T(8,128)} %copy-done.8) | copy-start | bytes 983044
  140.1 10.4 %collective-permute-start.10 = (f32[64,640]{1,0:T(8,128)}, f32[64,640]{1,0:T(8,128)S(1)}, u32[]{:S(2)}, u32[]{:S(2)}) collective-permute-start(f32[64,640]{1,0:T(8,128)} %get-tuple-element.17), channel_id=1, source_target_pairs={{0,16},{16,32},{32,48},{48,0},{1,17},{17,33},{33,49},{49,1},{2,18}... | collective-permute-start | bytes 491528 | tf_op jit(solution)/shard_map/ppermute | solution.py:365
  142.1 8.5 %collective-permute-start.8 = (f32[64,640]{1,0:T(8,128)}, f32[64,640]{1,0:T(8,128)S(1)}, u32[]{:S(2)}, u32[]{:S(2)}) collective-permute-start(f32[64,640]{1,0:T(8,128)} %get-tuple-element.15), channel_id=1, source_target_pairs={{0,48},{16,0},{32,16},{48,32},{1,49},{17,1},{33,17},{49,33},{2,50}... | collective-permute-start | bytes 491528 | tf_op jit(solution)/shard_map/ppermute | solution.py:365
  147.4 8.1 %collective-permute-start.9 = (f32[64,640]{1,0:T(8,128)}, f32[64,640]{1,0:T(8,128)S(1)}, u32[]{:S(2)}, u32[]{:S(2)}) collective-permute-start(f32[64,640]{1,0:T(8,128)} %get-tuple-element.16), channel_id=1, source_target_pairs={{0,32},{16,48},{32,0},{48,16},{1,33},{17,49},{33,1},{49,17},{2,34}... | collective-permute-start | bytes 491528 | tf_op jit(solution)/shard_map/ppermute | solution.py:365
  163.8 7.8 %copy-start.18 = (f32[640]{0:T(1024)S(1)}, f32[640]{0:T(1024)}, u32[]{:S(2)}) copy-start(f32[640]{0:T(1024)} %param.9) | copy-start | bytes 7684
  163.8 17.6 %copy-start.17 = (f32[64,640]{1,0:T(8,128)S(1)}, f32[64,640]{1,0:T(8,128)}, u32[]{:S(2)}) copy-start(f32[64,640]{1,0:T(8,128)} %get-tuple-element.18.refs_1_) | copy-start | bytes 491524
  163.8 17.6 %all-to-all-start.4 = ((f32[4,72,640]{2,1,0:T(8,128)}), f32[4,72,640]{2,1,0:T(8,128)S(1)}, u32[]{:S(2)}, u32[]{:S(2)}) async-start(f32[4,72,640]{2,1,0:T(8,128)} %shard_map.84), calls=%async_computation.4 | async-start | bytes 1474560 | tf_op jit(solution)/shard_map/all_to_all | solution.py:370
  183.2 14.7 %copy-start.12 = (f32[1,10,3,384]{3,0,2,1:T(1,128)S(1)}, f32[1,10,3,384]{3,0,2,1:T(1,128)}, u32[]{:S(2)}) copy-start(f32[1,10,3,384]{3,0,2,1:T(1,128)} %param.7) | copy-start | bytes 138244
  183.2 19.7 %all-to-all-start.5 = ((f32[8,8,128]{2,1,0:T(8,128)}), f32[8,8,128]{2,1,0:T(8,128)S(1)}, u32[]{:S(2)}, u32[]{:S(2)}) async-start(f32[8,8,128]{2,1,0:T(8,128)} %get-tuple-element.19.refs_2_), calls=%async_computation.5 | async-start | bytes 65536 | tf_op jit(solution)/shard_map/all_to_all | solution.py:370
  (11 other events, 39.2 us)

commit v6 on v5

--- a/solution.py
+++ b/solution.py
@@ -149,10 +149,19 @@
 
 
 def prepare_queries_body(args, lazy, results, scratch, need, send):
-    need()
-    (queries_ref,) = results
-    queries_ref[0:TOK, :] = lazy[0][0, 0]
-    queries_ref[TOK : 2 * TOK, :] = lazy[0][0, 1]
+    (position_ref,), (qkv_ref,), (queries_ref, tail_ref) = args, lazy, results
+    last = position_ref[0] == BLOCKS - 1
+    need()
+    queries_ref[0:TOK, :] = qkv_ref[0, 0]
+    queries_ref[TOK : 2 * TOK, :] = qkv_ref[0, 1]
+    send(0)
+    for a in range(2):
+        tail_ref[a] = jnp.where(last, qkv_ref[1 + a, 0], qkv_ref[1 + a, 1])
+
+
+def prepare_far_body(args, lazy, results, scratch, need, send):
+    need()
+    results[0][...] = lazy[0][...]
 
 
 def widened(part):
@@ -325,7 +334,7 @@
 
 
 def attention_body(args, lazy, results, scratch, need, send):
-    (position_ref,), (qkv_ref, near_ref, far_ref), (out_ref,) = args, lazy, results
+    (position_ref,), (qkv_ref, *near_refs, far_ref), (out_ref,) = args, lazy, results
     position = position_ref[0]
     row = lax.broadcasted_iota(jnp.int32, (TOK, 3 * TOK), 0) + 2 * TOK
     col = lax.broadcasted_iota(jnp.int32, (TOK, 3 * TOK), 1)
@@ -338,10 +347,9 @@
             at = slice(h * ATT, (h + 1) * ATT)
             parts = []
             for a in range(2):
-                far, near = far_ref[a, c, :, at], near_ref[a, c, :, at]
+                far, near = far_ref[a, c, :, at], near_refs[c][a, :, at]
                 if c == 1:
                     far = jnp.where(position >= 2, far, far_ref[a, 0, :, at])
-                    near = jnp.where(position >= 1, near, near_ref[a, 0, :, at])
                 parts.append(jnp.concatenate([far, near, qkv_ref[1 + a, c, :, at]], axis=0))
             keys, values = parts
             scores = dot(qkv_ref[0, c, :, at], keys, ((1,), (1,))) * (1.0 / math.sqrt(ATT))
@@ -391,20 +399,20 @@
     (spread,) = call(spread_body, [(NZ, NX * NY, 24, LANES)], 1, packs, fan=(0,), room=SMALL)
     recv1 = exchange(spread.reshape(NZ, NX * NY * 24, LANES), "z").reshape(BLOCKS * 24, LANES)
     pairs = from_neighbours(pairs)
-    near, far = behind(qkv[1:], 1), behind(qkv[1:], 2)
+    near0 = behind(qkv[1:, 0], 1)
     weights, send2 = call(
         gradient_body, [(3 * D, LANES), (BLOCKS * 24, LANES)], 5, recv1, lazy=whole(*pairs),
-        scratch=[(3 * D, LANES)], after=(near, far), room=ROOM - 1024 * 1024,
+        scratch=[(3 * D, LANES)], after=(near0,), room=ROOM - 512 * 1024,
     )
     recv2 = exchange(send2.reshape(NZ * NY, NX * 24, LANES), ("z", "yh"))
-    (queries,) = call(prepare_queries_body, [(2 * TOK, D)], 1, lazy=[(qkv, (0, 1))], after=(weights,))
+    queries, tail = call(
+        prepare_queries_body, [(2 * TOK, D), (2, TOK, D)], 1, position, lazy=whole(qkv), smem=(0,), after=(weights,)
+    )
     queries = from_neighbours(queries)
-    (attended,) = call(
-        attention_body, [(GROUPS, TOK, D)], 8, position, lazy=whole(qkv, near, far), smem=(0,)
-    )
+    near1 = behind(tail, 1)
     (send3,) = call(
         moment_body, [(NZ * NY, NX * 24, LANES)], 2, yh, recv2, packs, smem=(0,), fan=(0,),
-        after=(attended, *queries[1:]),
+        after=(near1, *queries[1:]),
         room=ROOM,
     )
     recv3 = exchange(send3, ("z", "yh")).reshape(BLOCKS * 24, LANES)
@@ -414,15 +422,21 @@
             after=(send3,),
         )
     )
+    (far,) = call(prepare_far_body, [(2, GROUPS, TOK, D)], 1, lazy=[(qkv, (1, 2))], after=(send3,))
+    far = behind(far, 2)
     (send_second,) = call(
         second_read_body, [(NX, TOK + 8, D)], 5, x, recv3,
         lazy=[*((q, (TOK, TOK)) for q in queries), (weights, None), (send3, (0, 1))], scratch=[(3 * D, LANES)],
-        smem=(0,), after=first[1:], room=ROOM,
+        smem=(0,), after=(far, *first[1:]), room=ROOM,
     )
     second = exchange(send_second, "x")
+    (attended,) = call(
+        attention_body, [(GROUPS, TOK, D)], 8, position, lazy=whole(qkv, near0, near1, far), smem=(0,),
+        after=(send_second,),
+    )
     readout, send5 = call(
         squares_body, [(GROUPS, TOK, D), (NARROW, 8, GROUPS * TOK)], 1, second, lazy=whole(*first), fan=(1,),
-        room=SMALL,
+        after=(attended,), room=SMALL,
     )
     recv5 = exchange(send5, "narrow")
     new_weights, new_moment = call(

time: 206 us -> 198 us (0.961)
  starting transfers between devices: 83.2 us -> 76.9 us
  waiting for transfers between devices: 61.1 us -> 58.6 us
    ppermute x6, waiting for transfers between devices: 40.3 us -> 13.3 us  [from_neighbours(): lax.ppermute(block, 'x', [((i - s) % NX, i) for i in range(NX)])]
    ppermute x2 -> x3, waiting for transfers between devices: 0.01 us -> 22.5 us  [behind(): lax.ppermute(block, axes, [((i - distance) % BLOCKS, i) for i in range(BL...]
    all_to_all x5, starting transfers between devices: 49.1 us -> 34.4 us  [exchange(): return lax.all_to_all(pieces, axes, split_axis=0, concat_axis=0, tiled=True)]
    ppermute x3, waiting for transfers between devices: 4.96 us -> 18.6 us  [back_to_neighbours(): lax.ppermute(blocks[s], 'x', [(i, (i - s) % NX) for i in range(NX)])]
    all_to_all x5, waiting for transfers between devices: 15.9 us -> 4.22 us  [exchange(): return lax.all_to_all(pieces, axes, split_axis=0, concat_axis=0, tiled=True)]
    ppermute x2 -> x3, starting transfers between devices: 4.84 us -> 12.7 us  [behind(): lax.ppermute(block, axes, [((i - distance) % BLOCKS, i) for i in range(BL...]
    ppermute x3, starting transfers between devices: 10.4 us -> 12.7 us  [back_to_neighbours(): lax.ppermute(blocks[s], 'x', [(i, (i - s) % NX) for i in range(NX)])]
    pallas_call x12 -> x13, Pallas kernels: 35.9 us -> 36.7 us  [call(): pl.pallas_call(kernel, out_shape=[jax.ShapeDtypeStruct(s, jnp.float32) fo...]
  transfers between devices with their start and end apart: 16 -> 17, of which waited for: 7 -> 8; matrix products, arithmetic and copies ran while one was open for 0% -> 0% of each run, Pallas kernels for 8% -> 10%
where the time goes in v6:
time: 198 us; the launch traced here: 197 us
  starting transfers between devices  76.9 us (39%)
  waiting for transfers between devices  58.6 us (30%)
  Pallas kernels  36.7 us (19%)
  blocking collectives  19.7 us (10%)
  local copies, waits for them, and re-layouts  3.44 us (2%)
    pallas_call x13, Pallas kernels, call(): pl.pallas_call(kernel, out_shape=[jax.ShapeDtypeStruct(s, jnp.float32) fo...  36.7 us
    all_to_all x5, starting transfers between devices, exchange(): return lax.all_to_all(pieces, axes, split_axis=0, concat_axis=0, tiled=True)  34.4 us
    ppermute x3, waiting for transfers between devices, behind(): lax.ppermute(block, axes, [((i - distance) % BLOCKS, i) for i in range(BL...  22.5 us
    all_to_all x1, blocking collectives, exchange(): return lax.all_to_all(pieces, axes, split_axis=0, concat_axis=0, tiled=True)  19.7 us
    ppermute x3, waiting for transfers between devices, back_to_neighbours(): lax.ppermute(blocks[s], 'x', [(i, (i - s) % NX) for i in range(NX)])  18.6 us
    ppermute x6, starting transfers between devices, from_neighbours(): lax.ppermute(block, 'x', [((i - s) % NX, i) for i in range(NX)])  17.1 us
    ppermute x6, waiting for transfers between devices, from_neighbours(): lax.ppermute(block, 'x', [((i - s) % NX, i) for i in range(NX)])  13.3 us
    ppermute x3, starting transfers between devices, behind(): lax.ppermute(block, axes, [((i - distance) % BLOCKS, i) for i in range(BL...  12.7 us
  transfers between devices with their start and end apart: 17, of which 8 were waited for; matrix products, arithmetic and copies ran while one was open for 0% of the time, Pallas kernels for 10%

profile of v6, /device:TPU:1, one launch (start us, length us, event | category | flops | bytes accessed | tf_op | source)
XLA Modules:
  0.0 196.7 jit_solution(7851099407604529928)
XLA Ops:
  2.6 19.7 %all_to_all.30.refs_0_.refs_2_ = f32[8,48,128]{2,1,0:T(8,128)S(1)} all-to-all(f32[8,48,128]{2,1,0:T(8,128)S(1)} %shard_map.76), channel_id=1, replica_groups=mesh['z'=8,'x'=4,'yh'=2,'narrow'=8] {'x','yh'}, dimensions={0} | all-to-all | bytes 393216 | tf_op jit(solution)/shard_map/all_to_all | solution.py:378
  23.4 10.2 %all-to-all-start.1 = ((f32[8,192,128]{2,1,0:T(8,128)}), f32[8,192,128]{2,1,0:T(8,128)S(1)}, u32[]{:S(2)}, u32[]{:S(2)}) async-start(f32[8,192,128]{2,1,0:T(8,128)} %bitcast.4), calls=%async_computation.1 | async-start | bytes 1572864 | tf_op jit(solution)/shard_map/all_to_all | solution.py:378
  35.7 3.7 %collective-permute-start.1 = (f32[128,640]{1,0:T(8,128)S(1)}, f32[128,640]{1,0:T(8,128)S(1)}, u32[]{:S(2)}, u32[]{:S(2)}) collective-permute-start(f32[128,640]{1,0:T(8,128)S(1)} %shard_map.78.refs_1_), channel_id=1, source_target_pairs={{32,0},{48,16},{0,32},{16,48},{33,1},{49,17},{1,33},{17,49},{34,2}... | collective-permute-start | bytes 983048 | tf_op jit(solution)/shard_map/ppermute | solution.py:368
  44.9 4.9 %collective-permute-done.1.refs_3_ = f32[128,640]{1,0:T(8,128)S(1)} collective-permute-done((f32[128,640]{1,0:T(8,128)S(1)}, f32[128,640]{1,0:T(8,128)S(1)}, u32[]{:S(2)}, u32[]{:S(2)}) %collective-permute-start.1) | collective-permute-done | bytes 327712 | tf_op jit(solution)/shard_map/ppermute | solution.py:368
  49.9 4.5 %collective-permute-done.2.refs_4_ = f32[128,640]{1,0:T(8,128)S(1)} collective-permute-done((f32[128,640]{1,0:T(8,128)S(1)}, f32[128,640]{1,0:T(8,128)S(1)}, u32[]{:S(2)}, u32[]{:S(2)}) %collective-permute-start.2) | collective-permute-done | bytes 327712 | tf_op jit(solution)/shard_map/ppermute | solution.py:368
  54.4 7.1 %collective-permute-done.3.refs_5_.refs_2_ = f32[2,64,640]{2,1,0:T(8,128)S(1)} collective-permute-done((f32[2,64,640]{2,1,0:T(8,128)S(1)}, f32[2,64,640]{2,1,0:T(8,128)S(1)}, u32[]{:S(2)}, u32[]{:S(2)}) %collective-permute-start.3) | collective-permute-done | bytes 327712 | tf_op jit(solution)/shard_map/ppermute | solution.py:364
  61.5 5.6 %shard_map.79 = (f32[1920,128]{1,0:T(8,128)}, f32[1536,128]{1,0:T(8,128)}) custom-call(f32[1536,128]{1,0:T(8,128)S(1)} %bitcast.16, f32[128,640]{1,0:T(8,128)S(1)} %shard_map.78.refs_1_, f32[128,640]{1,0:T(8,128)S(1)} %collective-permute-done.refs_2_, f32[128,640]{1,0:T(8,128)S(1)} %collective-permute-done.1.refs_3_, ...), custom_call_target="tpu_custom_call" | custom-call | flops 5000000000 | bytes 1000000 | tf_op jit(solution)/shard_map/pallas_call | solution.py:92
  67.1 9.6 %all-to-all-start.2 = ((f32[16,96,128]{2,1,0:T(8,128)}), f32[16,96,128]{2,1,0:T(8,128)S(1)}, u32[]{:S(2)}, u32[]{:S(2)}) async-start(f32[16,96,128]{2,1,0:T(8,128)} %bitcast.7), calls=%async_computation.2 | async-start | bytes 1572864 | tf_op jit(solution)/shard_map/all_to_all | solution.py:378
  83.5 3.8 %collective-permute-start.7 = (f32[128,640]{1,0:T(8,128)}, f32[128,640]{1,0:T(8,128)S(1)}, u32[]{:S(2)}, u32[]{:S(2)}) collective-permute-start(f32[128,640]{1,0:T(8,128)} %get-tuple-element.18.refs_0_.refs_2_), channel_id=1, source_target_pairs={{16,0},{32,16},{48,32},{0,48},{17,1},{33,17},{49,33},{1,49},{18,2}... | collective-permute-start | bytes 983048 | tf_op jit(solution)/shard_map/ppermute | solution.py:368
  87.3 7.2 %collective-permute-start.4 = (f32[2,64,640]{2,1,0:T(8,128)}, f32[2,64,640]{2,1,0:T(8,128)S(1)}, u32[]{:S(2)}, u32[]{:S(2)}) collective-permute-start(f32[2,64,640]{2,1,0:T(8,128)} %get-tuple-element.17), channel_id=1, source_target_pairs={{504,0},{0,8},{8,16},{16,24},{24,32},{32,40},{40,48},{48,56},{56,6... | collective-permute-start | bytes 983048 | tf_op jit(solution)/shard_map/ppermute | solution.py:364
  94.5 3.8 %collective-permute-done.7.refs_6_.refs_3_.refs_5_ = f32[128,640]{1,0:T(8,128)S(1)} collective-permute-done((f32[128,640]{1,0:T(8,128)}, f32[128,640]{1,0:T(8,128)S(1)}, u32[]{:S(2)}, u32[]{:S(2)}) %collective-permute-start.7) | collective-permute-done | bytes 327712 | tf_op jit(solution)/shard_map/ppermute | solution.py:368
  98.3 15.4 %collective-permute-done.4.refs_3_ = f32[2,64,640]{2,1,0:T(8,128)S(1)} collective-permute-done((f32[2,64,640]{2,1,0:T(8,128)}, f32[2,64,640]{2,1,0:T(8,128)S(1)}, u32[]{:S(2)}, u32[]{:S(2)}) %collective-permute-start.4) | collective-permute-done | bytes 327712 | tf_op jit(solution)/shard_map/ppermute | solution.py:364
  114.9 4.8 %all-to-all-start.3 = ((f32[16,96,128]{2,1,0:T(8,128)}), f32[16,96,128]{2,1,0:T(8,128)S(1)}, u32[]{:S(2)}, u32[]{:S(2)}) async-start(f32[16,96,128]{2,1,0:T(8,128)} %shard_map.81.refs_1_.refs_5_.refs_7_), calls=%async_computation.3 | async-start | bytes 1572864 | tf_op jit(solution)/shard_map/all_to_all | solution.py:378
  121.8 3.2 %collective-permute-start.8 = (f32[2,2,64,640]{3,2,1,0:T(8,128)}, f32[2,2,64,640]{3,2,1,0:T(8,128)S(1)}, u32[]{:S(2)}, u32[]{:S(2)}) collective-permute-start(f32[2,2,64,640]{3,2,1,0:T(8,128)} %shard_map.82), channel_id=1, source_target_pairs={{496,0},{504,8},{0,16},{8,24},{16,32},{24,40},{32,48},{40,56},{48,... | collective-permute-start | bytes 1966088 | tf_op jit(solution)/shard_map/ppermute | solution.py:364
  125.0 4.8 %shard_map.83 = (f32[64,640]{1,0:T(8,128)}, f32[64,640]{1,0:T(8,128)}, f32[64,640]{1,0:T(8,128)}, f32[64,640]{1,0:T(8,128)}) custom-call(f32[128,640]{1,0:T(8,128)} %get-tuple-element.18.refs_0_.refs_2_, f32[128,640]{1,0:T(8,128)} %copy-done.4, f32[128,640]{1,0:T(8,128)} %copy-done.7, f32[128,640]{1,0:T(8,128)} %copy-done.9, ...), custom_call_target="tpu_custom_call" | custom-call | flops 4000000000 | bytes 1000000 | tf_op jit(solution)/shard_map/pallas_call | solution.py:92
  129.8 6.2 %collective-permute-start.10 = (f32[64,640]{1,0:T(8,128)}, f32[64,640]{1,0:T(8,128)S(1)}, u32[]{:S(2)}, u32[]{:S(2)}) collective-permute-start(f32[64,640]{1,0:T(8,128)} %get-tuple-element.20), channel_id=1, source_target_pairs={{0,32},{16,48},{32,0},{48,16},{1,33},{17,49},{33,1},{49,17},{2,34}... | collective-permute-start | bytes 491528 | tf_op jit(solution)/shard_map/ppermute | solution.py:373
  137.9 4.6 %collective-permute-start.9 = (f32[64,640]{1,0:T(8,128)}, f32[64,640]{1,0:T(8,128)S(1)}, u32[]{:S(2)}, u32[]{:S(2)}) collective-permute-start(f32[64,640]{1,0:T(8,128)} %get-tuple-element.19), channel_id=1, source_target_pairs={{0,48},{16,0},{32,16},{48,32},{1,49},{17,1},{33,17},{49,33},{2,50}... | collective-permute-start | bytes 491528 | tf_op jit(solution)/shard_map/ppermute | solution.py:373
  142.5 3.3 %collective-permute-done.10.refs_10_.refs_3_ = f32[64,640]{1,0:T(8,128)S(1)} collective-permute-done((f32[64,640]{1,0:T(8,128)}, f32[64,640]{1,0:T(8,128)S(1)}, u32[]{:S(2)}, u32[]{:S(2)}) %collective-permute-start.10) | collective-permute-done | bytes 163872 | tf_op jit(solution)/shard_map/ppermute | solution.py:373
  145.9 15.3 %collective-permute-done.11.refs_11_.refs_4_ = f32[64,640]{1,0:T(8,128)S(1)} collective-permute-done((f32[64,640]{1,0:T(8,128)}, f32[64,640]{1,0:T(8,128)S(1)}, u32[]{:S(2)}, u32[]{:S(2)}) %collective-permute-start.11) | collective-permute-done | bytes 163872 | tf_op jit(solution)/shard_map/ppermute | solution.py:373
  161.2 6.3 %shard_map.84.refs_5_ = f32[4,72,640]{2,1,0:T(8,128)} custom-call(s32[1]{0:T(128)} %bitcast.refs_0_, f32[1536,128]{1,0:T(8,128)S(1)} %bitcast.15, f32[128,640]{1,0:T(8,128)S(1)} %copy-done.3, f32[128,640]{1,0:T(8,128)S(1)} %copy-done.5, f32[128,640]{1,0:T(8,128)S(1)} %copy-done.8, f32[128,640]{1,0:T(8,128)S(1)} %copy-done.10, ...), custom_call_target="tpu_custom_call" | custom-call | flops 5000000000 | bytes 1000000 | tf_op jit(solution)/shard_map/pallas_call | solution.py:92
  167.5 3.7 %all-to-all-start.4 = ((f32[4,72,640]{2,1,0:T(8,128)}), f32[4,72,640]{2,1,0:T(8,128)S(1)}, u32[]{:S(2)}, u32[]{:S(2)}) async-start(f32[4,72,640]{2,1,0:T(8,128)} %shard_map.84.refs_5_), calls=%async_computation.4 | async-start | bytes 1474560 | tf_op jit(solution)/shard_map/all_to_all | solution.py:378
  171.2 9.8 %shard_map.85.refs_5_.refs_3_ = f32[2,64,640]{2,1,0:T(8,128)} custom-call(s32[1]{0:T(128)} %bitcast.8.refs_0_, f32[3,2,64,640]{3,2,1,0:T(8,128)} %refs_1_.5, f32[2,64,640]{2,1,0:T(8,128)} %copy-done.2, f32[2,64,640]{2,1,0:T(8,128)} %copy-done.6, f32[2,2,64,640]{3,2,1,0:T(8,128)} %copy-done.1, f32[4,72,640]{2,1,0:T(8,128)} %shard_map.84.refs_5_), custom_call_target="tpu_custom_call" | custom-call | flops 8000000000 | bytes 1000000 | tf_op jit(solution)/shard_map/pallas_call | solution.py:92
  183.8 6.1 %all-to-all-start.5 = ((f32[8,8,128]{2,1,0:T(8,128)}), f32[8,8,128]{2,1,0:T(8,128)S(1)}, u32[]{:S(2)}, u32[]{:S(2)}) async-start(f32[8,8,128]{2,1,0:T(8,128)} %get-tuple-element.23.refs_2_), calls=%async_computation.5 | async-start | bytes 65536 | tf_op jit(solution)/shard_map/all_to_all | solution.py:378
  190.7 4.2 %all-to-all-done.5.refs_0_ = f32[8,8,128]{2,1,0:T(8,128)S(1)} async-done(((f32[8,8,128]{2,1,0:T(8,128)}), f32[8,8,128]{2,1,0:T(8,128)S(1)}, u32[]{:S(2)}, u32[]{:S(2)}) %all-to-all-start.5) | async-done | bytes 32800 | tf_op jit(solution)/shard_map/all_to_all | solution.py:378
  (66 shorter events, 27.7 us)
Async XLA Ops:
  23.4 38.2 %all-to-all-start.1 = ((f32[8,192,128]{2,1,0:T(8,128)}), f32[8,192,128]{2,1,0:T(8,128)S(1)}, u32[]{:S(2)}, u32[]{:S(2)}) async-start(f32[8,192,128]{2,1,0:T(8,128)} %bitcast.4), calls=%async_computation.1 | async-start | bytes 1572864 | tf_op jit(solution)/shard_map/all_to_all | solution.py:378
  33.8 11.1 %collective-permute-start = (f32[128,640]{1,0:T(8,128)S(1)}, f32[128,640]{1,0:T(8,128)S(1)}, u32[]{:S(2)}, u32[]{:S(2)}) collective-permute-start(f32[128,640]{1,0:T(8,128)S(1)} %shard_map.78.refs_1_), channel_id=1, source_target_pairs={{48,0},{0,16},{16,32},{32,48},{49,1},{1,17},{17,33},{33,49},{50,2}... | collective-permute-start | bytes 983048 | tf_op jit(solution)/shard_map/ppermute | solution.py:368
  35.7 14.1 %collective-permute-start.1 = (f32[128,640]{1,0:T(8,128)S(1)}, f32[128,640]{1,0:T(8,128)S(1)}, u32[]{:S(2)}, u32[]{:S(2)}) collective-permute-start(f32[128,640]{1,0:T(8,128)S(1)} %shard_map.78.refs_1_), channel_id=1, source_target_pairs={{32,0},{48,16},{0,32},{16,48},{33,1},{49,17},{1,33},{17,49},{34,2}... | collective-permute-start | bytes 983048 | tf_op jit(solution)/shard_map/ppermute | solution.py:368
  39.4 15.0 %collective-permute-start.2 = (f32[128,640]{1,0:T(8,128)S(1)}, f32[128,640]{1,0:T(8,128)S(1)}, u32[]{:S(2)}, u32[]{:S(2)}) collective-permute-start(f32[128,640]{1,0:T(8,128)S(1)} %shard_map.78.refs_1_), channel_id=1, source_target_pairs={{16,0},{32,16},{48,32},{0,48},{17,1},{33,17},{49,33},{1,49},{18,2}... | collective-permute-start | bytes 983048 | tf_op jit(solution)/shard_map/ppermute | solution.py:368
  42.5 19.0 %collective-permute-start.3 = (f32[2,64,640]{2,1,0:T(8,128)S(1)}, f32[2,64,640]{2,1,0:T(8,128)S(1)}, u32[]{:S(2)}, u32[]{:S(2)}) collective-permute-start(f32[2,64,640]{2,1,0:T(8,128)S(1)} %slice_bitcast_fusion), channel_id=1, source_target_pairs={{504,0},{0,8},{8,16},{16,24},{24,32},{32,40},{40,48},{48,56},{56,6... | collective-permute-start | bytes 983048 | tf_op jit(solution)/shard_map/ppermute | solution.py:364
  67.1 46.6 %all-to-all-start.2 = ((f32[16,96,128]{2,1,0:T(8,128)}), f32[16,96,128]{2,1,0:T(8,128)S(1)}, u32[]{:S(2)}, u32[]{:S(2)}) async-start(f32[16,96,128]{2,1,0:T(8,128)} %bitcast.7), calls=%async_computation.2 | async-start | bytes 1572864 | tf_op jit(solution)/shard_map/all_to_all | solution.py:378
  78.9 15.6 %collective-permute-start.5 = (f32[128,640]{1,0:T(8,128)}, f32[128,640]{1,0:T(8,128)S(1)}, u32[]{:S(2)}, u32[]{:S(2)}) collective-permute-start(f32[128,640]{1,0:T(8,128)} %get-tuple-element.18.refs_0_.refs_2_), channel_id=1, source_target_pairs={{48,0},{0,16},{16,32},{32,48},{49,1},{1,17},{17,33},{33,49},{50,2}... | collective-permute-start | bytes 983048 | tf_op jit(solution)/shard_map/ppermute | solution.py:368
  80.8 13.7 %collective-permute-start.6 = (f32[128,640]{1,0:T(8,128)}, f32[128,640]{1,0:T(8,128)S(1)}, u32[]{:S(2)}, u32[]{:S(2)}) collective-permute-start(f32[128,640]{1,0:T(8,128)} %get-tuple-element.18.refs_0_.refs_2_), channel_id=1, source_target_pairs={{32,0},{48,16},{0,32},{16,48},{33,1},{49,17},{1,33},{17,49},{34,2}... | collective-permute-start | bytes 983048 | tf_op jit(solution)/shard_map/ppermute | solution.py:368
  83.5 14.8 %collective-permute-start.7 = (f32[128,640]{1,0:T(8,128)}, f32[128,640]{1,0:T(8,128)S(1)}, u32[]{:S(2)}, u32[]{:S(2)}) collective-permute-start(f32[128,640]{1,0:T(8,128)} %get-tuple-element.18.refs_0_.refs_2_), channel_id=1, source_target_pairs={{16,0},{32,16},{48,32},{0,48},{17,1},{33,17},{49,33},{1,49},{18,2}... | collective-permute-start | bytes 983048 | tf_op jit(solution)/shard_map/ppermute | solution.py:368
  87.3 26.4 %collective-permute-start.4 = (f32[2,64,640]{2,1,0:T(8,128)}, f32[2,64,640]{2,1,0:T(8,128)S(1)}, u32[]{:S(2)}, u32[]{:S(2)}) collective-permute-start(f32[2,64,640]{2,1,0:T(8,128)} %get-tuple-element.17), channel_id=1, source_target_pairs={{504,0},{0,8},{8,16},{16,24},{24,32},{32,40},{40,48},{48,56},{56,6... | collective-permute-start | bytes 983048 | tf_op jit(solution)/shard_map/ppermute | solution.py:364
  94.5 20.4 %copy-start.4 = (f32[128,640]{1,0:T(8,128)}, f32[128,640]{1,0:T(8,128)S(1)}, u32[]{:S(2)}) copy-start(f32[128,640]{1,0:T(8,128)S(1)} %collective-permute-done.5.refs_4_.refs_1_.refs_3_) | copy-start | bytes 983044
  94.5 20.4 %copy-start.7 = (f32[128,640]{1,0:T(8,128)}, f32[128,640]{1,0:T(8,128)S(1)}, u32[]{:S(2)}) copy-start(f32[128,640]{1,0:T(8,128)S(1)} %collective-permute-done.6.refs_5_.refs_2_.refs_4_) | copy-start | bytes 983044
  98.3 16.6 %copy-start.9 = (f32[128,640]{1,0:T(8,128)}, f32[128,640]{1,0:T(8,128)S(1)}, u32[]{:S(2)}) copy-start(f32[128,640]{1,0:T(8,128)S(1)} %collective-permute-done.7.refs_6_.refs_3_.refs_5_) | copy-start | bytes 983044
  114.9 46.3 %all-to-all-start.3 = ((f32[16,96,128]{2,1,0:T(8,128)}), f32[16,96,128]{2,1,0:T(8,128)S(1)}, u32[]{:S(2)}, u32[]{:S(2)}) async-start(f32[16,96,128]{2,1,0:T(8,128)} %shard_map.81.refs_1_.refs_5_.refs_7_), calls=%async_computation.3 | async-start | bytes 1572864 | tf_op jit(solution)/shard_map/all_to_all | solution.py:378
  121.7 39.5 %copy-start.3 = (f32[128,640]{1,0:T(8,128)S(1)}, f32[128,640]{1,0:T(8,128)}, u32[]{:S(2)}) copy-start(f32[128,640]{1,0:T(8,128)} %get-tuple-element.18.refs_0_.refs_2_) | copy-start | bytes 983044
  121.7 39.4 %copy-start.5 = (f32[128,640]{1,0:T(8,128)S(1)}, f32[128,640]{1,0:T(8,128)}, u32[]{:S(2)}) copy-start(f32[128,640]{1,0:T(8,128)} %copy-done.4) | copy-start | bytes 983044
  121.8 39.4 %copy-start.8 = (f32[128,640]{1,0:T(8,128)S(1)}, f32[128,640]{1,0:T(8,128)}, u32[]{:S(2)}) copy-start(f32[128,640]{1,0:T(8,128)} %copy-done.7) | copy-start | bytes 983044
  121.8 39.4 %copy-start.10 = (f32[128,640]{1,0:T(8,128)S(1)}, f32[128,640]{1,0:T(8,128)}, u32[]{:S(2)}) copy-start(f32[128,640]{1,0:T(8,128)} %copy-done.9) | copy-start | bytes 983044
  121.8 39.4 %collective-permute-start.8 = (f32[2,2,64,640]{3,2,1,0:T(8,128)}, f32[2,2,64,640]{3,2,1,0:T(8,128)S(1)}, u32[]{:S(2)}, u32[]{:S(2)}) collective-permute-start(f32[2,2,64,640]{3,2,1,0:T(8,128)} %shard_map.82), channel_id=1, source_target_pairs={{496,0},{504,8},{0,16},{8,24},{16,32},{24,40},{32,48},{40,56},{48,... | collective-permute-start | bytes 1966088 | tf_op jit(solution)/shard_map/ppermute | solution.py:364
  129.8 16.1 %collective-permute-start.10 = (f32[64,640]{1,0:T(8,128)}, f32[64,640]{1,0:T(8,128)S(1)}, u32[]{:S(2)}, u32[]{:S(2)}) collective-permute-start(f32[64,640]{1,0:T(8,128)} %get-tuple-element.20), channel_id=1, source_target_pairs={{0,32},{16,48},{32,0},{48,16},{1,33},{17,49},{33,1},{49,17},{2,34}... | collective-permute-start | bytes 491528 | tf_op jit(solution)/shard_map/ppermute | solution.py:373
  136.0 25.1 %collective-permute-start.11 = (f32[64,640]{1,0:T(8,128)}, f32[64,640]{1,0:T(8,128)S(1)}, u32[]{:S(2)}, u32[]{:S(2)}) collective-permute-start(f32[64,640]{1,0:T(8,128)} %get-tuple-element.21), channel_id=1, source_target_pairs={{0,16},{16,32},{32,48},{48,0},{1,17},{17,33},{33,49},{49,1},{2,18}... | collective-permute-start | bytes 491528 | tf_op jit(solution)/shard_map/ppermute | solution.py:373
  137.9 23.2 %collective-permute-start.9 = (f32[64,640]{1,0:T(8,128)}, f32[64,640]{1,0:T(8,128)S(1)}, u32[]{:S(2)}, u32[]{:S(2)}) collective-permute-start(f32[64,640]{1,0:T(8,128)} %get-tuple-element.19), channel_id=1, source_target_pairs={{0,48},{16,0},{32,16},{48,32},{1,49},{17,1},{33,17},{49,33},{2,50}... | collective-permute-start | bytes 491528 | tf_op jit(solution)/shard_map/ppermute | solution.py:373
  167.5 13.5 %all-to-all-start.4 = ((f32[4,72,640]{2,1,0:T(8,128)}), f32[4,72,640]{2,1,0:T(8,128)S(1)}, u32[]{:S(2)}, u32[]{:S(2)}) async-start(f32[4,72,640]{2,1,0:T(8,128)} %shard_map.84.refs_5_), calls=%async_computation.4 | async-start | bytes 1474560 | tf_op jit(solution)/shard_map/all_to_all | solution.py:378
  183.8 11.1 %all-to-all-start.5 = ((f32[8,8,128]{2,1,0:T(8,128)}), f32[8,8,128]{2,1,0:T(8,128)S(1)}, u32[]{:S(2)}, u32[]{:S(2)}) async-start(f32[8,8,128]{2,1,0:T(8,128)} %get-tuple-element.23.refs_2_), calls=%async_computation.5 | async-start | bytes 65536 | tf_op jit(solution)/shard_map/all_to_all | solution.py:378
  (13 other events, 70.5 us)

commit v7 on v6

--- a/solution.py
+++ b/solution.py
@@ -28,6 +28,7 @@
 GROUPS = 2
 VMEM_LIMIT = 58 * 1024 * 1024
 ROOM = 8 * 1024 * 1024
+PAD = 8
 SMALL = 42 * 1024 * 1024
 
 
@@ -149,19 +150,21 @@
 
 
 def prepare_queries_body(args, lazy, results, scratch, need, send):
-    (position_ref,), (qkv_ref,), (queries_ref, tail_ref) = args, lazy, results
-    last = position_ref[0] == BLOCKS - 1
+    (qkv_ref,), (queries_ref, tail_ref) = lazy, results
     need()
     queries_ref[0:TOK, :] = qkv_ref[0, 0]
     queries_ref[TOK : 2 * TOK, :] = qkv_ref[0, 1]
     send(0)
     for a in range(2):
-        tail_ref[a] = jnp.where(last, qkv_ref[1 + a, 0], qkv_ref[1 + a, 1])
-
-
-def prepare_far_body(args, lazy, results, scratch, need, send):
-    need()
-    results[0][...] = lazy[0][...]
+        tail_ref[a] = qkv_ref[1 + a, 0]
+
+
+def prepare_tails_body(args, lazy, results, scratch, need, send):
+    (position_ref,), (qkv_ref,) = args, lazy
+    need()
+    for distance, ref in zip((1, 2), results):
+        for a in range(2):
+            ref[a] = jnp.where(position_ref[0] >= BLOCKS - distance, qkv_ref[a, 0], qkv_ref[a, 1])
 
 
 def widened(part):
@@ -324,39 +327,36 @@
 
 
 def mix_body(args, lazy, results, scratch, need, send):
-    (recv_ref, gain_ref, readout_ref, attended_ref), (mixed_ref,) = args, results
+    (recv_ref, gain_ref, readout_ref, *attended_refs), (mixed_ref,) = args, results
     total = recv_ref[0, 0:1, :]
     for n in range(1, NARROW):
         total = total + recv_ref[n, 0:1, :]
     scale = to_column(1.0 / jnp.sqrt(total / (D * NARROW) + EPSILON))
     for c in range(GROUPS):
-        mixed_ref[c] = attended_ref[c] + gain_ref[...] * (readout_ref[c] * scale[c * TOK : (c + 1) * TOK])
-
-
-def attention_body(args, lazy, results, scratch, need, send):
-    (position_ref,), (qkv_ref, *near_refs, far_ref), (out_ref,) = args, lazy, results
+        mixed_ref[c] = attended_refs[c][...] + gain_ref[...] * (readout_ref[c] * scale[c * TOK : (c + 1) * TOK])
+
+
+def attention_body(c, args, lazy, results, scratch, need, send):
+    (position_ref,), (qkv_ref, near_ref, far_ref), (out_ref,) = args, lazy, results
     position = position_ref[0]
     row = lax.broadcasted_iota(jnp.int32, (TOK, 3 * TOK), 0) + 2 * TOK
     col = lax.broadcasted_iota(jnp.int32, (TOK, 3 * TOK), 1)
-    window = (row - col >= 0) & (row - col < WINDOW)
-    first = jnp.where(position >= 2, 0, jnp.where(position >= 1, TOK, 2 * TOK))
-    need()
-    for c in range(GROUPS):
-        allowed = window & (col >= first) if c == 0 else window
-        for h in range(D // ATT):
-            at = slice(h * ATT, (h + 1) * ATT)
-            parts = []
-            for a in range(2):
-                far, near = far_ref[a, c, :, at], near_refs[c][a, :, at]
-                if c == 1:
-                    far = jnp.where(position >= 2, far, far_ref[a, 0, :, at])
-                parts.append(jnp.concatenate([far, near, qkv_ref[1 + a, c, :, at]], axis=0))
-            keys, values = parts
-            scores = dot(qkv_ref[0, c, :, at], keys, ((1,), (1,))) * (1.0 / math.sqrt(ATT))
-            scores = jnp.where(allowed, scores, -1e30)
-            weights = jnp.exp(scores - jnp.max(scores, axis=1, keepdims=True))
-            weights = weights / jnp.sum(weights, axis=1, keepdims=True)
-            out_ref[c, :, at] = dot(weights, values)
+    allowed = (row - col >= 0) & (row - col < WINDOW)
+    if c == 0:
+        first = jnp.where(position >= 2, 0, jnp.where(position >= 1, TOK, 2 * TOK))
+        allowed = allowed & (col >= first)
+    need()
+    for h in range(D // ATT):
+        at = slice(h * ATT, (h + 1) * ATT)
+        keys, values = (
+            jnp.concatenate([far_ref[a, :, at], near_ref[a, 0:TOK, at], qkv_ref[1 + a, c, :, at]], axis=0)
+            for a in range(2)
+        )
+        scores = dot(qkv_ref[0, c, :, at], keys, ((1,), (1,))) * (1.0 / math.sqrt(ATT))
+        scores = jnp.where(allowed, scores, -1e30)
+        weights = jnp.exp(scores - jnp.max(scores, axis=1, keepdims=True))
+        weights = weights / jnp.sum(weights, axis=1, keepdims=True)
+        out_ref[:, at] = dot(weights, values)
 
 
 def behind(block, distance):
@@ -399,44 +399,49 @@
     (spread,) = call(spread_body, [(NZ, NX * NY, 24, LANES)], 1, packs, fan=(0,), room=SMALL)
     recv1 = exchange(spread.reshape(NZ, NX * NY * 24, LANES), "z").reshape(BLOCKS * 24, LANES)
     pairs = from_neighbours(pairs)
-    near0 = behind(qkv[1:, 0], 1)
+    near0 = behind(jnp.pad(qkv[1:, 0], ((0, 0), (0, PAD), (0, 0))), 1)
     weights, send2 = call(
         gradient_body, [(3 * D, LANES), (BLOCKS * 24, LANES)], 5, recv1, lazy=whole(*pairs),
         scratch=[(3 * D, LANES)], after=(near0,), room=ROOM - 512 * 1024,
     )
     recv2 = exchange(send2.reshape(NZ * NY, NX * 24, LANES), ("z", "yh"))
     queries, tail = call(
-        prepare_queries_body, [(2 * TOK, D), (2, TOK, D)], 1, position, lazy=whole(qkv), smem=(0,), after=(weights,)
+        prepare_queries_body, [(2 * TOK, D), (2, TOK, D)], 1, lazy=whole(qkv), after=(weights,)
     )
     queries = from_neighbours(queries)
-    near1 = behind(tail, 1)
+    far0 = behind(tail, 2)
     (send3,) = call(
         moment_body, [(NZ * NY, NX * 24, LANES)], 2, yh, recv2, packs, smem=(0,), fan=(0,),
-        after=(near1, *queries[1:]),
+        after=(far0, *queries[1:]),
         room=ROOM,
     )
     recv3 = exchange(send3, ("z", "yh")).reshape(BLOCKS * 24, LANES)
-    first = back_to_neighbours(
-        call(
-            first_read_body, [(TOK, D)] * NX, 4, lazy=[*((q, (0, TOK)) for q in queries), (weights, None)],
-            after=(send3,),
-        )
-    )
-    (far,) = call(prepare_far_body, [(2, GROUPS, TOK, D)], 1, lazy=[(qkv, (1, 2))], after=(send3,))
-    far = behind(far, 2)
+    send_first = call(
+        first_read_body, [(TOK, D)] * NX, 4, lazy=[*((q, (0, TOK)) for q in queries), (weights, None)],
+        after=(send3,),
+    )
+    first = back_to_neighbours(send_first)
+    tails = call(
+        prepare_tails_body, [(2, TOK, D)] * 2, 1, position, lazy=[(qkv, (1, 2))], smem=(0,), after=(send_first[0],)
+    )
+    near1, far1 = behind(tails[0], 1), behind(tails[1], 2)
     (send_second,) = call(
         second_read_body, [(NX, TOK + 8, D)], 5, x, recv3,
         lazy=[*((q, (TOK, TOK)) for q in queries), (weights, None), (send3, (0, 1))], scratch=[(3 * D, LANES)],
-        smem=(0,), after=(far, *first[1:]), room=ROOM,
+        smem=(0,), after=(tails[0], *first[1:]), room=ROOM,
     )
     second = exchange(send_second, "x")
-    (attended,) = call(
-        attention_body, [(GROUPS, TOK, D)], 8, position, lazy=whole(qkv, near0, near1, far), smem=(0,),
+    (attended0,) = call(
+        functools.partial(attention_body, 0), [(TOK, D)], 5, position, lazy=whole(qkv, near0, far0), smem=(0,),
         after=(send_second,),
     )
     readout, send5 = call(
         squares_body, [(GROUPS, TOK, D), (NARROW, 8, GROUPS * TOK)], 1, second, lazy=whole(*first), fan=(1,),
-        after=(attended,), room=SMALL,
+        after=(attended0,), room=SMALL,
+    )
+    (attended1,) = call(
+        functools.partial(attention_body, 1), [(TOK, D)], 5, position, lazy=whole(qkv, near1, far1), smem=(0,),
+        after=(send5,),
     )
     recv5 = exchange(send5, "narrow")
     new_weights, new_moment = call(
@@ -444,7 +449,7 @@
         after=(send5,), room=SMALL,
     )
     (mixed,) = call(
-        mix_body, [(GROUPS, TOK, D)], 1, recv5, ttt_gain.reshape(1, D), readout, attended, after=(new_weights,),
+        mix_body, [(GROUPS, TOK, D)], 1, recv5, ttt_gain.reshape(1, D), readout, attended0, attended1, after=(new_weights,),
         room=SMALL,
     )
     return mixed, new_weights.reshape(1, ROWS, 3, H), new_moment.reshape(1, ROWS, 3, H)

time: 198 us -> 197 us (level)
  the two profiles are of different devices: /device:TPU:1 before, /device:TPU:73 now
where the time goes in v7:
time: 197 us; the launch traced here: 196 us
  starting transfers between devices  84.7 us (43%)
  waiting for transfers between devices  44.5 us (23%)
  Pallas kernels  38.4 us (19%)
  blocking collectives  20.9 us (11%)
  local copies, waits for them, and re-layouts  5.91 us (3%)
    all_to_all x5, starting transfers between devices, exchange(): return lax.all_to_all(pieces, axes, split_axis=0, concat_axis=0, tiled=True)  44 us
    pallas_call x14, Pallas kernels, call(): pl.pallas_call(kernel, out_shape=[jax.ShapeDtypeStruct(s, jnp.float32) fo...  38.4 us
    ppermute x6, waiting for transfers between devices, from_neighbours(): lax.ppermute(block, 'x', [((i - s) % NX, i) for i in range(NX)])  24 us
    all_to_all x1, blocking collectives, exchange(): return lax.all_to_all(pieces, axes, split_axis=0, concat_axis=0, tiled=True)  20.9 us
    ppermute x6, starting transfers between devices, from_neighbours(): lax.ppermute(block, 'x', [((i - s) % NX, i) for i in range(NX)])  18.9 us
    ppermute x4, starting transfers between devices, behind(): lax.ppermute(block, axes, [((i - distance) % BLOCKS, i) for i in range(BL...  13 us
    all_to_all x5, waiting for transfers between devices, exchange(): return lax.all_to_all(pieces, axes, split_axis=0, concat_axis=0, tiled=True)  11.3 us
    ppermute x3, starting transfers between devices, back_to_neighbours(): lax.ppermute(blocks[s], 'x', [(i, (i - s) % NX) for i in range(NX)])  8.85 us
  transfers between devices with their start and end apart: 18, of which 7 were waited for; matrix products, arithmetic and copies ran while one was open for 0% of the time, Pallas kernels for 12%

profile of v7, /device:TPU:73, one launch (start us, length us, event | category | flops | bytes accessed | tf_op | source)
XLA Modules:
  0.0 195.8 jit_solution(2712872998819021131)
XLA Ops:
  2.6 20.9 %all_to_all.30.refs_0_.refs_2_ = f32[8,48,128]{2,1,0:T(8,128)S(1)} all-to-all(f32[8,48,128]{2,1,0:T(8,128)S(1)} %shard_map.76), channel_id=1, replica_groups=mesh['z'=8,'x'=4,'yh'=2,'narrow'=8] {'x','yh'}, dimensions={0} | all-to-all | bytes 393216 | tf_op jit(solution)/shard_map/all_to_all | solution.py:378
  24.6 9.5 %all-to-all-start.1 = ((f32[8,192,128]{2,1,0:T(8,128)}), f32[8,192,128]{2,1,0:T(8,128)S(1)}, u32[]{:S(2)}, u32[]{:S(2)}) async-start(f32[8,192,128]{2,1,0:T(8,128)} %bitcast.4), calls=%async_computation.1 | async-start | bytes 1572864 | tf_op jit(solution)/shard_map/all_to_all | solution.py:378
  38.3 3.7 %collective-permute-start.1 = (f32[128,640]{1,0:T(8,128)S(1)}, f32[128,640]{1,0:T(8,128)S(1)}, u32[]{:S(2)}, u32[]{:S(2)}) collective-permute-start(f32[128,640]{1,0:T(8,128)S(1)} %shard_map.78.refs_1_), channel_id=1, source_target_pairs={{32,0},{48,16},{0,32},{16,48},{33,1},{49,17},{1,33},{17,49},{34,2}... | collective-permute-start | bytes 983048 | tf_op jit(solution)/shard_map/ppermute | solution.py:368
  44.9 3.5 %collective-permute-done.refs_2_ = f32[128,640]{1,0:T(8,128)S(1)} collective-permute-done((f32[128,640]{1,0:T(8,128)S(1)}, f32[128,640]{1,0:T(8,128)S(1)}, u32[]{:S(2)}, u32[]{:S(2)}) %collective-permute-start) | collective-permute-done | bytes 327712 | tf_op jit(solution)/shard_map/ppermute | solution.py:368
  48.4 12.3 %collective-permute-done.1.refs_3_ = f32[128,640]{1,0:T(8,128)S(1)} collective-permute-done((f32[128,640]{1,0:T(8,128)S(1)}, f32[128,640]{1,0:T(8,128)S(1)}, u32[]{:S(2)}, u32[]{:S(2)}) %collective-permute-start.1) | collective-permute-done | bytes 327712 | tf_op jit(solution)/shard_map/ppermute | solution.py:368
  60.8 5.5 %shard_map.79 = (f32[1920,128]{1,0:T(8,128)}, f32[1536,128]{1,0:T(8,128)}) custom-call(f32[1536,128]{1,0:T(8,128)S(1)} %bitcast.16, f32[128,640]{1,0:T(8,128)S(1)} %shard_map.78.refs_1_, f32[128,640]{1,0:T(8,128)S(1)} %collective-permute-done.refs_2_, f32[128,640]{1,0:T(8,128)S(1)} %collective-permute-done.1.refs_3_, ...), custom_call_target="tpu_custom_call" | custom-call | flops 5000000000 | bytes 1000000 | tf_op jit(solution)/shard_map/pallas_call | solution.py:93
  66.3 8.2 %all-to-all-start.2 = ((f32[16,96,128]{2,1,0:T(8,128)}), f32[16,96,128]{2,1,0:T(8,128)S(1)}, u32[]{:S(2)}, u32[]{:S(2)}) async-start(f32[16,96,128]{2,1,0:T(8,128)} %bitcast.7), calls=%async_computation.2 | async-start | bytes 1572864 | tf_op jit(solution)/shard_map/all_to_all | solution.py:378
  76.6 4.1 %collective-permute-start.5 = (f32[128,640]{1,0:T(8,128)}, f32[128,640]{1,0:T(8,128)S(1)}, u32[]{:S(2)}, u32[]{:S(2)}) collective-permute-start(f32[128,640]{1,0:T(8,128)} %get-tuple-element.20.refs_0_.refs_2_), channel_id=1, source_target_pairs={{48,0},{0,16},{16,32},{32,48},{49,1},{1,17},{17,33},{33,49},{50,2}... | collective-permute-start | bytes 983048 | tf_op jit(solution)/shard_map/ppermute | solution.py:368
  80.7 4.3 %collective-permute-start.6 = (f32[128,640]{1,0:T(8,128)}, f32[128,640]{1,0:T(8,128)S(1)}, u32[]{:S(2)}, u32[]{:S(2)}) collective-permute-start(f32[128,640]{1,0:T(8,128)} %get-tuple-element.20.refs_0_.refs_2_), channel_id=1, source_target_pairs={{32,0},{48,16},{0,32},{16,48},{33,1},{49,17},{1,33},{17,49},{34,2}... | collective-permute-start | bytes 983048 | tf_op jit(solution)/shard_map/ppermute | solution.py:368
  90.4 8.1 %collective-permute-done.6.refs_5_.refs_2_.refs_4_ = f32[128,640]{1,0:T(8,128)S(1)} collective-permute-done((f32[128,640]{1,0:T(8,128)}, f32[128,640]{1,0:T(8,128)S(1)}, u32[]{:S(2)}, u32[]{:S(2)}) %collective-permute-start.6) | collective-permute-done | bytes 327712 | tf_op jit(solution)/shard_map/ppermute | solution.py:368
  98.5 5.7 %collective-permute-done.4.refs_3_ = f32[2,64,640]{2,1,0:T(8,128)S(1)} collective-permute-done((f32[2,64,640]{2,1,0:T(8,128)}, f32[2,64,640]{2,1,0:T(8,128)S(1)}, u32[]{:S(2)}, u32[]{:S(2)}) %collective-permute-start.4) | collective-permute-done | bytes 327712 | tf_op jit(solution)/shard_map/ppermute | solution.py:364
  104.2 6.2 %all-to-all-done.2.refs_1_ = f32[16,96,128]{2,1,0:T(8,128)S(1)} async-done(((f32[16,96,128]{2,1,0:T(8,128)}), f32[16,96,128]{2,1,0:T(8,128)S(1)}, u32[]{:S(2)}, u32[]{:S(2)}) %all-to-all-start.2) | async-done | bytes 786464 | tf_op jit(solution)/shard_map/all_to_all | solution.py:378
  111.5 5.4 %all-to-all-start.3 = ((f32[16,96,128]{2,1,0:T(8,128)}), f32[16,96,128]{2,1,0:T(8,128)S(1)}, u32[]{:S(2)}, u32[]{:S(2)}) async-start(f32[16,96,128]{2,1,0:T(8,128)} %shard_map.81.refs_5_.refs_7_), calls=%async_computation.3 | async-start | bytes 1572864 | tf_op jit(solution)/shard_map/all_to_all | solution.py:378
  116.9 4.8 %shard_map.82 = (f32[64,640]{1,0:T(8,128)}, f32[64,640]{1,0:T(8,128)}, f32[64,640]{1,0:T(8,128)}, f32[64,640]{1,0:T(8,128)}) custom-call(f32[128,640]{1,0:T(8,128)} %get-tuple-element.20.refs_0_.refs_2_, f32[128,640]{1,0:T(8,128)} %copy-done.4, f32[128,640]{1,0:T(8,128)} %copy-done.6, f32[128,640]{1,0:T(8,128)} %copy-done.8, ...), custom_call_target="tpu_custom_call" | custom-call | flops 4000000000 | bytes 1000000 | tf_op jit(solution)/shard_map/pallas_call | solution.py:93
  123.6 4.6 %collective-permute-start.8 = (f32[64,640]{1,0:T(8,128)}, f32[64,640]{1,0:T(8,128)S(1)}, u32[]{:S(2)}, u32[]{:S(2)}) collective-permute-start(f32[64,640]{1,0:T(8,128)} %get-tuple-element.23), channel_id=1, source_target_pairs={{0,48},{16,0},{32,16},{48,32},{1,49},{17,1},{33,17},{49,33},{2,50}... | collective-permute-start | bytes 491528 | tf_op jit(solution)/shard_map/ppermute | solution.py:373
  132.7 3.5 %collective-permute-done.9.refs_10_.refs_3_ = f32[64,640]{1,0:T(8,128)S(1)} collective-permute-done((f32[64,640]{1,0:T(8,128)}, f32[64,640]{1,0:T(8,128)S(1)}, u32[]{:S(2)}, u32[]{:S(2)}) %collective-permute-start.9) | collective-permute-done | bytes 163872 | tf_op jit(solution)/shard_map/ppermute | solution.py:373
  136.3 5.1 %all-to-all-done.3 = f32[16,96,128]{2,1,0:T(8,128)S(1)} async-done(((f32[16,96,128]{2,1,0:T(8,128)}), f32[16,96,128]{2,1,0:T(8,128)S(1)}, u32[]{:S(2)}, u32[]{:S(2)}) %all-to-all-start.3) | async-done | bytes 786464 | tf_op jit(solution)/shard_map/all_to_all | solution.py:378
  142.3 6.2 %shard_map.84.refs_4_ = f32[4,72,640]{2,1,0:T(8,128)} custom-call(s32[1]{0:T(128)} %bitcast.refs_0_, f32[1536,128]{1,0:T(8,128)S(1)} %bitcast.15, f32[128,640]{1,0:T(8,128)S(1)} %copy-done.3, f32[128,640]{1,0:T(8,128)S(1)} %copy-done.5, f32[128,640]{1,0:T(8,128)S(1)} %copy-done.7, f32[128,640]{1,0:T(8,128)S(1)} %copy-done.9, ...), custom_call_target="tpu_custom_call" | custom-call | flops 5000000000 | bytes 1000000 | tf_op jit(solution)/shard_map/pallas_call | solution.py:93
  148.6 10.0 %all-to-all-start.4 = ((f32[4,72,640]{2,1,0:T(8,128)}), f32[4,72,640]{2,1,0:T(8,128)S(1)}, u32[]{:S(2)}, u32[]{:S(2)}) async-start(f32[4,72,640]{2,1,0:T(8,128)} %shard_map.84.refs_4_), calls=%async_computation.4 | async-start | bytes 1474560 | tf_op jit(solution)/shard_map/all_to_all | solution.py:378
  158.6 4.0 %collective-permute-start.11 = (f32[2,64,640]{2,1,0:T(8,128)S(1)}, f32[2,64,640]{2,1,0:T(8,128)S(1)}, u32[]{:S(2)}, u32[]{:S(2)}) collective-permute-start(f32[2,64,640]{2,1,0:T(8,128)S(1)} %copy-done.11), channel_id=1, source_target_pairs={{504,0},{0,8},{8,16},{16,24},{24,32},{32,40},{40,48},{48,56},{56,6... | collective-permute-start | bytes 983048 | tf_op jit(solution)/shard_map/ppermute | solution.py:364
  162.7 3.7 %collective-permute-start.12 = (f32[2,64,640]{2,1,0:T(8,128)S(1)}, f32[2,64,640]{2,1,0:T(8,128)S(1)}, u32[]{:S(2)}, u32[]{:S(2)}) collective-permute-start(f32[2,64,640]{2,1,0:T(8,128)S(1)} %copy-done.21), channel_id=1, source_target_pairs={{496,0},{504,8},{0,16},{8,24},{16,32},{24,40},{32,48},{40,56},{48,... | collective-permute-start | bytes 983048 | tf_op jit(solution)/shard_map/ppermute | solution.py:364
  166.4 5.8 %shard_map.85.refs_5_.refs_3_ = f32[64,640]{1,0:T(8,128)} custom-call(s32[1]{0:T(128)} %bitcast.9.refs_0_, f32[3,2,64,640]{3,2,1,0:T(8,128)} %refs_1_.7, f32[2,72,640]{2,1,0:T(8,128)} %copy-done.1, f32[2,64,640]{2,1,0:T(8,128)} %copy-done.2, f32[4,72,640]{2,1,0:T(8,128)} %shard_map.84.refs_4_), custom_call_target="tpu_custom_call" | custom-call | flops 5000000000 | bytes 1000000 | tf_op jit(solution)/shard_map/pallas_call | solution.py:93
  174.9 10.8 %all-to-all-start.5 = ((f32[8,8,128]{2,1,0:T(8,128)}), f32[8,8,128]{2,1,0:T(8,128)S(1)}, u32[]{:S(2)}, u32[]{:S(2)}) async-start(f32[8,8,128]{2,1,0:T(8,128)} %get-tuple-element.26.refs_4_.refs_2_), calls=%async_computation.5 | async-start | bytes 65536 | tf_op jit(solution)/shard_map/all_to_all | solution.py:378
  187.2 5.8 %shard_map.87.refs_4_ = f32[64,640]{1,0:T(8,128)} custom-call(s32[1]{0:T(128)} %bitcast.9.refs_0_, f32[3,2,64,640]{3,2,1,0:T(8,128)} %refs_1_.7, f32[2,64,640]{2,1,0:T(8,128)} %copy-done.22, f32[2,64,640]{2,1,0:T(8,128)} %copy-done.23, f32[8,8,128]{2,1,0:T(8,128)} %get-tuple-element.26.refs_4_.refs_2_), custom_call_target="tpu_custom_call" | custom-call | flops 5000000000 | bytes 1000000 | tf_op jit(solution)/shard_map/pallas_call | solution.py:93
  (78 shorter events, 32.6 us)
Async XLA Ops:
  24.6 36.2 %all-to-all-start.1 = ((f32[8,192,128]{2,1,0:T(8,128)}), f32[8,192,128]{2,1,0:T(8,128)S(1)}, u32[]{:S(2)}, u32[]{:S(2)}) async-start(f32[8,192,128]{2,1,0:T(8,128)} %bitcast.4), calls=%async_computation.1 | async-start | bytes 1572864 | tf_op jit(solution)/shard_map/all_to_all | solution.py:378
  34.2 26.6 %collective-permute-start.3 = (f32[2,72,640]{2,1,0:T(8,128)S(1)}, f32[2,72,640]{2,1,0:T(8,128)S(1)}, u32[]{:S(2)}, u32[]{:S(2)}) collective-permute-start(f32[2,72,640]{2,1,0:T(8,128)S(1)} %pad.4), channel_id=1, source_target_pairs={{504,0},{0,8},{8,16},{16,24},{24,32},{32,40},{40,48},{48,56},{56,6... | collective-permute-start | bytes 1105928 | tf_op jit(solution)/shard_map/ppermute | solution.py:364
  36.3 12.1 %collective-permute-start = (f32[128,640]{1,0:T(8,128)S(1)}, f32[128,640]{1,0:T(8,128)S(1)}, u32[]{:S(2)}, u32[]{:S(2)}) collective-permute-start(f32[128,640]{1,0:T(8,128)S(1)} %shard_map.78.refs_1_), channel_id=1, source_target_pairs={{48,0},{0,16},{16,32},{32,48},{49,1},{1,17},{17,33},{33,49},{50,2}... | collective-permute-start | bytes 983048 | tf_op jit(solution)/shard_map/ppermute | solution.py:368
  38.3 22.5 %collective-permute-start.1 = (f32[128,640]{1,0:T(8,128)S(1)}, f32[128,640]{1,0:T(8,128)S(1)}, u32[]{:S(2)}, u32[]{:S(2)}) collective-permute-start(f32[128,640]{1,0:T(8,128)S(1)} %shard_map.78.refs_1_), channel_id=1, source_target_pairs={{32,0},{48,16},{0,32},{16,48},{33,1},{49,17},{1,33},{17,49},{34,2}... | collective-permute-start | bytes 983048 | tf_op jit(solution)/shard_map/ppermute | solution.py:368
  42.0 18.8 %collective-permute-start.2 = (f32[128,640]{1,0:T(8,128)S(1)}, f32[128,640]{1,0:T(8,128)S(1)}, u32[]{:S(2)}, u32[]{:S(2)}) collective-permute-start(f32[128,640]{1,0:T(8,128)S(1)} %shard_map.78.refs_1_), channel_id=1, source_target_pairs={{16,0},{32,16},{48,32},{0,48},{17,1},{33,17},{49,33},{1,49},{18,2}... | collective-permute-start | bytes 983048 | tf_op jit(solution)/shard_map/ppermute | solution.py:368
  66.3 44.1 %all-to-all-start.2 = ((f32[16,96,128]{2,1,0:T(8,128)}), f32[16,96,128]{2,1,0:T(8,128)S(1)}, u32[]{:S(2)}, u32[]{:S(2)}) async-start(f32[16,96,128]{2,1,0:T(8,128)} %bitcast.7), calls=%async_computation.2 | async-start | bytes 1572864 | tf_op jit(solution)/shard_map/all_to_all | solution.py:378
  76.6 13.7 %collective-permute-start.5 = (f32[128,640]{1,0:T(8,128)}, f32[128,640]{1,0:T(8,128)S(1)}, u32[]{:S(2)}, u32[]{:S(2)}) collective-permute-start(f32[128,640]{1,0:T(8,128)} %get-tuple-element.20.refs_0_.refs_2_), channel_id=1, source_target_pairs={{48,0},{0,16},{16,32},{32,48},{49,1},{1,17},{17,33},{33,49},{50,2}... | collective-permute-start | bytes 983048 | tf_op jit(solution)/shard_map/ppermute | solution.py:368
  80.7 17.7 %collective-permute-start.6 = (f32[128,640]{1,0:T(8,128)}, f32[128,640]{1,0:T(8,128)S(1)}, u32[]{:S(2)}, u32[]{:S(2)}) collective-permute-start(f32[128,640]{1,0:T(8,128)} %get-tuple-element.20.refs_0_.refs_2_), channel_id=1, source_target_pairs={{32,0},{48,16},{0,32},{16,48},{33,1},{49,17},{1,33},{17,49},{34,2}... | collective-permute-start | bytes 983048 | tf_op jit(solution)/shard_map/ppermute | solution.py:368
  85.0 13.4 %collective-permute-start.7 = (f32[128,640]{1,0:T(8,128)}, f32[128,640]{1,0:T(8,128)S(1)}, u32[]{:S(2)}, u32[]{:S(2)}) collective-permute-start(f32[128,640]{1,0:T(8,128)} %get-tuple-element.20.refs_0_.refs_2_), channel_id=1, source_target_pairs={{16,0},{32,16},{48,32},{0,48},{17,1},{33,17},{49,33},{1,49},{18,2}... | collective-permute-start | bytes 983048 | tf_op jit(solution)/shard_map/ppermute | solution.py:368
  87.0 17.3 %collective-permute-start.4 = (f32[2,64,640]{2,1,0:T(8,128)}, f32[2,64,640]{2,1,0:T(8,128)S(1)}, u32[]{:S(2)}, u32[]{:S(2)}) collective-permute-start(f32[2,64,640]{2,1,0:T(8,128)} %get-tuple-element.19), channel_id=1, source_target_pairs={{496,0},{504,8},{0,16},{8,24},{16,32},{24,40},{32,48},{40,56},{48,... | collective-permute-start | bytes 983048 | tf_op jit(solution)/shard_map/ppermute | solution.py:364
  90.4 21.2 %copy-start.4 = (f32[128,640]{1,0:T(8,128)}, f32[128,640]{1,0:T(8,128)S(1)}, u32[]{:S(2)}) copy-start(f32[128,640]{1,0:T(8,128)S(1)} %collective-permute-done.5.refs_4_.refs_1_.refs_3_) | copy-start | bytes 983044
  98.5 13.1 %copy-start.6 = (f32[128,640]{1,0:T(8,128)}, f32[128,640]{1,0:T(8,128)S(1)}, u32[]{:S(2)}) copy-start(f32[128,640]{1,0:T(8,128)S(1)} %collective-permute-done.6.refs_5_.refs_2_.refs_4_) | copy-start | bytes 983044
  98.5 13.1 %copy-start.8 = (f32[128,640]{1,0:T(8,128)}, f32[128,640]{1,0:T(8,128)S(1)}, u32[]{:S(2)}) copy-start(f32[128,640]{1,0:T(8,128)S(1)} %collective-permute-done.7.refs_6_.refs_3_.refs_5_) | copy-start | bytes 983044
  111.5 29.8 %all-to-all-start.3 = ((f32[16,96,128]{2,1,0:T(8,128)}), f32[16,96,128]{2,1,0:T(8,128)S(1)}, u32[]{:S(2)}, u32[]{:S(2)}) async-start(f32[16,96,128]{2,1,0:T(8,128)} %shard_map.81.refs_5_.refs_7_), calls=%async_computation.3 | async-start | bytes 1572864 | tf_op jit(solution)/shard_map/all_to_all | solution.py:378
  121.7 11.0 %collective-permute-start.10 = (f32[64,640]{1,0:T(8,128)}, f32[64,640]{1,0:T(8,128)S(1)}, u32[]{:S(2)}, u32[]{:S(2)}) collective-permute-start(f32[64,640]{1,0:T(8,128)} %get-tuple-element.25), channel_id=1, source_target_pairs={{0,16},{16,32},{32,48},{48,0},{1,17},{17,33},{33,49},{49,1},{2,18}... | collective-permute-start | bytes 491528 | tf_op jit(solution)/shard_map/ppermute | solution.py:373
  123.6 9.1 %collective-permute-start.8 = (f32[64,640]{1,0:T(8,128)}, f32[64,640]{1,0:T(8,128)S(1)}, u32[]{:S(2)}, u32[]{:S(2)}) collective-permute-start(f32[64,640]{1,0:T(8,128)} %get-tuple-element.23), channel_id=1, source_target_pairs={{0,48},{16,0},{32,16},{48,32},{1,49},{17,1},{33,17},{49,33},{2,50}... | collective-permute-start | bytes 491528 | tf_op jit(solution)/shard_map/ppermute | solution.py:373
  128.2 8.1 %collective-permute-start.9 = (f32[64,640]{1,0:T(8,128)}, f32[64,640]{1,0:T(8,128)S(1)}, u32[]{:S(2)}, u32[]{:S(2)}) collective-permute-start(f32[64,640]{1,0:T(8,128)} %get-tuple-element.24), channel_id=1, source_target_pairs={{0,32},{16,48},{32,0},{48,16},{1,33},{17,49},{33,1},{49,17},{2,34}... | collective-permute-start | bytes 491528 | tf_op jit(solution)/shard_map/ppermute | solution.py:373
  130.6 10.8 %copy-start.3 = (f32[128,640]{1,0:T(8,128)S(1)}, f32[128,640]{1,0:T(8,128)}, u32[]{:S(2)}) copy-start(f32[128,640]{1,0:T(8,128)} %get-tuple-element.20.refs_0_.refs_2_) | copy-start | bytes 983044
  130.6 10.7 %copy-start.5 = (f32[128,640]{1,0:T(8,128)S(1)}, f32[128,640]{1,0:T(8,128)}, u32[]{:S(2)}) copy-start(f32[128,640]{1,0:T(8,128)} %copy-done.4) | copy-start | bytes 983044
  148.6 14.1 %copy-start.21 = (f32[2,64,640]{2,1,0:T(8,128)S(1)}, f32[2,64,640]{2,1,0:T(8,128)}, u32[]{:S(2)}) copy-start(f32[2,64,640]{2,1,0:T(8,128)} %get-tuple-element.28) | copy-start | bytes 983044
  148.6 23.6 %all-to-all-start.4 = ((f32[4,72,640]{2,1,0:T(8,128)}), f32[4,72,640]{2,1,0:T(8,128)S(1)}, u32[]{:S(2)}, u32[]{:S(2)}) async-start(f32[4,72,640]{2,1,0:T(8,128)} %shard_map.84.refs_4_), calls=%async_computation.4 | async-start | bytes 1474560 | tf_op jit(solution)/shard_map/all_to_all | solution.py:378
  158.6 27.1 %collective-permute-start.11 = (f32[2,64,640]{2,1,0:T(8,128)S(1)}, f32[2,64,640]{2,1,0:T(8,128)S(1)}, u32[]{:S(2)}, u32[]{:S(2)}) collective-permute-start(f32[2,64,640]{2,1,0:T(8,128)S(1)} %copy-done.11), channel_id=1, source_target_pairs={{504,0},{0,8},{8,16},{16,24},{24,32},{32,40},{40,48},{48,56},{56,6... | collective-permute-start | bytes 983048 | tf_op jit(solution)/shard_map/ppermute | solution.py:364
  162.7 23.1 %collective-permute-start.12 = (f32[2,64,640]{2,1,0:T(8,128)S(1)}, f32[2,64,640]{2,1,0:T(8,128)S(1)}, u32[]{:S(2)}, u32[]{:S(2)}) collective-permute-start(f32[2,64,640]{2,1,0:T(8,128)S(1)} %copy-done.21), channel_id=1, source_target_pairs={{496,0},{504,8},{0,16},{8,24},{16,32},{24,40},{32,48},{40,56},{48,... | collective-permute-start | bytes 983048 | tf_op jit(solution)/shard_map/ppermute | solution.py:364
  174.9 18.9 %all-to-all-start.5 = ((f32[8,8,128]{2,1,0:T(8,128)}), f32[8,8,128]{2,1,0:T(8,128)S(1)}, u32[]{:S(2)}, u32[]{:S(2)}) async-start(f32[8,8,128]{2,1,0:T(8,128)} %get-tuple-element.26.refs_4_.refs_2_), calls=%async_computation.5 | async-start | bytes 65536 | tf_op jit(solution)/shard_map/all_to_all | solution.py:378
  (18 other events, 89.4 us)

commit v8 on v5

--- a/solution.py
+++ b/solution.py
@@ -129,17 +129,13 @@
     ]
 
 
-def prepare_packs_body(args, lazy, results, scratch, need, send):
-    for half, ref in enumerate(args):
-        for x, block in enumerate(own_packs(ref, scratch[0])):
+def prepare_weights_body(args, lazy, results, scratch, need, send):
+    packs = own_packs(args[0], scratch[0])
+    for z in range(NZ):
+        for x in range(NX):
             for y in range(NY):
                 for t in range(3):
-                    rows = slice(24 * half + 8 * t, 24 * half + 8 * t + 8)
-                    results[0][x * NY + y, rows, :] = block[:, LANES * t : LANES * (t + 1)]
-
-
-def spread_body(args, lazy, results, scratch, need, send):
-    results[0][...] = args[0][:, 0:24, :]
+                    results[0][(z * NX + x) * NY + y, 8 * t : 8 * t + 8, :] = packs[x][:, LANES * t : LANES * (t + 1)]
 
 
 def prepare_pairs_body(args, lazy, results, scratch, need, send):
@@ -149,10 +145,14 @@
 
 
 def prepare_queries_body(args, lazy, results, scratch, need, send):
-    need()
-    (queries_ref,) = results
-    queries_ref[0:TOK, :] = lazy[0][0, 0]
-    queries_ref[TOK : 2 * TOK, :] = lazy[0][0, 1]
+    (mom_ref,), (qkv_ref,), (queries_ref,) = args, lazy, results
+    packs = own_packs(mom_ref, scratch[0])
+    for x in range(NX):
+        queries_ref[2 * TOK + 8 * x : 2 * TOK + 8 * x + 8, 0:H] = packs[x]
+        queries_ref[2 * TOK + 8 * x : 2 * TOK + 8 * x + 8, H:D] = jnp.zeros((8, D - H), jnp.float32)
+    need()
+    queries_ref[0:TOK, :] = qkv_ref[0, 0]
+    queries_ref[TOK : 2 * TOK, :] = qkv_ref[0, 1]
 
 
 def widened(part):
@@ -229,13 +229,19 @@
     return lax.rem(x_ref[0] + NX - s, NX)
 
 
-def moment_body(args, lazy, results, scratch, need, send):
-    (yh_ref, recv_ref, packs_ref), (own_ref,) = args, results
+def moment_body(args, tails, results, scratch, need, send):
+    (x_ref, recv_ref), (own_ref,) = args, results
     total = recv_ref[0]
     for j in range(1, NZ * NY):
         total = total + recv_ref[j]
-    old = jnp.concatenate([packs_ref[x * NY + yh_ref[0], 24:48, :] for x in range(NX)], axis=0)
-    own_ref[...] = total + MOMENTUM_RATE * old
+    own_ref[...] = total
+    need()
+    mine = pl.ds(pl.multiple_of(8 * x_ref[0], 8), 8)
+    for s, ref in enumerate(tails):
+        old = ref[mine, :]
+        old = jnp.concatenate([old[:, LANES * t : LANES * (t + 1)] for t in range(3)], axis=0)
+        rows = pl.ds(pl.multiple_of(24 * source(x_ref, s), 8), 24)
+        own_ref[rows, :] = own_ref[rows, :] + MOMENTUM_RATE * old
 
 
 def hidden_of(inputs, w1, w3):
@@ -360,6 +366,13 @@
     return [block] + [lax.ppermute(block, "x", [((i - s) % NX, i) for i in range(NX)]) for s in range(1, NX)]
 
 
+def relayed_from_neighbours(block):
+    behind_one = lax.ppermute(block, "x", [((i - 1) % NX, i) for i in range(NX)])
+    from_ahead = [((i + 1) % NX, i) for i in range(NX)]
+    ahead_one = lax.ppermute(block, "x", from_ahead)
+    return [block, behind_one, lax.ppermute(ahead_one, "x", from_ahead), ahead_one]
+
+
 def back_to_neighbours(blocks):
     return [blocks[0]] + [
         lax.ppermute(blocks[s], "x", [(i, (i - s) % NX) for i in range(NX)]) for s in range(1, NX)
@@ -380,32 +393,30 @@
 
 def local(qkv, eta, fast_weights, momentum, ttt_gain):
     own_weights, own_moment = fast_weights.reshape(3 * ROWS, 1, H), momentum.reshape(3 * ROWS, 1, H)
-    x, yh = lax.axis_index("x"), lax.axis_index("yh")
-    position = scalar((lax.axis_index("z") * NX + x) * NY + yh)
-    x, yh = scalar(x), scalar(yh)
-    (packs,) = call(
-        prepare_packs_body, [(NX * NY, 48, LANES)], 1, own_weights, own_moment, scratch=[(32, H)], room=SMALL
-    )
+    x = lax.axis_index("x")
+    position = scalar((lax.axis_index("z") * NX + x) * NY + lax.axis_index("yh"))
+    x = scalar(x)
+    (send1,) = call(prepare_weights_body, [(BLOCKS, 24, LANES)], 1, own_weights, scratch=[(32, H)], room=SMALL)
     (pairs,) = call(prepare_pairs_body, [(2 * TOK, D)], 1, eta, qkv, room=SMALL)
-    packs = exchange(packs, ("x", "yh"))
-    (spread,) = call(spread_body, [(NZ, NX * NY, 24, LANES)], 1, packs, fan=(0,), room=SMALL)
-    recv1 = exchange(spread.reshape(NZ, NX * NY * 24, LANES), "z").reshape(BLOCKS * 24, LANES)
-    pairs = from_neighbours(pairs)
+    recv1 = exchange(send1, ("z", "x", "yh")).reshape(BLOCKS * 24, LANES)
+    pairs = relayed_from_neighbours(pairs)
     near, far = behind(qkv[1:], 1), behind(qkv[1:], 2)
     weights, send2 = call(
         gradient_body, [(3 * D, LANES), (BLOCKS * 24, LANES)], 5, recv1, lazy=whole(*pairs),
-        scratch=[(3 * D, LANES)], after=(near, far), room=ROOM - 1024 * 1024,
+        scratch=[(3 * D, LANES)], room=ROOM - 512 * 1024,
     )
     recv2 = exchange(send2.reshape(NZ * NY, NX * 24, LANES), ("z", "yh"))
-    (queries,) = call(prepare_queries_body, [(2 * TOK, D)], 1, lazy=[(qkv, (0, 1))], after=(weights,))
+    (queries,) = call(
+        prepare_queries_body, [(2 * TOK + 32, D)], 0.1, own_moment, lazy=[(qkv, (0, 1))], scratch=[(32, H)],
+        after=(weights,),
+    )
     queries = from_neighbours(queries)
     (attended,) = call(
-        attention_body, [(GROUPS, TOK, D)], 8, position, lazy=whole(qkv, near, far), smem=(0,)
+        attention_body, [(GROUPS, TOK, D)], 12, position, lazy=whole(qkv, near, far), smem=(0,)
     )
     (send3,) = call(
-        moment_body, [(NZ * NY, NX * 24, LANES)], 2, yh, recv2, packs, smem=(0,), fan=(0,),
-        after=(attended, *queries[1:]),
-        room=ROOM,
+        moment_body, [(NZ * NY, NX * 24, LANES)], 2, x, recv2, lazy=[(q, (2 * TOK, 32)) for q in queries],
+        smem=(0,), fan=(0,), after=(attended,), room=ROOM,
     )
     recv3 = exchange(send3, ("z", "yh")).reshape(BLOCKS * 24, LANES)
     first = back_to_neighbours(

time: 206 us -> 183 us (0.89)
  waiting for transfers between devices: 61.1 us -> 40.7 us
  blocking collectives: 19.7 us -> 0 us
  starting transfers between devices: 83.2 us -> 101 us
    ppermute x6 -> x3, waiting for transfers between devices: 40.3 us -> 8.25 us  [from_neighbours(): lax.ppermute(block, 'x', [((i - s) % NX, i) for i in range(NX)])]
    all_to_all x1 -> x0, blocking collectives: 19.7 us -> none  [exchange(): return lax.all_to_all(pieces, axes, split_axis=0, concat_axis=0, tiled=True)]
    all_to_all x5, starting transfers between devices: 49.1 us -> 62.6 us  [exchange(): return lax.all_to_all(pieces, axes, split_axis=0, concat_axis=0, tiled=True)]
    ppermute x0 -> x3, starting transfers between devices: none -> 10.5 us  [the longest x1 4.45 us: relayed_from_neighbours(): lax.ppermute(ahead_one, 'x', from_ahead)]
    ppermute x0 -> x3, waiting for transfers between devices: none -> 9.87 us  [the longest x1 9.86 us: relayed_from_neighbours(): ahead_one = lax.ppermute(block, 'x', from_ahead)]
    ppermute x6 -> x3, starting transfers between devices: 18.9 us -> 10.3 us  [from_neighbours(): lax.ppermute(block, 'x', [((i - s) % NX, i) for i in range(NX)])]
    ppermute x2, starting transfers between devices: 4.84 us -> 9.19 us  [behind(): lax.ppermute(block, axes, [((i - distance) % BLOCKS, i) for i in range(BL...]
    ppermute x2, waiting for transfers between devices: 0.01 us -> 4.25 us  [behind(): lax.ppermute(block, axes, [((i - distance) % BLOCKS, i) for i in range(BL...]
  transfers between devices with their start and end apart: 16 -> 16, of which waited for: 7 -> 7; matrix products, arithmetic and copies ran while one was open for 0% -> 0% of each run, Pallas kernels for 8% -> 13%
where the time goes in v8:
time: 183 us; the launch traced here: 182 us
  starting transfers between devices  101 us (55%)
  waiting for transfers between devices  40.7 us (22%)
  Pallas kernels  35.3 us (19%)
  local copies, waits for them, and re-layouts  3.77 us (2%)
    all_to_all x5, starting transfers between devices, exchange(): return lax.all_to_all(pieces, axes, split_axis=0, concat_axis=0, tiled=True)  62.6 us
    pallas_call x11, Pallas kernels, call(): pl.pallas_call(kernel, out_shape=[jax.ShapeDtypeStruct(s, jnp.float32) fo...  35.3 us
    all_to_all x5, waiting for transfers between devices, exchange(): return lax.all_to_all(pieces, axes, split_axis=0, concat_axis=0, tiled=True)  12.2 us
    ppermute x3, starting transfers between devices, from_neighbours(): lax.ppermute(block, 'x', [((i - s) % NX, i) for i in range(NX)])  10.3 us
    ppermute x1, waiting for transfers between devices, relayed_from_neighbours(): ahead_one = lax.ppermute(block, 'x', from_ahead)  9.86 us
    ppermute x2, starting transfers between devices, behind(): lax.ppermute(block, axes, [((i - distance) % BLOCKS, i) for i in range(BL...  9.19 us
    ppermute x3, starting transfers between devices, back_to_neighbours(): lax.ppermute(blocks[s], 'x', [(i, (i - s) % NX) for i in range(NX)])  8.41 us
    ppermute x3, waiting for transfers between devices, from_neighbours(): lax.ppermute(block, 'x', [((i - s) % NX, i) for i in range(NX)])  8.25 us
  transfers between devices with their start and end apart: 16, of which 7 were waited for; matrix products, arithmetic and copies ran while one was open for 0% of the time, Pallas kernels for 13%

profile of v8, /device:TPU:1, one launch (start us, length us, event | category | flops | bytes accessed | tf_op | source)
XLA Modules:
  0.0 182.1 jit_solution(15805367049213229700)
XLA Ops:
  2.5 19.7 %all-to-all-start = ((f32[64,24,128]{2,1,0:T(8,128)}), f32[64,24,128]{2,1,0:T(8,128)S(1)}, u32[]{:S(2)}, u32[]{:S(2)}) async-start(f32[64,24,128]{2,1,0:T(8,128)} %shard_map.76), calls=%async_computation | async-start | bytes 1572864 | tf_op jit(solution)/shard_map/all_to_all | solution.py:383
  22.5 4.1 %collective-permute-start.1 = (f32[128,640]{1,0:T(8,128)S(1)}, f32[128,640]{1,0:T(8,128)S(1)}, u32[]{:S(2)}, u32[]{:S(2)}) collective-permute-start(f32[128,640]{1,0:T(8,128)S(1)} %shard_map.77.refs_1_), channel_id=1, source_target_pairs={{16,0},{32,16},{48,32},{0,48},{17,1},{33,17},{49,33},{1,49},{18,2}... | collective-permute-start | bytes 983048 | tf_op jit(solution)/shard_map/ppermute | solution.py:372
  26.6 1.9 %collective-permute-start = (f32[128,640]{1,0:T(8,128)S(1)}, f32[128,640]{1,0:T(8,128)S(1)}, u32[]{:S(2)}, u32[]{:S(2)}) collective-permute-start(f32[128,640]{1,0:T(8,128)S(1)} %shard_map.77.refs_1_), channel_id=1, source_target_pairs={{48,0},{0,16},{16,32},{32,48},{49,1},{1,17},{17,33},{33,49},{50,2}... | collective-permute-start | bytes 983048 | tf_op jit(solution)/shard_map/ppermute | solution.py:370
  28.6 9.9 %collective-permute-done.1.refs_4_ = f32[128,640]{1,0:T(8,128)S(1)} collective-permute-done((f32[128,640]{1,0:T(8,128)S(1)}, f32[128,640]{1,0:T(8,128)S(1)}, u32[]{:S(2)}, u32[]{:S(2)}) %collective-permute-start.1) | collective-permute-done | bytes 327712 | tf_op jit(solution)/shard_map/ppermute | solution.py:372
  38.4 4.5 %collective-permute-start.2 = (f32[128,640]{1,0:T(8,128)S(1)}, f32[128,640]{1,0:T(8,128)S(1)}, u32[]{:S(2)}, u32[]{:S(2)}) collective-permute-start(f32[128,640]{1,0:T(8,128)S(1)} %collective-permute-done.1.refs_4_), channel_id=1, source_target_pairs={{16,0},{32,16},{48,32},{0,48},{17,1},{33,17},{49,33},{1,49},{18,2}... | collective-permute-start | bytes 983048 | tf_op jit(solution)/shard_map/ppermute | solution.py:373
  43.8 7.3 %collective-permute-start.6 = (f32[2,2,64,640]{3,2,1,0:T(8,128)}, f32[2,2,64,640]{3,2,1,0:T(8,128)}, u32[]{:S(2)}, u32[]{:S(2)}) collective-permute-start(f32[2,2,64,640]{3,2,1,0:T(8,128)} %slice.4), channel_id=1, source_target_pairs={{504,0},{0,8},{8,16},{16,24},{24,32},{32,40},{40,48},{48,56},{56,6... | collective-permute-start | bytes 1966088 | tf_op jit(solution)/shard_map/ppermute | solution.py:362
  51.0 1.9 %collective-permute-start.7 = (f32[2,2,64,640]{3,2,1,0:T(8,128)}, f32[2,2,64,640]{3,2,1,0:T(8,128)}, u32[]{:S(2)}, u32[]{:S(2)}) collective-permute-start(f32[2,2,64,640]{3,2,1,0:T(8,128)} %slice.4), channel_id=1, source_target_pairs={{496,0},{504,8},{0,16},{8,24},{16,32},{24,40},{32,48},{40,56},{48,... | collective-permute-start | bytes 1966088 | tf_op jit(solution)/shard_map/ppermute | solution.py:362
  53.0 5.6 %shard_map.78 = (f32[1920,128]{1,0:T(8,128)}, f32[1536,128]{1,0:T(8,128)}) custom-call(f32[1536,128]{1,0:T(8,128)S(1)} %bitcast.10, f32[128,640]{1,0:T(8,128)S(1)} %shard_map.77.refs_1_, f32[128,640]{1,0:T(8,128)S(1)} %collective-permute-done.refs_2_, f32[128,640]{1,0:T(8,128)S(1)} %collective-permute-done.2.refs_3_, ...), custom_call_target="tpu_custom_call" | custom-call | flops 5000000000 | bytes 1000000 | tf_op jit(solution)/shard_map/pallas_call | solution.py:92
  58.6 8.3 %all-to-all-start.1 = ((f32[16,96,128]{2,1,0:T(8,128)}), f32[16,96,128]{2,1,0:T(8,128)S(1)}, u32[]{:S(2)}, u32[]{:S(2)}) async-start(f32[16,96,128]{2,1,0:T(8,128)} %bitcast.3), calls=%async_computation.1 | async-start | bytes 1572864 | tf_op jit(solution)/shard_map/all_to_all | solution.py:383
  66.9 2.6 %shard_map.79.refs_2_.refs_0_ = f32[160,640]{1,0:T(8,128)} custom-call(f32[30,1,384]{2,1,0:T(1,128)} %bitcast.14, f32[3,2,64,640]{3,2,1,0:T(8,128)} %refs_1_.5, f32[1920,128]{1,0:T(8,128)} %get-tuple-element.14.refs_2_.refs_4_.refs_6_), custom_call_target="tpu_custom_call" | custom-call | flops 100000000 | bytes 1000000 | tf_op jit(solution)/shard_map/pallas_call | solution.py:92
  69.5 1.9 %collective-permute-start.3 = (f32[160,640]{1,0:T(8,128)}, f32[160,640]{1,0:T(8,128)S(1)}, u32[]{:S(2)}, u32[]{:S(2)}) collective-permute-start(f32[160,640]{1,0:T(8,128)} %shard_map.79.refs_2_.refs_0_), channel_id=1, source_target_pairs={{48,0},{0,16},{16,32},{32,48},{49,1},{1,17},{17,33},{33,49},{50,2}... | collective-permute-start | bytes 1228808 | tf_op jit(solution)/shard_map/ppermute | solution.py:366
  71.5 6.5 %collective-permute-start.4 = (f32[160,640]{1,0:T(8,128)}, f32[160,640]{1,0:T(8,128)S(1)}, u32[]{:S(2)}, u32[]{:S(2)}) collective-permute-start(f32[160,640]{1,0:T(8,128)} %shard_map.79.refs_2_.refs_0_), channel_id=1, source_target_pairs={{32,0},{48,16},{0,32},{16,48},{33,1},{49,17},{1,33},{17,49},{34,2}... | collective-permute-start | bytes 1228808 | tf_op jit(solution)/shard_map/ppermute | solution.py:366
  79.9 4.2 %collective-permute-done.6.refs_2_ = f32[2,2,64,640]{3,2,1,0:T(8,128)} collective-permute-done((f32[2,2,64,640]{3,2,1,0:T(8,128)}, f32[2,2,64,640]{3,2,1,0:T(8,128)}, u32[]{:S(2)}, u32[]{:S(2)}) %collective-permute-start.6) | collective-permute-done | bytes 655392 | tf_op jit(solution)/shard_map/ppermute | solution.py:362
  84.1 9.8 %shard_map.80.refs_6_.refs_3_ = f32[2,64,640]{2,1,0:T(8,128)} custom-call(s32[1]{0:T(128)} %bitcast.5.refs_0_, f32[3,2,64,640]{3,2,1,0:T(8,128)} %refs_1_.5, f32[2,2,64,640]{3,2,1,0:T(8,128)} %collective-permute-done.6.refs_2_, f32[2,2,64,640]{3,2,1,0:T(8,128)} %collective-permute-done.7.refs_3_), custom_call_target="tpu_custom_call" | custom-call | flops 12000000000 | bytes 1000000 | tf_op jit(solution)/shard_map/pallas_call | solution.py:92
  93.9 8.2 %collective-permute-done.3.refs_3_.refs_1_ = f32[160,640]{1,0:T(8,128)S(1)} collective-permute-done((f32[160,640]{1,0:T(8,128)}, f32[160,640]{1,0:T(8,128)S(1)}, u32[]{:S(2)}, u32[]{:S(2)}) %collective-permute-start.3) | collective-permute-done | bytes 409632 | tf_op jit(solution)/shard_map/ppermute | solution.py:366
  105.0 10.2 %all-to-all-start.2 = ((f32[16,96,128]{2,1,0:T(8,128)}), f32[16,96,128]{2,1,0:T(8,128)S(1)}, u32[]{:S(2)}, u32[]{:S(2)}) async-start(f32[16,96,128]{2,1,0:T(8,128)} %shard_map.81.refs_5_.refs_7_), calls=%async_computation.2 | async-start | bytes 1572864 | tf_op jit(solution)/shard_map/all_to_all | solution.py:383
  115.2 4.9 %shard_map.82 = (f32[64,640]{1,0:T(8,128)}, f32[64,640]{1,0:T(8,128)}, f32[64,640]{1,0:T(8,128)}, f32[64,640]{1,0:T(8,128)}) custom-call(f32[160,640]{1,0:T(8,128)} %shard_map.79.refs_2_.refs_0_, f32[160,640]{1,0:T(8,128)} %copy-done.3, f32[160,640]{1,0:T(8,128)} %copy-done.5, f32[160,640]{1,0:T(8,128)} %copy-done.7, ...), custom_call_target="tpu_custom_call" | custom-call | flops 4000000000 | bytes 1000000 | tf_op jit(solution)/shard_map/pallas_call | solution.py:92
  122.0 4.6 %collective-permute-start.8 = (f32[64,640]{1,0:T(8,128)}, f32[64,640]{1,0:T(8,128)S(1)}, u32[]{:S(2)}, u32[]{:S(2)}) collective-permute-start(f32[64,640]{1,0:T(8,128)} %get-tuple-element.15), channel_id=1, source_target_pairs={{0,48},{16,0},{32,16},{48,32},{1,49},{17,1},{33,17},{49,33},{2,50}... | collective-permute-start | bytes 491528 | tf_op jit(solution)/shard_map/ppermute | solution.py:378
  129.2 5.5 %collective-permute-done.9.refs_9_.refs_3_ = f32[64,640]{1,0:T(8,128)S(1)} collective-permute-done((f32[64,640]{1,0:T(8,128)}, f32[64,640]{1,0:T(8,128)S(1)}, u32[]{:S(2)}, u32[]{:S(2)}) %collective-permute-start.9) | collective-permute-done | bytes 163872 | tf_op jit(solution)/shard_map/ppermute | solution.py:378
  134.8 6.3 %shard_map.83 = f32[4,72,640]{2,1,0:T(8,128)} custom-call(s32[1]{0:T(128)} %bitcast.refs_0_, f32[1536,128]{1,0:T(8,128)S(1)} %bitcast.9, f32[160,640]{1,0:T(8,128)S(1)} %copy-done.2, f32[160,640]{1,0:T(8,128)S(1)} %copy-done.4, f32[160,640]{1,0:T(8,128)S(1)} %copy-done.6, f32[160,640]{1,0:T(8,128)S(1)} %copy-done.8, ...), custom_call_target="tpu_custom_call" | custom-call | flops 5000000000 | bytes 1000000 | tf_op jit(solution)/shard_map/pallas_call | solution.py:92
  141.1 3.6 %all-to-all-start.3 = ((f32[4,72,640]{2,1,0:T(8,128)}), f32[4,72,640]{2,1,0:T(8,128)S(1)}, u32[]{:S(2)}, u32[]{:S(2)}) async-start(f32[4,72,640]{2,1,0:T(8,128)} %shard_map.83), calls=%async_computation.3 | async-start | bytes 1474560 | tf_op jit(solution)/shard_map/all_to_all | solution.py:383
  144.7 8.0 %all-to-all-done.3.refs_0_ = f32[4,72,640]{2,1,0:T(8,128)S(1)} async-done(((f32[4,72,640]{2,1,0:T(8,128)}), f32[4,72,640]{2,1,0:T(8,128)S(1)}, u32[]{:S(2)}, u32[]{:S(2)}) %all-to-all-start.3) | async-done | bytes 737312 | tf_op jit(solution)/shard_map/all_to_all | solution.py:383
  154.6 20.7 %all-to-all-start.4 = ((f32[8,8,128]{2,1,0:T(8,128)}), f32[8,8,128]{2,1,0:T(8,128)S(1)}, u32[]{:S(2)}, u32[]{:S(2)}) async-start(f32[8,8,128]{2,1,0:T(8,128)} %get-tuple-element.19.refs_2_), calls=%async_computation.4 | async-start | bytes 65536 | tf_op jit(solution)/shard_map/all_to_all | solution.py:383
  176.1 4.2 %all-to-all-done.4.refs_0_ = f32[8,8,128]{2,1,0:T(8,128)S(1)} async-done(((f32[8,8,128]{2,1,0:T(8,128)}), f32[8,8,128]{2,1,0:T(8,128)S(1)}, u32[]{:S(2)}, u32[]{:S(2)}) %all-to-all-start.4) | async-done | bytes 32800 | tf_op jit(solution)/shard_map/all_to_all | solution.py:383
  (55 shorter events, 16.5 us)
Async XLA Ops:
  2.5 19.8 %copy-start = (f32[3,2,64,640]{3,2,1,0:T(8,128)S(1)}, f32[3,2,64,640]{3,2,1,0:T(8,128)}, u32[]{:S(2)}) copy-start(f32[3,2,64,640]{3,2,1,0:T(8,128)} %refs_1_.5) | copy-start | bytes 2949124
  2.5 19.8 %copy-start.11 = (f32[1,64]{1,0:T(1,128)S(1)}, f32[1,64]{1,0:T(1,128)}, u32[]{:S(2)}) copy-start(f32[1,64]{1,0:T(1,128)} %refs_0_.1) | copy-start | bytes 772
  2.5 50.5 %all-to-all-start = ((f32[64,24,128]{2,1,0:T(8,128)}), f32[64,24,128]{2,1,0:T(8,128)S(1)}, u32[]{:S(2)}, u32[]{:S(2)}) async-start(f32[64,24,128]{2,1,0:T(8,128)} %shard_map.76), calls=%async_computation | async-start | bytes 1572864 | tf_op jit(solution)/shard_map/all_to_all | solution.py:383
  22.5 15.9 %collective-permute-start.1 = (f32[128,640]{1,0:T(8,128)S(1)}, f32[128,640]{1,0:T(8,128)S(1)}, u32[]{:S(2)}, u32[]{:S(2)}) collective-permute-start(f32[128,640]{1,0:T(8,128)S(1)} %shard_map.77.refs_1_), channel_id=1, source_target_pairs={{16,0},{32,16},{48,32},{0,48},{17,1},{33,17},{49,33},{1,49},{18,2}... | collective-permute-start | bytes 983048 | tf_op jit(solution)/shard_map/ppermute | solution.py:372
  26.6 26.4 %collective-permute-start = (f32[128,640]{1,0:T(8,128)S(1)}, f32[128,640]{1,0:T(8,128)S(1)}, u32[]{:S(2)}, u32[]{:S(2)}) collective-permute-start(f32[128,640]{1,0:T(8,128)S(1)} %shard_map.77.refs_1_), channel_id=1, source_target_pairs={{48,0},{0,16},{16,32},{32,48},{49,1},{1,17},{17,33},{33,49},{50,2}... | collective-permute-start | bytes 983048 | tf_op jit(solution)/shard_map/ppermute | solution.py:370
  38.4 14.6 %collective-permute-start.2 = (f32[128,640]{1,0:T(8,128)S(1)}, f32[128,640]{1,0:T(8,128)S(1)}, u32[]{:S(2)}, u32[]{:S(2)}) collective-permute-start(f32[128,640]{1,0:T(8,128)S(1)} %collective-permute-done.1.refs_4_), channel_id=1, source_target_pairs={{16,0},{32,16},{48,32},{0,48},{17,1},{33,17},{49,33},{1,49},{18,2}... | collective-permute-start | bytes 983048 | tf_op jit(solution)/shard_map/ppermute | solution.py:373
  43.8 40.4 %collective-permute-start.6 = (f32[2,2,64,640]{3,2,1,0:T(8,128)}, f32[2,2,64,640]{3,2,1,0:T(8,128)}, u32[]{:S(2)}, u32[]{:S(2)}) collective-permute-start(f32[2,2,64,640]{3,2,1,0:T(8,128)} %slice.4), channel_id=1, source_target_pairs={{504,0},{0,8},{8,16},{16,24},{24,32},{32,40},{40,48},{48,56},{56,6... | collective-permute-start | bytes 1966088 | tf_op jit(solution)/shard_map/ppermute | solution.py:362
  51.0 33.1 %collective-permute-start.7 = (f32[2,2,64,640]{3,2,1,0:T(8,128)}, f32[2,2,64,640]{3,2,1,0:T(8,128)}, u32[]{:S(2)}, u32[]{:S(2)}) collective-permute-start(f32[2,2,64,640]{3,2,1,0:T(8,128)} %slice.4), channel_id=1, source_target_pairs={{496,0},{504,8},{0,16},{8,24},{16,32},{24,40},{32,48},{40,56},{48,... | collective-permute-start | bytes 1966088 | tf_op jit(solution)/shard_map/ppermute | solution.py:362
  58.6 43.6 %all-to-all-start.1 = ((f32[16,96,128]{2,1,0:T(8,128)}), f32[16,96,128]{2,1,0:T(8,128)S(1)}, u32[]{:S(2)}, u32[]{:S(2)}) async-start(f32[16,96,128]{2,1,0:T(8,128)} %bitcast.3), calls=%async_computation.1 | async-start | bytes 1572864 | tf_op jit(solution)/shard_map/all_to_all | solution.py:383
  69.5 32.6 %collective-permute-start.3 = (f32[160,640]{1,0:T(8,128)}, f32[160,640]{1,0:T(8,128)S(1)}, u32[]{:S(2)}, u32[]{:S(2)}) collective-permute-start(f32[160,640]{1,0:T(8,128)} %shard_map.79.refs_2_.refs_0_), channel_id=1, source_target_pairs={{48,0},{0,16},{16,32},{32,48},{49,1},{1,17},{17,33},{33,49},{50,2}... | collective-permute-start | bytes 1228808 | tf_op jit(solution)/shard_map/ppermute | solution.py:366
  71.5 30.7 %collective-permute-start.4 = (f32[160,640]{1,0:T(8,128)}, f32[160,640]{1,0:T(8,128)S(1)}, u32[]{:S(2)}, u32[]{:S(2)}) collective-permute-start(f32[160,640]{1,0:T(8,128)} %shard_map.79.refs_2_.refs_0_), channel_id=1, source_target_pairs={{32,0},{48,16},{0,32},{16,48},{33,1},{49,17},{1,33},{17,49},{34,2}... | collective-permute-start | bytes 1228808 | tf_op jit(solution)/shard_map/ppermute | solution.py:366
  78.0 24.2 %collective-permute-start.5 = (f32[160,640]{1,0:T(8,128)}, f32[160,640]{1,0:T(8,128)S(1)}, u32[]{:S(2)}, u32[]{:S(2)}) collective-permute-start(f32[160,640]{1,0:T(8,128)} %shard_map.79.refs_2_.refs_0_), channel_id=1, source_target_pairs={{16,0},{32,16},{48,32},{0,48},{17,1},{33,17},{49,33},{1,49},{18,2}... | collective-permute-start | bytes 1228808 | tf_op jit(solution)/shard_map/ppermute | solution.py:366
  84.1 18.1 %copy-start.1 = (f32[160,640]{1,0:T(8,128)S(1)}, f32[160,640]{1,0:T(8,128)}, u32[]{:S(2)}) copy-start(f32[160,640]{1,0:T(8,128)} %shard_map.79.refs_2_.refs_0_) | copy-start | bytes 1228804
  105.0 29.7 %all-to-all-start.2 = ((f32[16,96,128]{2,1,0:T(8,128)}), f32[16,96,128]{2,1,0:T(8,128)S(1)}, u32[]{:S(2)}, u32[]{:S(2)}) async-start(f32[16,96,128]{2,1,0:T(8,128)} %shard_map.81.refs_5_.refs_7_), calls=%async_computation.2 | async-start | bytes 1572864 | tf_op jit(solution)/shard_map/all_to_all | solution.py:383
  115.2 19.5 %copy-start.2 = (f32[160,640]{1,0:T(8,128)S(1)}, f32[160,640]{1,0:T(8,128)}, u32[]{:S(2)}) copy-start(f32[160,640]{1,0:T(8,128)} %shard_map.79.refs_2_.refs_0_) | copy-start | bytes 1228804
  115.2 19.5 %copy-start.4 = (f32[160,640]{1,0:T(8,128)S(1)}, f32[160,640]{1,0:T(8,128)}, u32[]{:S(2)}) copy-start(f32[160,640]{1,0:T(8,128)} %copy-done.3) | copy-start | bytes 1228804
  115.2 19.5 %copy-start.6 = (f32[160,640]{1,0:T(8,128)S(1)}, f32[160,640]{1,0:T(8,128)}, u32[]{:S(2)}) copy-start(f32[160,640]{1,0:T(8,128)} %copy-done.5) | copy-start | bytes 1228804
  115.2 19.5 %copy-start.8 = (f32[160,640]{1,0:T(8,128)S(1)}, f32[160,640]{1,0:T(8,128)}, u32[]{:S(2)}) copy-start(f32[160,640]{1,0:T(8,128)} %copy-done.7) | copy-start | bytes 1228804
  120.1 8.4 %collective-permute-start.10 = (f32[64,640]{1,0:T(8,128)}, f32[64,640]{1,0:T(8,128)S(1)}, u32[]{:S(2)}, u32[]{:S(2)}) collective-permute-start(f32[64,640]{1,0:T(8,128)} %get-tuple-element.17), channel_id=1, source_target_pairs={{0,16},{16,32},{32,48},{48,0},{1,17},{17,33},{33,49},{49,1},{2,18}... | collective-permute-start | bytes 491528 | tf_op jit(solution)/shard_map/ppermute | solution.py:378
  122.0 7.1 %collective-permute-start.8 = (f32[64,640]{1,0:T(8,128)}, f32[64,640]{1,0:T(8,128)S(1)}, u32[]{:S(2)}, u32[]{:S(2)}) collective-permute-start(f32[64,640]{1,0:T(8,128)} %get-tuple-element.15), channel_id=1, source_target_pairs={{0,48},{16,0},{32,16},{48,32},{1,49},{17,1},{33,17},{49,33},{2,50}... | collective-permute-start | bytes 491528 | tf_op jit(solution)/shard_map/ppermute | solution.py:378
  126.6 8.1 %collective-permute-start.9 = (f32[64,640]{1,0:T(8,128)}, f32[64,640]{1,0:T(8,128)S(1)}, u32[]{:S(2)}, u32[]{:S(2)}) collective-permute-start(f32[64,640]{1,0:T(8,128)} %get-tuple-element.16), channel_id=1, source_target_pairs={{0,32},{16,48},{32,0},{48,16},{1,33},{17,49},{33,1},{49,17},{2,34}... | collective-permute-start | bytes 491528 | tf_op jit(solution)/shard_map/ppermute | solution.py:378
  141.1 11.7 %all-to-all-start.3 = ((f32[4,72,640]{2,1,0:T(8,128)}), f32[4,72,640]{2,1,0:T(8,128)S(1)}, u32[]{:S(2)}, u32[]{:S(2)}) async-start(f32[4,72,640]{2,1,0:T(8,128)} %shard_map.83), calls=%async_computation.3 | async-start | bytes 1474560 | tf_op jit(solution)/shard_map/all_to_all | solution.py:383
  154.6 20.7 %copy-start.10 = (f32[1,10,3,384]{3,0,2,1:T(1,128)S(1)}, f32[1,10,3,384]{3,0,2,1:T(1,128)}, u32[]{:S(2)}) copy-start(f32[1,10,3,384]{3,0,2,1:T(1,128)} %param.7) | copy-start | bytes 138244
  154.6 25.6 %all-to-all-start.4 = ((f32[8,8,128]{2,1,0:T(8,128)}), f32[8,8,128]{2,1,0:T(8,128)S(1)}, u32[]{:S(2)}, u32[]{:S(2)}) async-start(f32[8,8,128]{2,1,0:T(8,128)} %get-tuple-element.19.refs_2_), calls=%async_computation.4 | async-start | bytes 65536 | tf_op jit(solution)/shard_map/all_to_all | solution.py:383
  (9 other events, 31.6 us)

commit v9 on v8

--- a/solution.py
+++ b/solution.py
@@ -155,6 +155,10 @@
     queries_ref[TOK : 2 * TOK, :] = qkv_ref[0, 1]
 
 
+def marker_body(args, lazy, results, scratch, need, send):
+    results[0][...] = jnp.zeros((8, LANES), jnp.float32)
+
+
 def widened(part):
     return jnp.concatenate([part, jnp.zeros((part.shape[0], LANES - SLICE), jnp.float32)], axis=1)
 
@@ -411,12 +415,10 @@
         after=(weights,),
     )
     queries = from_neighbours(queries)
-    (attended,) = call(
-        attention_body, [(GROUPS, TOK, D)], 12, position, lazy=whole(qkv, near, far), smem=(0,)
-    )
+    (marker,) = call(marker_body, [(8, LANES)], 12, after=(near, far))
     (send3,) = call(
         moment_body, [(NZ * NY, NX * 24, LANES)], 2, x, recv2, lazy=[(q, (2 * TOK, 32)) for q in queries],
-        smem=(0,), fan=(0,), after=(attended,), room=ROOM,
+        smem=(0,), fan=(0,), after=(marker,), room=ROOM,
     )
     recv3 = exchange(send3, ("z", "yh")).reshape(BLOCKS * 24, LANES)
     first = back_to_neighbours(
@@ -431,9 +433,12 @@
         smem=(0,), after=first[1:], room=ROOM,
     )
     second = exchange(send_second, "x")
+    (attended,) = call(
+        attention_body, [(GROUPS, TOK, D)], 8, position, lazy=whole(qkv, near, far), smem=(0,), after=(send_second,)
+    )
     readout, send5 = call(
         squares_body, [(GROUPS, TOK, D), (NARROW, 8, GROUPS * TOK)], 1, second, lazy=whole(*first), fan=(1,),
-        room=SMALL,
+        after=(attended,), room=SMALL,
     )
     recv5 = exchange(send5, "narrow")
     new_weights, new_moment = call(

time: 183 us -> 181 us (0.989)
  starting transfers between devices: 101 us -> 89.2 us
  waiting for transfers between devices: 40.7 us -> 48 us
    all_to_all x5, starting transfers between devices: 62.6 us -> 50.5 us  [exchange(): return lax.all_to_all(pieces, axes, split_axis=0, concat_axis=0, tiled=True)]
    ppermute x3, waiting for transfers between devices: 8.25 us -> 17.4 us  [from_neighbours(): lax.ppermute(block, 'x', [((i - s) % NX, i) for i in range(NX)])]
    unnamed x34 -> x36, local copies, waits for them, and re-layouts: 2.87 us -> 4.01 us
    pallas_call x11 -> x12, Pallas kernels: 35.3 us -> 35.9 us  [call(): pl.pallas_call(kernel, out_shape=[jax.ShapeDtypeStruct(s, jnp.float32) fo...]
  transfers between devices with their start and end apart: 16 -> 16, of which waited for: 7 -> 7; matrix products, arithmetic and copies ran while one was open for 0% -> 1% of each run, Pallas kernels for 13% -> 14%
where the time goes in v9:
time: 181 us; the launch traced here: 179 us
  starting transfers between devices  89.2 us (49%)
  waiting for transfers between devices  48 us (27%)
  Pallas kernels  35.9 us (20%)
  local copies, waits for them, and re-layouts  4.92 us (3%)
    all_to_all x5, starting transfers between devices, exchange(): return lax.all_to_all(pieces, axes, split_axis=0, concat_axis=0, tiled=True)  50.5 us
    pallas_call x12, Pallas kernels, call(): pl.pallas_call(kernel, out_shape=[jax.ShapeDtypeStruct(s, jnp.float32) fo...  35.9 us
    ppermute x3, waiting for transfers between devices, from_neighbours(): lax.ppermute(block, 'x', [((i - s) % NX, i) for i in range(NX)])  17.4 us
    all_to_all x5, waiting for transfers between devices, exchange(): return lax.all_to_all(pieces, axes, split_axis=0, concat_axis=0, tiled=True)  11.6 us
    ppermute x3, starting transfers between devices, from_neighbours(): lax.ppermute(block, 'x', [((i - s) % NX, i) for i in range(NX)])  10.5 us
    ppermute x1, waiting for transfers between devices, relayed_from_neighbours(): ahead_one = lax.ppermute(block, 'x', from_ahead)  9.86 us
    ppermute x2, starting transfers between devices, behind(): lax.ppermute(block, axes, [((i - distance) % BLOCKS, i) for i in range(BL...  9.19 us
    ppermute x3, starting transfers between devices, back_to_neighbours(): lax.ppermute(blocks[s], 'x', [(i, (i - s) % NX) for i in range(NX)])  8.59 us
  transfers between devices with their start and end apart: 16, of which 7 were waited for; matrix products, arithmetic and copies ran while one was open for 1% of the time, Pallas kernels for 14%

profile of v9, /device:TPU:1, one launch (start us, length us, event | category | flops | bytes accessed | tf_op | source)
XLA Modules:
  0.0 179.3 jit_solution(3982954445709975381)
XLA Ops:
  2.5 19.7 %all-to-all-start = ((f32[64,24,128]{2,1,0:T(8,128)}), f32[64,24,128]{2,1,0:T(8,128)S(1)}, u32[]{:S(2)}, u32[]{:S(2)}) async-start(f32[64,24,128]{2,1,0:T(8,128)} %shard_map.76), calls=%async_computation | async-start | bytes 1572864 | tf_op jit(solution)/shard_map/all_to_all | solution.py:387
  22.5 4.1 %collective-permute-start.1 = (f32[128,640]{1,0:T(8,128)S(1)}, f32[128,640]{1,0:T(8,128)S(1)}, u32[]{:S(2)}, u32[]{:S(2)}) collective-permute-start(f32[128,640]{1,0:T(8,128)S(1)} %shard_map.77.refs_1_), channel_id=1, source_target_pairs={{16,0},{32,16},{48,32},{0,48},{17,1},{33,17},{49,33},{1,49},{18,2}... | collective-permute-start | bytes 983048 | tf_op jit(solution)/shard_map/ppermute | solution.py:376
  28.6 9.9 %collective-permute-done.1.refs_4_ = f32[128,640]{1,0:T(8,128)S(1)} collective-permute-done((f32[128,640]{1,0:T(8,128)S(1)}, f32[128,640]{1,0:T(8,128)S(1)}, u32[]{:S(2)}, u32[]{:S(2)}) %collective-permute-start.1) | collective-permute-done | bytes 327712 | tf_op jit(solution)/shard_map/ppermute | solution.py:376
  38.4 4.5 %collective-permute-start.2 = (f32[128,640]{1,0:T(8,128)S(1)}, f32[128,640]{1,0:T(8,128)S(1)}, u32[]{:S(2)}, u32[]{:S(2)}) collective-permute-start(f32[128,640]{1,0:T(8,128)S(1)} %collective-permute-done.1.refs_4_), channel_id=1, source_target_pairs={{16,0},{32,16},{48,32},{0,48},{17,1},{33,17},{49,33},{1,49},{18,2}... | collective-permute-start | bytes 983048 | tf_op jit(solution)/shard_map/ppermute | solution.py:377
  43.8 7.3 %collective-permute-start.6 = (f32[2,2,64,640]{3,2,1,0:T(8,128)}, f32[2,2,64,640]{3,2,1,0:T(8,128)}, u32[]{:S(2)}, u32[]{:S(2)}) collective-permute-start(f32[2,2,64,640]{3,2,1,0:T(8,128)} %slice.4), channel_id=1, source_target_pairs={{504,0},{0,8},{8,16},{16,24},{24,32},{32,40},{40,48},{48,56},{56,6... | collective-permute-start | bytes 1966088 | tf_op jit(solution)/shard_map/ppermute | solution.py:366
  51.1 1.9 %collective-permute-start.7 = (f32[2,2,64,640]{3,2,1,0:T(8,128)}, f32[2,2,64,640]{3,2,1,0:T(8,128)}, u32[]{:S(2)}, u32[]{:S(2)}) collective-permute-start(f32[2,2,64,640]{3,2,1,0:T(8,128)} %slice.4), channel_id=1, source_target_pairs={{496,0},{504,8},{0,16},{8,24},{16,32},{24,40},{32,48},{40,56},{48,... | collective-permute-start | bytes 1966088 | tf_op jit(solution)/shard_map/ppermute | solution.py:366
  53.0 5.6 %shard_map.78 = (f32[1920,128]{1,0:T(8,128)}, f32[1536,128]{1,0:T(8,128)}) custom-call(f32[1536,128]{1,0:T(8,128)S(1)} %bitcast.10, f32[128,640]{1,0:T(8,128)S(1)} %shard_map.77.refs_1_, f32[128,640]{1,0:T(8,128)S(1)} %collective-permute-done.refs_2_, f32[128,640]{1,0:T(8,128)S(1)} %collective-permute-done.2.refs_3_, ...), custom_call_target="tpu_custom_call" | custom-call | flops 5000000000 | bytes 1000000 | tf_op jit(solution)/shard_map/pallas_call | solution.py:92
  58.6 8.3 %all-to-all-start.1 = ((f32[16,96,128]{2,1,0:T(8,128)}), f32[16,96,128]{2,1,0:T(8,128)S(1)}, u32[]{:S(2)}, u32[]{:S(2)}) async-start(f32[16,96,128]{2,1,0:T(8,128)} %bitcast.3), calls=%async_computation.1 | async-start | bytes 1572864 | tf_op jit(solution)/shard_map/all_to_all | solution.py:387
  66.9 2.6 %shard_map.79.refs_2_.refs_0_ = f32[160,640]{1,0:T(8,128)} custom-call(f32[30,1,384]{2,1,0:T(1,128)} %bitcast.14, f32[3,2,64,640]{3,2,1,0:T(8,128)} %refs_1_.5, f32[1920,128]{1,0:T(8,128)} %get-tuple-element.14.refs_2_.refs_4_.refs_6_), custom_call_target="tpu_custom_call" | custom-call | flops 100000000 | bytes 1000000 | tf_op jit(solution)/shard_map/pallas_call | solution.py:92
  69.5 2.1 %collective-permute-start.3 = (f32[160,640]{1,0:T(8,128)}, f32[160,640]{1,0:T(8,128)S(1)}, u32[]{:S(2)}, u32[]{:S(2)}) collective-permute-start(f32[160,640]{1,0:T(8,128)} %shard_map.79.refs_2_.refs_0_), channel_id=1, source_target_pairs={{48,0},{0,16},{16,32},{32,48},{49,1},{1,17},{17,33},{33,49},{50,2}... | collective-permute-start | bytes 1228808 | tf_op jit(solution)/shard_map/ppermute | solution.py:370
  71.6 6.5 %collective-permute-start.4 = (f32[160,640]{1,0:T(8,128)}, f32[160,640]{1,0:T(8,128)S(1)}, u32[]{:S(2)}, u32[]{:S(2)}) collective-permute-start(f32[160,640]{1,0:T(8,128)} %shard_map.79.refs_2_.refs_0_), channel_id=1, source_target_pairs={{32,0},{48,16},{0,32},{16,48},{33,1},{49,17},{1,33},{17,49},{34,2}... | collective-permute-start | bytes 1228808 | tf_op jit(solution)/shard_map/ppermute | solution.py:370
  80.0 4.1 %collective-permute-done.6.refs_0_.refs_2_ = f32[2,2,64,640]{3,2,1,0:T(8,128)} collective-permute-done((f32[2,2,64,640]{3,2,1,0:T(8,128)}, f32[2,2,64,640]{3,2,1,0:T(8,128)}, u32[]{:S(2)}, u32[]{:S(2)}) %collective-permute-start.6) | collective-permute-done | bytes 655392 | tf_op jit(solution)/shard_map/ppermute | solution.py:366
  84.8 17.4 %collective-permute-done.3.refs_3_.refs_1_ = f32[160,640]{1,0:T(8,128)S(1)} collective-permute-done((f32[160,640]{1,0:T(8,128)}, f32[160,640]{1,0:T(8,128)S(1)}, u32[]{:S(2)}, u32[]{:S(2)}) %collective-permute-start.3) | collective-permute-done | bytes 409632 | tf_op jit(solution)/shard_map/ppermute | solution.py:370
  104.5 10.2 %all-to-all-start.2 = ((f32[16,96,128]{2,1,0:T(8,128)}), f32[16,96,128]{2,1,0:T(8,128)S(1)}, u32[]{:S(2)}, u32[]{:S(2)}) async-start(f32[16,96,128]{2,1,0:T(8,128)} %shard_map.81.refs_5_.refs_7_), calls=%async_computation.2 | async-start | bytes 1572864 | tf_op jit(solution)/shard_map/all_to_all | solution.py:387
  114.7 4.9 %shard_map.82 = (f32[64,640]{1,0:T(8,128)}, f32[64,640]{1,0:T(8,128)}, f32[64,640]{1,0:T(8,128)}, f32[64,640]{1,0:T(8,128)}) custom-call(f32[160,640]{1,0:T(8,128)} %shard_map.79.refs_2_.refs_0_, f32[160,640]{1,0:T(8,128)} %copy-done.3, f32[160,640]{1,0:T(8,128)} %copy-done.5, f32[160,640]{1,0:T(8,128)} %copy-done.7, ...), custom_call_target="tpu_custom_call" | custom-call | flops 4000000000 | bytes 1000000 | tf_op jit(solution)/shard_map/pallas_call | solution.py:92
  121.6 4.6 %collective-permute-start.8 = (f32[64,640]{1,0:T(8,128)}, f32[64,640]{1,0:T(8,128)S(1)}, u32[]{:S(2)}, u32[]{:S(2)}) collective-permute-start(f32[64,640]{1,0:T(8,128)} %get-tuple-element.15), channel_id=1, source_target_pairs={{0,48},{16,0},{32,16},{48,32},{1,49},{17,1},{33,17},{49,33},{2,50}... | collective-permute-start | bytes 491528 | tf_op jit(solution)/shard_map/ppermute | solution.py:382
  126.1 2.1 %collective-permute-start.9 = (f32[64,640]{1,0:T(8,128)}, f32[64,640]{1,0:T(8,128)S(1)}, u32[]{:S(2)}, u32[]{:S(2)}) collective-permute-start(f32[64,640]{1,0:T(8,128)} %get-tuple-element.16), channel_id=1, source_target_pairs={{0,32},{16,48},{32,0},{48,16},{1,33},{17,49},{33,1},{49,17},{2,34}... | collective-permute-start | bytes 491528 | tf_op jit(solution)/shard_map/ppermute | solution.py:382
  128.9 5.0 %collective-permute-done.9.refs_9_.refs_3_ = f32[64,640]{1,0:T(8,128)S(1)} collective-permute-done((f32[64,640]{1,0:T(8,128)}, f32[64,640]{1,0:T(8,128)S(1)}, u32[]{:S(2)}, u32[]{:S(2)}) %collective-permute-start.9) | collective-permute-done | bytes 163872 | tf_op jit(solution)/shard_map/ppermute | solution.py:382
  133.9 6.5 %all-to-all-done.2 = f32[16,96,128]{2,1,0:T(8,128)S(1)} async-done(((f32[16,96,128]{2,1,0:T(8,128)}), f32[16,96,128]{2,1,0:T(8,128)S(1)}, u32[]{:S(2)}, u32[]{:S(2)}) %all-to-all-start.2) | async-done | bytes 786464 | tf_op jit(solution)/shard_map/all_to_all | solution.py:387
  140.5 6.3 %shard_map.83.refs_4_ = f32[4,72,640]{2,1,0:T(8,128)} custom-call(s32[1]{0:T(128)} %bitcast.refs_0_, f32[1536,128]{1,0:T(8,128)S(1)} %bitcast.9, f32[160,640]{1,0:T(8,128)S(1)} %copy-done.2, f32[160,640]{1,0:T(8,128)S(1)} %copy-done.4, f32[160,640]{1,0:T(8,128)S(1)} %copy-done.6, f32[160,640]{1,0:T(8,128)S(1)} %copy-done.8, ...), custom_call_target="tpu_custom_call" | custom-call | flops 5000000000 | bytes 1000000 | tf_op jit(solution)/shard_map/pallas_call | solution.py:92
  146.7 3.5 %all-to-all-start.3 = ((f32[4,72,640]{2,1,0:T(8,128)}), f32[4,72,640]{2,1,0:T(8,128)S(1)}, u32[]{:S(2)}, u32[]{:S(2)}) async-start(f32[4,72,640]{2,1,0:T(8,128)} %shard_map.83.refs_4_), calls=%async_computation.3 | async-start | bytes 1474560 | tf_op jit(solution)/shard_map/all_to_all | solution.py:387
  150.3 9.7 %shard_map.84.refs_5_.refs_3_ = f32[2,64,640]{2,1,0:T(8,128)} custom-call(s32[1]{0:T(128)} %bitcast.6.refs_0_, f32[3,2,64,640]{3,2,1,0:T(8,128)} %refs_1_.5, f32[2,2,64,640]{3,2,1,0:T(8,128)} %collective-permute-done.6.refs_0_.refs_2_, f32[2,2,64,640]{3,2,1,0:T(8,128)} %collective-permute-done.7.refs_1_.refs_3_, f32[4,72,640]{2,1,0:T(8,128)} %shard_map.83.refs_4_), custom_call_target="tpu_custom_call" | custom-call | flops 8000000000 | bytes 1000000 | tf_op jit(solution)/shard_map/pallas_call | solution.py:92
  163.8 8.7 %all-to-all-start.4 = ((f32[8,8,128]{2,1,0:T(8,128)}), f32[8,8,128]{2,1,0:T(8,128)S(1)}, u32[]{:S(2)}, u32[]{:S(2)}) async-start(f32[8,8,128]{2,1,0:T(8,128)} %get-tuple-element.19.refs_2_), calls=%async_computation.4 | async-start | bytes 65536 | tf_op jit(solution)/shard_map/all_to_all | solution.py:387
  173.3 4.2 %all-to-all-done.4.refs_0_ = f32[8,8,128]{2,1,0:T(8,128)S(1)} async-done(((f32[8,8,128]{2,1,0:T(8,128)}), f32[8,8,128]{2,1,0:T(8,128)S(1)}, u32[]{:S(2)}, u32[]{:S(2)}) %all-to-all-start.4) | async-done | bytes 32800 | tf_op jit(solution)/shard_map/all_to_all | solution.py:387
  (58 shorter events, 18.5 us)
Async XLA Ops:
  2.5 19.8 %copy-start = (f32[3,2,64,640]{3,2,1,0:T(8,128)S(1)}, f32[3,2,64,640]{3,2,1,0:T(8,128)}, u32[]{:S(2)}) copy-start(f32[3,2,64,640]{3,2,1,0:T(8,128)} %refs_1_.5) | copy-start | bytes 2949124
  2.5 19.8 %copy-start.11 = (f32[1,64]{1,0:T(1,128)S(1)}, f32[1,64]{1,0:T(1,128)}, u32[]{:S(2)}) copy-start(f32[1,64]{1,0:T(1,128)} %refs_0_.1) | copy-start | bytes 772
  2.5 50.5 %all-to-all-start = ((f32[64,24,128]{2,1,0:T(8,128)}), f32[64,24,128]{2,1,0:T(8,128)S(1)}, u32[]{:S(2)}, u32[]{:S(2)}) async-start(f32[64,24,128]{2,1,0:T(8,128)} %shard_map.76), calls=%async_computation | async-start | bytes 1572864 | tf_op jit(solution)/shard_map/all_to_all | solution.py:387
  22.5 15.9 %collective-permute-start.1 = (f32[128,640]{1,0:T(8,128)S(1)}, f32[128,640]{1,0:T(8,128)S(1)}, u32[]{:S(2)}, u32[]{:S(2)}) collective-permute-start(f32[128,640]{1,0:T(8,128)S(1)} %shard_map.77.refs_1_), channel_id=1, source_target_pairs={{16,0},{32,16},{48,32},{0,48},{17,1},{33,17},{49,33},{1,49},{18,2}... | collective-permute-start | bytes 983048 | tf_op jit(solution)/shard_map/ppermute | solution.py:376
  26.6 26.4 %collective-permute-start = (f32[128,640]{1,0:T(8,128)S(1)}, f32[128,640]{1,0:T(8,128)S(1)}, u32[]{:S(2)}, u32[]{:S(2)}) collective-permute-start(f32[128,640]{1,0:T(8,128)S(1)} %shard_map.77.refs_1_), channel_id=1, source_target_pairs={{48,0},{0,16},{16,32},{32,48},{49,1},{1,17},{17,33},{33,49},{50,2}... | collective-permute-start | bytes 983048 | tf_op jit(solution)/shard_map/ppermute | solution.py:374
  38.4 14.6 %collective-permute-start.2 = (f32[128,640]{1,0:T(8,128)S(1)}, f32[128,640]{1,0:T(8,128)S(1)}, u32[]{:S(2)}, u32[]{:S(2)}) collective-permute-start(f32[128,640]{1,0:T(8,128)S(1)} %collective-permute-done.1.refs_4_), channel_id=1, source_target_pairs={{16,0},{32,16},{48,32},{0,48},{17,1},{33,17},{49,33},{1,49},{18,2}... | collective-permute-start | bytes 983048 | tf_op jit(solution)/shard_map/ppermute | solution.py:377
  43.8 40.4 %collective-permute-start.6 = (f32[2,2,64,640]{3,2,1,0:T(8,128)}, f32[2,2,64,640]{3,2,1,0:T(8,128)}, u32[]{:S(2)}, u32[]{:S(2)}) collective-permute-start(f32[2,2,64,640]{3,2,1,0:T(8,128)} %slice.4), channel_id=1, source_target_pairs={{504,0},{0,8},{8,16},{16,24},{24,32},{32,40},{40,48},{48,56},{56,6... | collective-permute-start | bytes 1966088 | tf_op jit(solution)/shard_map/ppermute | solution.py:366
  51.1 33.1 %collective-permute-start.7 = (f32[2,2,64,640]{3,2,1,0:T(8,128)}, f32[2,2,64,640]{3,2,1,0:T(8,128)}, u32[]{:S(2)}, u32[]{:S(2)}) collective-permute-start(f32[2,2,64,640]{3,2,1,0:T(8,128)} %slice.4), channel_id=1, source_target_pairs={{496,0},{504,8},{0,16},{8,24},{16,32},{24,40},{32,48},{40,56},{48,... | collective-permute-start | bytes 1966088 | tf_op jit(solution)/shard_map/ppermute | solution.py:366
  58.6 43.6 %all-to-all-start.1 = ((f32[16,96,128]{2,1,0:T(8,128)}), f32[16,96,128]{2,1,0:T(8,128)S(1)}, u32[]{:S(2)}, u32[]{:S(2)}) async-start(f32[16,96,128]{2,1,0:T(8,128)} %bitcast.3), calls=%async_computation.1 | async-start | bytes 1572864 | tf_op jit(solution)/shard_map/all_to_all | solution.py:387
  69.5 32.7 %copy-start.1 = (f32[160,640]{1,0:T(8,128)S(1)}, f32[160,640]{1,0:T(8,128)}, u32[]{:S(2)}) copy-start(f32[160,640]{1,0:T(8,128)} %shard_map.79.refs_2_.refs_0_) | copy-start | bytes 1228804
  69.5 32.6 %collective-permute-start.3 = (f32[160,640]{1,0:T(8,128)}, f32[160,640]{1,0:T(8,128)S(1)}, u32[]{:S(2)}, u32[]{:S(2)}) collective-permute-start(f32[160,640]{1,0:T(8,128)} %shard_map.79.refs_2_.refs_0_), channel_id=1, source_target_pairs={{48,0},{0,16},{16,32},{32,48},{49,1},{1,17},{17,33},{33,49},{50,2}... | collective-permute-start | bytes 1228808 | tf_op jit(solution)/shard_map/ppermute | solution.py:370
  71.6 30.6 %collective-permute-start.4 = (f32[160,640]{1,0:T(8,128)}, f32[160,640]{1,0:T(8,128)S(1)}, u32[]{:S(2)}, u32[]{:S(2)}) collective-permute-start(f32[160,640]{1,0:T(8,128)} %shard_map.79.refs_2_.refs_0_), channel_id=1, source_target_pairs={{32,0},{48,16},{0,32},{16,48},{33,1},{49,17},{1,33},{17,49},{34,2}... | collective-permute-start | bytes 1228808 | tf_op jit(solution)/shard_map/ppermute | solution.py:370
  78.1 24.1 %collective-permute-start.5 = (f32[160,640]{1,0:T(8,128)}, f32[160,640]{1,0:T(8,128)S(1)}, u32[]{:S(2)}, u32[]{:S(2)}) collective-permute-start(f32[160,640]{1,0:T(8,128)} %shard_map.79.refs_2_.refs_0_), channel_id=1, source_target_pairs={{16,0},{32,16},{48,32},{0,48},{17,1},{33,17},{49,33},{1,49},{18,2}... | collective-permute-start | bytes 1228808 | tf_op jit(solution)/shard_map/ppermute | solution.py:370
  104.5 35.9 %all-to-all-start.2 = ((f32[16,96,128]{2,1,0:T(8,128)}), f32[16,96,128]{2,1,0:T(8,128)S(1)}, u32[]{:S(2)}, u32[]{:S(2)}) async-start(f32[16,96,128]{2,1,0:T(8,128)} %shard_map.81.refs_5_.refs_7_), calls=%async_computation.2 | async-start | bytes 1572864 | tf_op jit(solution)/shard_map/all_to_all | solution.py:387
  114.7 25.7 %copy-start.2 = (f32[160,640]{1,0:T(8,128)S(1)}, f32[160,640]{1,0:T(8,128)}, u32[]{:S(2)}) copy-start(f32[160,640]{1,0:T(8,128)} %shard_map.79.refs_2_.refs_0_) | copy-start | bytes 1228804
  114.7 25.7 %copy-start.4 = (f32[160,640]{1,0:T(8,128)S(1)}, f32[160,640]{1,0:T(8,128)}, u32[]{:S(2)}) copy-start(f32[160,640]{1,0:T(8,128)} %copy-done.3) | copy-start | bytes 1228804
  114.7 25.7 %copy-start.6 = (f32[160,640]{1,0:T(8,128)S(1)}, f32[160,640]{1,0:T(8,128)}, u32[]{:S(2)}) copy-start(f32[160,640]{1,0:T(8,128)} %copy-done.5) | copy-start | bytes 1228804
  114.7 25.7 %copy-start.8 = (f32[160,640]{1,0:T(8,128)S(1)}, f32[160,640]{1,0:T(8,128)}, u32[]{:S(2)}) copy-start(f32[160,640]{1,0:T(8,128)} %copy-done.7) | copy-start | bytes 1228804
  119.6 9.3 %collective-permute-start.10 = (f32[64,640]{1,0:T(8,128)}, f32[64,640]{1,0:T(8,128)S(1)}, u32[]{:S(2)}, u32[]{:S(2)}) collective-permute-start(f32[64,640]{1,0:T(8,128)} %get-tuple-element.17), channel_id=1, source_target_pairs={{0,16},{16,32},{32,48},{48,0},{1,17},{17,33},{33,49},{49,1},{2,18}... | collective-permute-start | bytes 491528 | tf_op jit(solution)/shard_map/ppermute | solution.py:382
  121.6 7.4 %collective-permute-start.8 = (f32[64,640]{1,0:T(8,128)}, f32[64,640]{1,0:T(8,128)S(1)}, u32[]{:S(2)}, u32[]{:S(2)}) collective-permute-start(f32[64,640]{1,0:T(8,128)} %get-tuple-element.15), channel_id=1, source_target_pairs={{0,48},{16,0},{32,16},{48,32},{1,49},{17,1},{33,17},{49,33},{2,50}... | collective-permute-start | bytes 491528 | tf_op jit(solution)/shard_map/ppermute | solution.py:382
  126.1 7.8 %collective-permute-start.9 = (f32[64,640]{1,0:T(8,128)}, f32[64,640]{1,0:T(8,128)S(1)}, u32[]{:S(2)}, u32[]{:S(2)}) collective-permute-start(f32[64,640]{1,0:T(8,128)} %get-tuple-element.16), channel_id=1, source_target_pairs={{0,32},{16,48},{32,0},{48,16},{1,33},{17,49},{33,1},{49,17},{2,34}... | collective-permute-start | bytes 491528 | tf_op jit(solution)/shard_map/ppermute | solution.py:382
  146.7 14.2 %all-to-all-start.3 = ((f32[4,72,640]{2,1,0:T(8,128)}), f32[4,72,640]{2,1,0:T(8,128)S(1)}, u32[]{:S(2)}, u32[]{:S(2)}) async-start(f32[4,72,640]{2,1,0:T(8,128)} %shard_map.83.refs_4_), calls=%async_computation.3 | async-start | bytes 1474560 | tf_op jit(solution)/shard_map/all_to_all | solution.py:387
  150.3 10.7 %copy-start.15 = (f32[64,640]{1,0:T(8,128)S(1)}, f32[64,640]{1,0:T(8,128)}, u32[]{:S(2)}) copy-start(f32[64,640]{1,0:T(8,128)} %get-tuple-element.18.refs_1_) | copy-start | bytes 491524
  163.8 13.7 %all-to-all-start.4 = ((f32[8,8,128]{2,1,0:T(8,128)}), f32[8,8,128]{2,1,0:T(8,128)S(1)}, u32[]{:S(2)}, u32[]{:S(2)}) async-start(f32[8,8,128]{2,1,0:T(8,128)} %get-tuple-element.19.refs_2_), calls=%async_computation.4 | async-start | bytes 65536 | tf_op jit(solution)/shard_map/all_to_all | solution.py:387
  (10 other events, 24.6 us)

commit v10 on v9

--- a/solution.py
+++ b/solution.py
@@ -139,20 +139,20 @@
 
 
 def prepare_pairs_body(args, lazy, results, scratch, need, send):
-    eta_ref, qkv_ref = args
-    results[0][0:TOK, :] = qkv_ref[1, 0]
-    results[0][TOK : 2 * TOK, :] = to_column(eta_ref[...]) * qkv_ref[2, 0]
-
-
-def prepare_queries_body(args, lazy, results, scratch, need, send):
-    (mom_ref,), (qkv_ref,), (queries_ref,) = args, lazy, results
+    (eta_ref, qkv_ref, mom_ref), (pairs_ref,) = args, results
+    pairs_ref[0:TOK, :] = qkv_ref[1, 0]
+    pairs_ref[TOK : 2 * TOK, :] = to_column(eta_ref[...]) * qkv_ref[2, 0]
     packs = own_packs(mom_ref, scratch[0])
     for x in range(NX):
-        queries_ref[2 * TOK + 8 * x : 2 * TOK + 8 * x + 8, 0:H] = packs[x]
-        queries_ref[2 * TOK + 8 * x : 2 * TOK + 8 * x + 8, H:D] = jnp.zeros((8, D - H), jnp.float32)
-    need()
-    queries_ref[0:TOK, :] = qkv_ref[0, 0]
-    queries_ref[TOK : 2 * TOK, :] = qkv_ref[0, 1]
+        pairs_ref[2 * TOK + 8 * x : 2 * TOK + 8 * x + 8, 0:H] = packs[x]
+        pairs_ref[2 * TOK + 8 * x : 2 * TOK + 8 * x + 8, H:D] = jnp.zeros((8, D - H), jnp.float32)
+
+
+def prepare_queries_body(args, lazy, results, scratch, need, send):
+    need()
+    (queries_ref,) = results
+    queries_ref[0:TOK, :] = lazy[0][0, 0]
+    queries_ref[TOK : 2 * TOK, :] = lazy[0][0, 1]
 
 
 def marker_body(args, lazy, results, scratch, need, send):
@@ -366,10 +366,6 @@
     return lax.ppermute(block, axes, [((i - distance) % BLOCKS, i) for i in range(BLOCKS)])
 
 
-def from_neighbours(block):
-    return [block] + [lax.ppermute(block, "x", [((i - s) % NX, i) for i in range(NX)]) for s in range(1, NX)]
-
-
 def relayed_from_neighbours(block):
     behind_one = lax.ppermute(block, "x", [((i - 1) % NX, i) for i in range(NX)])
     from_ahead = [((i + 1) % NX, i) for i in range(NX)]
@@ -401,24 +397,23 @@
     position = scalar((lax.axis_index("z") * NX + x) * NY + lax.axis_index("yh"))
     x = scalar(x)
     (send1,) = call(prepare_weights_body, [(BLOCKS, 24, LANES)], 1, own_weights, scratch=[(32, H)], room=SMALL)
-    (pairs,) = call(prepare_pairs_body, [(2 * TOK, D)], 1, eta, qkv, room=SMALL)
+    (pairs,) = call(
+        prepare_pairs_body, [(2 * TOK + 32, D)], 1, eta, qkv, own_moment, scratch=[(32, H)], room=SMALL
+    )
     recv1 = exchange(send1, ("z", "x", "yh")).reshape(BLOCKS * 24, LANES)
     pairs = relayed_from_neighbours(pairs)
     near, far = behind(qkv[1:], 1), behind(qkv[1:], 2)
     weights, send2 = call(
-        gradient_body, [(3 * D, LANES), (BLOCKS * 24, LANES)], 5, recv1, lazy=whole(*pairs),
+        gradient_body, [(3 * D, LANES), (BLOCKS * 24, LANES)], 5, recv1, lazy=[(p, (0, 2 * TOK)) for p in pairs],
         scratch=[(3 * D, LANES)], room=ROOM - 512 * 1024,
     )
     recv2 = exchange(send2.reshape(NZ * NY, NX * 24, LANES), ("z", "yh"))
-    (queries,) = call(
-        prepare_queries_body, [(2 * TOK + 32, D)], 0.1, own_moment, lazy=[(qkv, (0, 1))], scratch=[(32, H)],
-        after=(weights,),
-    )
-    queries = from_neighbours(queries)
+    (queries,) = call(prepare_queries_body, [(2 * TOK, D)], 0.1, lazy=[(qkv, (0, 1))], after=(weights,))
+    queries = relayed_from_neighbours(queries)
     (marker,) = call(marker_body, [(8, LANES)], 12, after=(near, far))
     (send3,) = call(
-        moment_body, [(NZ * NY, NX * 24, LANES)], 2, x, recv2, lazy=[(q, (2 * TOK, 32)) for q in queries],
-        smem=(0,), fan=(0,), after=(marker,), room=ROOM,
+        moment_body, [(NZ * NY, NX * 24, LANES)], 2, x, recv2, lazy=[(p, (2 * TOK, 32)) for p in pairs],
+        smem=(0,), fan=(0,), after=(marker, *queries[1:]), room=ROOM,
     )
     recv3 = exchange(send3, ("z", "yh")).reshape(BLOCKS * 24, LANES)
     first = back_to_neighbours(

time: 181 us -> 187 us (1.033)
  starting transfers between devices: 89.2 us -> 104 us
  waiting for transfers between devices: 48 us -> 39.1 us
    ppermute x3 -> x0, waiting for transfers between devices: 17.4 us -> none  [from_neighbours(): lax.ppermute(block, 'x', [((i - s) % NX, i) for i in range(NX)])]
    all_to_all x5, starting transfers between devices: 50.5 us -> 62.1 us  [exchange(): return lax.all_to_all(pieces, axes, split_axis=0, concat_axis=0, tiled=True)]
    ppermute x3 -> x0, starting transfers between devices: 10.5 us -> none  [from_neighbours(): lax.ppermute(block, 'x', [((i - s) % NX, i) for i in range(NX)])]
    ppermute x1 -> x2, waiting for transfers between devices: 0.01 us -> 7.18 us  [relayed_from_neighbours(): lax.ppermute(block, 'x', [((i - 1) % NX, i) for i in range(NX)])]
    ppermute x1 -> x2, waiting for transfers between devices: 9.86 us -> 16 us  [relayed_from_neighbours(): ahead_one = lax.ppermute(block, 'x', from_ahead)]
    ppermute x1 -> x2, starting transfers between devices: 4.45 us -> 10.6 us  [relayed_from_neighbours(): lax.ppermute(ahead_one, 'x', from_ahead)]
    ppermute x1 -> x2, starting transfers between devices: 4.13 us -> 9.56 us  [relayed_from_neighbours(): ahead_one = lax.ppermute(block, 'x', from_ahead)]
    ppermute x2, waiting for transfers between devices: 4.14 us -> 0.14 us  [behind(): lax.ppermute(block, axes, [((i - distance) % BLOCKS, i) for i in range(BL...]
  transfers between devices with their start and end apart: 16 -> 16, of which waited for: 7 -> 7; matrix products, arithmetic and copies ran while one was open for 1% -> 0% of each run, Pallas kernels for 14% -> 13%
where the time goes in v10:
time: 187 us; the launch traced here: 186 us
  starting transfers between devices  104 us (56%)
  waiting for transfers between devices  39.1 us (21%)
  Pallas kernels  36.3 us (19%)
  local copies, waits for them, and re-layouts  5.51 us (3%)
    all_to_all x5, starting transfers between devices, exchange(): return lax.all_to_all(pieces, axes, split_axis=0, concat_axis=0, tiled=True)  62.1 us
    pallas_call x12, Pallas kernels, call(): pl.pallas_call(kernel, out_shape=[jax.ShapeDtypeStruct(s, jnp.float32) fo...  36.3 us
    ppermute x2, waiting for transfers between devices, relayed_from_neighbours(): ahead_one = lax.ppermute(block, 'x', from_ahead)  16 us
    ppermute x2, starting transfers between devices, relayed_from_neighbours(): lax.ppermute(ahead_one, 'x', from_ahead)  10.6 us
    all_to_all x5, waiting for transfers between devices, exchange(): return lax.all_to_all(pieces, axes, split_axis=0, concat_axis=0, tiled=True)  10 us
    ppermute x2, starting transfers between devices, relayed_from_neighbours(): ahead_one = lax.ppermute(block, 'x', from_ahead)  9.56 us
    ppermute x2, starting transfers between devices, behind(): lax.ppermute(block, axes, [((i - distance) % BLOCKS, i) for i in range(BL...  8.89 us
    ppermute x3, starting transfers between devices, back_to_neighbours(): lax.ppermute(blocks[s], 'x', [(i, (i - s) % NX) for i in range(NX)])  8.87 us
  transfers between devices with their start and end apart: 16, of which 7 were waited for; matrix products, arithmetic and copies ran while one was open for 0% of the time, Pallas kernels for 13%

profile of v10, /device:TPU:1, one launch (start us, length us, event | category | flops | bytes accessed | tf_op | source)
XLA Modules:
  0.0 185.9 jit_solution(6631210144536794331)
XLA Ops:
  2.5 19.7 %all-to-all-start = ((f32[64,24,128]{2,1,0:T(8,128)}), f32[64,24,128]{2,1,0:T(8,128)S(1)}, u32[]{:S(2)}, u32[]{:S(2)}) async-start(f32[64,24,128]{2,1,0:T(8,128)} %shard_map.76), calls=%async_computation | async-start | bytes 1572864 | tf_op jit(solution)/shard_map/all_to_all | solution.py:383
  23.3 4.1 %collective-permute-start.1 = (f32[160,640]{1,0:T(8,128)S(1)}, f32[160,640]{1,0:T(8,128)S(1)}, u32[]{:S(2)}, u32[]{:S(2)}) collective-permute-start(f32[160,640]{1,0:T(8,128)S(1)} %shard_map.77.refs_1_.refs_2_), channel_id=1, source_target_pairs={{16,0},{32,16},{48,32},{0,48},{17,1},{33,17},{49,33},{1,49},{18,2}... | collective-permute-start | bytes 1228808 | tf_op jit(solution)/shard_map/ppermute | solution.py:372
  29.3 12.8 %collective-permute-done.1.refs_4_.refs_5_ = f32[160,640]{1,0:T(8,128)S(1)} collective-permute-done((f32[160,640]{1,0:T(8,128)S(1)}, f32[160,640]{1,0:T(8,128)S(1)}, u32[]{:S(2)}, u32[]{:S(2)}) %collective-permute-start.1) | collective-permute-done | bytes 409632 | tf_op jit(solution)/shard_map/ppermute | solution.py:372
  42.1 5.3 %collective-permute-start.2 = (f32[160,640]{1,0:T(8,128)S(1)}, f32[160,640]{1,0:T(8,128)S(1)}, u32[]{:S(2)}, u32[]{:S(2)}) collective-permute-start(f32[160,640]{1,0:T(8,128)S(1)} %collective-permute-done.1.refs_4_.refs_5_), channel_id=1, source_target_pairs={{16,0},{32,16},{48,32},{0,48},{17,1},{33,17},{49,33},{1,49},{18,2}... | collective-permute-start | bytes 1228808 | tf_op jit(solution)/shard_map/ppermute | solution.py:373
  48.3 7.0 %collective-permute-start.3 = (f32[2,2,64,640]{3,2,1,0:T(8,128)}, f32[2,2,64,640]{3,2,1,0:T(8,128)}, u32[]{:S(2)}, u32[]{:S(2)}) collective-permute-start(f32[2,2,64,640]{3,2,1,0:T(8,128)} %slice.4), channel_id=1, source_target_pairs={{504,0},{0,8},{8,16},{16,24},{24,32},{32,40},{40,48},{48,56},{56,6... | collective-permute-start | bytes 1966088 | tf_op jit(solution)/shard_map/ppermute | solution.py:366
  55.3 1.9 %collective-permute-start.4 = (f32[2,2,64,640]{3,2,1,0:T(8,128)}, f32[2,2,64,640]{3,2,1,0:T(8,128)}, u32[]{:S(2)}, u32[]{:S(2)}) collective-permute-start(f32[2,2,64,640]{3,2,1,0:T(8,128)} %slice.4), channel_id=1, source_target_pairs={{496,0},{504,8},{0,16},{8,24},{16,32},{24,40},{32,48},{40,56},{48,... | collective-permute-start | bytes 1966088 | tf_op jit(solution)/shard_map/ppermute | solution.py:366
  57.2 5.6 %shard_map.78 = (f32[1920,128]{1,0:T(8,128)}, f32[1536,128]{1,0:T(8,128)}) custom-call(f32[1536,128]{1,0:T(8,128)S(1)} %bitcast.10, f32[160,640]{1,0:T(8,128)S(1)} %shard_map.77.refs_1_.refs_2_, f32[160,640]{1,0:T(8,128)S(1)} %collective-permute-done.refs_2_.refs_3_, f32[160,640]{1,0:T(8,128)S(1)} %collective-permute-done.2.refs_3_.refs_4_, ...), custom_call_target="tpu_custom_call" | custom-call | flops 5000000000 | bytes 1000000 | tf_op jit(solution)/shard_map/pallas_call | solution.py:92
  62.8 8.1 %all-to-all-start.1 = ((f32[16,96,128]{2,1,0:T(8,128)}), f32[16,96,128]{2,1,0:T(8,128)}, u32[]{:S(2)}, u32[]{:S(2)}) async-start(f32[16,96,128]{2,1,0:T(8,128)} %bitcast.4), calls=%async_computation.1 | async-start | bytes 1572864 | tf_op jit(solution)/shard_map/all_to_all | solution.py:383
  72.6 5.4 %collective-permute-start.6 = (f32[128,640]{1,0:T(8,128)}, f32[128,640]{1,0:T(8,128)S(1)}, u32[]{:S(2)}, u32[]{:S(2)}) collective-permute-start(f32[128,640]{1,0:T(8,128)} %shard_map.80.refs_0_.refs_2_), channel_id=1, source_target_pairs={{16,0},{32,16},{48,32},{0,48},{17,1},{33,17},{49,33},{1,49},{18,2}... | collective-permute-start | bytes 983048 | tf_op jit(solution)/shard_map/ppermute | solution.py:372
  80.0 3.3 %collective-permute-done.6.refs_9_.refs_3_.refs_5_ = f32[128,640]{1,0:T(8,128)S(1)} collective-permute-done((f32[128,640]{1,0:T(8,128)}, f32[128,640]{1,0:T(8,128)S(1)}, u32[]{:S(2)}, u32[]{:S(2)}) %collective-permute-start.6) | collective-permute-done | bytes 327712 | tf_op jit(solution)/shard_map/ppermute | solution.py:372
  83.2 5.3 %collective-permute-start.7 = (f32[128,640]{1,0:T(8,128)S(1)}, f32[128,640]{1,0:T(8,128)S(1)}, u32[]{:S(2)}, u32[]{:S(2)}) collective-permute-start(f32[128,640]{1,0:T(8,128)S(1)} %collective-permute-done.6.refs_9_.refs_3_.refs_5_), channel_id=1, source_target_pairs={{16,0},{32,16},{48,32},{0,48},{17,1},{33,17},{49,33},{1,49},{18,2}... | collective-permute-start | bytes 983048 | tf_op jit(solution)/shard_map/ppermute | solution.py:373
  89.3 7.2 %collective-permute-done.5.refs_7_.refs_1_.refs_3_ = f32[128,640]{1,0:T(8,128)S(1)} collective-permute-done((f32[128,640]{1,0:T(8,128)}, f32[128,640]{1,0:T(8,128)S(1)}, u32[]{:S(2)}, u32[]{:S(2)}) %collective-permute-start.5) | collective-permute-done | bytes 327712 | tf_op jit(solution)/shard_map/ppermute | solution.py:370
  96.5 5.8 %all-to-all-done.1.refs_1_ = f32[16,96,128]{2,1,0:T(8,128)} async-done(((f32[16,96,128]{2,1,0:T(8,128)}), f32[16,96,128]{2,1,0:T(8,128)}, u32[]{:S(2)}, u32[]{:S(2)}) %all-to-all-start.1) | async-done | bytes 786464 | tf_op jit(solution)/shard_map/all_to_all | solution.py:383
  103.0 2.7 %shard_map.81.refs_5_.refs_7_ = f32[16,96,128]{2,1,0:T(8,128)} custom-call(s32[1]{0:T(128)} %bitcast.refs_0_, f32[16,96,128]{2,1,0:T(8,128)} %all-to-all-done.1.refs_1_, f32[160,640]{1,0:T(8,128)S(1)} %shard_map.77.refs_1_.refs_2_, f32[160,640]{1,0:T(8,128)S(1)} %collective-permute-done.refs_2_.refs_3_, ...), custom_call_target="tpu_custom_call" | custom-call | flops 2000000000 | bytes 1000000 | tf_op jit(solution)/shard_map/pallas_call | solution.py:92
  105.7 6.6 %all-to-all-start.2 = ((f32[16,96,128]{2,1,0:T(8,128)}), f32[16,96,128]{2,1,0:T(8,128)S(1)}, u32[]{:S(2)}, u32[]{:S(2)}) async-start(f32[16,96,128]{2,1,0:T(8,128)} %shard_map.81.refs_5_.refs_7_), calls=%async_computation.2 | async-start | bytes 1572864 | tf_op jit(solution)/shard_map/all_to_all | solution.py:383
  112.3 4.9 %shard_map.82 = (f32[64,640]{1,0:T(8,128)}, f32[64,640]{1,0:T(8,128)}, f32[64,640]{1,0:T(8,128)}, f32[64,640]{1,0:T(8,128)}) custom-call(f32[128,640]{1,0:T(8,128)} %shard_map.80.refs_0_.refs_2_, f32[128,640]{1,0:T(8,128)} %copy-done.4, f32[128,640]{1,0:T(8,128)} %copy-done.6, f32[128,640]{1,0:T(8,128)} %copy-done.2, ...), custom_call_target="tpu_custom_call" | custom-call | flops 4000000000 | bytes 1000000 | tf_op jit(solution)/shard_map/pallas_call | solution.py:92
  119.1 4.6 %collective-permute-start.8 = (f32[64,640]{1,0:T(8,128)}, f32[64,640]{1,0:T(8,128)S(1)}, u32[]{:S(2)}, u32[]{:S(2)}) collective-permute-start(f32[64,640]{1,0:T(8,128)} %get-tuple-element.15), channel_id=1, source_target_pairs={{0,48},{16,0},{32,16},{48,32},{1,49},{17,1},{33,17},{49,33},{2,50}... | collective-permute-start | bytes 491528 | tf_op jit(solution)/shard_map/ppermute | solution.py:378
  123.7 2.4 %collective-permute-start.9 = (f32[64,640]{1,0:T(8,128)}, f32[64,640]{1,0:T(8,128)S(1)}, u32[]{:S(2)}, u32[]{:S(2)}) collective-permute-start(f32[64,640]{1,0:T(8,128)} %get-tuple-element.16), channel_id=1, source_target_pairs={{0,32},{16,48},{32,0},{48,16},{1,33},{17,49},{33,1},{49,17},{2,34}... | collective-permute-start | bytes 491528 | tf_op jit(solution)/shard_map/ppermute | solution.py:378
  126.8 5.7 %collective-permute-done.9.refs_9_.refs_3_ = f32[64,640]{1,0:T(8,128)S(1)} collective-permute-done((f32[64,640]{1,0:T(8,128)}, f32[64,640]{1,0:T(8,128)S(1)}, u32[]{:S(2)}, u32[]{:S(2)}) %collective-permute-start.9) | collective-permute-done | bytes 163872 | tf_op jit(solution)/shard_map/ppermute | solution.py:378
  132.5 6.3 %shard_map.83.refs_4_ = f32[4,72,640]{2,1,0:T(8,128)} custom-call(s32[1]{0:T(128)} %bitcast.refs_0_, f32[1536,128]{1,0:T(8,128)S(1)} %bitcast.9, f32[128,640]{1,0:T(8,128)S(1)} %copy-done.1, f32[128,640]{1,0:T(8,128)S(1)} %copy-done.5, f32[128,640]{1,0:T(8,128)S(1)} %copy-done.7, f32[128,640]{1,0:T(8,128)S(1)} %copy-done.3, ...), custom_call_target="tpu_custom_call" | custom-call | flops 5000000000 | bytes 1000000 | tf_op jit(solution)/shard_map/pallas_call | solution.py:92
  138.8 3.5 %all-to-all-start.3 = ((f32[4,72,640]{2,1,0:T(8,128)}), f32[4,72,640]{2,1,0:T(8,128)S(1)}, u32[]{:S(2)}, u32[]{:S(2)}) async-start(f32[4,72,640]{2,1,0:T(8,128)} %shard_map.83.refs_4_), calls=%async_computation.3 | async-start | bytes 1474560 | tf_op jit(solution)/shard_map/all_to_all | solution.py:383
  142.3 9.7 %shard_map.84.refs_5_.refs_3_ = f32[2,64,640]{2,1,0:T(8,128)} custom-call(s32[1]{0:T(128)} %bitcast.6.refs_0_, f32[3,2,64,640]{3,2,1,0:T(8,128)} %refs_1_.3, f32[2,2,64,640]{3,2,1,0:T(8,128)} %collective-permute-done.3.refs_0_.refs_2_, f32[2,2,64,640]{3,2,1,0:T(8,128)} %collective-permute-done.4.refs_1_.refs_3_, f32[4,72,640]{2,1,0:T(8,128)} %shard_map.83.refs_4_), custom_call_target="tpu_custom_call" | custom-call | flops 8000000000 | bytes 1000000 | tf_op jit(solution)/shard_map/pallas_call | solution.py:92
  154.9 24.2 %all-to-all-start.4 = ((f32[8,8,128]{2,1,0:T(8,128)}), f32[8,8,128]{2,1,0:T(8,128)S(1)}, u32[]{:S(2)}, u32[]{:S(2)}) async-start(f32[8,8,128]{2,1,0:T(8,128)} %get-tuple-element.19.refs_2_), calls=%async_computation.4 | async-start | bytes 65536 | tf_op jit(solution)/shard_map/all_to_all | solution.py:383
  179.9 4.2 %all-to-all-done.4.refs_0_ = f32[8,8,128]{2,1,0:T(8,128)S(1)} async-done(((f32[8,8,128]{2,1,0:T(8,128)}), f32[8,8,128]{2,1,0:T(8,128)S(1)}, u32[]{:S(2)}, u32[]{:S(2)}) %all-to-all-start.4) | async-done | bytes 32800 | tf_op jit(solution)/shard_map/all_to_all | solution.py:383
  (58 shorter events, 18.7 us)
Async XLA Ops:
  2.5 19.8 %copy-start = (f32[3,2,64,640]{3,2,1,0:T(8,128)S(1)}, f32[3,2,64,640]{3,2,1,0:T(8,128)}, u32[]{:S(2)}) copy-start(f32[3,2,64,640]{3,2,1,0:T(8,128)} %refs_1_.3) | copy-start | bytes 2949124
  2.5 19.8 %copy-start.8 = (f32[1,10,3,384]{3,0,2,1:T(1,128)S(1)}, f32[1,10,3,384]{3,0,2,1:T(1,128)}, u32[]{:S(2)}) copy-start(f32[1,10,3,384]{3,0,2,1:T(1,128)} %param.8) | copy-start | bytes 138244
  2.5 54.7 %all-to-all-start = ((f32[64,24,128]{2,1,0:T(8,128)}), f32[64,24,128]{2,1,0:T(8,128)S(1)}, u32[]{:S(2)}, u32[]{:S(2)}) async-start(f32[64,24,128]{2,1,0:T(8,128)} %shard_map.76), calls=%async_computation | async-start | bytes 1572864 | tf_op jit(solution)/shard_map/all_to_all | solution.py:383
  23.3 18.9 %collective-permute-start.1 = (f32[160,640]{1,0:T(8,128)S(1)}, f32[160,640]{1,0:T(8,128)S(1)}, u32[]{:S(2)}, u32[]{:S(2)}) collective-permute-start(f32[160,640]{1,0:T(8,128)S(1)} %shard_map.77.refs_1_.refs_2_), channel_id=1, source_target_pairs={{16,0},{32,16},{48,32},{0,48},{17,1},{33,17},{49,33},{1,49},{18,2}... | collective-permute-start | bytes 1228808 | tf_op jit(solution)/shard_map/ppermute | solution.py:372
  27.4 29.8 %collective-permute-start = (f32[160,640]{1,0:T(8,128)S(1)}, f32[160,640]{1,0:T(8,128)S(1)}, u32[]{:S(2)}, u32[]{:S(2)}) collective-permute-start(f32[160,640]{1,0:T(8,128)S(1)} %shard_map.77.refs_1_.refs_2_), channel_id=1, source_target_pairs={{48,0},{0,16},{16,32},{32,48},{49,1},{1,17},{17,33},{33,49},{50,2}... | collective-permute-start | bytes 1228808 | tf_op jit(solution)/shard_map/ppermute | solution.py:370
  42.1 15.1 %collective-permute-start.2 = (f32[160,640]{1,0:T(8,128)S(1)}, f32[160,640]{1,0:T(8,128)S(1)}, u32[]{:S(2)}, u32[]{:S(2)}) collective-permute-start(f32[160,640]{1,0:T(8,128)S(1)} %collective-permute-done.1.refs_4_.refs_5_), channel_id=1, source_target_pairs={{16,0},{32,16},{48,32},{0,48},{17,1},{33,17},{49,33},{1,49},{18,2}... | collective-permute-start | bytes 1228808 | tf_op jit(solution)/shard_map/ppermute | solution.py:373
  48.3 40.4 %collective-permute-start.3 = (f32[2,2,64,640]{3,2,1,0:T(8,128)}, f32[2,2,64,640]{3,2,1,0:T(8,128)}, u32[]{:S(2)}, u32[]{:S(2)}) collective-permute-start(f32[2,2,64,640]{3,2,1,0:T(8,128)} %slice.4), channel_id=1, source_target_pairs={{504,0},{0,8},{8,16},{16,24},{24,32},{32,40},{40,48},{48,56},{56,6... | collective-permute-start | bytes 1966088 | tf_op jit(solution)/shard_map/ppermute | solution.py:366
  55.3 33.4 %collective-permute-start.4 = (f32[2,2,64,640]{3,2,1,0:T(8,128)}, f32[2,2,64,640]{3,2,1,0:T(8,128)}, u32[]{:S(2)}, u32[]{:S(2)}) collective-permute-start(f32[2,2,64,640]{3,2,1,0:T(8,128)} %slice.4), channel_id=1, source_target_pairs={{496,0},{504,8},{0,16},{8,24},{16,32},{24,40},{32,48},{40,56},{48,... | collective-permute-start | bytes 1966088 | tf_op jit(solution)/shard_map/ppermute | solution.py:366
  62.8 39.5 %all-to-all-start.1 = ((f32[16,96,128]{2,1,0:T(8,128)}), f32[16,96,128]{2,1,0:T(8,128)}, u32[]{:S(2)}, u32[]{:S(2)}) async-start(f32[16,96,128]{2,1,0:T(8,128)} %bitcast.4), calls=%async_computation.1 | async-start | bytes 1572864 | tf_op jit(solution)/shard_map/all_to_all | solution.py:383
  72.6 10.6 %collective-permute-start.6 = (f32[128,640]{1,0:T(8,128)}, f32[128,640]{1,0:T(8,128)S(1)}, u32[]{:S(2)}, u32[]{:S(2)}) collective-permute-start(f32[128,640]{1,0:T(8,128)} %shard_map.80.refs_0_.refs_2_), channel_id=1, source_target_pairs={{16,0},{32,16},{48,32},{0,48},{17,1},{33,17},{49,33},{1,49},{18,2}... | collective-permute-start | bytes 983048 | tf_op jit(solution)/shard_map/ppermute | solution.py:372
  78.0 18.5 %collective-permute-start.5 = (f32[128,640]{1,0:T(8,128)}, f32[128,640]{1,0:T(8,128)S(1)}, u32[]{:S(2)}, u32[]{:S(2)}) collective-permute-start(f32[128,640]{1,0:T(8,128)} %shard_map.80.refs_0_.refs_2_), channel_id=1, source_target_pairs={{48,0},{0,16},{16,32},{32,48},{49,1},{1,17},{17,33},{33,49},{50,2}... | collective-permute-start | bytes 983048 | tf_op jit(solution)/shard_map/ppermute | solution.py:370
  83.2 19.1 %copy-start.2 = (f32[128,640]{1,0:T(8,128)}, f32[128,640]{1,0:T(8,128)S(1)}, u32[]{:S(2)}) copy-start(f32[128,640]{1,0:T(8,128)S(1)} %collective-permute-done.6.refs_9_.refs_3_.refs_5_) | copy-start | bytes 983044
  83.2 13.3 %collective-permute-start.7 = (f32[128,640]{1,0:T(8,128)S(1)}, f32[128,640]{1,0:T(8,128)S(1)}, u32[]{:S(2)}, u32[]{:S(2)}) collective-permute-start(f32[128,640]{1,0:T(8,128)S(1)} %collective-permute-done.6.refs_9_.refs_3_.refs_5_), channel_id=1, source_target_pairs={{16,0},{32,16},{48,32},{0,48},{17,1},{33,17},{49,33},{1,49},{18,2}... | collective-permute-start | bytes 983048 | tf_op jit(solution)/shard_map/ppermute | solution.py:373
  105.7 26.8 %all-to-all-start.2 = ((f32[16,96,128]{2,1,0:T(8,128)}), f32[16,96,128]{2,1,0:T(8,128)S(1)}, u32[]{:S(2)}, u32[]{:S(2)}) async-start(f32[16,96,128]{2,1,0:T(8,128)} %shard_map.81.refs_5_.refs_7_), calls=%async_computation.2 | async-start | bytes 1572864 | tf_op jit(solution)/shard_map/all_to_all | solution.py:383
  112.3 20.2 %copy-start.1 = (f32[128,640]{1,0:T(8,128)S(1)}, f32[128,640]{1,0:T(8,128)}, u32[]{:S(2)}) copy-start(f32[128,640]{1,0:T(8,128)} %shard_map.80.refs_0_.refs_2_) | copy-start | bytes 983044
  112.3 20.2 %copy-start.3 = (f32[128,640]{1,0:T(8,128)S(1)}, f32[128,640]{1,0:T(8,128)}, u32[]{:S(2)}) copy-start(f32[128,640]{1,0:T(8,128)} %copy-done.2) | copy-start | bytes 983044
  112.3 20.2 %copy-start.5 = (f32[128,640]{1,0:T(8,128)S(1)}, f32[128,640]{1,0:T(8,128)}, u32[]{:S(2)}) copy-start(f32[128,640]{1,0:T(8,128)} %copy-done.4) | copy-start | bytes 983044
  112.3 20.2 %copy-start.7 = (f32[128,640]{1,0:T(8,128)S(1)}, f32[128,640]{1,0:T(8,128)}, u32[]{:S(2)}) copy-start(f32[128,640]{1,0:T(8,128)} %copy-done.6) | copy-start | bytes 983044
  117.2 9.6 %collective-permute-start.10 = (f32[64,640]{1,0:T(8,128)}, f32[64,640]{1,0:T(8,128)S(1)}, u32[]{:S(2)}, u32[]{:S(2)}) collective-permute-start(f32[64,640]{1,0:T(8,128)} %get-tuple-element.17), channel_id=1, source_target_pairs={{0,16},{16,32},{32,48},{48,0},{1,17},{17,33},{33,49},{49,1},{2,18}... | collective-permute-start | bytes 491528 | tf_op jit(solution)/shard_map/ppermute | solution.py:378
  119.1 7.7 %collective-permute-start.8 = (f32[64,640]{1,0:T(8,128)}, f32[64,640]{1,0:T(8,128)S(1)}, u32[]{:S(2)}, u32[]{:S(2)}) collective-permute-start(f32[64,640]{1,0:T(8,128)} %get-tuple-element.15), channel_id=1, source_target_pairs={{0,48},{16,0},{32,16},{48,32},{1,49},{17,1},{33,17},{49,33},{2,50}... | collective-permute-start | bytes 491528 | tf_op jit(solution)/shard_map/ppermute | solution.py:378
  123.7 8.8 %collective-permute-start.9 = (f32[64,640]{1,0:T(8,128)}, f32[64,640]{1,0:T(8,128)S(1)}, u32[]{:S(2)}, u32[]{:S(2)}) collective-permute-start(f32[64,640]{1,0:T(8,128)} %get-tuple-element.16), channel_id=1, source_target_pairs={{0,32},{16,48},{32,0},{48,16},{1,33},{17,49},{33,1},{49,17},{2,34}... | collective-permute-start | bytes 491528 | tf_op jit(solution)/shard_map/ppermute | solution.py:378
  138.8 13.3 %all-to-all-start.3 = ((f32[4,72,640]{2,1,0:T(8,128)}), f32[4,72,640]{2,1,0:T(8,128)S(1)}, u32[]{:S(2)}, u32[]{:S(2)}) async-start(f32[4,72,640]{2,1,0:T(8,128)} %shard_map.83.refs_4_), calls=%async_computation.3 | async-start | bytes 1474560 | tf_op jit(solution)/shard_map/all_to_all | solution.py:383
  154.9 24.2 %copy-start.10 = (f32[1,10,3,384]{3,0,2,1:T(1,128)S(1)}, f32[1,10,3,384]{3,0,2,1:T(1,128)}, u32[]{:S(2)}) copy-start(f32[1,10,3,384]{3,0,2,1:T(1,128)} %param.7) | copy-start | bytes 138244
  154.9 29.1 %all-to-all-start.4 = ((f32[8,8,128]{2,1,0:T(8,128)}), f32[8,8,128]{2,1,0:T(8,128)S(1)}, u32[]{:S(2)}, u32[]{:S(2)}) async-start(f32[8,8,128]{2,1,0:T(8,128)} %get-tuple-element.19.refs_2_), calls=%async_computation.4 | async-start | bytes 65536 | tf_op jit(solution)/shard_map/all_to_all | solution.py:383
  (10 other events, 37.7 us)

commit v11 on v9

--- a/solution.py
+++ b/solution.py
@@ -35,6 +35,20 @@
     return lax.dot_general(
         left, right, (dims, ((), ())), precision=PRECISION, preferred_element_type=jnp.float32
     )
+
+
+def halves(x):
+    high = x.astype(jnp.bfloat16)
+    return high, (x - high.astype(jnp.float32)).astype(jnp.bfloat16)
+
+
+def split_dot(left, right, dims=((1,), (0,))):
+    def one(a, b):
+        return lax.dot_general(a, b, (dims, ((), ())), preferred_element_type=jnp.float32)
+
+    left_high, left_low = halves(left)
+    right_high, right_low = halves(right)
+    return one(left_high, right_high) + (one(left_high, right_low) + one(left_low, right_high))
 
 
 def entry(group, sublane):
@@ -214,18 +228,18 @@
     need()
     keys = token_rows(pairs, 0)
     weighted = token_rows(pairs, TOK)
-    pre = dot(keys, jnp.concatenate([matrix(w_ref, 0), matrix(w_ref, 1)], axis=1))
+    pre = split_dot(keys, jnp.concatenate([matrix(w_ref, 0), matrix(w_ref, 1)], axis=1))
     gate_pre, up_pre = pre[:, :LANES], pre[:, LANES:]
-    back = -dot(weighted, matrix(w_ref, 2))
+    back = -split_dot(weighted, matrix(w_ref, 2))
     sigmoid = jax.nn.sigmoid(gate_pre)
     gated = gate_pre * sigmoid
     hidden = gated * up_pre
     gate_back = back * up_pre * sigmoid * (1.0 + gate_pre * (1.0 - sigmoid))
     up_back = back * gated
-    both = dot(keys, jnp.concatenate([gate_back, up_back], axis=1), ((0,), (0,)))
+    both = split_dot(keys, jnp.concatenate([gate_back, up_back], axis=1), ((0,), (0,)))
     g_ref[0:D, :] = both[:, :LANES]
     g_ref[D : 2 * D, :] = both[:, LANES:]
-    g_ref[2 * D : 3 * D, :] = -dot(weighted, hidden, ((0,), (0,)))
+    g_ref[2 * D : 3 * D, :] = -split_dot(weighted, hidden, ((0,), (0,)))
     pack(g_ref, send_ref, 24, 96, 192)
 
 
@@ -249,7 +263,7 @@
 
 
 def hidden_of(inputs, w1, w3):
-    pre = dot(inputs, jnp.concatenate([w1, w3], axis=1))
+    pre = split_dot(inputs, jnp.concatenate([w1, w3], axis=1))
     gate_pre, up_pre = pre[:, :LANES], pre[:, LANES:]
     return gate_pre * jax.nn.sigmoid(gate_pre) * up_pre
 
@@ -258,7 +272,7 @@
     need()
     *queries, w_ref = lazy
     hidden = hidden_of(token_rows(queries, 0), matrix(w_ref, 0), matrix(w_ref, 1))
-    partial = dot(hidden, matrix(w_ref, 2), ((1,), (1,)))
+    partial = split_dot(hidden, matrix(w_ref, 2), ((1,), (1,)))
     for s in range(NX):
         results[s][...] = partial[s * TOK : (s + 1) * TOK]
 
@@ -280,7 +294,7 @@
     new3, rate3, ratio3 = renormalized(matrix(w_ref, 1), matrix(m_ref, 1))
     new2, rate2, ratio2 = renormalized(matrix(w_ref, 2), matrix(m_ref, 2))
     hidden = hidden_of(token_rows(queries, 0), new1, new3)
-    partial = dot(hidden, new2, ((1,), (1,)))
+    partial = split_dot(hidden, new2, ((1,), (1,)))
     stats = [rate1, rate3, rate2, ratio1, ratio3, ratio2, jnp.zeros((2, LANES), jnp.float32)]
     stats = jnp.concatenate(stats, axis=0)
     for x in range(NX):

time: 181 us -> 180 us (level)
  Pallas kernels: 35.9 us -> 32.6 us
  waiting for transfers between devices: 48 us -> 50.4 us
    pallas_call x12, Pallas kernels: 35.9 us -> 32.6 us  [call(): pl.pallas_call(kernel, out_shape=[jax.ShapeDtypeStruct(s, jnp.float32) fo...]
  transfers between devices with their start and end apart: 16 -> 16, of which waited for: 7 -> 8; matrix products, arithmetic and copies ran while one was open for 1% -> 1% of each run, Pallas kernels for 14% -> 12%
where the time goes in v11:
time: 180 us; the launch traced here: 178 us
  starting transfers between devices  89.1 us (50%)
  waiting for transfers between devices  50.4 us (28%)
  Pallas kernels  32.6 us (18%)
  local copies, waits for them, and re-layouts  4.92 us (3%)
    all_to_all x5, starting transfers between devices, exchange(): return lax.all_to_all(pieces, axes, split_axis=0, concat_axis=0, tiled=True)  50.6 us
    pallas_call x12, Pallas kernels, call(): pl.pallas_call(kernel, out_shape=[jax.ShapeDtypeStruct(s, jnp.float32) fo...  32.6 us
    ppermute x3, waiting for transfers between devices, from_neighbours(): lax.ppermute(block, 'x', [((i - s) % NX, i) for i in range(NX)])  17.4 us
    all_to_all x5, waiting for transfers between devices, exchange(): return lax.all_to_all(pieces, axes, split_axis=0, concat_axis=0, tiled=True)  12.2 us
    ppermute x3, starting transfers between devices, from_neighbours(): lax.ppermute(block, 'x', [((i - s) % NX, i) for i in range(NX)])  10.5 us
    ppermute x1, waiting for transfers between devices, relayed_from_neighbours(): ahead_one = lax.ppermute(block, 'x', from_ahead)  9.86 us
    ppermute x2, starting transfers between devices, behind(): lax.ppermute(block, axes, [((i - distance) % BLOCKS, i) for i in range(BL...  9.19 us
    ppermute x3, starting transfers between devices, back_to_neighbours(): lax.ppermute(blocks[s], 'x', [(i, (i - s) % NX) for i in range(NX)])  8.41 us
  transfers between devices with their start and end apart: 16, of which 8 were waited for; matrix products, arithmetic and copies ran while one was open for 1% of the time, Pallas kernels for 12%

profile of v11, /device:TPU:1, one launch (start us, length us, event | category | flops | bytes accessed | tf_op | source)
XLA Modules:
  0.0 178.3 jit_solution(15148837803364023866)
XLA Ops:
  2.5 19.7 %all-to-all-start = ((f32[64,24,128]{2,1,0:T(8,128)}), f32[64,24,128]{2,1,0:T(8,128)S(1)}, u32[]{:S(2)}, u32[]{:S(2)}) async-start(f32[64,24,128]{2,1,0:T(8,128)} %shard_map.76), calls=%async_computation | async-start | bytes 1572864 | tf_op jit(solution)/shard_map/all_to_all | solution.py:401
  22.5 4.1 %collective-permute-start.1 = (f32[128,640]{1,0:T(8,128)S(1)}, f32[128,640]{1,0:T(8,128)S(1)}, u32[]{:S(2)}, u32[]{:S(2)}) collective-permute-start(f32[128,640]{1,0:T(8,128)S(1)} %shard_map.77.refs_1_), channel_id=1, source_target_pairs={{16,0},{32,16},{48,32},{0,48},{17,1},{33,17},{49,33},{1,49},{18,2}... | collective-permute-start | bytes 983048 | tf_op jit(solution)/shard_map/ppermute | solution.py:390
  26.6 1.9 %collective-permute-start = (f32[128,640]{1,0:T(8,128)S(1)}, f32[128,640]{1,0:T(8,128)S(1)}, u32[]{:S(2)}, u32[]{:S(2)}) collective-permute-start(f32[128,640]{1,0:T(8,128)S(1)} %shard_map.77.refs_1_), channel_id=1, source_target_pairs={{48,0},{0,16},{16,32},{32,48},{49,1},{1,17},{17,33},{33,49},{50,2}... | collective-permute-start | bytes 983048 | tf_op jit(solution)/shard_map/ppermute | solution.py:388
  28.6 9.9 %collective-permute-done.1.refs_4_ = f32[128,640]{1,0:T(8,128)S(1)} collective-permute-done((f32[128,640]{1,0:T(8,128)S(1)}, f32[128,640]{1,0:T(8,128)S(1)}, u32[]{:S(2)}, u32[]{:S(2)}) %collective-permute-start.1) | collective-permute-done | bytes 327712 | tf_op jit(solution)/shard_map/ppermute | solution.py:390
  38.4 4.5 %collective-permute-start.2 = (f32[128,640]{1,0:T(8,128)S(1)}, f32[128,640]{1,0:T(8,128)S(1)}, u32[]{:S(2)}, u32[]{:S(2)}) collective-permute-start(f32[128,640]{1,0:T(8,128)S(1)} %collective-permute-done.1.refs_4_), channel_id=1, source_target_pairs={{16,0},{32,16},{48,32},{0,48},{17,1},{33,17},{49,33},{1,49},{18,2}... | collective-permute-start | bytes 983048 | tf_op jit(solution)/shard_map/ppermute | solution.py:391
  43.8 7.3 %collective-permute-start.6 = (f32[2,2,64,640]{3,2,1,0:T(8,128)}, f32[2,2,64,640]{3,2,1,0:T(8,128)}, u32[]{:S(2)}, u32[]{:S(2)}) collective-permute-start(f32[2,2,64,640]{3,2,1,0:T(8,128)} %slice.4), channel_id=1, source_target_pairs={{504,0},{0,8},{8,16},{16,24},{24,32},{32,40},{40,48},{48,56},{56,6... | collective-permute-start | bytes 1966088 | tf_op jit(solution)/shard_map/ppermute | solution.py:380
  51.1 1.9 %collective-permute-start.7 = (f32[2,2,64,640]{3,2,1,0:T(8,128)}, f32[2,2,64,640]{3,2,1,0:T(8,128)}, u32[]{:S(2)}, u32[]{:S(2)}) collective-permute-start(f32[2,2,64,640]{3,2,1,0:T(8,128)} %slice.4), channel_id=1, source_target_pairs={{496,0},{504,8},{0,16},{8,24},{16,32},{24,40},{32,48},{40,56},{48,... | collective-permute-start | bytes 1966088 | tf_op jit(solution)/shard_map/ppermute | solution.py:380
  53.0 4.3 %shard_map.78 = (f32[1920,128]{1,0:T(8,128)}, f32[1536,128]{1,0:T(8,128)}) custom-call(f32[1536,128]{1,0:T(8,128)S(1)} %bitcast.10, f32[128,640]{1,0:T(8,128)S(1)} %shard_map.77.refs_1_, f32[128,640]{1,0:T(8,128)S(1)} %collective-permute-done.refs_2_, f32[128,640]{1,0:T(8,128)S(1)} %collective-permute-done.2.refs_3_, ...), custom_call_target="tpu_custom_call" | custom-call | flops 5000000000 | bytes 1000000 | tf_op jit(solution)/shard_map/pallas_call | solution.py:106
  57.3 8.3 %all-to-all-start.1 = ((f32[16,96,128]{2,1,0:T(8,128)}), f32[16,96,128]{2,1,0:T(8,128)S(1)}, u32[]{:S(2)}, u32[]{:S(2)}) async-start(f32[16,96,128]{2,1,0:T(8,128)} %bitcast.3), calls=%async_computation.1 | async-start | bytes 1572864 | tf_op jit(solution)/shard_map/all_to_all | solution.py:401
  65.7 2.6 %shard_map.79.refs_2_.refs_0_ = f32[160,640]{1,0:T(8,128)} custom-call(f32[30,1,384]{2,1,0:T(1,128)} %bitcast.14, f32[3,2,64,640]{3,2,1,0:T(8,128)} %refs_1_.5, f32[1920,128]{1,0:T(8,128)} %get-tuple-element.14.refs_2_.refs_4_.refs_6_), custom_call_target="tpu_custom_call" | custom-call | flops 100000000 | bytes 1000000 | tf_op jit(solution)/shard_map/pallas_call | solution.py:106
  68.3 2.1 %collective-permute-start.3 = (f32[160,640]{1,0:T(8,128)}, f32[160,640]{1,0:T(8,128)S(1)}, u32[]{:S(2)}, u32[]{:S(2)}) collective-permute-start(f32[160,640]{1,0:T(8,128)} %shard_map.79.refs_2_.refs_0_), channel_id=1, source_target_pairs={{48,0},{0,16},{16,32},{32,48},{49,1},{1,17},{17,33},{33,49},{50,2}... | collective-permute-start | bytes 1228808 | tf_op jit(solution)/shard_map/ppermute | solution.py:384
  70.3 6.5 %collective-permute-start.4 = (f32[160,640]{1,0:T(8,128)}, f32[160,640]{1,0:T(8,128)S(1)}, u32[]{:S(2)}, u32[]{:S(2)}) collective-permute-start(f32[160,640]{1,0:T(8,128)} %shard_map.79.refs_2_.refs_0_), channel_id=1, source_target_pairs={{32,0},{48,16},{0,32},{16,48},{33,1},{49,17},{1,33},{17,49},{34,2}... | collective-permute-start | bytes 1228808 | tf_op jit(solution)/shard_map/ppermute | solution.py:384
  78.8 5.5 %collective-permute-done.6.refs_0_.refs_2_ = f32[2,2,64,640]{3,2,1,0:T(8,128)} collective-permute-done((f32[2,2,64,640]{3,2,1,0:T(8,128)}, f32[2,2,64,640]{3,2,1,0:T(8,128)}, u32[]{:S(2)}, u32[]{:S(2)}) %collective-permute-start.6) | collective-permute-done | bytes 655392 | tf_op jit(solution)/shard_map/ppermute | solution.py:380
  84.9 17.4 %collective-permute-done.3.refs_3_.refs_1_ = f32[160,640]{1,0:T(8,128)S(1)} collective-permute-done((f32[160,640]{1,0:T(8,128)}, f32[160,640]{1,0:T(8,128)S(1)}, u32[]{:S(2)}, u32[]{:S(2)}) %collective-permute-start.3) | collective-permute-done | bytes 409632 | tf_op jit(solution)/shard_map/ppermute | solution.py:384
  104.6 10.1 %all-to-all-start.2 = ((f32[16,96,128]{2,1,0:T(8,128)}), f32[16,96,128]{2,1,0:T(8,128)S(1)}, u32[]{:S(2)}, u32[]{:S(2)}) async-start(f32[16,96,128]{2,1,0:T(8,128)} %shard_map.81.refs_5_.refs_7_), calls=%async_computation.2 | async-start | bytes 1572864 | tf_op jit(solution)/shard_map/all_to_all | solution.py:401
  114.8 3.8 %shard_map.82 = (f32[64,640]{1,0:T(8,128)}, f32[64,640]{1,0:T(8,128)}, f32[64,640]{1,0:T(8,128)}, f32[64,640]{1,0:T(8,128)}) custom-call(f32[160,640]{1,0:T(8,128)} %shard_map.79.refs_2_.refs_0_, f32[160,640]{1,0:T(8,128)} %copy-done.3, f32[160,640]{1,0:T(8,128)} %copy-done.5, f32[160,640]{1,0:T(8,128)} %copy-done.7, ...), custom_call_target="tpu_custom_call" | custom-call | flops 4000000000 | bytes 1000000 | tf_op jit(solution)/shard_map/pallas_call | solution.py:106
  120.5 4.6 %collective-permute-start.8 = (f32[64,640]{1,0:T(8,128)}, f32[64,640]{1,0:T(8,128)S(1)}, u32[]{:S(2)}, u32[]{:S(2)}) collective-permute-start(f32[64,640]{1,0:T(8,128)} %get-tuple-element.15), channel_id=1, source_target_pairs={{0,48},{16,0},{32,16},{48,32},{1,49},{17,1},{33,17},{49,33},{2,50}... | collective-permute-start | bytes 491528 | tf_op jit(solution)/shard_map/ppermute | solution.py:396
  127.9 5.3 %collective-permute-done.9.refs_9_.refs_3_ = f32[64,640]{1,0:T(8,128)S(1)} collective-permute-done((f32[64,640]{1,0:T(8,128)}, f32[64,640]{1,0:T(8,128)S(1)}, u32[]{:S(2)}, u32[]{:S(2)}) %collective-permute-start.9) | collective-permute-done | bytes 163872 | tf_op jit(solution)/shard_map/ppermute | solution.py:396
  133.2 7.3 %all-to-all-done.2 = f32[16,96,128]{2,1,0:T(8,128)S(1)} async-done(((f32[16,96,128]{2,1,0:T(8,128)}), f32[16,96,128]{2,1,0:T(8,128)S(1)}, u32[]{:S(2)}, u32[]{:S(2)}) %all-to-all-start.2) | async-done | bytes 786464 | tf_op jit(solution)/shard_map/all_to_all | solution.py:401
  140.5 5.3 %shard_map.83.refs_4_ = f32[4,72,640]{2,1,0:T(8,128)} custom-call(s32[1]{0:T(128)} %bitcast.refs_0_, f32[1536,128]{1,0:T(8,128)S(1)} %bitcast.9, f32[160,640]{1,0:T(8,128)S(1)} %copy-done.2, f32[160,640]{1,0:T(8,128)S(1)} %copy-done.4, f32[160,640]{1,0:T(8,128)S(1)} %copy-done.6, f32[160,640]{1,0:T(8,128)S(1)} %copy-done.8, ...), custom_call_target="tpu_custom_call" | custom-call | flops 5000000000 | bytes 1000000 | tf_op jit(solution)/shard_map/pallas_call | solution.py:106
  145.8 3.7 %all-to-all-start.3 = ((f32[4,72,640]{2,1,0:T(8,128)}), f32[4,72,640]{2,1,0:T(8,128)S(1)}, u32[]{:S(2)}, u32[]{:S(2)}) async-start(f32[4,72,640]{2,1,0:T(8,128)} %shard_map.83.refs_4_), calls=%async_computation.3 | async-start | bytes 1474560 | tf_op jit(solution)/shard_map/all_to_all | solution.py:401
  149.5 9.7 %shard_map.84.refs_5_.refs_3_ = f32[2,64,640]{2,1,0:T(8,128)} custom-call(s32[1]{0:T(128)} %bitcast.6.refs_0_, f32[3,2,64,640]{3,2,1,0:T(8,128)} %refs_1_.5, f32[2,2,64,640]{3,2,1,0:T(8,128)} %collective-permute-done.6.refs_0_.refs_2_, f32[2,2,64,640]{3,2,1,0:T(8,128)} %collective-permute-done.7.refs_1_.refs_3_, f32[4,72,640]{2,1,0:T(8,128)} %shard_map.83.refs_4_), custom_call_target="tpu_custom_call" | custom-call | flops 8000000000 | bytes 1000000 | tf_op jit(solution)/shard_map/pallas_call | solution.py:106
  162.8 8.7 %all-to-all-start.4 = ((f32[8,8,128]{2,1,0:T(8,128)}), f32[8,8,128]{2,1,0:T(8,128)S(1)}, u32[]{:S(2)}, u32[]{:S(2)}) async-start(f32[8,8,128]{2,1,0:T(8,128)} %get-tuple-element.19.refs_2_), calls=%async_computation.4 | async-start | bytes 65536 | tf_op jit(solution)/shard_map/all_to_all | solution.py:401
  172.3 4.2 %all-to-all-done.4.refs_0_ = f32[8,8,128]{2,1,0:T(8,128)S(1)} async-done(((f32[8,8,128]{2,1,0:T(8,128)}), f32[8,8,128]{2,1,0:T(8,128)S(1)}, u32[]{:S(2)}, u32[]{:S(2)}) %all-to-all-start.4) | async-done | bytes 32800 | tf_op jit(solution)/shard_map/all_to_all | solution.py:401
  (58 shorter events, 18.4 us)
Async XLA Ops:
  2.5 19.8 %copy-start = (f32[3,2,64,640]{3,2,1,0:T(8,128)S(1)}, f32[3,2,64,640]{3,2,1,0:T(8,128)}, u32[]{:S(2)}) copy-start(f32[3,2,64,640]{3,2,1,0:T(8,128)} %refs_1_.5) | copy-start | bytes 2949124
  2.5 19.8 %copy-start.11 = (f32[1,64]{1,0:T(1,128)S(1)}, f32[1,64]{1,0:T(1,128)}, u32[]{:S(2)}) copy-start(f32[1,64]{1,0:T(1,128)} %refs_0_.1) | copy-start | bytes 772
  2.5 50.5 %all-to-all-start = ((f32[64,24,128]{2,1,0:T(8,128)}), f32[64,24,128]{2,1,0:T(8,128)S(1)}, u32[]{:S(2)}, u32[]{:S(2)}) async-start(f32[64,24,128]{2,1,0:T(8,128)} %shard_map.76), calls=%async_computation | async-start | bytes 1572864 | tf_op jit(solution)/shard_map/all_to_all | solution.py:401
  22.5 15.9 %collective-permute-start.1 = (f32[128,640]{1,0:T(8,128)S(1)}, f32[128,640]{1,0:T(8,128)S(1)}, u32[]{:S(2)}, u32[]{:S(2)}) collective-permute-start(f32[128,640]{1,0:T(8,128)S(1)} %shard_map.77.refs_1_), channel_id=1, source_target_pairs={{16,0},{32,16},{48,32},{0,48},{17,1},{33,17},{49,33},{1,49},{18,2}... | collective-permute-start | bytes 983048 | tf_op jit(solution)/shard_map/ppermute | solution.py:390
  26.6 26.4 %collective-permute-start = (f32[128,640]{1,0:T(8,128)S(1)}, f32[128,640]{1,0:T(8,128)S(1)}, u32[]{:S(2)}, u32[]{:S(2)}) collective-permute-start(f32[128,640]{1,0:T(8,128)S(1)} %shard_map.77.refs_1_), channel_id=1, source_target_pairs={{48,0},{0,16},{16,32},{32,48},{49,1},{1,17},{17,33},{33,49},{50,2}... | collective-permute-start | bytes 983048 | tf_op jit(solution)/shard_map/ppermute | solution.py:388
  38.4 14.6 %collective-permute-start.2 = (f32[128,640]{1,0:T(8,128)S(1)}, f32[128,640]{1,0:T(8,128)S(1)}, u32[]{:S(2)}, u32[]{:S(2)}) collective-permute-start(f32[128,640]{1,0:T(8,128)S(1)} %collective-permute-done.1.refs_4_), channel_id=1, source_target_pairs={{16,0},{32,16},{48,32},{0,48},{17,1},{33,17},{49,33},{1,49},{18,2}... | collective-permute-start | bytes 983048 | tf_op jit(solution)/shard_map/ppermute | solution.py:391
  43.8 40.5 %collective-permute-start.6 = (f32[2,2,64,640]{3,2,1,0:T(8,128)}, f32[2,2,64,640]{3,2,1,0:T(8,128)}, u32[]{:S(2)}, u32[]{:S(2)}) collective-permute-start(f32[2,2,64,640]{3,2,1,0:T(8,128)} %slice.4), channel_id=1, source_target_pairs={{504,0},{0,8},{8,16},{16,24},{24,32},{32,40},{40,48},{48,56},{56,6... | collective-permute-start | bytes 1966088 | tf_op jit(solution)/shard_map/ppermute | solution.py:380
  51.1 33.2 %collective-permute-start.7 = (f32[2,2,64,640]{3,2,1,0:T(8,128)}, f32[2,2,64,640]{3,2,1,0:T(8,128)}, u32[]{:S(2)}, u32[]{:S(2)}) collective-permute-start(f32[2,2,64,640]{3,2,1,0:T(8,128)} %slice.4), channel_id=1, source_target_pairs={{496,0},{504,8},{0,16},{8,24},{16,32},{24,40},{32,48},{40,56},{48,... | collective-permute-start | bytes 1966088 | tf_op jit(solution)/shard_map/ppermute | solution.py:380
  57.3 45.0 %all-to-all-start.1 = ((f32[16,96,128]{2,1,0:T(8,128)}), f32[16,96,128]{2,1,0:T(8,128)S(1)}, u32[]{:S(2)}, u32[]{:S(2)}) async-start(f32[16,96,128]{2,1,0:T(8,128)} %bitcast.3), calls=%async_computation.1 | async-start | bytes 1572864 | tf_op jit(solution)/shard_map/all_to_all | solution.py:401
  68.3 34.1 %copy-start.1 = (f32[160,640]{1,0:T(8,128)S(1)}, f32[160,640]{1,0:T(8,128)}, u32[]{:S(2)}) copy-start(f32[160,640]{1,0:T(8,128)} %shard_map.79.refs_2_.refs_0_) | copy-start | bytes 1228804
  68.3 34.0 %collective-permute-start.3 = (f32[160,640]{1,0:T(8,128)}, f32[160,640]{1,0:T(8,128)S(1)}, u32[]{:S(2)}, u32[]{:S(2)}) collective-permute-start(f32[160,640]{1,0:T(8,128)} %shard_map.79.refs_2_.refs_0_), channel_id=1, source_target_pairs={{48,0},{0,16},{16,32},{32,48},{49,1},{1,17},{17,33},{33,49},{50,2}... | collective-permute-start | bytes 1228808 | tf_op jit(solution)/shard_map/ppermute | solution.py:384
  70.3 32.0 %collective-permute-start.4 = (f32[160,640]{1,0:T(8,128)}, f32[160,640]{1,0:T(8,128)S(1)}, u32[]{:S(2)}, u32[]{:S(2)}) collective-permute-start(f32[160,640]{1,0:T(8,128)} %shard_map.79.refs_2_.refs_0_), channel_id=1, source_target_pairs={{32,0},{48,16},{0,32},{16,48},{33,1},{49,17},{1,33},{17,49},{34,2}... | collective-permute-start | bytes 1228808 | tf_op jit(solution)/shard_map/ppermute | solution.py:384
  76.8 25.5 %collective-permute-start.5 = (f32[160,640]{1,0:T(8,128)}, f32[160,640]{1,0:T(8,128)S(1)}, u32[]{:S(2)}, u32[]{:S(2)}) collective-permute-start(f32[160,640]{1,0:T(8,128)} %shard_map.79.refs_2_.refs_0_), channel_id=1, source_target_pairs={{16,0},{32,16},{48,32},{0,48},{17,1},{33,17},{49,33},{1,49},{18,2}... | collective-permute-start | bytes 1228808 | tf_op jit(solution)/shard_map/ppermute | solution.py:384
  104.6 35.9 %all-to-all-start.2 = ((f32[16,96,128]{2,1,0:T(8,128)}), f32[16,96,128]{2,1,0:T(8,128)S(1)}, u32[]{:S(2)}, u32[]{:S(2)}) async-start(f32[16,96,128]{2,1,0:T(8,128)} %shard_map.81.refs_5_.refs_7_), calls=%async_computation.2 | async-start | bytes 1572864 | tf_op jit(solution)/shard_map/all_to_all | solution.py:401
  114.7 25.7 %copy-start.2 = (f32[160,640]{1,0:T(8,128)S(1)}, f32[160,640]{1,0:T(8,128)}, u32[]{:S(2)}) copy-start(f32[160,640]{1,0:T(8,128)} %shard_map.79.refs_2_.refs_0_) | copy-start | bytes 1228804
  114.7 25.7 %copy-start.4 = (f32[160,640]{1,0:T(8,128)S(1)}, f32[160,640]{1,0:T(8,128)}, u32[]{:S(2)}) copy-start(f32[160,640]{1,0:T(8,128)} %copy-done.3) | copy-start | bytes 1228804
  114.7 25.7 %copy-start.6 = (f32[160,640]{1,0:T(8,128)S(1)}, f32[160,640]{1,0:T(8,128)}, u32[]{:S(2)}) copy-start(f32[160,640]{1,0:T(8,128)} %copy-done.5) | copy-start | bytes 1228804
  114.8 25.7 %copy-start.8 = (f32[160,640]{1,0:T(8,128)S(1)}, f32[160,640]{1,0:T(8,128)}, u32[]{:S(2)}) copy-start(f32[160,640]{1,0:T(8,128)} %copy-done.7) | copy-start | bytes 1228804
  118.6 9.1 %collective-permute-start.10 = (f32[64,640]{1,0:T(8,128)}, f32[64,640]{1,0:T(8,128)S(1)}, u32[]{:S(2)}, u32[]{:S(2)}) collective-permute-start(f32[64,640]{1,0:T(8,128)} %get-tuple-element.17), channel_id=1, source_target_pairs={{0,16},{16,32},{32,48},{48,0},{1,17},{17,33},{33,49},{49,1},{2,18}... | collective-permute-start | bytes 491528 | tf_op jit(solution)/shard_map/ppermute | solution.py:396
  120.5 7.3 %collective-permute-start.8 = (f32[64,640]{1,0:T(8,128)}, f32[64,640]{1,0:T(8,128)S(1)}, u32[]{:S(2)}, u32[]{:S(2)}) collective-permute-start(f32[64,640]{1,0:T(8,128)} %get-tuple-element.15), channel_id=1, source_target_pairs={{0,48},{16,0},{32,16},{48,32},{1,49},{17,1},{33,17},{49,33},{2,50}... | collective-permute-start | bytes 491528 | tf_op jit(solution)/shard_map/ppermute | solution.py:396
  125.1 8.1 %collective-permute-start.9 = (f32[64,640]{1,0:T(8,128)}, f32[64,640]{1,0:T(8,128)S(1)}, u32[]{:S(2)}, u32[]{:S(2)}) collective-permute-start(f32[64,640]{1,0:T(8,128)} %get-tuple-element.16), channel_id=1, source_target_pairs={{0,32},{16,48},{32,0},{48,16},{1,33},{17,49},{33,1},{49,17},{2,34}... | collective-permute-start | bytes 491528 | tf_op jit(solution)/shard_map/ppermute | solution.py:396
  145.8 14.2 %all-to-all-start.3 = ((f32[4,72,640]{2,1,0:T(8,128)}), f32[4,72,640]{2,1,0:T(8,128)S(1)}, u32[]{:S(2)}, u32[]{:S(2)}) async-start(f32[4,72,640]{2,1,0:T(8,128)} %shard_map.83.refs_4_), calls=%async_computation.3 | async-start | bytes 1474560 | tf_op jit(solution)/shard_map/all_to_all | solution.py:401
  149.5 10.5 %copy-start.15 = (f32[64,640]{1,0:T(8,128)S(1)}, f32[64,640]{1,0:T(8,128)}, u32[]{:S(2)}) copy-start(f32[64,640]{1,0:T(8,128)} %get-tuple-element.18.refs_1_) | copy-start | bytes 491524
  162.8 13.7 %all-to-all-start.4 = ((f32[8,8,128]{2,1,0:T(8,128)}), f32[8,8,128]{2,1,0:T(8,128)S(1)}, u32[]{:S(2)}, u32[]{:S(2)}) async-start(f32[8,8,128]{2,1,0:T(8,128)} %get-tuple-element.19.refs_2_), calls=%async_computation.4 | async-start | bytes 65536 | tf_op jit(solution)/shard_map/all_to_all | solution.py:401
  (10 other events, 24.6 us)

commit v12 on v11

--- a/solution.py
+++ b/solution.py
@@ -339,16 +339,16 @@
 
 
 def mix_body(args, lazy, results, scratch, need, send):
-    (recv_ref, gain_ref, readout_ref, attended_ref), (mixed_ref,) = args, results
+    (recv_ref, gain_ref, readout_ref, *attended_refs), (mixed_ref,) = args, results
     total = recv_ref[0, 0:1, :]
     for n in range(1, NARROW):
         total = total + recv_ref[n, 0:1, :]
     scale = to_column(1.0 / jnp.sqrt(total / (D * NARROW) + EPSILON))
     for c in range(GROUPS):
-        mixed_ref[c] = attended_ref[c] + gain_ref[...] * (readout_ref[c] * scale[c * TOK : (c + 1) * TOK])
-
-
-def attention_body(args, lazy, results, scratch, need, send):
+        mixed_ref[c] = attended_refs[c][...] + gain_ref[...] * (readout_ref[c] * scale[c * TOK : (c + 1) * TOK])
+
+
+def attention_body(c, args, lazy, results, scratch, need, send):
     (position_ref,), (qkv_ref, near_ref, far_ref), (out_ref,) = args, lazy, results
     position = position_ref[0]
     row = lax.broadcasted_iota(jnp.int32, (TOK, 3 * TOK), 0) + 2 * TOK
@@ -356,23 +356,22 @@
     window = (row - col >= 0) & (row - col < WINDOW)
     first = jnp.where(position >= 2, 0, jnp.where(position >= 1, TOK, 2 * TOK))
     need()
-    for c in range(GROUPS):
-        allowed = window & (col >= first) if c == 0 else window
-        for h in range(D // ATT):
-            at = slice(h * ATT, (h + 1) * ATT)
-            parts = []
-            for a in range(2):
-                far, near = far_ref[a, c, :, at], near_ref[a, c, :, at]
-                if c == 1:
-                    far = jnp.where(position >= 2, far, far_ref[a, 0, :, at])
-                    near = jnp.where(position >= 1, near, near_ref[a, 0, :, at])
-                parts.append(jnp.concatenate([far, near, qkv_ref[1 + a, c, :, at]], axis=0))
-            keys, values = parts
-            scores = dot(qkv_ref[0, c, :, at], keys, ((1,), (1,))) * (1.0 / math.sqrt(ATT))
-            scores = jnp.where(allowed, scores, -1e30)
-            weights = jnp.exp(scores - jnp.max(scores, axis=1, keepdims=True))
-            weights = weights / jnp.sum(weights, axis=1, keepdims=True)
-            out_ref[c, :, at] = dot(weights, values)
+    allowed = window & (col >= first) if c == 0 else window
+    for h in range(D // ATT):
+        at = slice(h * ATT, (h + 1) * ATT)
+        parts = []
+        for a in range(2):
+            far, near = far_ref[a, c, :, at], near_ref[a, c, :, at]
+            if c == 1:
+                far = jnp.where(position >= 2, far, far_ref[a, 0, :, at])
+                near = jnp.where(position >= 1, near, near_ref[a, 0, :, at])
+            parts.append(jnp.concatenate([far, near, qkv_ref[1 + a, c, :, at]], axis=0))
+        keys, values = parts
+        scores = dot(qkv_ref[0, c, :, at], keys, ((1,), (1,))) * (1.0 / math.sqrt(ATT))
+        scores = jnp.where(allowed, scores, -1e30)
+        weights = jnp.exp(scores - jnp.max(scores, axis=1, keepdims=True))
+        weights = weights / jnp.sum(weights, axis=1, keepdims=True)
+        out_ref[:, at] = dot(weights, values)
 
 
 def behind(block, distance):
@@ -435,24 +434,28 @@
         smem=(0,), fan=(0,), after=(marker,), room=ROOM,
     )
     recv3 = exchange(send3, ("z", "yh")).reshape(BLOCKS * 24, LANES)
-    first = back_to_neighbours(
-        call(
-            first_read_body, [(TOK, D)] * NX, 4, lazy=[*((q, (0, TOK)) for q in queries), (weights, None)],
-            after=(send3,),
-        )
+    send_first = call(
+        first_read_body, [(TOK, D)] * NX, 4, lazy=[*((q, (0, TOK)) for q in queries), (weights, None)],
+        after=(send3,),
+    )
+    first = back_to_neighbours(send_first)
+    (attended0,) = call(
+        functools.partial(attention_body, 0), [(TOK, D)], 1, position, lazy=whole(qkv, near, far), smem=(0,),
+        after=(send_first[0],),
     )
     (send_second,) = call(
         second_read_body, [(NX, TOK + 8, D)], 5, x, recv3,
         lazy=[*((q, (TOK, TOK)) for q in queries), (weights, None), (send3, (0, 1))], scratch=[(3 * D, LANES)],
-        smem=(0,), after=first[1:], room=ROOM,
+        smem=(0,), after=(attended0, *first[1:]), room=ROOM,
     )
     second = exchange(send_second, "x")
-    (attended,) = call(
-        attention_body, [(GROUPS, TOK, D)], 8, position, lazy=whole(qkv, near, far), smem=(0,), after=(send_second,)
+    (attended1,) = call(
+        functools.partial(attention_body, 1), [(TOK, D)], 5, position, lazy=whole(qkv, near, far), smem=(0,),
+        after=(send_second,),
     )
     readout, send5 = call(
         squares_body, [(GROUPS, TOK, D), (NARROW, 8, GROUPS * TOK)], 1, second, lazy=whole(*first), fan=(1,),
-        after=(attended,), room=SMALL,
+        after=(attended1,), room=SMALL,
     )
     recv5 = exchange(send5, "narrow")
     new_weights, new_moment = call(
@@ -460,7 +463,7 @@
         after=(send5,), room=SMALL,
     )
     (mixed,) = call(
-        mix_body, [(GROUPS, TOK, D)], 1, recv5, ttt_gain.reshape(1, D), readout, attended, after=(new_weights,),
+        mix_body, [(GROUPS, TOK, D)], 1, recv5, ttt_gain.reshape(1, D), readout, attended0, attended1, after=(new_weights,),
         room=SMALL,
     )
     return mixed, new_weights.reshape(1, ROWS, 3, H), new_moment.reshape(1, ROWS, 3, H)

time: 180 us -> 180 us (level)
  Pallas kernels: 32.6 us -> 34.8 us
    ppermute x3, waiting for transfers between devices: 5.44 us -> 0.01 us  [back_to_neighbours(): lax.ppermute(blocks[s], 'x', [(i, (i - s) % NX) for i in range(NX)])]
    all_to_all x5, waiting for transfers between devices: 12.2 us -> 16.1 us  [exchange(): return lax.all_to_all(pieces, axes, split_axis=0, concat_axis=0, tiled=True)]
    pallas_call x12 -> x13, Pallas kernels: 32.6 us -> 34.8 us  [call(): pl.pallas_call(kernel, out_shape=[jax.ShapeDtypeStruct(s, jnp.float32) fo...]
    unnamed x36 -> x38, local copies, waits for them, and re-layouts: 4.01 us -> 4.2 us
  transfers between devices with their start and end apart: 16 -> 16, of which waited for: 8 -> 6; matrix products, arithmetic and copies ran while one was open for 1% -> 1% of each run, Pallas kernels for 12% -> 14%
where the time goes in v12:
time: 180 us; the launch traced here: 179 us
  starting transfers between devices  89 us (49%)
  waiting for transfers between devices  48.9 us (27%)
  Pallas kernels  34.8 us (19%)
  local copies, waits for them, and re-layouts  5.1 us (3%)
    all_to_all x5, starting transfers between devices, exchange(): return lax.all_to_all(pieces, axes, split_axis=0, concat_axis=0, tiled=True)  50.4 us
    pallas_call x13, Pallas kernels, call(): pl.pallas_call(kernel, out_shape=[jax.ShapeDtypeStruct(s, jnp.float32) fo...  34.8 us
    ppermute x3, waiting for transfers between devices, from_neighbours(): lax.ppermute(block, 'x', [((i - s) % NX, i) for i in range(NX)])  17.4 us
    all_to_all x5, waiting for transfers between devices, exchange(): return lax.all_to_all(pieces, axes, split_axis=0, concat_axis=0, tiled=True)  16.1 us
    ppermute x3, starting transfers between devices, from_neighbours(): lax.ppermute(block, 'x', [((i - s) % NX, i) for i in range(NX)])  10.5 us
    ppermute x1, waiting for transfers between devices, relayed_from_neighbours(): ahead_one = lax.ppermute(block, 'x', from_ahead)  9.86 us
    ppermute x2, starting transfers between devices, behind(): lax.ppermute(block, axes, [((i - distance) % BLOCKS, i) for i in range(BL...  9.19 us
    ppermute x3, starting transfers between devices, back_to_neighbours(): lax.ppermute(blocks[s], 'x', [(i, (i - s) % NX) for i in range(NX)])  8.41 us
  transfers between devices with their start and end apart: 16, of which 6 were waited for; matrix products, arithmetic and copies ran while one was open for 1% of the time, Pallas kernels for 14%

profile of v12, /device:TPU:1, one launch (start us, length us, event | category | flops | bytes accessed | tf_op | source)
XLA Modules:
  0.0 179.0 jit_solution(12032278391885436870)
XLA Ops:
  2.5 19.7 %all-to-all-start = ((f32[64,24,128]{2,1,0:T(8,128)}), f32[64,24,128]{2,1,0:T(8,128)S(1)}, u32[]{:S(2)}, u32[]{:S(2)}) async-start(f32[64,24,128]{2,1,0:T(8,128)} %shard_map.76), calls=%async_computation | async-start | bytes 1572864 | tf_op jit(solution)/shard_map/all_to_all | solution.py:400
  22.5 4.1 %collective-permute-start.1 = (f32[128,640]{1,0:T(8,128)S(1)}, f32[128,640]{1,0:T(8,128)S(1)}, u32[]{:S(2)}, u32[]{:S(2)}) collective-permute-start(f32[128,640]{1,0:T(8,128)S(1)} %shard_map.77.refs_1_), channel_id=1, source_target_pairs={{16,0},{32,16},{48,32},{0,48},{17,1},{33,17},{49,33},{1,49},{18,2}... | collective-permute-start | bytes 983048 | tf_op jit(solution)/shard_map/ppermute | solution.py:389
  28.6 9.9 %collective-permute-done.1.refs_4_ = f32[128,640]{1,0:T(8,128)S(1)} collective-permute-done((f32[128,640]{1,0:T(8,128)S(1)}, f32[128,640]{1,0:T(8,128)S(1)}, u32[]{:S(2)}, u32[]{:S(2)}) %collective-permute-start.1) | collective-permute-done | bytes 327712 | tf_op jit(solution)/shard_map/ppermute | solution.py:389
  38.4 4.5 %collective-permute-start.2 = (f32[128,640]{1,0:T(8,128)S(1)}, f32[128,640]{1,0:T(8,128)S(1)}, u32[]{:S(2)}, u32[]{:S(2)}) collective-permute-start(f32[128,640]{1,0:T(8,128)S(1)} %collective-permute-done.1.refs_4_), channel_id=1, source_target_pairs={{16,0},{32,16},{48,32},{0,48},{17,1},{33,17},{49,33},{1,49},{18,2}... | collective-permute-start | bytes 983048 | tf_op jit(solution)/shard_map/ppermute | solution.py:390
  43.8 7.3 %collective-permute-start.6 = (f32[2,2,64,640]{3,2,1,0:T(8,128)}, f32[2,2,64,640]{3,2,1,0:T(8,128)}, u32[]{:S(2)}, u32[]{:S(2)}) collective-permute-start(f32[2,2,64,640]{3,2,1,0:T(8,128)} %slice.4), channel_id=1, source_target_pairs={{504,0},{0,8},{8,16},{16,24},{24,32},{32,40},{40,48},{48,56},{56,6... | collective-permute-start | bytes 1966088 | tf_op jit(solution)/shard_map/ppermute | solution.py:379
  51.1 1.9 %collective-permute-start.7 = (f32[2,2,64,640]{3,2,1,0:T(8,128)}, f32[2,2,64,640]{3,2,1,0:T(8,128)}, u32[]{:S(2)}, u32[]{:S(2)}) collective-permute-start(f32[2,2,64,640]{3,2,1,0:T(8,128)} %slice.4), channel_id=1, source_target_pairs={{496,0},{504,8},{0,16},{8,24},{16,32},{24,40},{32,48},{40,56},{48,... | collective-permute-start | bytes 1966088 | tf_op jit(solution)/shard_map/ppermute | solution.py:379
  53.0 4.3 %shard_map.78 = (f32[1920,128]{1,0:T(8,128)}, f32[1536,128]{1,0:T(8,128)}) custom-call(f32[1536,128]{1,0:T(8,128)S(1)} %bitcast.10, f32[128,640]{1,0:T(8,128)S(1)} %shard_map.77.refs_1_, f32[128,640]{1,0:T(8,128)S(1)} %collective-permute-done.refs_2_, f32[128,640]{1,0:T(8,128)S(1)} %collective-permute-done.2.refs_3_, ...), custom_call_target="tpu_custom_call" | custom-call | flops 5000000000 | bytes 1000000 | tf_op jit(solution)/shard_map/pallas_call | solution.py:106
  57.3 8.3 %all-to-all-start.1 = ((f32[16,96,128]{2,1,0:T(8,128)}), f32[16,96,128]{2,1,0:T(8,128)S(1)}, u32[]{:S(2)}, u32[]{:S(2)}) async-start(f32[16,96,128]{2,1,0:T(8,128)} %bitcast.3), calls=%async_computation.1 | async-start | bytes 1572864 | tf_op jit(solution)/shard_map/all_to_all | solution.py:400
  65.7 2.6 %shard_map.79.refs_2_.refs_0_ = f32[160,640]{1,0:T(8,128)} custom-call(f32[30,1,384]{2,1,0:T(1,128)} %bitcast.14, f32[3,2,64,640]{3,2,1,0:T(8,128)} %refs_1_.7, f32[1920,128]{1,0:T(8,128)} %get-tuple-element.14.refs_2_.refs_4_.refs_6_), custom_call_target="tpu_custom_call" | custom-call | flops 100000000 | bytes 1000000 | tf_op jit(solution)/shard_map/pallas_call | solution.py:106
  68.2 2.1 %collective-permute-start.3 = (f32[160,640]{1,0:T(8,128)}, f32[160,640]{1,0:T(8,128)S(1)}, u32[]{:S(2)}, u32[]{:S(2)}) collective-permute-start(f32[160,640]{1,0:T(8,128)} %shard_map.79.refs_2_.refs_0_), channel_id=1, source_target_pairs={{48,0},{0,16},{16,32},{32,48},{49,1},{1,17},{17,33},{33,49},{50,2}... | collective-permute-start | bytes 1228808 | tf_op jit(solution)/shard_map/ppermute | solution.py:383
  70.3 6.5 %collective-permute-start.4 = (f32[160,640]{1,0:T(8,128)}, f32[160,640]{1,0:T(8,128)S(1)}, u32[]{:S(2)}, u32[]{:S(2)}) collective-permute-start(f32[160,640]{1,0:T(8,128)} %shard_map.79.refs_2_.refs_0_), channel_id=1, source_target_pairs={{32,0},{48,16},{0,32},{16,48},{33,1},{49,17},{1,33},{17,49},{34,2}... | collective-permute-start | bytes 1228808 | tf_op jit(solution)/shard_map/ppermute | solution.py:383
  78.7 5.5 %collective-permute-done.6.refs_0_.refs_2_ = f32[2,2,64,640]{3,2,1,0:T(8,128)} collective-permute-done((f32[2,2,64,640]{3,2,1,0:T(8,128)}, f32[2,2,64,640]{3,2,1,0:T(8,128)}, u32[]{:S(2)}, u32[]{:S(2)}) %collective-permute-start.6) | collective-permute-done | bytes 655392 | tf_op jit(solution)/shard_map/ppermute | solution.py:379
  84.9 17.4 %collective-permute-done.3.refs_3_.refs_1_ = f32[160,640]{1,0:T(8,128)S(1)} collective-permute-done((f32[160,640]{1,0:T(8,128)}, f32[160,640]{1,0:T(8,128)S(1)}, u32[]{:S(2)}, u32[]{:S(2)}) %collective-permute-start.3) | collective-permute-done | bytes 409632 | tf_op jit(solution)/shard_map/ppermute | solution.py:383
  104.6 10.1 %all-to-all-start.2 = ((f32[16,96,128]{2,1,0:T(8,128)}), f32[16,96,128]{2,1,0:T(8,128)S(1)}, u32[]{:S(2)}, u32[]{:S(2)}) async-start(f32[16,96,128]{2,1,0:T(8,128)} %shard_map.81.refs_5_.refs_7_), calls=%async_computation.2 | async-start | bytes 1572864 | tf_op jit(solution)/shard_map/all_to_all | solution.py:400
  114.7 3.7 %shard_map.82 = (f32[64,640]{1,0:T(8,128)}, f32[64,640]{1,0:T(8,128)}, f32[64,640]{1,0:T(8,128)}, f32[64,640]{1,0:T(8,128)}) custom-call(f32[160,640]{1,0:T(8,128)} %shard_map.79.refs_2_.refs_0_, f32[160,640]{1,0:T(8,128)} %copy-done.3, f32[160,640]{1,0:T(8,128)} %copy-done.5, f32[160,640]{1,0:T(8,128)} %copy-done.7, ...), custom_call_target="tpu_custom_call" | custom-call | flops 4000000000 | bytes 1000000 | tf_op jit(solution)/shard_map/pallas_call | solution.py:106
  120.4 4.6 %collective-permute-start.8 = (f32[64,640]{1,0:T(8,128)}, f32[64,640]{1,0:T(8,128)S(1)}, u32[]{:S(2)}, u32[]{:S(2)}) collective-permute-start(f32[64,640]{1,0:T(8,128)} %get-tuple-element.16), channel_id=1, source_target_pairs={{0,48},{16,0},{32,16},{48,32},{1,49},{17,1},{33,17},{49,33},{2,50}... | collective-permute-start | bytes 491528 | tf_op jit(solution)/shard_map/ppermute | solution.py:395
  126.9 6.1 %shard_map.83.refs_8_.refs_3_ = f32[64,640]{1,0:T(8,128)} custom-call(s32[1]{0:T(128)} %bitcast.6.refs_0_, f32[3,2,64,640]{3,2,1,0:T(8,128)} %refs_1_.7, f32[2,2,64,640]{3,2,1,0:T(8,128)} %collective-permute-done.6.refs_0_.refs_2_, f32[2,2,64,640]{3,2,1,0:T(8,128)} %collective-permute-done.7.refs_1_.refs_3_, f32[64,640]{1,0:T(8,128)} %get-tuple-element.15.refs_4_.refs_1_), custom_call_target="tpu_custom_call" | custom-call | flops 1000000000 | bytes 1000000 | tf_op jit(solution)/shard_map/pallas_call | solution.py:106
  133.1 7.4 %all-to-all-done.2 = f32[16,96,128]{2,1,0:T(8,128)S(1)} async-done(((f32[16,96,128]{2,1,0:T(8,128)}), f32[16,96,128]{2,1,0:T(8,128)S(1)}, u32[]{:S(2)}, u32[]{:S(2)}) %all-to-all-start.2) | async-done | bytes 786464 | tf_op jit(solution)/shard_map/all_to_all | solution.py:400
  141.4 5.2 %shard_map.84.refs_4_ = f32[4,72,640]{2,1,0:T(8,128)} custom-call(s32[1]{0:T(128)} %bitcast.refs_0_, f32[1536,128]{1,0:T(8,128)S(1)} %bitcast.9, f32[160,640]{1,0:T(8,128)S(1)} %copy-done.2, f32[160,640]{1,0:T(8,128)S(1)} %copy-done.4, f32[160,640]{1,0:T(8,128)S(1)} %copy-done.6, f32[160,640]{1,0:T(8,128)S(1)} %copy-done.8, ...), custom_call_target="tpu_custom_call" | custom-call | flops 5000000000 | bytes 1000000 | tf_op jit(solution)/shard_map/pallas_call | solution.py:106
  146.6 3.5 %all-to-all-start.3 = ((f32[4,72,640]{2,1,0:T(8,128)}), f32[4,72,640]{2,1,0:T(8,128)S(1)}, u32[]{:S(2)}, u32[]{:S(2)}) async-start(f32[4,72,640]{2,1,0:T(8,128)} %shard_map.84.refs_4_), calls=%async_computation.3 | async-start | bytes 1474560 | tf_op jit(solution)/shard_map/all_to_all | solution.py:400
  150.2 6.0 %shard_map.85.refs_5_.refs_4_ = f32[64,640]{1,0:T(8,128)} custom-call(s32[1]{0:T(128)} %bitcast.6.refs_0_, f32[3,2,64,640]{3,2,1,0:T(8,128)} %refs_1_.7, f32[2,2,64,640]{3,2,1,0:T(8,128)} %collective-permute-done.6.refs_0_.refs_2_, f32[2,2,64,640]{3,2,1,0:T(8,128)} %collective-permute-done.7.refs_1_.refs_3_, f32[4,72,640]{2,1,0:T(8,128)} %shard_map.84.refs_4_), custom_call_target="tpu_custom_call" | custom-call | flops 5000000000 | bytes 1000000 | tf_op jit(solution)/shard_map/pallas_call | solution.py:106
  156.2 4.6 %all-to-all-done.3.refs_0_ = f32[4,72,640]{2,1,0:T(8,128)S(1)} async-done(((f32[4,72,640]{2,1,0:T(8,128)}), f32[4,72,640]{2,1,0:T(8,128)S(1)}, u32[]{:S(2)}, u32[]{:S(2)}) %all-to-all-start.3) | async-done | bytes 737312 | tf_op jit(solution)/shard_map/all_to_all | solution.py:400
  163.6 8.7 %all-to-all-start.4 = ((f32[8,8,128]{2,1,0:T(8,128)}), f32[8,8,128]{2,1,0:T(8,128)S(1)}, u32[]{:S(2)}, u32[]{:S(2)}) async-start(f32[8,8,128]{2,1,0:T(8,128)} %get-tuple-element.19.refs_2_), calls=%async_computation.4 | async-start | bytes 65536 | tf_op jit(solution)/shard_map/all_to_all | solution.py:400
  173.1 4.2 %all-to-all-done.4.refs_0_ = f32[8,8,128]{2,1,0:T(8,128)S(1)} async-done(((f32[8,8,128]{2,1,0:T(8,128)}), f32[8,8,128]{2,1,0:T(8,128)S(1)}, u32[]{:S(2)}, u32[]{:S(2)}) %all-to-all-start.4) | async-done | bytes 32800 | tf_op jit(solution)/shard_map/all_to_all | solution.py:400
  (61 shorter events, 19.7 us)
Async XLA Ops:
  2.5 19.8 %copy-start = (f32[3,2,64,640]{3,2,1,0:T(8,128)S(1)}, f32[3,2,64,640]{3,2,1,0:T(8,128)}, u32[]{:S(2)}) copy-start(f32[3,2,64,640]{3,2,1,0:T(8,128)} %refs_1_.7) | copy-start | bytes 2949124
  2.5 19.8 %copy-start.11 = (f32[1,64]{1,0:T(1,128)S(1)}, f32[1,64]{1,0:T(1,128)}, u32[]{:S(2)}) copy-start(f32[1,64]{1,0:T(1,128)} %refs_0_.1) | copy-start | bytes 772
  2.5 50.5 %all-to-all-start = ((f32[64,24,128]{2,1,0:T(8,128)}), f32[64,24,128]{2,1,0:T(8,128)S(1)}, u32[]{:S(2)}, u32[]{:S(2)}) async-start(f32[64,24,128]{2,1,0:T(8,128)} %shard_map.76), calls=%async_computation | async-start | bytes 1572864 | tf_op jit(solution)/shard_map/all_to_all | solution.py:400
  22.5 15.9 %collective-permute-start.1 = (f32[128,640]{1,0:T(8,128)S(1)}, f32[128,640]{1,0:T(8,128)S(1)}, u32[]{:S(2)}, u32[]{:S(2)}) collective-permute-start(f32[128,640]{1,0:T(8,128)S(1)} %shard_map.77.refs_1_), channel_id=1, source_target_pairs={{16,0},{32,16},{48,32},{0,48},{17,1},{33,17},{49,33},{1,49},{18,2}... | collective-permute-start | bytes 983048 | tf_op jit(solution)/shard_map/ppermute | solution.py:389
  26.6 26.4 %collective-permute-start = (f32[128,640]{1,0:T(8,128)S(1)}, f32[128,640]{1,0:T(8,128)S(1)}, u32[]{:S(2)}, u32[]{:S(2)}) collective-permute-start(f32[128,640]{1,0:T(8,128)S(1)} %shard_map.77.refs_1_), channel_id=1, source_target_pairs={{48,0},{0,16},{16,32},{32,48},{49,1},{1,17},{17,33},{33,49},{50,2}... | collective-permute-start | bytes 983048 | tf_op jit(solution)/shard_map/ppermute | solution.py:387
  38.4 14.6 %collective-permute-start.2 = (f32[128,640]{1,0:T(8,128)S(1)}, f32[128,640]{1,0:T(8,128)S(1)}, u32[]{:S(2)}, u32[]{:S(2)}) collective-permute-start(f32[128,640]{1,0:T(8,128)S(1)} %collective-permute-done.1.refs_4_), channel_id=1, source_target_pairs={{16,0},{32,16},{48,32},{0,48},{17,1},{33,17},{49,33},{1,49},{18,2}... | collective-permute-start | bytes 983048 | tf_op jit(solution)/shard_map/ppermute | solution.py:390
  43.8 40.5 %collective-permute-start.6 = (f32[2,2,64,640]{3,2,1,0:T(8,128)}, f32[2,2,64,640]{3,2,1,0:T(8,128)}, u32[]{:S(2)}, u32[]{:S(2)}) collective-permute-start(f32[2,2,64,640]{3,2,1,0:T(8,128)} %slice.4), channel_id=1, source_target_pairs={{504,0},{0,8},{8,16},{16,24},{24,32},{32,40},{40,48},{48,56},{56,6... | collective-permute-start | bytes 1966088 | tf_op jit(solution)/shard_map/ppermute | solution.py:379
  51.1 33.2 %collective-permute-start.7 = (f32[2,2,64,640]{3,2,1,0:T(8,128)}, f32[2,2,64,640]{3,2,1,0:T(8,128)}, u32[]{:S(2)}, u32[]{:S(2)}) collective-permute-start(f32[2,2,64,640]{3,2,1,0:T(8,128)} %slice.4), channel_id=1, source_target_pairs={{496,0},{504,8},{0,16},{8,24},{16,32},{24,40},{32,48},{40,56},{48,... | collective-permute-start | bytes 1966088 | tf_op jit(solution)/shard_map/ppermute | solution.py:379
  57.3 45.0 %all-to-all-start.1 = ((f32[16,96,128]{2,1,0:T(8,128)}), f32[16,96,128]{2,1,0:T(8,128)S(1)}, u32[]{:S(2)}, u32[]{:S(2)}) async-start(f32[16,96,128]{2,1,0:T(8,128)} %bitcast.3), calls=%async_computation.1 | async-start | bytes 1572864 | tf_op jit(solution)/shard_map/all_to_all | solution.py:400
  68.2 34.1 %copy-start.1 = (f32[160,640]{1,0:T(8,128)S(1)}, f32[160,640]{1,0:T(8,128)}, u32[]{:S(2)}) copy-start(f32[160,640]{1,0:T(8,128)} %shard_map.79.refs_2_.refs_0_) | copy-start | bytes 1228804
  68.2 34.0 %collective-permute-start.3 = (f32[160,640]{1,0:T(8,128)}, f32[160,640]{1,0:T(8,128)S(1)}, u32[]{:S(2)}, u32[]{:S(2)}) collective-permute-start(f32[160,640]{1,0:T(8,128)} %shard_map.79.refs_2_.refs_0_), channel_id=1, source_target_pairs={{48,0},{0,16},{16,32},{32,48},{49,1},{1,17},{17,33},{33,49},{50,2}... | collective-permute-start | bytes 1228808 | tf_op jit(solution)/shard_map/ppermute | solution.py:383
  70.3 32.0 %collective-permute-start.4 = (f32[160,640]{1,0:T(8,128)}, f32[160,640]{1,0:T(8,128)S(1)}, u32[]{:S(2)}, u32[]{:S(2)}) collective-permute-start(f32[160,640]{1,0:T(8,128)} %shard_map.79.refs_2_.refs_0_), channel_id=1, source_target_pairs={{32,0},{48,16},{0,32},{16,48},{33,1},{49,17},{1,33},{17,49},{34,2}... | collective-permute-start | bytes 1228808 | tf_op jit(solution)/shard_map/ppermute | solution.py:383
  76.8 25.5 %collective-permute-start.5 = (f32[160,640]{1,0:T(8,128)}, f32[160,640]{1,0:T(8,128)S(1)}, u32[]{:S(2)}, u32[]{:S(2)}) collective-permute-start(f32[160,640]{1,0:T(8,128)} %shard_map.79.refs_2_.refs_0_), channel_id=1, source_target_pairs={{16,0},{32,16},{48,32},{0,48},{17,1},{33,17},{49,33},{1,49},{18,2}... | collective-permute-start | bytes 1228808 | tf_op jit(solution)/shard_map/ppermute | solution.py:383
  104.6 35.8 %all-to-all-start.2 = ((f32[16,96,128]{2,1,0:T(8,128)}), f32[16,96,128]{2,1,0:T(8,128)S(1)}, u32[]{:S(2)}, u32[]{:S(2)}) async-start(f32[16,96,128]{2,1,0:T(8,128)} %shard_map.81.refs_5_.refs_7_), calls=%async_computation.2 | async-start | bytes 1572864 | tf_op jit(solution)/shard_map/all_to_all | solution.py:400
  118.5 14.6 %collective-permute-start.10 = (f32[64,640]{1,0:T(8,128)}, f32[64,640]{1,0:T(8,128)S(1)}, u32[]{:S(2)}, u32[]{:S(2)}) collective-permute-start(f32[64,640]{1,0:T(8,128)} %get-tuple-element.18), channel_id=1, source_target_pairs={{0,16},{16,32},{32,48},{48,0},{1,17},{17,33},{33,49},{49,1},{2,18}... | collective-permute-start | bytes 491528 | tf_op jit(solution)/shard_map/ppermute | solution.py:395
  120.4 12.7 %collective-permute-start.8 = (f32[64,640]{1,0:T(8,128)}, f32[64,640]{1,0:T(8,128)S(1)}, u32[]{:S(2)}, u32[]{:S(2)}) collective-permute-start(f32[64,640]{1,0:T(8,128)} %get-tuple-element.16), channel_id=1, source_target_pairs={{0,48},{16,0},{32,16},{48,32},{1,49},{17,1},{33,17},{49,33},{2,50}... | collective-permute-start | bytes 491528 | tf_op jit(solution)/shard_map/ppermute | solution.py:395
  125.0 8.1 %collective-permute-start.9 = (f32[64,640]{1,0:T(8,128)}, f32[64,640]{1,0:T(8,128)S(1)}, u32[]{:S(2)}, u32[]{:S(2)}) collective-permute-start(f32[64,640]{1,0:T(8,128)} %get-tuple-element.17), channel_id=1, source_target_pairs={{0,32},{16,48},{32,0},{48,16},{1,33},{17,49},{33,1},{49,17},{2,34}... | collective-permute-start | bytes 491528 | tf_op jit(solution)/shard_map/ppermute | solution.py:395
  126.9 13.5 %copy-start.2 = (f32[160,640]{1,0:T(8,128)S(1)}, f32[160,640]{1,0:T(8,128)}, u32[]{:S(2)}) copy-start(f32[160,640]{1,0:T(8,128)} %shard_map.79.refs_2_.refs_0_) | copy-start | bytes 1228804
  126.9 13.5 %copy-start.4 = (f32[160,640]{1,0:T(8,128)S(1)}, f32[160,640]{1,0:T(8,128)}, u32[]{:S(2)}) copy-start(f32[160,640]{1,0:T(8,128)} %copy-done.3) | copy-start | bytes 1228804
  126.9 13.5 %copy-start.6 = (f32[160,640]{1,0:T(8,128)S(1)}, f32[160,640]{1,0:T(8,128)}, u32[]{:S(2)}) copy-start(f32[160,640]{1,0:T(8,128)} %copy-done.5) | copy-start | bytes 1228804
  126.9 13.5 %copy-start.8 = (f32[160,640]{1,0:T(8,128)S(1)}, f32[160,640]{1,0:T(8,128)}, u32[]{:S(2)}) copy-start(f32[160,640]{1,0:T(8,128)} %copy-done.7) | copy-start | bytes 1228804
  146.6 14.2 %all-to-all-start.3 = ((f32[4,72,640]{2,1,0:T(8,128)}), f32[4,72,640]{2,1,0:T(8,128)S(1)}, u32[]{:S(2)}, u32[]{:S(2)}) async-start(f32[4,72,640]{2,1,0:T(8,128)} %shard_map.84.refs_4_), calls=%async_computation.3 | async-start | bytes 1474560 | tf_op jit(solution)/shard_map/all_to_all | solution.py:400
  150.2 10.7 %copy-start.13 = (f32[64,640]{1,0:T(8,128)S(1)}, f32[64,640]{1,0:T(8,128)}, u32[]{:S(2)}) copy-start(f32[64,640]{1,0:T(8,128)} %get-tuple-element.15.refs_4_.refs_1_) | copy-start | bytes 491524
  163.6 13.7 %all-to-all-start.4 = ((f32[8,8,128]{2,1,0:T(8,128)}), f32[8,8,128]{2,1,0:T(8,128)S(1)}, u32[]{:S(2)}, u32[]{:S(2)}) async-start(f32[8,8,128]{2,1,0:T(8,128)} %get-tuple-element.19.refs_2_), calls=%async_computation.4 | async-start | bytes 65536 | tf_op jit(solution)/shard_map/all_to_all | solution.py:400
  (11 other events, 28.3 us)
